TPU v7x, 32 devices: a whole 2x2x4 slice. The times are simulated.
32 devices in a mesh: groups: 2 (over x), ctx: 8 (over z, y), exp: 2 (over core).
Axes of the slice: x: 2, y: 2, z: 4, core: 2. Of those that a mesh axis runs over, the one named last changes fastest.
Arguments:
- tokens: bfloat16 [4096, 2048], P(('groups', 'ctx', 'exp')), parts along dimension 0, may hold values from -6 to 152
- norm_gain: float32 [2048], replicated, may hold values from 0.1 to 1.9
- router_weight: float32 [2048, 8], replicated, may hold values from -0.125 to 5.1
- routes: int32 [4096, 2], P(('groups', 'ctx', 'exp')), parts along dimension 0, may hold values from 0 to 7, all different within a row; in each aligned block of 128 rows (0 to 127, 128 to 255, ...) at most 40 rows name the same one
- key_weight: bfloat16 [2048, 1024], replicated, may hold values from -0.125 to 0.125
- value_weight: bfloat16 [2048, 1024], replicated, may hold values from -0.125 to 0.125
- query_weight: bfloat16 [8, 2048, 1024], P('ctx'), may hold values from -0.125 to 0.125
- output_weight: bfloat16 [8, 1024, 2048], P('ctx'), may hold values from -3 to 3
Outputs:
- attention_out: bfloat16 [4096, 2048], P(('groups', 'ctx', 'exp')), parts along dimension 0
There are 2 independent parts, one for each index of `groups`. A program takes and returns all parts, laid end to end along the dimension named above; an argument that names none is the same for every part. Nothing has to cross between parts.
Inputs may be any that keep to these rules, and one draw needn't show every extreme that they name: `routes`: each row names 2 different experts; among the 128 rows of one device no expert is named more than 40 times, a bound that some block reaches.
All inputs are finite; a program needn't handle non-finite values.
Results may differ from a plain program's by a relative error of at most 0.006.
The roundings to bfloat16 on the way count: a program that leaves them out, or rounds other values in their place, can miss the bound.
Values may be sent and summed in bfloat16 or wider, within the bound.
No kernel may reach another device: no remote copies, remote signals or barrier semaphores. Data moves between devices by JAX's collectives and lax.ppermute only.
A program may use at most 128 MiB of HBM per device.

v0:
```python
import math

import jax
import jax.numpy as jnp
from jax import lax
from jax.sharding import PartitionSpec as P

HS = 128
EXPERTS = 8
TOPK = 2
MOST = 40


def norm_rows(tokens, norm_gain):
    floats = tokens.astype(jnp.float32)
    factor = lax.rsqrt(jnp.mean(floats * floats, axis=1, keepdims=True) + 1e-06)
    return (floats * factor * norm_gain).astype(jnp.bfloat16)


def split_blocks(row_count):
    pieces = max(1, row_count // 512)
    while row_count % pieces != 0:
        pieces = pieces - 1
    return pieces


def attend_block(queries, positions, key_rows, value_rows, head_count, head_size):
    key_index = jnp.arange(key_rows.shape[0], dtype=jnp.int32)
    allowed = key_index[None, :] <= positions[:, None]
    outputs = []
    for head_id in range(head_count):
        start_col = head_id * head_size
        query_part = queries[:, start_col : start_col + head_size]
        key_part = key_rows[:, start_col : start_col + head_size]
        scores = lax.dot_general(
            query_part, key_part, (((1,), (1,)), ((), ())), preferred_element_type=jnp.float32
        )
        scores = jnp.where(allowed, scores * (1.0 / math.sqrt(head_size)), -1e30)
        peak_val = jnp.max(scores, axis=1, keepdims=True)
        raised = jnp.exp(scores - peak_val)
        weights = (raised / jnp.sum(raised, axis=1, keepdims=True)).astype(jnp.bfloat16)
        value_part = value_rows[:, start_col : start_col + head_size]
        outputs.append(
            jnp.dot(weights, value_part, preferred_element_type=jnp.float32).astype(jnp.bfloat16)
        )
    return jnp.concatenate(outputs, axis=1)


def serve_flat(rows, positions, query_slab, output_slab, key_panel, value_panel):
    head_width = query_slab.shape[1]
    row_count = rows.shape[0]
    queries = jnp.dot(rows, query_slab, preferred_element_type=jnp.float32).astype(jnp.bfloat16)
    block_total = split_blocks(row_count)

    def run_block(packed):
        return attend_block(packed[0], packed[1], key_panel, value_panel, head_width // HS, HS)

    attended = lax.map(
        run_block,
        (queries.reshape(block_total, -1, head_width), positions.reshape(block_total, -1)),
    )
    attended = attended.reshape(row_count, head_width)
    return jnp.dot(attended, output_slab, preferred_element_type=jnp.float32).astype(jnp.bfloat16)


def serve_grouped(rows, positions, query_slab, output_slab, key_panel, value_panel):
    outer = rows.shape[0]
    source_count = rows.shape[1]
    slot_width = rows.shape[2]
    model_width = rows.shape[3]
    group_count = 8
    per_group = source_count // group_count
    key_span = key_panel.shape[0] // group_count
    results = []
    for group_id in range(group_count):
        lo_src = group_id * per_group
        part_rows = rows[:, lo_src : lo_src + per_group].reshape(
            outer * per_group * slot_width, model_width
        )
        part_pos = positions[:, lo_src : lo_src + per_group].reshape(outer * per_group * slot_width)
        reach = (group_id + 1) * key_span
        served = serve_flat(
            part_rows, part_pos, query_slab, output_slab, key_panel[:reach], value_panel[:reach]
        )
        results.append(served.reshape(outer, per_group, slot_width, model_width))
    return jnp.concatenate(results, axis=1)


def per_device(
    tokens, norm_gain, router_weight, routes, key_weight, value_weight, query_weight, output_weight
):
    tok_count = tokens.shape[0]
    model_width = tokens.shape[1]
    ctx_count = lax.axis_size("ctx")
    exp_count = lax.axis_size("exp")
    quarter_count = ctx_count // EXPERTS
    head_width = query_weight.shape[2]
    normed = norm_rows(tokens, norm_gain)
    logits = jnp.dot(normed.astype(jnp.float32), router_weight, precision=lax.Precision.HIGHEST)
    gating = jax.nn.softmax(jnp.take_along_axis(logits, routes, axis=1), axis=1)
    key_rows = jnp.dot(normed, key_weight, preferred_element_type=jnp.float32).astype(jnp.bfloat16)
    value_rows = jnp.dot(normed, value_weight, preferred_element_type=jnp.float32).astype(
        jnp.bfloat16
    )
    stacked = jnp.stack([key_rows, value_rows], axis=0)
    gathered = lax.all_gather(stacked, "exp", axis=1, tiled=True)
    row_count = gathered.shape[1]
    split_up = gathered.reshape(2, row_count, quarter_count, head_width).transpose(2, 0, 1, 3)
    panels = lax.all_to_all(
        jnp.tile(split_up, (EXPERTS, 1, 1, 1)), "ctx", split_axis=0, concat_axis=2, tiled=True
    )[0]
    key_panel = panels[0]
    value_panel = panels[1]
    own_index = lax.axis_index("ctx") * exp_count + lax.axis_index("exp")
    pair_count = tok_count * TOPK
    slot_total = EXPERTS * MOST
    flat_expert = routes.reshape(pair_count)
    onehot = (flat_expert[:, None] == jnp.arange(EXPERTS, dtype=jnp.int32)[None, :]).astype(
        jnp.int32
    )
    slot_rank = jnp.sum((jnp.cumsum(onehot, axis=0) - 1) * onehot, axis=1)
    slot_index = flat_expert * MOST + slot_rank
    chosen_mask = slot_index[None, :] == jnp.arange(slot_total, dtype=jnp.int32)[:, None]
    pair_token = jnp.arange(pair_count, dtype=jnp.int32) // TOPK
    token_select = chosen_mask.reshape(slot_total, tok_count, TOPK).astype(jnp.bfloat16).sum(axis=2)
    buffer = jnp.dot(token_select, normed, preferred_element_type=jnp.float32).astype(jnp.bfloat16)
    slot_pos = jnp.max(
        jnp.where(chosen_mask, own_index * tok_count + pair_token[None, :], 0), axis=1
    )
    query_slab = query_weight[0]
    output_slab = output_weight[0]
    send_rows = jnp.repeat(buffer.reshape(EXPERTS, MOST, model_width), quarter_count, axis=0)
    send_pos = jnp.repeat(slot_pos.reshape(EXPERTS, MOST), quarter_count, axis=0)
    got_rows = lax.all_to_all(send_rows, "ctx", split_axis=0, concat_axis=0, tiled=True)
    got_pos = lax.all_to_all(send_pos, "ctx", split_axis=0, concat_axis=0, tiled=True)
    partial_value = serve_grouped(
        got_rows[None], got_pos[None], query_slab, output_slab, key_panel, value_panel
    )
    partials = partial_value[0]
    returned = lax.all_to_all(partials, "ctx", split_axis=0, concat_axis=0, tiled=True)
    summed = (
        returned.astype(jnp.float32).reshape(EXPERTS, quarter_count, MOST, model_width).sum(axis=1)
    )
    summed = summed.reshape(slot_total, model_width)
    gate_flat = gating.reshape(pair_count)
    combine_mat = (
        jnp.where(chosen_mask, gate_flat[None, :], 0.0)
        .reshape(slot_total, tok_count, TOPK)
        .sum(axis=2)
    )
    combined = lax.dot_general(
        combine_mat, summed, (((0,), (0,)), ((), ())), precision=lax.Precision.HIGHEST
    )
    return combined.astype(jnp.bfloat16)


def solution(mesh):
    in_specs = (
        P(("groups", "ctx", "exp"), None),
        P(),
        P(),
        P(("groups", "ctx", "exp"), None),
        P(),
        P(),
        P("ctx", None, None),
        P("ctx", None, None),
    )
    out_specs = P(("groups", "ctx", "exp"), None)
    return jax.shard_map(
        per_device, mesh=mesh, in_specs=in_specs, out_specs=out_specs, check_vma=False
    )
```

profile of v0, /device:TPU:0, one launch (start us, length us, event | category | flops | bytes accessed | tf_op | source)
XLA Modules:
  0.0 388.7 jit_solution(6817668088077099973)
XLA Ops:
  6.5 0.8 copy.40
  7.7 0.6 reduce-window.6
  8.8 0.7 all_to_all.23
  9.5 7.3 %all-to-all-start = ((s32[8,1,40]{2,1,0:T(1,128)}), s32[8,1,40]{2,1,0:T(1,128)S(1)}, u32[]{:S(2)}, u32[]{:S(2)}) async-start(s32[8,1,40]{2,1,0:T(1,128)} %all_to_all.23), calls=%async_computation | async-start | bytes 8192 | tf_op jit(solution)/shard_map/all_to_all | solution.py:135
  17.0 0.7 multiply_add_fusion.1
  17.7 1.2 fusion.258
  19.0 2.7 convolution_convert_fusion
  21.7 1.5 all-to-all-done
  23.2 4.5 %all-to-all-start.1 = ((bf16[8,40,2048]{2,1,0:T(8,128)(2,1)}), bf16[8,40,2048]{2,1,0:T(8,128)(2,1)S(1)}, u32[]{:S(2)}, u32[]{:S(2)}) async-start(bf16[8,40,2048]{2,1,0:T(8,128)(2,1)} %bitcast.5), calls=%async_computation.1 | async-start | bytes 2621440 | tf_op jit(solution)/shard_map/all_to_all | solution.py:134
  27.7 3.1 fusion.136
  31.2 0.8 fusion.137
  32.0 0.8 pad_maximum_fusion
  32.8 10.6 %all-gather.2.cloned.1.call-done = bf16[2,256,1024]{2,1,0:T(8,128)(2,1)} async-done(((bf16[2,128,1024]{2,1,0:T(8,128)(2,1)}), bf16[2,256,1024]{2,1,0:T(8,128)(2,1)}) %all-gather.2.cloned.1.call-update) | async-done | bytes 1048592 | tf_op jit(solution)/shard_map/all_gather | solution.py:106
  43.4 15.2 %all-to-all-done.1 = bf16[8,40,2048]{2,1,0:T(8,128)(2,1)S(1)} async-done(((bf16[8,40,2048]{2,1,0:T(8,128)(2,1)}), bf16[8,40,2048]{2,1,0:T(8,128)(2,1)S(1)}, u32[]{:S(2)}, u32[]{:S(2)}) %all-to-all-start.1) | async-done | bytes 1310752 | tf_op jit(solution)/shard_map/all_to_all | solution.py:134
  58.6 5.5 %tile.2 = bf16[8,2,256,1024]{3,2,1,0:T(8,128)(2,1)} broadcast(bf16[2,256,1024]{2,1,0:T(8,128)(2,1)} %all-gather.2.cloned.1.call-done), dimensions={1,2,3} | broadcast | bytes 9437184 | tf_op jit(solution)/shard_map/tile | solution.py:110
  64.1 5.0 %all-to-all-start.2 = ((bf16[8,2,256,1024]{3,2,1,0:T(8,128)(2,1)}), bf16[8,2,256,1024]{3,2,1,0:T(8,128)(2,1)}, u32[]{:S(2)}, u32[]{:S(2)}) async-start(bf16[8,2,256,1024]{3,2,1,0:T(8,128)(2,1)} %tile.2), calls=%async_computation.2 | async-start | bytes 16777216 | tf_op jit(solution)/shard_map/all_to_all | solution.py:109
  69.2 3.2 fusion.167
  72.6 0.8 fusion.164
  73.5 0.8 fusion.161
  74.3 0.8 fusion.158
  75.2 0.8 fusion.155
  76.0 0.8 fusion.152
  76.8 0.8 fusion.149
  77.7 0.8 fusion.146
  78.5 172.4 %all-to-all-done.2 = bf16[8,2,256,1024]{3,2,1,0:T(8,128)(2,1)} async-done(((bf16[8,2,256,1024]{3,2,1,0:T(8,128)(2,1)}), bf16[8,2,256,1024]{3,2,1,0:T(8,128)(2,1)}, u32[]{:S(2)}, u32[]{:S(2)}) %all-to-all-start.2) | async-done | bytes 8388640 | tf_op jit(solution)/shard_map/all_to_all | solution.py:109
  250.9 4.1 %fusion.658 = (bf16[1,1,8,256,1024]{4,3,1,2,0:T(8,128)(2,1)S(1)}, bf16[1,1,8,256,1024]{4,3,1,2,0:T(8,128)(2,1)S(1)}) fusion(bf16[1,2,8,256,1024]{4,3,1,2,0:T(8,128)(2,1)} %bitcast.12), kind=kLoop, calls=%fused_computation.899 | loop fusion | bytes 16777216 | tf_op jit(solution)/shard_map/slice | solution.py:112
  255.1 0.5 fusion.721
  255.6 0.5 fusion.722
  256.1 0.5 fusion.723
  256.7 0.5 fusion.724
  257.2 0.5 fusion.725
  257.7 0.5 fusion.726
  258.3 0.5 fusion.727
  258.8 0.5 fusion.728
  259.3 4.0 %fusion.659 = (bf16[1,1,7,256,1024]{4,3,1,2,0:T(8,128)(2,1)S(1)}, bf16[1,1,7,256,1024]{4,3,1,2,0:T(8,128)(2,1)S(1)}) fusion(bf16[1,2,8,256,1024]{4,3,1,2,0:T(8,128)(2,1)} %bitcast.12), kind=kLoop, calls=%fused_computation.900 | loop fusion | bytes 14680064 | tf_op jit(solution)/shard_map/slice | solution.py:83
  263.3 0.5 fusion.713
  263.9 0.5 fusion.714
  264.4 0.5 fusion.715
  264.9 0.5 fusion.716
  265.5 0.5 fusion.717
  266.0 0.5 fusion.718
  266.5 0.5 fusion.719
  267.1 0.5 fusion.720
  267.6 4.2 %fusion.660 = (bf16[1,1,6,256,1024]{4,3,1,2,0:T(8,128)(2,1)S(1)}, bf16[1,1,6,256,1024]{4,3,1,2,0:T(8,128)(2,1)S(1)}) fusion(bf16[1,2,8,256,1024]{4,3,1,2,0:T(8,128)(2,1)} %bitcast.12), kind=kLoop, calls=%fused_computation.901 | loop fusion | bytes 12582912 | tf_op jit(solution)/shard_map/slice | solution.py:83
  272.2 0.5 fusion.706
  275.4 3.2 fusion.661
  282.2 2.7 fusion.662
  287.6 0.6 fusion.696
  288.2 2.3 fusion.663
  293.4 1.7 fusion.664
  297.6 1.3 slice_bitcast_fusion.1
  332.5 1.5 fusion.133
  334.0 1.5 fusion.127
  335.5 1.5 fusion.121
  337.0 1.5 fusion.115
  338.5 1.5 fusion.109
  340.0 1.5 fusion.103
  341.5 1.5 fusion.97
  343.0 1.5 fusion.91
  344.5 3.6 all-to-all-start.3
  348.4 0.6 fusion.655
  349.0 1.4 gather_fusion
  350.7 28.9 %all-to-all-done.3 = bf16[8,40,2048]{2,1,0:T(8,128)(2,1)S(1)} async-done(((bf16[8,40,2048]{2,1,0:T(8,128)(2,1)}), bf16[8,40,2048]{2,1,0:T(8,128)(2,1)S(1)}, u32[]{:S(2)}, u32[]{:S(2)}) %all-to-all-start.3) | async-done | bytes 1310752 | tf_op jit(solution)/shard_map/all_to_all | solution.py:140
  379.6 1.8 convolution_convert_fusion.1
  (213 shorter events, 50.5 us)
Async XLA Ops:
  6.5 341.9 %copy-start = (f32[2048,8]{0,1:T(8,128)S(1)}, f32[2048,8]{0,1:T(8,128)}, u32[]{:S(2)}) copy-start(f32[2048,8]{0,1:T(8,128)} %param.10) | copy-start | bytes 196612
  6.5 21.2 %copy-start.3 = (bf16[128,2048]{1,0:T(8,128)(2,1)S(1)}, bf16[128,2048]{1,0:T(8,128)(2,1)}, u32[]{:S(2)}) copy-start(bf16[128,2048]{1,0:T(8,128)(2,1)} %param.8) | copy-start | bytes 1572868
  6.5 21.2 %copy-start.5 = (f32[2048]{0:T(1024)S(1)}, f32[2048]{0:T(1024)}, u32[]{:S(2)}) copy-start(f32[2048]{0:T(1024)} %param.9) | copy-start | bytes 24580
  9.5 13.7 %all-to-all-start = ((s32[8,1,40]{2,1,0:T(1,128)}), s32[8,1,40]{2,1,0:T(1,128)S(1)}, u32[]{:S(2)}, u32[]{:S(2)}) async-start(s32[8,1,40]{2,1,0:T(1,128)} %all_to_all.23), calls=%async_computation | async-start | bytes 8192 | tf_op jit(solution)/shard_map/all_to_all | solution.py:135
  23.2 35.4 %all-to-all-start.1 = ((bf16[8,40,2048]{2,1,0:T(8,128)(2,1)}), bf16[8,40,2048]{2,1,0:T(8,128)(2,1)S(1)}, u32[]{:S(2)}, u32[]{:S(2)}) async-start(bf16[8,40,2048]{2,1,0:T(8,128)(2,1)} %bitcast.5), calls=%async_computation.1 | async-start | bytes 2621440 | tf_op jit(solution)/shard_map/all_to_all | solution.py:134
  27.7 15.7 %all-gather.2.cloned.1.call-start = ((), (), s32[]{:S(2)}) async-start(), calls=%async_computation.4 | async-start | bytes 1572864 | tf_op jit(solution)/shard_map/all_gather | solution.py:106
  27.7 3.5 copy-start.4
  64.1 186.8 %all-to-all-start.2 = ((bf16[8,2,256,1024]{3,2,1,0:T(8,128)(2,1)}), bf16[8,2,256,1024]{3,2,1,0:T(8,128)(2,1)}, u32[]{:S(2)}, u32[]{:S(2)}) async-start(bf16[8,2,256,1024]{3,2,1,0:T(8,128)(2,1)} %tile.2), calls=%async_computation.2 | async-start | bytes 16777216 | tf_op jit(solution)/shard_map/all_to_all | solution.py:109
  69.2 3.5 copy-start.1
  326.4 6.1 %copy-start.2 = (bf16[1,1024,2048]{2,1,0:T(8,128)(2,1)S(1)}, bf16[1,1024,2048]{2,1,0:T(8,128)(2,1)}, u32[]{:S(2)}) copy-start(bf16[1,1024,2048]{2,1,0:T(8,128)(2,1)} %param.15) | copy-start | bytes 12582916
  343.0 5.1 %copy-start.6 = (s32[128,2]{0,1:T(2,128)S(1)}, s32[128,2]{0,1:T(2,128)}, u32[]{:S(2)}) copy-start(s32[128,2]{0,1:T(2,128)} %param.11) | copy-start | bytes 3076
  344.5 35.1 %all-to-all-start.3 = ((bf16[8,40,2048]{2,1,0:T(8,128)(2,1)}), bf16[8,40,2048]{2,1,0:T(8,128)(2,1)S(1)}, u32[]{:S(2)}, u32[]{:S(2)}) async-start(bf16[8,40,2048]{2,1,0:T(8,128)(2,1)} %bitcast.53), calls=%async_computation.3 | async-start | bytes 2621440 | tf_op jit(solution)/shard_map/all_to_all | solution.py:140
Sparse Core Ops, SparseCore 0:
  33.0 10.3 all-gather.1
where the time goes:
time: 396 us; the launch traced here: 389 us
  waiting for transfers between devices  229 us (58%)
  matrix products  74.1 us (19%)
  local copies, waits for them, and re-layouts  33.6 us (8%)
  starting transfers between devices  20.5 us (5%)
  other arithmetic  17.4 us (4%)
  between operations  14.5 us (4%)
    all_to_all x1, waiting for transfers between devices, per_device(): lax.all_to_all(jnp.tile(split_up, (EXPERTS, 1, 1, 1)), 'ctx', split_axis=...  172 us
    all_to_all x1, waiting for transfers between devices, per_device(): lax.all_to_all(partials, 'ctx', split_axis=0, concat_axis=0, tiled=True)  28.9 us
    dot_general x64, matrix products, attend_block(): lax.dot_general(query_part, key_part, (((1,), (1,)), ((), ())), preferred...  26.8 us
    slice x7, local copies, waits for them, and re-layouts, serve_grouped(): key_panel[:reach]  19.3 us
    dot_general x64, matrix products, attend_block(): jnp.dot(weights, value_part, preferred_element_type=jnp.float32)  17.4 us
    all_to_all x1, waiting for transfers between devices, per_device(): lax.all_to_all(send_rows, 'ctx', split_axis=0, concat_axis=0, tiled=True)  15.2 us
    reduce_sum x64, other arithmetic, attend_block(): jnp.sum(raised, axis=1, keepdims=True)  13.6 us
    dot_general x8, matrix products, serve_flat(): jnp.dot(attended, output_slab, preferred_element_type=jnp.float32)  12 us
  transfers between devices with their start and end apart: 5, of which 5 were waited for; matrix products, arithmetic and copies ran while one was open for 5% of the time, Pallas kernels for 0%

commit v1 on v0

v1 whole, which is shorter than its diff:
```python
import functools
import math

import jax
import jax.numpy as jnp
from jax import lax
from jax.experimental import pallas as pl
from jax.experimental.pallas import tpu as pltpu
from jax.sharding import PartitionSpec as P

HS = 128
EXPERTS = 8
TOPK = 2
MOST = 40
MASKED = -1e30


def norm_rows(tokens, norm_gain):
    floats = tokens.astype(jnp.float32)
    factor = lax.rsqrt(jnp.mean(floats * floats, axis=1, keepdims=True) + 1e-06)
    return (floats * factor * norm_gain).astype(jnp.bfloat16)


def ring_order(count):
    return list(range(0, count, 2)) + list(range(1, count, 2))[::-1]


def attend_kernel(tile, span, pos_ref, q_ref, k_ref, v_ref, out_ref):
    scale = 1.0 / math.sqrt(HS)
    for i in range(q_ref.shape[0] // tile):
        rows = pl.ds(i * tile, tile)
        reach = (i + 1) * span
        scores = lax.dot_general(
            q_ref[rows, :],
            k_ref[pl.ds(0, reach), :],
            (((1,), (1,)), ((), ())),
            preferred_element_type=jnp.float32,
        )
        scores = scores * scale
        last = scores[:, reach - span :]
        key_index = lax.broadcasted_iota(jnp.int32, last.shape, 1) + (reach - span)
        last = jnp.where(key_index <= pos_ref[rows, :], last, MASKED)
        if i > 0:
            scores = jnp.concatenate([scores[:, : reach - span], last], axis=1)
        else:
            scores = last
        peak = jnp.max(scores, axis=1, keepdims=True)
        raised = jnp.exp(scores - peak)
        total = jnp.sum(raised, axis=1, keepdims=True)
        weights = (raised * (1.0 / total)).astype(jnp.bfloat16)
        out_ref[rows, :] = jnp.dot(
            weights, v_ref[pl.ds(0, reach), :], preferred_element_type=jnp.float32
        ).astype(jnp.bfloat16)


def attend(queries, positions, keys, values, tile, span):
    row_count, width = queries.shape
    length = keys.shape[0]
    heads = width // HS
    body = functools.partial(attend_kernel, tile, span)
    return pl.pallas_call(
        body,
        grid=(heads,),
        in_specs=[
            pl.BlockSpec((row_count, 1), lambda h: (0, 0)),
            pl.BlockSpec((row_count, HS), lambda h: (0, h)),
            pl.BlockSpec((length, HS), lambda h: (0, h)),
            pl.BlockSpec((length, HS), lambda h: (0, h)),
        ],
        out_specs=pl.BlockSpec((row_count, HS), lambda h: (0, h)),
        out_shape=jax.ShapeDtypeStruct((row_count, width), jnp.bfloat16),
        compiler_params=pltpu.CompilerParams(vmem_limit_bytes=48 * 1024 * 1024),
        cost_estimate=pl.CostEstimate(
            flops=2 * row_count * length * width,
            bytes_accessed=4 * length * width,
            transcendentals=row_count * length * heads // 2,
        ),
        name="attend",
    )(positions, queries, keys, values)


def per_device(
    tokens, norm_gain, router_weight, routes, key_weight, value_weight, query_weight, output_weight
):
    tok_count, model_width = tokens.shape
    ctx_count = lax.axis_size("ctx")
    exp_count = lax.axis_size("exp")
    quarter_count = ctx_count // EXPERTS
    head_width = query_weight.shape[2]
    ctx_index = lax.axis_index("ctx")
    exp_index = lax.axis_index("exp")
    order = ring_order(ctx_count)
    order_table = jnp.array(order, jnp.int32)
    place_table = jnp.array([order.index(c) for c in range(ctx_count)], jnp.int32)
    place = place_table[ctx_index]
    forward = [(order[p], order[(p + 1) % ctx_count]) for p in range(ctx_count)]
    backward = [(b, a) for a, b in forward]
    sibling = [(e, (e + 1) % exp_count) for e in range(exp_count)]
    query_slab = query_weight[0]
    output_slab = output_weight[0]
    if quarter_count > 1:
        first = (ctx_index % quarter_count) * head_width
        key_weight = lax.dynamic_slice_in_dim(key_weight, first, head_width, axis=1)
        value_weight = lax.dynamic_slice_in_dim(value_weight, first, head_width, axis=1)

    normed = norm_rows(tokens, norm_gain)
    half = tok_count // 2

    pair_count = tok_count * TOPK
    slot_total = EXPERTS * MOST
    flat_expert = routes.reshape(pair_count)
    onehot = (flat_expert[:, None] == jnp.arange(EXPERTS, dtype=jnp.int32)[None, :]).astype(
        jnp.int32
    )
    slot_rank = jnp.sum((jnp.cumsum(onehot, axis=0) - 1) * onehot, axis=1)
    slot_index = flat_expert * MOST + slot_rank
    chosen_mask = slot_index[None, :] == jnp.arange(slot_total, dtype=jnp.int32)[:, None]
    pair_token = jnp.arange(pair_count, dtype=jnp.int32) // TOPK
    slot_token = jnp.max(jnp.where(chosen_mask, pair_token[None, :], -1), axis=1)
    send_token = jnp.repeat(slot_token.reshape(EXPERTS, MOST), quarter_count, axis=0)
    got_token = lax.all_to_all(send_token, "ctx", split_axis=0, concat_axis=0, tiled=True)

    def project(rows):
        keys = jnp.dot(rows, key_weight, preferred_element_type=jnp.float32)
        values = jnp.dot(rows, value_weight, preferred_element_type=jnp.float32)
        return jnp.stack([keys.astype(jnp.bfloat16), values.astype(jnp.bfloat16)], axis=0)

    all_rows = jnp.zeros((ctx_count, tok_count, model_width), jnp.bfloat16)
    all_panels = jnp.zeros((2, ctx_count, exp_count, tok_count, head_width), jnp.bfloat16)
    panels = []

    def place_blocks(blocks, owners):
        nonlocal all_rows, all_panels
        rows = jnp.concatenate(blocks, axis=0)
        own = project(rows)
        others = lax.ppermute(own, "exp", sibling)
        for b, owner in enumerate(owners):
            part = slice(b * tok_count, (b + 1) * tok_count)
            all_rows = lax.dynamic_update_slice(
                all_rows, rows[part][None], (owner, 0, 0)
            )
            all_panels = lax.dynamic_update_slice(
                all_panels, own[:, None, None, part], (0, owner, exp_index, 0, 0)
            )
            all_panels = lax.dynamic_update_slice(
                all_panels, others[:, None, None, part], (0, owner, 1 - exp_index, 0, 0)
            )

    place_blocks([normed], [ctx_index])
    ahead = [normed[:half], normed[half:]]
    behind = [normed[:half], normed[half:]]
    steps = ctx_count // 2
    for step in range(1, steps + 1):
        if step < steps:
            ahead = [lax.ppermute(part, "ctx", forward) for part in ahead]
            behind = [lax.ppermute(part, "ctx", backward) for part in behind]
            owners = [
                order_table[(place - step) % ctx_count],
                order_table[(place + step) % ctx_count],
            ]
            place_blocks(ahead + behind, owners)
        else:
            one = lax.ppermute(ahead[0], "ctx", forward)
            two = lax.ppermute(behind[1], "ctx", backward)
            place_blocks([one, two], [order_table[(place + step) % ctx_count]])

    select = (
        got_token[:, :, None] == jnp.arange(tok_count, dtype=jnp.int32)[None, None, :]
    ).astype(jnp.bfloat16)
    slot_rows = lax.dot_general(
        select, all_rows, (((2,), (1,)), ((0,), (0,))), preferred_element_type=jnp.float32
    ).astype(jnp.bfloat16)
    row_count = ctx_count * MOST
    slot_rows = slot_rows.reshape(row_count, model_width)
    queries = jnp.dot(slot_rows, query_slab, preferred_element_type=jnp.float32).astype(
        jnp.bfloat16
    )
    source = jnp.arange(ctx_count, dtype=jnp.int32)[:, None] * exp_count + exp_index
    positions = (jnp.maximum(got_token, 0) + source * tok_count).reshape(row_count, 1)
    length = ctx_count * exp_count * tok_count
    attended = attend(
        queries,
        positions,
        all_panels[0].reshape(length, head_width),
        all_panels[1].reshape(length, head_width),
        2 * MOST,
        2 * exp_count * tok_count,
    )
    pieces = jnp.dot(attended, output_slab, preferred_element_type=jnp.float32).astype(
        jnp.bfloat16
    )
    returned = lax.all_to_all(
        pieces.reshape(ctx_count, MOST, model_width), "ctx", split_axis=0, concat_axis=0, tiled=True
    )

    logits = jnp.dot(normed.astype(jnp.float32), router_weight, precision=lax.Precision.HIGHEST)
    gating = jax.nn.softmax(jnp.take_along_axis(logits, routes, axis=1), axis=1)
    summed = (
        returned.astype(jnp.float32).reshape(EXPERTS, quarter_count, MOST, model_width).sum(axis=1)
    )
    summed = summed.reshape(slot_total, model_width)
    gate_flat = gating.reshape(pair_count)
    combine_mat = (
        jnp.where(chosen_mask, gate_flat[None, :], 0.0)
        .reshape(slot_total, tok_count, TOPK)
        .sum(axis=2)
    )
    combined = lax.dot_general(
        combine_mat, summed, (((0,), (0,)), ((), ())), precision=lax.Precision.HIGHEST
    )
    return combined.astype(jnp.bfloat16)


def solution(mesh):
    in_specs = (
        P(("groups", "ctx", "exp"), None),
        P(),
        P(),
        P(("groups", "ctx", "exp"), None),
        P(),
        P(),
        P("ctx", None, None),
        P("ctx", None, None),
    )
    out_specs = P(("groups", "ctx", "exp"), None)
    return jax.shard_map(
        per_device, mesh=mesh, in_specs=in_specs, out_specs=out_specs, check_vma=False
    )
```

time: 396 us -> 198 us (0.50); the launches traced: 389 us -> 198 us
  waiting for transfers between devices: 229 us -> 64.9 us
  matrix products: 74.1 us -> 25.2 us
  Pallas kernels: 0 us -> 18.9 us
  starting transfers between devices: 20.5 us -> 29.6 us
  local copies, waits for them, and re-layouts: 33.6 us -> 26.2 us
    all_to_all x4 -> x2, waiting for transfers between devices: 218 us -> 28.9 us  [the longest x1 28.9 us: per_device(): lax.all_to_all(pieces.reshape(ctx_count, MOST, model_width), 'ctx', split...]
    dot_general x147 -> x13, matrix products: 71.7 us -> 22.8 us  [the longest x5 7.66 us: project(): values = jnp.dot(rows, value_weight, preferred_element_type=jnp.float32)]
    ppermute x0 -> x19, waiting for transfers between devices: none -> 36 us  [the longest x6 17.6 us: per_device(): ahead = [lax.ppermute(part, 'ctx', forward) for part in ahead]]
    pallas_call x0 -> x1, Pallas kernels: none -> 18.9 us  [attend(): pl.pallas_call(body, grid=(heads,), in_specs=[pl.BlockSpec((row_count, 1)...]
    ppermute x0 -> x19, starting transfers between devices: none -> 18.6 us  [the longest x6 11.4 us: per_device(): ahead = [lax.ppermute(part, 'ctx', forward) for part in ahead]]
    slice x8 -> x3, local copies, waits for them, and re-layouts: 23.4 us -> 6.44 us  [the longest x1 5.41 us: per_device(): all_panels[1].reshape(length, head_width)]
    reduce_sum x65 -> x0, other arithmetic: 13.6 us -> none  [the longest x64 13.6 us: attend_block(): jnp.sum(raised, axis=1, keepdims=True)]
    dynamic_update_slice x0 -> x15, other arithmetic: none -> 12.7 us  [the longest x8 6.55 us: place_blocks(): lax.dynamic_update_slice(all_panels, own[:, None, None, part], (0, owner,...]
  transfers between devices with their start and end apart: 5 -> 21, of which waited for: 5 -> 7; matrix products, arithmetic and copies ran while one was open for 5% -> 25% of each run, Pallas kernels for 0% -> 0%
where the time goes in v1:
time: 198 us
  waiting for transfers between devices  64.9 us (33%)
  starting transfers between devices  29.6 us (15%)
  local copies, waits for them, and re-layouts  26.2 us (13%)
  matrix products  25.2 us (13%)
  Pallas kernels  18.9 us (10%)
  between operations  17.8 us (9%)
  other arithmetic  15.4 us (8%)
    all_to_all x1, waiting for transfers between devices, per_device(): lax.all_to_all(pieces.reshape(ctx_count, MOST, model_width), 'ctx', split...  28.9 us
    pallas_call x1, Pallas kernels, attend(): pl.pallas_call(body, grid=(heads,), in_specs=[pl.BlockSpec((row_count, 1)...  18.9 us
    ppermute x6, waiting for transfers between devices, per_device(): ahead = [lax.ppermute(part, 'ctx', forward) for part in ahead]  17.6 us
    ppermute x6, waiting for transfers between devices, per_device(): behind = [lax.ppermute(part, 'ctx', backward) for part in behind]  12.4 us
    ppermute x6, starting transfers between devices, per_device(): ahead = [lax.ppermute(part, 'ctx', forward) for part in ahead]  11.4 us
    dot_general x5, matrix products, project(): values = jnp.dot(rows, value_weight, preferred_element_type=jnp.float32)  7.66 us
    dot_general x5, matrix products, project(): keys = jnp.dot(rows, key_weight, preferred_element_type=jnp.float32)  7.64 us
    dynamic_update_slice x8, local copies, waits for them, and re-layouts, place_blocks(): lax.dynamic_update_slice(all_panels, others[:, None, None, part], (0, own...  6.64 us
  transfers between devices with their start and end apart: 21, of which 7 were waited for; matrix products, arithmetic and copies ran while one was open for 25% of the time, Pallas kernels for 0%

profile of v1, /device:TPU:0, one launch (start us, length us, event | category | flops | bytes accessed | tf_op | source)
XLA Modules:
  0.0 197.9 jit_solution(5294327355834301626)
XLA Ops:
  0.0 1.3 fusion.20
  1.3 2.5 %broadcast_in_dim.122 = bf16[8,128,2048]{2,1,0:T(8,128)(2,1)} broadcast(bf16[]{:T(256)} %constant.119.clone.1), dimensions={} | broadcast | bytes 4194306 | tf_op jit(solution)/shard_map/broadcast_in_dim | solution.py:128
  3.8 1.0 bitcast_dynamic-update-slice_fusion.5
  4.9 0.8 fusion.61
  5.7 3.0 %collective-permute-start.1 = (bf16[64,2048]{1,0:T(8,128)(2,1)}, bf16[64,2048]{1,0:T(8,128)(2,1)S(1)}, u32[]{:S(2)}, u32[]{:S(2)}) collective-permute-start(bf16[64,2048]{1,0:T(8,128)(2,1)} %get-tuple-element.12), channel_id=1, source_target_pairs={{0,4},{4,8},{8,12},{12,14},{14,10},{10,6},{6,2},{2,0},{1,5},{5,9},... | collective-permute-start | bytes 786440 | tf_op jit(solution)/shard_map/ppermute | solution.py:155
  8.7 2.0 %collective-permute-start = (bf16[64,2048]{1,0:T(8,128)(2,1)}, bf16[64,2048]{1,0:T(8,128)(2,1)S(1)}, u32[]{:S(2)}, u32[]{:S(2)}) collective-permute-start(bf16[64,2048]{1,0:T(8,128)(2,1)} %get-tuple-element.11), channel_id=1, source_target_pairs={{0,4},{4,8},{8,12},{12,14},{14,10},{10,6},{6,2},{2,0},{1,5},{5,9},... | collective-permute-start | bytes 786440 | tf_op jit(solution)/shard_map/ppermute | solution.py:155
  12.2 0.7 all_to_all.9
  12.9 6.3 %all-to-all-start = ((s32[8,1,40]{2,1,0:T(1,128)}), s32[8,1,40]{2,1,0:T(1,128)S(1)}, u32[]{:S(2)}, u32[]{:S(2)}) async-start(s32[8,1,40]{2,1,0:T(1,128)} %all_to_all.9), calls=%async_computation | async-start | bytes 8192 | tf_op jit(solution)/shard_map/all_to_all | solution.py:121
  19.2 3.1 %fusion.17 = bf16[1,128,1024]{2,1,0:T(8,128)(2,1)S(1)} fusion(bf16[128,2048]{1,0:T(8,128)(2,1)S(1)} %get-tuple-element.6, bf16[2048,1024]{1,0:T(8,128)(2,1)} %param.15), kind=kOutput, calls=%fused_computation.43 | convolution fusion | flops 537001984 | bytes 4980736 | tf_op jit(solution)/shard_map/dot_general | solution.py:125
  22.6 0.7 fusion.16
  28.7 4.3 %broadcast_in_dim.131 = bf16[2,8,2,128,1024]{4,3,2,1,0:T(8,128)(2,1)} broadcast(bf16[]{:T(256)} %constant.119.clone.1), dimensions={} | broadcast | bytes 8388610 | tf_op jit(solution)/shard_map/broadcast_in_dim | solution.py:129
  33.0 0.8 bitcast_dynamic-update-slice_fusion.3
  47.8 3.6 %fusion.10 = bf16[1,256,1024]{2,1,0:T(8,128)(2,1)S(1)} fusion(bf16[256,2048]{1,0:T(8,128)(2,1)S(1)} %constant_dynamic-update-slice_fusion.2, bf16[2048,1024]{1,0:T(8,128)(2,1)} %param.14), kind=kOutput, calls=%fused_computation.32 | convolution fusion | flops 1074003968 | bytes 5767168 | tf_op jit(solution)/shard_map/dot_general | solution.py:124
  51.4 1.3 fusion.11
  53.3 2.0 %collective-permute-start.5 = (bf16[64,2048]{1,0:T(8,128)(2,1)S(1)}, bf16[64,2048]{1,0:T(8,128)(2,1)S(1)}, u32[]{:S(2)}, u32[]{:S(2)}) collective-permute-start(bf16[64,2048]{1,0:T(8,128)(2,1)S(1)} %collective-permute-done.1), channel_id=1, source_target_pairs={{0,4},{4,8},{8,12},{12,14},{14,10},{10,6},{6,2},{2,0},{1,5},{5,9},... | collective-permute-start | bytes 786440 | tf_op jit(solution)/shard_map/ppermute | solution.py:155
  55.4 1.5 collective-permute-start.4
  57.4 0.9 fusion.47
  58.3 0.8 fusion.48
  59.1 8.4 %collective-permute-done.4 = bf16[64,2048]{1,0:T(8,128)(2,1)S(1)} collective-permute-done((bf16[64,2048]{1,0:T(8,128)(2,1)S(1)}, bf16[64,2048]{1,0:T(8,128)(2,1)S(1)}, u32[]{:S(2)}, u32[]{:S(2)}) %collective-permute-start.4) | collective-permute-done | bytes 262176 | tf_op jit(solution)/shard_map/ppermute | solution.py:155
  67.5 1.7 collective-permute-start.6
  69.3 6.0 %collective-permute-done.6 = bf16[64,2048]{1,0:T(8,128)(2,1)S(1)} collective-permute-done((bf16[64,2048]{1,0:T(8,128)(2,1)S(1)}, bf16[64,2048]{1,0:T(8,128)(2,1)S(1)}, u32[]{:S(2)}, u32[]{:S(2)}) %collective-permute-start.6) | collective-permute-done | bytes 262176 | tf_op jit(solution)/shard_map/ppermute | solution.py:156
  75.3 1.3 fusion.12
  76.6 1.3 fusion.13
  77.9 0.8 bitcast_dynamic-update-slice_fusion.2
  78.8 0.8 fusion.37
  79.8 1.5 collective-permute-start.9
  81.2 1.5 collective-permute-start.8
  83.3 0.8 fusion.49
  84.1 0.8 fusion.50
  84.9 9.1 %collective-permute-done.8 = bf16[64,2048]{1,0:T(8,128)(2,1)S(1)} collective-permute-done((bf16[64,2048]{1,0:T(8,128)(2,1)S(1)}, bf16[64,2048]{1,0:T(8,128)(2,1)S(1)}, u32[]{:S(2)}, u32[]{:S(2)}) %collective-permute-start.8) | collective-permute-done | bytes 262176 | tf_op jit(solution)/shard_map/ppermute | solution.py:155
  94.1 1.4 collective-permute-start.10
  95.6 6.4 %collective-permute-done.10 = bf16[64,2048]{1,0:T(8,128)(2,1)S(1)} collective-permute-done((bf16[64,2048]{1,0:T(8,128)(2,1)S(1)}, bf16[64,2048]{1,0:T(8,128)(2,1)S(1)}, u32[]{:S(2)}, u32[]{:S(2)}) %collective-permute-start.10) | collective-permute-done | bytes 262176 | tf_op jit(solution)/shard_map/ppermute | solution.py:156
  102.0 1.3 fusion.14
  103.3 1.3 fusion.15
  104.8 1.5 collective-permute-start.12
  106.9 0.8 fusion.51
  107.7 0.8 fusion.52
  108.6 4.9 %collective-permute-done.12 = bf16[64,2048]{1,0:T(8,128)(2,1)S(1)} collective-permute-done((bf16[64,2048]{1,0:T(8,128)(2,1)S(1)}, bf16[64,2048]{1,0:T(8,128)(2,1)S(1)}, u32[]{:S(2)}, u32[]{:S(2)}) %collective-permute-start.12) | collective-permute-done | bytes 262176 | tf_op jit(solution)/shard_map/ppermute | solution.py:163
  113.5 1.1 collective-permute-done.13
  114.7 0.7 fusion.19
  115.4 0.7 fusion.18
  116.3 0.9 bitcast_dynamic-update-slice_fusion.4
  117.2 3.3 %convolution_convert_fusion = bf16[8,40,2048]{2,1,0:T(8,128)(2,1)S(1)} fusion(bf16[8,128,2048]{2,1,0:T(8,128)(2,1)} %bitcast_dynamic-update-slice_fusion.4, s32[8,40]{1,0:T(8,128)S(1)} %bitcast.207), kind=kOutput, calls=%fused_computation.5 | convolution fusion | flops 168468480 | bytes 5506304 | tf_op jit(solution)/shard_map/dot_general | solution.py:170
  120.5 1.6 fusion.7.q_ref
  122.1 0.8 fusion.46
  122.9 0.8 fusion.40
  123.8 0.8 fusion.45
  124.6 0.8 fusion.31
  125.4 0.8 fusion.44
  126.2 0.8 fusion.34
  127.1 0.8 fusion.43
  127.9 0.8 fusion.25
  128.7 0.8 fusion.42
  129.5 0.8 fusion.28
  130.3 0.8 fusion.41
  131.2 0.8 bitcast_dynamic-update-slice_fusion.1
  132.0 0.9 bitcast_dynamic-update-slice_fusion
  132.9 5.4 %fusion.60 = (bf16[1,8,2,128,1024]{4,3,2,1,0:T(8,128)(2,1)}, bf16[1,8,2,128,1024]{4,3,2,1,0:T(8,128)(2,1)S(1)}) fusion(bf16[2,8,2,128,1024]{4,3,2,1,0:T(8,128)(2,1)} %bitcast_dynamic-update-slice_fusion), kind=kLoop, calls=%fused_computation.141 | loop fusion | bytes 16777216 | tf_op jit(solution)/shard_map/slice | solution.py:185
  138.3 18.9 %attend.1 = bf16[320,1024]{1,0:T(8,128)(2,1)S(1)} custom-call(s32[320,1]{1,0:T(8,128)S(1)} %copy.133.pos_ref, bf16[320,1024]{1,0:T(8,128)(2,1)S(1)} %fusion.7.q_ref, bf16[2048,1024]{1,0:T(8,128)(2,1)S(1)} %bitcast.203, bf16[2048,1024]{1,0:T(8,128)(2,1)} %bitcast.204), custom_call_target="tpu_custom_call" | custom-call | flops 1342177280 | bytes 8388608 | tf_op jit(solution)/shard_map/attend/pallas_call | solution.py:61
  157.2 2.6 %fusion.4 = bf16[320,2048]{1,0:T(8,128)(2,1)} fusion(bf16[320,1024]{1,0:T(8,128)(2,1)S(1)} %attend.1, bf16[1,1024,2048]{2,1,0:T(8,128)(2,1)S(1)} %copy-done.9), kind=kOutput, calls=%fused_computation.6 | convolution fusion | flops 1342832640 | bytes 6160384 | tf_op jit(solution)/shard_map/dot_general | solution.py:189
  159.8 4.6 %all-to-all-start.1 = ((bf16[8,40,2048]{2,1,0:T(8,128)(2,1)}), bf16[8,40,2048]{2,1,0:T(8,128)(2,1)S(1)}, u32[]{:S(2)}, u32[]{:S(2)}) async-start(bf16[8,40,2048]{2,1,0:T(8,128)(2,1)} %bitcast.73), calls=%async_computation.1 | async-start | bytes 2621440 | tf_op jit(solution)/shard_map/all_to_all | solution.py:192
  165.4 1.4 gather_fusion
  167.2 28.9 %all-to-all-done.1 = bf16[8,40,2048]{2,1,0:T(8,128)(2,1)S(1)} async-done(((bf16[8,40,2048]{2,1,0:T(8,128)(2,1)}), bf16[8,40,2048]{2,1,0:T(8,128)(2,1)S(1)}, u32[]{:S(2)}, u32[]{:S(2)}) %all-to-all-start.1) | async-done | bytes 1310752 | tf_op jit(solution)/shard_map/all_to_all | solution.py:192
  196.1 1.8 convolution_convert_fusion.1
  (99 shorter events, 8.1 us)
Async XLA Ops:
  0.0 164.8 %copy-start = (f32[2048,8]{0,1:T(8,128)S(1)}, f32[2048,8]{0,1:T(8,128)}, u32[]{:S(2)}) copy-start(f32[2048,8]{0,1:T(8,128)} %param.12) | copy-start | bytes 196612
  0.0 3.8 %copy-start.4 = (bf16[128,2048]{1,0:T(8,128)(2,1)S(1)}, bf16[128,2048]{1,0:T(8,128)(2,1)}, u32[]{:S(2)}) copy-start(bf16[128,2048]{1,0:T(8,128)(2,1)} %param.10) | copy-start | bytes 1572868
  0.0 3.8 %copy-start.7 = (f32[2048]{0:T(1024)S(1)}, f32[2048]{0:T(1024)}, u32[]{:S(2)}) copy-start(f32[2048]{0:T(1024)} %param.11) | copy-start | bytes 24580
  0.0 10.7 %copy-start.6 = (s32[128,2]{0,1:T(2,128)S(1)}, s32[128,2]{0,1:T(2,128)}, u32[]{:S(2)}) copy-start(s32[128,2]{0,1:T(2,128)} %param.13) | copy-start | bytes 3076
  5.7 42.0 %collective-permute-start.1 = (bf16[64,2048]{1,0:T(8,128)(2,1)}, bf16[64,2048]{1,0:T(8,128)(2,1)S(1)}, u32[]{:S(2)}, u32[]{:S(2)}) collective-permute-start(bf16[64,2048]{1,0:T(8,128)(2,1)} %get-tuple-element.12), channel_id=1, source_target_pairs={{0,4},{4,8},{8,12},{12,14},{14,10},{10,6},{6,2},{2,0},{1,5},{5,9},... | collective-permute-start | bytes 786440 | tf_op jit(solution)/shard_map/ppermute | solution.py:155
  8.7 39.1 %collective-permute-start.3 = (bf16[64,2048]{1,0:T(8,128)(2,1)}, bf16[64,2048]{1,0:T(8,128)(2,1)S(1)}, u32[]{:S(2)}, u32[]{:S(2)}) collective-permute-start(bf16[64,2048]{1,0:T(8,128)(2,1)} %get-tuple-element.12), channel_id=1, source_target_pairs={{4,0},{8,4},{12,8},{14,12},{10,14},{6,10},{2,6},{0,2},{5,1},{9,5},... | collective-permute-start | bytes 786440 | tf_op jit(solution)/shard_map/ppermute | solution.py:156
  8.7 38.9 %collective-permute-start = (bf16[64,2048]{1,0:T(8,128)(2,1)}, bf16[64,2048]{1,0:T(8,128)(2,1)S(1)}, u32[]{:S(2)}, u32[]{:S(2)}) collective-permute-start(bf16[64,2048]{1,0:T(8,128)(2,1)} %get-tuple-element.11), channel_id=1, source_target_pairs={{0,4},{4,8},{8,12},{12,14},{14,10},{10,6},{6,2},{2,0},{1,5},{5,9},... | collective-permute-start | bytes 786440 | tf_op jit(solution)/shard_map/ppermute | solution.py:155
  10.7 37.0 %collective-permute-start.2 = (bf16[64,2048]{1,0:T(8,128)(2,1)}, bf16[64,2048]{1,0:T(8,128)(2,1)S(1)}, u32[]{:S(2)}, u32[]{:S(2)}) collective-permute-start(bf16[64,2048]{1,0:T(8,128)(2,1)} %get-tuple-element.11), channel_id=1, source_target_pairs={{4,0},{8,4},{12,8},{14,12},{10,14},{6,10},{2,6},{0,2},{5,1},{9,5},... | collective-permute-start | bytes 786440 | tf_op jit(solution)/shard_map/ppermute | solution.py:156
  12.9 34.4 %all-to-all-start = ((s32[8,1,40]{2,1,0:T(1,128)}), s32[8,1,40]{2,1,0:T(1,128)S(1)}, u32[]{:S(2)}, u32[]{:S(2)}) async-start(s32[8,1,40]{2,1,0:T(1,128)} %all_to_all.9), calls=%async_computation | async-start | bytes 8192 | tf_op jit(solution)/shard_map/all_to_all | solution.py:121
  19.2 3.4 %copy-start.2 = (bf16[2048,1024]{1,0:T(8,128)(2,1)S(1)}, bf16[2048,1024]{1,0:T(8,128)(2,1)}, u32[]{:S(2)}) copy-start(bf16[2048,1024]{1,0:T(8,128)(2,1)} %param.14) | copy-start | bytes 12582916
  22.6 0.9 copy-start.10
  23.4 54.5 %collective-permute-start.14 = (bf16[2,128,1024]{2,1,0:T(8,128)(2,1)S(1)}, bf16[2,128,1024]{2,1,0:T(8,128)(2,1)S(1)}, u32[]{:S(2)}, u32[]{:S(2)}) collective-permute-start(bf16[2,128,1024]{2,1,0:T(8,128)(2,1)S(1)} %pad_maximum_fusion.3), channel_id=1, source_target_pairs={{0,1},{1,0},{2,3},{3,2},{4,5},{5,4},{6,7},{7,6},{8,9},{9,8},{10,11... | collective-permute-start | bytes 1572872 | tf_op jit(solution)/shard_map/ppermute | solution.py:136
  28.7 5.1 %copy-start.5 = (s32[8]{0:T(128)S(1)}, s32[8]{0:T(128)}, u32[]{:S(2)}) copy-start(s32[8]{0:T(128)} %constant.129.clone) | copy-start | bytes 100
  47.7 3.7 %copy-start.1 = (bf16[2048,1024]{1,0:T(8,128)(2,1)S(1)}, bf16[2048,1024]{1,0:T(8,128)(2,1)}, u32[]{:S(2)}) copy-start(bf16[2048,1024]{1,0:T(8,128)(2,1)} %param.15) | copy-start | bytes 12582916
  52.7 22.7 %copy-start.3 = (bf16[2048,1024]{1,0:T(8,128)(2,1)S(1)}, bf16[2048,1024]{1,0:T(8,128)(2,1)}, u32[]{:S(2)}) copy-start(bf16[2048,1024]{1,0:T(8,128)(2,1)} %param.14) | copy-start | bytes 12582916
  52.8 69.3 %collective-permute-start.15 = (bf16[2,256,1024]{2,1,0:T(8,128)(2,1)S(1)}, bf16[2,256,1024]{2,1,0:T(8,128)(2,1)S(1)}, u32[]{:S(2)}, u32[]{:S(2)}) collective-permute-start(bf16[2,256,1024]{2,1,0:T(8,128)(2,1)S(1)} %pad_maximum_fusion), channel_id=1, source_target_pairs={{0,1},{1,0},{2,3},{3,2},{4,5},{5,4},{6,7},{7,6},{8,9},{9,8},{10,11... | collective-permute-start | bytes 3145736 | tf_op jit(solution)/shard_map/ppermute | solution.py:136
  53.3 15.9 %collective-permute-start.5 = (bf16[64,2048]{1,0:T(8,128)(2,1)S(1)}, bf16[64,2048]{1,0:T(8,128)(2,1)S(1)}, u32[]{:S(2)}, u32[]{:S(2)}) collective-permute-start(bf16[64,2048]{1,0:T(8,128)(2,1)S(1)} %collective-permute-done.1), channel_id=1, source_target_pairs={{0,4},{4,8},{8,12},{12,14},{14,10},{10,6},{6,2},{2,0},{1,5},{5,9},... | collective-permute-start | bytes 786440 | tf_op jit(solution)/shard_map/ppermute | solution.py:155
  55.4 12.1 %collective-permute-start.4 = (bf16[64,2048]{1,0:T(8,128)(2,1)S(1)}, bf16[64,2048]{1,0:T(8,128)(2,1)S(1)}, u32[]{:S(2)}, u32[]{:S(2)}) collective-permute-start(bf16[64,2048]{1,0:T(8,128)(2,1)S(1)} %collective-permute-done), channel_id=1, source_target_pairs={{0,4},{4,8},{8,12},{12,14},{14,10},{10,6},{6,2},{2,0},{1,5},{5,9},... | collective-permute-start | bytes 786440 | tf_op jit(solution)/shard_map/ppermute | solution.py:155
  56.8 18.5 %collective-permute-start.7 = (bf16[64,2048]{1,0:T(8,128)(2,1)S(1)}, bf16[64,2048]{1,0:T(8,128)(2,1)S(1)}, u32[]{:S(2)}, u32[]{:S(2)}) collective-permute-start(bf16[64,2048]{1,0:T(8,128)(2,1)S(1)} %collective-permute-done.3), channel_id=1, source_target_pairs={{4,0},{8,4},{12,8},{14,12},{10,14},{6,10},{2,6},{0,2},{5,1},{9,5},... | collective-permute-start | bytes 786440 | tf_op jit(solution)/shard_map/ppermute | solution.py:156
  67.5 7.8 %collective-permute-start.6 = (bf16[64,2048]{1,0:T(8,128)(2,1)S(1)}, bf16[64,2048]{1,0:T(8,128)(2,1)S(1)}, u32[]{:S(2)}, u32[]{:S(2)}) collective-permute-start(bf16[64,2048]{1,0:T(8,128)(2,1)S(1)} %collective-permute-done.2), channel_id=1, source_target_pairs={{4,0},{8,4},{12,8},{14,12},{10,14},{6,10},{2,6},{0,2},{5,1},{9,5},... | collective-permute-start | bytes 786440 | tf_op jit(solution)/shard_map/ppermute | solution.py:156
  79.7 45.7 %collective-permute-start.16 = (bf16[2,256,1024]{2,1,0:T(8,128)(2,1)S(1)}, bf16[2,256,1024]{2,1,0:T(8,128)(2,1)S(1)}, u32[]{:S(2)}, u32[]{:S(2)}) collective-permute-start(bf16[2,256,1024]{2,1,0:T(8,128)(2,1)S(1)} %pad_maximum_fusion.1), channel_id=1, source_target_pairs={{0,1},{1,0},{2,3},{3,2},{4,5},{5,4},{6,7},{7,6},{8,9},{9,8},{10,11... | collective-permute-start | bytes 3145736 | tf_op jit(solution)/shard_map/ppermute | solution.py:136
  79.8 15.8 %collective-permute-start.9 = (bf16[64,2048]{1,0:T(8,128)(2,1)S(1)}, bf16[64,2048]{1,0:T(8,128)(2,1)S(1)}, u32[]{:S(2)}, u32[]{:S(2)}) collective-permute-start(bf16[64,2048]{1,0:T(8,128)(2,1)S(1)} %collective-permute-done.5), channel_id=1, source_target_pairs={{0,4},{4,8},{8,12},{12,14},{14,10},{10,6},{6,2},{2,0},{1,5},{5,9},... | collective-permute-start | bytes 786440 | tf_op jit(solution)/shard_map/ppermute | solution.py:155
  81.2 12.9 %collective-permute-start.8 = (bf16[64,2048]{1,0:T(8,128)(2,1)S(1)}, bf16[64,2048]{1,0:T(8,128)(2,1)S(1)}, u32[]{:S(2)}, u32[]{:S(2)}) collective-permute-start(bf16[64,2048]{1,0:T(8,128)(2,1)S(1)} %collective-permute-done.4), channel_id=1, source_target_pairs={{0,4},{4,8},{8,12},{12,14},{14,10},{10,6},{6,2},{2,0},{1,5},{5,9},... | collective-permute-start | bytes 786440 | tf_op jit(solution)/shard_map/ppermute | solution.py:155
  82.7 19.3 %collective-permute-start.11 = (bf16[64,2048]{1,0:T(8,128)(2,1)S(1)}, bf16[64,2048]{1,0:T(8,128)(2,1)S(1)}, u32[]{:S(2)}, u32[]{:S(2)}) collective-permute-start(bf16[64,2048]{1,0:T(8,128)(2,1)S(1)} %collective-permute-done.7), channel_id=1, source_target_pairs={{4,0},{8,4},{12,8},{14,12},{10,14},{6,10},{2,6},{0,2},{5,1},{9,5},... | collective-permute-start | bytes 786440 | tf_op jit(solution)/shard_map/ppermute | solution.py:156
  94.1 7.9 %collective-permute-start.10 = (bf16[64,2048]{1,0:T(8,128)(2,1)S(1)}, bf16[64,2048]{1,0:T(8,128)(2,1)S(1)}, u32[]{:S(2)}, u32[]{:S(2)}) collective-permute-start(bf16[64,2048]{1,0:T(8,128)(2,1)S(1)} %collective-permute-done.6), channel_id=1, source_target_pairs={{4,0},{8,4},{12,8},{14,12},{10,14},{6,10},{2,6},{0,2},{5,1},{9,5},... | collective-permute-start | bytes 786440 | tf_op jit(solution)/shard_map/ppermute | solution.py:156
  104.7 24.0 %collective-permute-start.17 = (bf16[2,256,1024]{2,1,0:T(8,128)(2,1)S(1)}, bf16[2,256,1024]{2,1,0:T(8,128)(2,1)S(1)}, u32[]{:S(2)}, u32[]{:S(2)}) collective-permute-start(bf16[2,256,1024]{2,1,0:T(8,128)(2,1)S(1)} %pad_maximum_fusion.2), channel_id=1, source_target_pairs={{0,1},{1,0},{2,3},{3,2},{4,5},{5,4},{6,7},{7,6},{8,9},{9,8},{10,11... | collective-permute-start | bytes 3145736 | tf_op jit(solution)/shard_map/ppermute | solution.py:136
  104.8 8.7 %collective-permute-start.12 = (bf16[64,2048]{1,0:T(8,128)(2,1)S(1)}, bf16[64,2048]{1,0:T(8,128)(2,1)S(1)}, u32[]{:S(2)}, u32[]{:S(2)}) collective-permute-start(bf16[64,2048]{1,0:T(8,128)(2,1)S(1)} %collective-permute-done.8), channel_id=1, source_target_pairs={{0,4},{4,8},{8,12},{12,14},{14,10},{10,6},{6,2},{2,0},{1,5},{5,9},... | collective-permute-start | bytes 786440 | tf_op jit(solution)/shard_map/ppermute | solution.py:163
  106.3 8.4 %collective-permute-start.13 = (bf16[64,2048]{1,0:T(8,128)(2,1)S(1)}, bf16[64,2048]{1,0:T(8,128)(2,1)S(1)}, u32[]{:S(2)}, u32[]{:S(2)}) collective-permute-start(bf16[64,2048]{1,0:T(8,128)(2,1)S(1)} %collective-permute-done.11), channel_id=1, source_target_pairs={{4,0},{8,4},{12,8},{14,12},{10,14},{6,10},{2,6},{0,2},{5,1},{9,5},... | collective-permute-start | bytes 786440 | tf_op jit(solution)/shard_map/ppermute | solution.py:164
  116.1 4.4 %copy-start.8 = (bf16[1,2048,1024]{2,1,0:T(8,128)(2,1)S(1)}, bf16[1,2048,1024]{2,1,0:T(8,128)(2,1)}, u32[]{:S(2)}) copy-start(bf16[1,2048,1024]{2,1,0:T(8,128)(2,1)} %param.16) | copy-start | bytes 12582916
  116.2 15.8 %collective-permute-start.18 = (bf16[2,128,1024]{2,1,0:T(8,128)(2,1)S(1)}, bf16[2,128,1024]{2,1,0:T(8,128)(2,1)S(1)}, u32[]{:S(2)}, u32[]{:S(2)}) collective-permute-start(bf16[2,128,1024]{2,1,0:T(8,128)(2,1)S(1)} %pad_maximum_fusion.4), channel_id=1, source_target_pairs={{0,1},{1,0},{2,3},{3,2},{4,5},{5,4},{6,7},{7,6},{8,9},{9,8},{10,11... | collective-permute-start | bytes 1572872 | tf_op jit(solution)/shard_map/ppermute | solution.py:136
  138.3 18.9 %copy-start.9 = (bf16[1,1024,2048]{2,1,0:T(8,128)(2,1)S(1)}, bf16[1,1024,2048]{2,1,0:T(8,128)(2,1)}, u32[]{:S(2)}) copy-start(bf16[1,1024,2048]{2,1,0:T(8,128)(2,1)} %param.17) | copy-start | bytes 12582916
  159.8 36.3 %all-to-all-start.1 = ((bf16[8,40,2048]{2,1,0:T(8,128)(2,1)}), bf16[8,40,2048]{2,1,0:T(8,128)(2,1)S(1)}, u32[]{:S(2)}, u32[]{:S(2)}) async-start(bf16[8,40,2048]{2,1,0:T(8,128)(2,1)} %bitcast.73), calls=%async_computation.1 | async-start | bytes 2621440 | tf_op jit(solution)/shard_map/all_to_all | solution.py:192

commit v2 on v1

v2 whole, which is shorter than its diff:
```python
import functools
import math

import jax
import jax.numpy as jnp
from jax import lax
from jax.experimental import pallas as pl
from jax.experimental.pallas import tpu as pltpu
from jax.sharding import PartitionSpec as P

HS = 128
EXPERTS = 8
TOPK = 2
MOST = 40
SLOTS = 48
MASKED = -1e30
VMEM = 48 * 1024 * 1024


def ring_rank(place, count):
    place = lax.rem(place + 2 * count, count)
    return jnp.where(place < count // 2, 2 * place, 2 * (count - 1 - place) + 1)


def ring_place(rank, count):
    return jnp.where(rank % 2 == 0, rank // 2, count - 1 - rank // 2)


def ring_owner(offset):
    count = lax.axis_size("ctx")
    return ring_rank(ring_place(lax.axis_index("ctx"), count) + offset, count)


def norm_kernel(tokens_ref, gain_ref, out_ref):
    floats = tokens_ref[...].astype(jnp.float32)
    factor = lax.rsqrt(jnp.mean(floats * floats, axis=1, keepdims=True) + 1e-06)
    out_ref[...] = (floats * factor * gain_ref[...]).astype(jnp.bfloat16)


def norm_rows(tokens, norm_gain):
    return pl.pallas_call(
        norm_kernel,
        out_shape=jax.ShapeDtypeStruct(tokens.shape, jnp.bfloat16),
        name="norm_rows",
    )(tokens, norm_gain.reshape(1, -1))


def project_kernel(offsets, count, token_ref, *refs):
    blocks = refs[:count]
    key_ref, value_ref, query_ref, panel_ref, out_ref, picked = refs[count:]
    rows = jnp.concatenate([block[...] for block in blocks], axis=0)
    tok_count = rows.shape[0] // len(offsets)

    @pl.when(pl.program_id(0) == 0)
    def _():
        for g, offset in enumerate(offsets):
            wanted = token_ref[ring_owner(offset)]
            lane = lax.broadcasted_iota(jnp.int32, (SLOTS, tok_count), 1)
            select = (lane == wanted).astype(jnp.bfloat16)
            picked[pl.ds(g * SLOTS, SLOTS), :] = jnp.dot(
                select,
                rows[g * tok_count : (g + 1) * tok_count],
                preferred_element_type=jnp.float32,
            ).astype(jnp.bfloat16)

    panel_ref[0] = jnp.dot(
        rows, key_ref[...], preferred_element_type=jnp.float32
    ).astype(jnp.bfloat16)
    panel_ref[1] = jnp.dot(
        rows, value_ref[...], preferred_element_type=jnp.float32
    ).astype(jnp.bfloat16)
    queries = jnp.dot(picked[...], query_ref[...], preferred_element_type=jnp.float32)
    for g in range(len(offsets)):
        out_ref[g] = queries[g * SLOTS : (g + 1) * SLOTS].astype(jnp.bfloat16)


def project(blocks, offsets, slot_token, key_weight, value_weight, query_slab):
    row_count = sum(block.shape[0] for block in blocks)
    model_width, width = key_weight.shape
    step = min(width, 512)
    weight_spec = pl.BlockSpec((model_width, step), lambda n: (0, n))
    return pl.pallas_call(
        functools.partial(project_kernel, offsets, len(blocks)),
        grid=(width // step,),
        in_specs=[pl.BlockSpec(slot_token.shape, lambda n: (0, 0, 0))]
        + [pl.BlockSpec(block.shape, lambda n: (0, 0)) for block in blocks]
        + [weight_spec] * 3,
        out_specs=[
            pl.BlockSpec((2, row_count, step), lambda n: (0, 0, n)),
            pl.BlockSpec((len(offsets), SLOTS, step), lambda n: (0, 0, n)),
        ],
        out_shape=[
            jax.ShapeDtypeStruct((2, row_count, width), jnp.bfloat16),
            jax.ShapeDtypeStruct((len(offsets), SLOTS, width), jnp.bfloat16),
        ],
        scratch_shapes=[pltpu.VMEM((len(offsets) * SLOTS, model_width), jnp.bfloat16)],
        compiler_params=pltpu.CompilerParams(vmem_limit_bytes=VMEM),
        name="project",
    )(slot_token, *blocks, key_weight, value_weight, query_slab)


def attend_kernel(plan, tok_count, pos_ref, *refs):
    count = len(plan)
    query_refs = refs[:count]
    own_refs = refs[count : 2 * count]
    other_refs = refs[2 * count : 3 * count]
    out_ref, queries, keys, values, scores, weights = refs[3 * count :]
    side = lax.axis_index("exp")
    exp_count = 2
    rate = math.log2(math.e) / math.sqrt(HS)
    tile = 2 * MOST
    span = 2 * exp_count * tok_count
    tiles = queries.shape[0] // 2
    group = min(tiles, 4)

    for offsets, query_ref, own_ref, other_ref in zip(plan, query_refs, own_refs, other_refs):
        for g, offset in enumerate(offsets):
            owner = ring_owner(offset)
            part = pl.ds(g * tok_count, tok_count)
            queries[owner] = query_ref[g].astype(jnp.float32)[:MOST]
            keys[owner * exp_count + side] = own_ref[0, part]
            values[owner * exp_count + side] = own_ref[1, part]
            keys[owner * exp_count + 1 - side] = other_ref[0, part]
            values[owner * exp_count + 1 - side] = other_ref[1, part]

    per_span = 2 * exp_count
    for lead in range(0, tiles, group):
        top = lead + group
        base = lead * tile
        held = queries[2 * lead : 2 * top].reshape(group * tile, HS).astype(jnp.bfloat16)
        for j in range(top):
            skip = max(0, j - lead) * tile
            key_part = keys[per_span * j : per_span * (j + 1)].reshape(span, HS)
            scores[pl.ds(skip, group * tile - skip), pl.ds(j * span, span)] = lax.dot_general(
                held[skip:], key_part, (((1,), (1,)), ((), ())), preferred_element_type=jnp.float32
            )
        for i in range(lead, top):
            reach = (i + 1) * span
            for sub in range(0, tile, 16):
                rows = pl.ds((i - lead) * tile + sub, 16)
                part = scores[rows, pl.ds(0, reach)]
                last = part[:, reach - span :]
                key_index = lax.broadcasted_iota(jnp.int32, last.shape, 1) + (reach - span)
                allowed = key_index <= pos_ref[pl.ds(i * tile + sub, 16), :]
                last = jnp.where(allowed, last, MASKED)
                if i > 0:
                    part = jnp.concatenate([part[:, : reach - span], last], axis=1)
                else:
                    part = last
                peak = jnp.max(part, axis=1, keepdims=True)
                raised = jnp.exp2((part - peak) * rate)
                total = jnp.sum(raised, axis=1, keepdims=True)
                weights[rows, pl.ds(0, reach)] = (raised * (1.0 / total)).astype(jnp.bfloat16)
        sums = [None] * group
        for j in range(top):
            skip = max(0, j - lead)
            value_part = values[per_span * j : per_span * (j + 1)].reshape(span, HS)
            product = jnp.dot(
                weights[pl.ds(skip * tile, (group - skip) * tile), pl.ds(j * span, span)],
                value_part,
                preferred_element_type=jnp.float32,
            )
            for i in range(skip, group):
                piece = product[(i - skip) * tile : (i - skip + 1) * tile]
                sums[i] = piece if sums[i] is None else sums[i] + piece
        for i in range(group):
            out_ref[pl.ds(base + i * tile, tile), :] = sums[i].astype(jnp.bfloat16)


def attend(plan, positions, queries, own, other):
    row_count = positions.shape[0]
    width = queries[0].shape[-1]
    heads = width // HS
    ctx_count = row_count // MOST
    tok_count = own[0].shape[1] // len(plan[0])
    length = ctx_count * 2 * tok_count
    group_rows = min(row_count, 8 * MOST)
    query_specs = [pl.BlockSpec((q.shape[0], SLOTS, HS), lambda h: (0, 0, h)) for q in queries]
    panel_specs = [pl.BlockSpec((2, p.shape[1], HS), lambda h: (0, 0, h)) for p in own]
    return pl.pallas_call(
        functools.partial(attend_kernel, plan, tok_count),
        grid=(heads,),
        in_specs=[pl.BlockSpec((row_count, 1), lambda h: (0, 0))]
        + query_specs
        + panel_specs
        + panel_specs,
        out_specs=pl.BlockSpec((row_count, HS), lambda h: (0, h)),
        out_shape=jax.ShapeDtypeStruct((row_count, width), jnp.bfloat16),
        scratch_shapes=[
            pltpu.VMEM((ctx_count, MOST, HS), jnp.float32),
            pltpu.VMEM((2 * ctx_count, tok_count, HS), jnp.bfloat16),
            pltpu.VMEM((2 * ctx_count, tok_count, HS), jnp.bfloat16),
            pltpu.VMEM((group_rows, length), jnp.float32),
            pltpu.VMEM((group_rows, length), jnp.bfloat16),
        ],
        compiler_params=pltpu.CompilerParams(vmem_limit_bytes=VMEM),
        name="attend",
    )(positions, *queries, *own, *other)


def per_device(
    tokens, norm_gain, router_weight, routes, key_weight, value_weight, query_weight, output_weight
):
    tok_count, model_width = tokens.shape
    ctx_count = lax.axis_size("ctx")
    exp_count = lax.axis_size("exp")
    quarter_count = ctx_count // EXPERTS
    head_width = query_weight.shape[2]
    ctx_index = lax.axis_index("ctx")
    exp_index = lax.axis_index("exp")
    ranks = list(range(0, ctx_count, 2)) + list(range(1, ctx_count, 2))[::-1]
    forward = [(ranks[p], ranks[(p + 1) % ctx_count]) for p in range(ctx_count)]
    backward = [(b, a) for a, b in forward]
    sibling = [(e, 1 - e) for e in range(exp_count)]
    query_slab = query_weight[0]
    output_slab = output_weight[0]
    if quarter_count > 1:
        first = (ctx_index % quarter_count) * head_width
        key_weight = lax.dynamic_slice_in_dim(key_weight, first, head_width, axis=1)
        value_weight = lax.dynamic_slice_in_dim(value_weight, first, head_width, axis=1)

    normed = norm_rows(tokens, norm_gain)
    half = tok_count // 2

    pair_count = tok_count * TOPK
    slot_total = EXPERTS * MOST
    flat_expert = routes.reshape(pair_count)
    onehot = (flat_expert[:, None] == jnp.arange(EXPERTS, dtype=jnp.int32)[None, :]).astype(
        jnp.int32
    )
    slot_rank = jnp.sum((jnp.cumsum(onehot, axis=0) - 1) * onehot, axis=1)
    slot_index = flat_expert * MOST + slot_rank
    chosen_mask = slot_index[None, :] == jnp.arange(slot_total, dtype=jnp.int32)[:, None]
    pair_token = jnp.arange(pair_count, dtype=jnp.int32) // TOPK
    slot_token = jnp.max(jnp.where(chosen_mask, pair_token[None, :], -1), axis=1)
    send_token = jnp.repeat(slot_token.reshape(EXPERTS, MOST), quarter_count, axis=0)
    got_token = lax.all_to_all(send_token, "ctx", split_axis=0, concat_axis=0, tiled=True)
    wanted = jnp.pad(got_token, ((0, 0), (0, SLOTS - MOST)), constant_values=-1)[:, :, None]
    source = jnp.arange(ctx_count, dtype=jnp.int32)[:, None] * exp_count + exp_index
    positions = (got_token + source * tok_count).reshape(ctx_count * MOST, 1)

    plan, queries, own, other = [], [], [], []

    def serve(blocks, offsets):
        panel, query = project(blocks, offsets, wanted, key_weight, value_weight, query_slab)
        plan.append(offsets)
        queries.append(query)
        own.append(panel)
        other.append(lax.ppermute(panel, "exp", sibling))

    serve([normed], [0])
    ahead = behind = normed
    steps = ctx_count // 2
    for step in range(1, steps):
        ahead = lax.ppermute(ahead, "ctx", forward)
        behind = lax.ppermute(behind, "ctx", backward)
        serve([ahead, behind], [-step, step])
    one = lax.ppermute(ahead[:half], "ctx", forward)
    two = lax.ppermute(behind[half:], "ctx", backward)
    serve([one, two], [steps])

    attended = attend(plan, positions, queries, own, other)
    pieces = jnp.dot(attended, output_slab, preferred_element_type=jnp.float32).astype(
        jnp.bfloat16
    )
    returned = lax.all_to_all(
        pieces.reshape(ctx_count, MOST, model_width), "ctx", split_axis=0, concat_axis=0, tiled=True
    )

    logits = jnp.dot(normed.astype(jnp.float32), router_weight, precision=lax.Precision.HIGHEST)
    gating = jax.nn.softmax(jnp.take_along_axis(logits, routes, axis=1), axis=1)
    summed = (
        returned.astype(jnp.float32).reshape(EXPERTS, quarter_count, MOST, model_width).sum(axis=1)
    )
    summed = summed.reshape(slot_total, model_width)
    gate_flat = gating.reshape(pair_count)
    combine_mat = (
        jnp.where(chosen_mask, gate_flat[None, :], 0.0)
        .reshape(slot_total, tok_count, TOPK)
        .sum(axis=2)
    )
    combined = lax.dot_general(
        combine_mat, summed, (((0,), (0,)), ((), ())), precision=lax.Precision.HIGHEST
    )
    return combined.astype(jnp.bfloat16)


def solution(mesh):
    in_specs = (
        P(("groups", "ctx", "exp"), None),
        P(),
        P(),
        P(("groups", "ctx", "exp"), None),
        P(),
        P(),
        P("ctx", None, None),
        P("ctx", None, None),
    )
    out_specs = P(("groups", "ctx", "exp"), None)
    return jax.shard_map(
        per_device, mesh=mesh, in_specs=in_specs, out_specs=out_specs, check_vma=False
    )
```

time: 198 us -> 144 us (0.73)
  Pallas kernels: 18.9 us -> 44.8 us
  matrix products: 25.2 us -> 4.97 us
  between operations: 17.8 us -> 0.25 us
  starting transfers between devices: 29.6 us -> 13.4 us
  local copies, waits for them, and re-layouts: 26.2 us -> 12 us
  blocking collectives: 0 us -> 14 us
  other arithmetic: 15.4 us -> 1.57 us
  waiting for transfers between devices: 64.9 us -> 52.2 us
    pallas_call x1 -> x7, Pallas kernels: 18.9 us -> 44.8 us  [the longest x5 31.2 us: project(): pl.pallas_call(functools.partial(project_kernel, offsets, len(blocks)), g...]
    dot_general x12 -> x0, matrix products: 20.2 us -> none  [the longest x5 7.66 us: project(): values = jnp.dot(rows, value_weight, preferred_element_type=jnp.float32)]
    all_to_all x0 -> x1, blocking collectives: none -> 14 us  [per_device(): lax.all_to_all(send_token, 'ctx', split_axis=0, concat_axis=0, tiled=True)]
    ppermute x19 -> x13, waiting for transfers between devices: 36 us -> 23 us  [the longest x3 20.5 us: per_device(): behind = lax.ppermute(behind, 'ctx', backward)]
    dynamic_update_slice x15 -> x0, other arithmetic: 12.7 us -> none  [the longest x8 6.55 us: place_blocks(): lax.dynamic_update_slice(all_panels, own[:, None, None, part], (0, owner,...]
    ppermute x19 -> x13, starting transfers between devices: 18.6 us -> 9.84 us  [the longest x3 6.02 us: per_device(): behind = lax.ppermute(behind, 'ctx', backward)]
    unnamed x33 -> x31, local copies, waits for them, and re-layouts: 0.73 us -> 8.33 us
    dynamic_update_slice x9 -> x0, local copies, waits for them, and re-layouts: 7.51 us -> none  [the longest x8 6.64 us: place_blocks(): lax.dynamic_update_slice(all_panels, others[:, None, None, part], (0, own...]
  transfers between devices with their start and end apart: 21 -> 14, of which waited for: 7 -> 6; matrix products, arithmetic and copies ran while one was open for 25% -> 4% of each run, Pallas kernels for 0% -> 22%
where the time goes in v2:
time: 144 us; the launch traced here: 143 us
  waiting for transfers between devices  52.2 us (36%)
  Pallas kernels  44.8 us (31%)
  blocking collectives  14 us (10%)
  starting transfers between devices  13.4 us (9%)
  local copies, waits for them, and re-layouts  12 us (8%)
  matrix products  4.97 us (3%)
  other arithmetic  1.57 us (1%)
    pallas_call x5, Pallas kernels, project(): pl.pallas_call(functools.partial(project_kernel, offsets, len(blocks)), g...  31.2 us
    all_to_all x1, waiting for transfers between devices, per_device(): lax.all_to_all(pieces.reshape(ctx_count, MOST, model_width), 'ctx', split...  29.1 us
    ppermute x3, waiting for transfers between devices, per_device(): behind = lax.ppermute(behind, 'ctx', backward)  20.5 us
    all_to_all x1, blocking collectives, per_device(): lax.all_to_all(send_token, 'ctx', split_axis=0, concat_axis=0, tiled=True)  14 us
    pallas_call x1, Pallas kernels, attend(): pl.pallas_call(functools.partial(attend_kernel, plan, tok_count), grid=(h...  11.5 us
    unnamed x31, local copies, waits for them, and re-layouts  8.33 us
    ppermute x3, starting transfers between devices, per_device(): behind = lax.ppermute(behind, 'ctx', backward)  6.02 us
    all_to_all x1, starting transfers between devices, per_device(): lax.all_to_all(pieces.reshape(ctx_count, MOST, model_width), 'ctx', split...  3.57 us
  transfers between devices with their start and end apart: 14, of which 6 were waited for; matrix products, arithmetic and copies ran while one was open for 4% of the time, Pallas kernels for 22%

profile of v2, /device:TPU:0, one launch (start us, length us, event | category | flops | bytes accessed | tf_op | source)
XLA Modules:
  0.0 143.2 jit_solution(17652266074440592545)
XLA Ops:
  0.0 2.1 %norm_rows.1.refs_0_ = bf16[128,2048]{1,0:T(8,128)(2,1)} custom-call(bf16[128,2048]{1,0:T(8,128)(2,1)} %tokens_ref.1, f32[1,2048]{1,0:T(1,128)} %bitcast.34), custom_call_target="tpu_custom_call" | custom-call | tf_op jit(solution)/shard_map/norm_rows/pallas_call | solution.py:41
  2.1 3.0 %collective-permute-start.1 = (bf16[128,2048]{1,0:T(8,128)(2,1)}, bf16[128,2048]{1,0:T(8,128)(2,1)S(1)}, u32[]{:S(2)}, u32[]{:S(2)}) collective-permute-start(bf16[128,2048]{1,0:T(8,128)(2,1)} %norm_rows.1.refs_0_), channel_id=1, source_target_pairs={{4,0},{8,4},{12,8},{14,12},{10,14},{6,10},{2,6},{0,2},{5,1},{9,5},... | collective-permute-start | bytes 1572872 | tf_op jit(solution)/shard_map/ppermute | solution.py:256
  5.1 0.1 collective-permute-start
  5.1 12.1 %collective-permute-done.1.refs_1_ = bf16[128,2048]{1,0:T(8,128)(2,1)S(1)} collective-permute-done((bf16[128,2048]{1,0:T(8,128)(2,1)}, bf16[128,2048]{1,0:T(8,128)(2,1)S(1)}, u32[]{:S(2)}, u32[]{:S(2)}) %collective-permute-start.1) | collective-permute-done | bytes 524320 | tf_op jit(solution)/shard_map/ppermute | solution.py:256
  17.3 1.7 %collective-permute-start.3 = (bf16[128,2048]{1,0:T(8,128)(2,1)S(1)}, bf16[128,2048]{1,0:T(8,128)(2,1)S(1)}, u32[]{:S(2)}, u32[]{:S(2)}) collective-permute-start(bf16[128,2048]{1,0:T(8,128)(2,1)S(1)} %collective-permute-done.1.refs_1_), channel_id=1, source_target_pairs={{4,0},{8,4},{12,8},{14,12},{10,14},{6,10},{2,6},{0,2},{5,1},{9,5},... | collective-permute-start | bytes 1572872 | tf_op jit(solution)/shard_map/ppermute | solution.py:256
  18.9 0.3 collective-permute-start.2
  19.3 0.8 copy-done.3
  20.1 0.8 copy.61
  20.9 0.1 eq.45
  21.0 0.1 eq.49
  21.2 0.6 reduce-window.6
  21.7 0.2 slice_reduce_fusion
  22.0 8.4 %collective-permute-done.3.refs_1_ = bf16[128,2048]{1,0:T(8,128)(2,1)S(1)} collective-permute-done((bf16[128,2048]{1,0:T(8,128)(2,1)S(1)}, bf16[128,2048]{1,0:T(8,128)(2,1)S(1)}, u32[]{:S(2)}, u32[]{:S(2)}) %collective-permute-start.3) | collective-permute-done | bytes 524320 | tf_op jit(solution)/shard_map/ppermute | solution.py:256
  30.4 1.4 collective-permute-start.5
  31.7 0.0 collective-permute-done.2.refs_0_
  31.7 0.7 collective-permute-start.4
  32.4 0.1 fusion.5
  32.5 0.1 select_reduce_fusion
  32.6 0.1 all_to_all.13
  32.7 14.0 %all_to_all.20 = s32[8,1,40]{2,1,0:T(1,128)S(1)} all-to-all(s32[8,1,40]{2,1,0:T(1,128)S(1)} %all_to_all.13), channel_id=1, replica_groups=mesh['groups'=2,'ctx'=8,'exp'=2] {'ctx'}, dimensions={0} | all-to-all | bytes 2560 | tf_op jit(solution)/shard_map/all_to_all | solution.py:237
  46.7 0.1 copy.66.token_ref
  46.9 1.0 copy-done.4
  47.9 6.6 %project.6 = (bf16[2,256,1024]{2,1,0:T(8,128)(2,1)S(1)}, bf16[2,48,1024]{2,1,0:T(8,128)(2,1)S(1)}) custom-call(s32[8,48,1]{2,1,0:T(8,128)S(1)} %copy.66.token_ref, bf16[128,2048]{1,0:T(8,128)(2,1)S(1)} %copy-done.4, bf16[128,2048]{1,0:T(8,128)(2,1)S(1)} %collective-permute-done.1.refs_1_, bf16[2048,1024]{1,0:T(8,128)(2,1)} %refs_2_.9, ...), custom_call_target="tpu_custom_call" | custom-call | tf_op jit(solution)/shard_map/project/pallas_call | solution.py:82
  54.5 0.7 copy-done.5
  55.2 0.0 collective-permute-start.9
  55.2 7.7 %project.7 = (bf16[2,256,1024]{2,1,0:T(8,128)(2,1)}, bf16[2,48,1024]{2,1,0:T(8,128)(2,1)S(1)}) custom-call(s32[8,48,1]{2,1,0:T(8,128)S(1)} %copy.66.token_ref, bf16[128,2048]{1,0:T(8,128)(2,1)} %collective-permute-done.2.refs_0_, bf16[128,2048]{1,0:T(8,128)(2,1)S(1)} %collective-permute-done.3.refs_1_, bf16[2048,1024]{1,0:T(8,128)(2,1)} %refs_2_.9, ...), custom_call_target="tpu_custom_call" | custom-call | tf_op jit(solution)/shard_map/project/pallas_call | solution.py:82
  62.9 0.7 copy-done.7
  63.6 0.5 collective-permute-start.10
  64.1 7.3 %project.8 = (bf16[2,256,1024]{2,1,0:T(8,128)(2,1)}, bf16[2,48,1024]{2,1,0:T(8,128)(2,1)S(1)}) custom-call(s32[8,48,1]{2,1,0:T(8,128)S(1)} %copy.66.token_ref, bf16[128,2048]{1,0:T(8,128)(2,1)S(1)} %collective-permute-done.4.refs_0_, bf16[128,2048]{1,0:T(8,128)(2,1)S(1)} %collective-permute-done.5.refs_1_, bf16[2048,1024]{1,0:T(8,128)(2,1)} %refs_2_.9, ...), custom_call_target="tpu_custom_call" | custom-call | tf_op jit(solution)/shard_map/project/pallas_call | solution.py:82
  71.4 0.6 collective-permute-start.7
  72.0 0.0 copy-done.9
  72.0 1.5 %collective-permute-start.6 = (bf16[64,2048]{1,0:T(8,128)(2,1)S(1)}, bf16[64,2048]{1,0:T(8,128)(2,1)S(1)}, u32[]{:S(2)}, u32[]{:S(2)}) collective-permute-start(bf16[64,2048]{1,0:T(8,128)(2,1)S(1)} %slice.19), channel_id=1, source_target_pairs={{0,4},{4,8},{8,12},{12,14},{14,10},{10,6},{6,2},{2,0},{1,5},{5,9},... | collective-permute-start | bytes 786440 | tf_op jit(solution)/shard_map/ppermute | solution.py:258
  73.5 4.8 %project.5 = (bf16[2,128,1024]{2,1,0:T(8,128)(2,1)S(1)}, bf16[1,48,1024]{2,1,0:T(8,128)(2,1)S(1)}) custom-call(s32[8,48,1]{2,1,0:T(8,128)S(1)} %copy.66.token_ref, bf16[128,2048]{1,0:T(8,128)(2,1)S(1)} %copy-done.2, bf16[2048,1024]{1,0:T(8,128)(2,1)S(1)} %copy-done.1, bf16[2048,1024]{1,0:T(8,128)(2,1)} %refs_3_.7, bf16[2048,1024]{1,0:T(8,128)(2,1)} %bitcast.30), custom_call_target="tpu_custom_call" | custom-call | tf_op jit(solution)/shard_map/project/pallas_call | solution.py:82
  78.4 1.8 %collective-permute-done.7.refs_1_ = bf16[64,2048]{1,0:T(8,128)(2,1)S(1)} collective-permute-done((bf16[64,2048]{1,0:T(8,128)(2,1)S(1)}, bf16[64,2048]{1,0:T(8,128)(2,1)S(1)}, u32[]{:S(2)}, u32[]{:S(2)}) %collective-permute-start.7) | collective-permute-done | bytes 262176 | tf_op jit(solution)/shard_map/ppermute | solution.py:259
  80.1 0.4 collective-permute-done.6.refs_0_
  80.5 4.8 %project.9 = (bf16[2,128,1024]{2,1,0:T(8,128)(2,1)S(1)}, bf16[1,48,1024]{2,1,0:T(8,128)(2,1)S(1)}) custom-call(s32[8,48,1]{2,1,0:T(8,128)S(1)} %copy.66.token_ref, bf16[64,2048]{1,0:T(8,128)(2,1)S(1)} %collective-permute-done.6.refs_0_, bf16[64,2048]{1,0:T(8,128)(2,1)S(1)} %collective-permute-done.7.refs_1_, bf16[2048,1024]{1,0:T(8,128)(2,1)S(1)} %copy-done.1, ...), custom_call_target="tpu_custom_call" | custom-call | tf_op jit(solution)/shard_map/project/pallas_call | solution.py:82
  85.3 0.0 copy-start.11
  85.4 0.6 copy-done.11
  86.0 0.1 collective-permute-start.12
  86.1 0.1 add.62
  86.2 0.1 add.63
  86.3 0.5 broadcast.139
  86.8 0.6 reduce.5
  87.4 0.1 all_to_all.15
  87.5 0.1 copy.71.pos_ref
  87.6 0.4 collective-permute-done.12.refs_14_
  88.0 0.9 copy-done.6
  89.0 0.9 copy-done.8
  89.9 0.9 copy-done.10
  90.8 0.9 copy-done.12
  91.7 11.5 %attend.1 = bf16[320,1024]{1,0:T(8,128)(2,1)S(1)} custom-call(s32[320,1]{1,0:T(8,128)S(1)} %copy.71.pos_ref, bf16[1,48,1024]{2,1,0:T(8,128)(2,1)S(1)} %get-tuple-element.15.refs_0_, bf16[2,48,1024]{2,1,0:T(8,128)(2,1)S(1)} %copy-done.6, bf16[2,48,1024]{2,1,0:T(8,128)(2,1)S(1)} %copy-done.8, bf16[2,48,1024]{2,1,0:T(8,128)(2,1)S(1)} %copy-done.10, ...), custom_call_target="tpu_custom_call" | custom-call | tf_op jit(solution)/shard_map/attend/pallas_call | solution.py:180
  103.3 0.0 copy-start.13
  103.3 2.6 %fusion.2 = bf16[320,2048]{1,0:T(8,128)(2,1)} fusion(bf16[320,1024]{1,0:T(8,128)(2,1)S(1)} %attend.1, bf16[1,1024,2048]{2,1,0:T(8,128)(2,1)S(1)} %copy-done.14), kind=kOutput, calls=%fused_computation.3 | convolution fusion | flops 1342832640 | bytes 6160384 | tf_op jit(solution)/shard_map/dot_general | solution.py:263
  105.9 3.6 %all-to-all-start.1 = ((bf16[8,40,2048]{2,1,0:T(8,128)(2,1)}), bf16[8,40,2048]{2,1,0:T(8,128)(2,1)S(1)}, u32[]{:S(2)}, u32[]{:S(2)}) async-start(bf16[8,40,2048]{2,1,0:T(8,128)(2,1)} %bitcast.8), calls=%async_computation.1 | async-start | bytes 2621440 | tf_op jit(solution)/shard_map/all_to_all | solution.py:266
  109.5 0.1 reduce_sum.34
  109.6 0.1 copy.64
  109.8 0.1 reshape.138
  109.9 0.1 copy.63
  110.0 0.5 fusion.10
  110.5 1.4 gather_fusion
  111.9 0.1 reshape.141
  112.0 0.1 copy.65
  112.2 29.1 %all-to-all-done.1 = bf16[8,40,2048]{2,1,0:T(8,128)(2,1)S(1)} async-done(((bf16[8,40,2048]{2,1,0:T(8,128)(2,1)}), bf16[8,40,2048]{2,1,0:T(8,128)(2,1)S(1)}, u32[]{:S(2)}, u32[]{:S(2)}) %all-to-all-start.1) | async-done | bytes 1310752 | tf_op jit(solution)/shard_map/all_to_all | solution.py:266
  141.3 1.8 %convolution_convert_fusion = bf16[128,2048]{1,0:T(8,128)(2,1)} fusion(f32[320,128]{1,0:T(8,128)S(1)} %select_reduce_fusion.1, bf16[320,2048]{1,0:T(8,128)(2,1)S(1)} %bitcast.32), kind=kOutput, calls=%fused_computation.4 | convolution fusion | flops 1006895104 | bytes 1998848 | tf_op jit(solution)/shard_map/dot_general | solution.py:282
  (42 shorter events, 0.3 us)
Async XLA Ops:
  0.0 110.0 %copy-start = (f32[2048,8]{0,1:T(8,128)S(1)}, f32[2048,8]{0,1:T(8,128)}, u32[]{:S(2)}) copy-start(f32[2048,8]{0,1:T(8,128)} %param.10) | copy-start | bytes 196612
  2.1 15.2 %collective-permute-start.1 = (bf16[128,2048]{1,0:T(8,128)(2,1)}, bf16[128,2048]{1,0:T(8,128)(2,1)S(1)}, u32[]{:S(2)}, u32[]{:S(2)}) collective-permute-start(bf16[128,2048]{1,0:T(8,128)(2,1)} %norm_rows.1.refs_0_), channel_id=1, source_target_pairs={{4,0},{8,4},{12,8},{14,12},{10,14},{6,10},{2,6},{0,2},{5,1},{9,5},... | collective-permute-start | bytes 1572872 | tf_op jit(solution)/shard_map/ppermute | solution.py:256
  5.1 13.9 %collective-permute-start = (bf16[128,2048]{1,0:T(8,128)(2,1)}, bf16[128,2048]{1,0:T(8,128)(2,1)S(1)}, u32[]{:S(2)}, u32[]{:S(2)}) collective-permute-start(bf16[128,2048]{1,0:T(8,128)(2,1)} %norm_rows.1.refs_0_), channel_id=1, source_target_pairs={{0,4},{4,8},{8,12},{12,14},{14,10},{10,6},{6,2},{2,0},{1,5},{5,9},... | collective-permute-start | bytes 1572872 | tf_op jit(solution)/shard_map/ppermute | solution.py:255
  17.3 13.1 %collective-permute-start.3 = (bf16[128,2048]{1,0:T(8,128)(2,1)S(1)}, bf16[128,2048]{1,0:T(8,128)(2,1)S(1)}, u32[]{:S(2)}, u32[]{:S(2)}) collective-permute-start(bf16[128,2048]{1,0:T(8,128)(2,1)S(1)} %collective-permute-done.1.refs_1_), channel_id=1, source_target_pairs={{4,0},{8,4},{12,8},{14,12},{10,14},{6,10},{2,6},{0,2},{5,1},{9,5},... | collective-permute-start | bytes 1572872 | tf_op jit(solution)/shard_map/ppermute | solution.py:256
  18.9 12.8 %collective-permute-start.2 = (bf16[128,2048]{1,0:T(8,128)(2,1)S(1)}, bf16[128,2048]{1,0:T(8,128)(2,1)}, u32[]{:S(2)}, u32[]{:S(2)}) collective-permute-start(bf16[128,2048]{1,0:T(8,128)(2,1)S(1)} %collective-permute-done.refs_0_), channel_id=1, source_target_pairs={{0,4},{4,8},{8,12},{12,14},{14,10},{10,6},{6,2},{2,0},{1,5},{5,9},... | collective-permute-start | bytes 1572872 | tf_op jit(solution)/shard_map/ppermute | solution.py:255
  19.3 0.8 copy-start.3
  30.4 33.7 %collective-permute-start.5 = (bf16[128,2048]{1,0:T(8,128)(2,1)S(1)}, bf16[128,2048]{1,0:T(8,128)(2,1)S(1)}, u32[]{:S(2)}, u32[]{:S(2)}) collective-permute-start(bf16[128,2048]{1,0:T(8,128)(2,1)S(1)} %collective-permute-done.3.refs_1_), channel_id=1, source_target_pairs={{4,0},{8,4},{12,8},{14,12},{10,14},{6,10},{2,6},{0,2},{5,1},{9,5},... | collective-permute-start | bytes 1572872 | tf_op jit(solution)/shard_map/ppermute | solution.py:256
  31.7 32.4 %collective-permute-start.4 = (bf16[128,2048]{1,0:T(8,128)(2,1)}, bf16[128,2048]{1,0:T(8,128)(2,1)S(1)}, u32[]{:S(2)}, u32[]{:S(2)}) collective-permute-start(bf16[128,2048]{1,0:T(8,128)(2,1)} %collective-permute-done.2.refs_0_), channel_id=1, source_target_pairs={{0,4},{4,8},{8,12},{12,14},{14,10},{10,6},{6,2},{2,0},{1,5},{5,9},... | collective-permute-start | bytes 1572872 | tf_op jit(solution)/shard_map/ppermute | solution.py:255
  46.9 1.0 copy-start.4
  54.5 0.7 copy-start.5
  55.2 32.5 %collective-permute-start.9 = (bf16[2,256,1024]{2,1,0:T(8,128)(2,1)S(1)}, bf16[2,256,1024]{2,1,0:T(8,128)(2,1)}, u32[]{:S(2)}, u32[]{:S(2)}) collective-permute-start(bf16[2,256,1024]{2,1,0:T(8,128)(2,1)S(1)} %get-tuple-element.21.refs_6_), channel_id=1, source_target_pairs={{0,1},{1,0},{2,3},{3,2},{4,5},{5,4},{6,7},{7,6},{8,9},{9,8},{10,11... | collective-permute-start | bytes 3145736 | tf_op jit(solution)/shard_map/ppermute | solution.py:249
  62.9 0.7 copy-start.7
  63.6 10.0 %copy-start.1 = (bf16[2048,1024]{1,0:T(8,128)(2,1)S(1)}, bf16[2048,1024]{1,0:T(8,128)(2,1)}, u32[]{:S(2)}) copy-start(bf16[2048,1024]{1,0:T(8,128)(2,1)} %refs_2_.9) | copy-start | bytes 12582916
  63.6 10.0 %copy-start.2 = (bf16[128,2048]{1,0:T(8,128)(2,1)S(1)}, bf16[128,2048]{1,0:T(8,128)(2,1)}, u32[]{:S(2)}) copy-start(bf16[128,2048]{1,0:T(8,128)(2,1)} %norm_rows.1.refs_0_) | copy-start | bytes 1572868
  63.6 24.1 %collective-permute-start.10 = (bf16[2,256,1024]{2,1,0:T(8,128)(2,1)}, bf16[2,256,1024]{2,1,0:T(8,128)(2,1)}, u32[]{:S(2)}, u32[]{:S(2)}) collective-permute-start(bf16[2,256,1024]{2,1,0:T(8,128)(2,1)} %get-tuple-element.22.refs_7_), channel_id=1, source_target_pairs={{0,1},{1,0},{2,3},{3,2},{4,5},{5,4},{6,7},{7,6},{8,9},{9,8},{10,11... | collective-permute-start | bytes 3145736 | tf_op jit(solution)/shard_map/ppermute | solution.py:249
  71.3 0.7 copy-start.9
  71.3 16.7 %collective-permute-start.11 = (bf16[2,256,1024]{2,1,0:T(8,128)(2,1)}, bf16[2,256,1024]{2,1,0:T(8,128)(2,1)}, u32[]{:S(2)}, u32[]{:S(2)}) collective-permute-start(bf16[2,256,1024]{2,1,0:T(8,128)(2,1)} %get-tuple-element.23.refs_8_), channel_id=1, source_target_pairs={{0,1},{1,0},{2,3},{3,2},{4,5},{5,4},{6,7},{7,6},{8,9},{9,8},{10,11... | collective-permute-start | bytes 3145736 | tf_op jit(solution)/shard_map/ppermute | solution.py:249
  71.4 8.8 %collective-permute-start.7 = (bf16[64,2048]{1,0:T(8,128)(2,1)S(1)}, bf16[64,2048]{1,0:T(8,128)(2,1)S(1)}, u32[]{:S(2)}, u32[]{:S(2)}) collective-permute-start(bf16[64,2048]{1,0:T(8,128)(2,1)S(1)} %slice.20), channel_id=1, source_target_pairs={{4,0},{8,4},{12,8},{14,12},{10,14},{6,10},{2,6},{0,2},{5,1},{9,5},... | collective-permute-start | bytes 786440 | tf_op jit(solution)/shard_map/ppermute | solution.py:259
  72.0 8.5 %collective-permute-start.6 = (bf16[64,2048]{1,0:T(8,128)(2,1)S(1)}, bf16[64,2048]{1,0:T(8,128)(2,1)S(1)}, u32[]{:S(2)}, u32[]{:S(2)}) collective-permute-start(bf16[64,2048]{1,0:T(8,128)(2,1)S(1)} %slice.19), channel_id=1, source_target_pairs={{0,4},{4,8},{8,12},{12,14},{14,10},{10,6},{6,2},{2,0},{1,5},{5,9},... | collective-permute-start | bytes 786440 | tf_op jit(solution)/shard_map/ppermute | solution.py:258
  80.1 7.5 %collective-permute-start.8 = (bf16[2,128,1024]{2,1,0:T(8,128)(2,1)S(1)}, bf16[2,128,1024]{2,1,0:T(8,128)(2,1)S(1)}, u32[]{:S(2)}, u32[]{:S(2)}) collective-permute-start(bf16[2,128,1024]{2,1,0:T(8,128)(2,1)S(1)} %get-tuple-element.20.refs_5_), channel_id=1, source_target_pairs={{0,1},{1,0},{2,3},{3,2},{4,5},{5,4},{6,7},{7,6},{8,9},{9,8},{10,11... | collective-permute-start | bytes 1572872 | tf_op jit(solution)/shard_map/ppermute | solution.py:249
  85.3 0.6 copy-start.11
  86.0 2.0 %collective-permute-start.12 = (bf16[2,128,1024]{2,1,0:T(8,128)(2,1)S(1)}, bf16[2,128,1024]{2,1,0:T(8,128)(2,1)}, u32[]{:S(2)}, u32[]{:S(2)}) collective-permute-start(bf16[2,128,1024]{2,1,0:T(8,128)(2,1)S(1)} %get-tuple-element.24.refs_9_), channel_id=1, source_target_pairs={{0,1},{1,0},{2,3},{3,2},{4,5},{5,4},{6,7},{7,6},{8,9},{9,8},{10,11... | collective-permute-start | bytes 1572872 | tf_op jit(solution)/shard_map/ppermute | solution.py:249
  88.0 0.9 copy-start.6
  89.0 0.9 copy-start.8
  89.9 0.9 copy-start.10
  90.8 0.9 copy-start.12
  91.7 11.5 %copy-start.14 = (bf16[1,1024,2048]{2,1,0:T(8,128)(2,1)S(1)}, bf16[1,1024,2048]{2,1,0:T(8,128)(2,1)}, u32[]{:S(2)}) copy-start(bf16[1,1024,2048]{2,1,0:T(8,128)(2,1)} %param.15) | copy-start | bytes 12582916
  103.3 6.4 %copy-start.13 = (s32[128,2]{0,1:T(2,128)S(1)}, s32[128,2]{0,1:T(2,128)}, u32[]{:S(2)}) copy-start(s32[128,2]{0,1:T(2,128)} %param.11) | copy-start | bytes 3076
  105.9 35.4 %all-to-all-start.1 = ((bf16[8,40,2048]{2,1,0:T(8,128)(2,1)}), bf16[8,40,2048]{2,1,0:T(8,128)(2,1)S(1)}, u32[]{:S(2)}, u32[]{:S(2)}) async-start(bf16[8,40,2048]{2,1,0:T(8,128)(2,1)} %bitcast.8), calls=%async_computation.1 | async-start | bytes 2621440 | tf_op jit(solution)/shard_map/all_to_all | solution.py:266

commit v3 on v2

v3 whole, which is shorter than its diff:
```python
import functools
import math

import jax
import jax.numpy as jnp
from jax import lax
from jax.experimental import pallas as pl
from jax.experimental.pallas import tpu as pltpu
from jax.sharding import PartitionSpec as P

HS = 128
EXPERTS = 8
MOST = 40
SLOTS = 48
MASKED = -1e30
LANES = 128
MIB = 1 << 20


def ring_rank(place, count):
    place = lax.rem(place + 2 * count, count)
    return jnp.where(place < count // 2, 2 * place, 2 * (count - 1 - place) + 1)


def ring_place(rank, count):
    return jnp.where(rank % 2 == 0, rank // 2, count - 1 - rank // 2)


def ring_owner(offset):
    count = lax.axis_size("ctx")
    return ring_rank(ring_place(lax.axis_index("ctx"), count) + offset, count)


def norm_kernel(tokens_ref, gain_ref, routes_ref, top_ref, bottom_ref):
    floats = tokens_ref[...].astype(jnp.float32)
    count, width = floats.shape
    factor = lax.rsqrt(jnp.mean(floats * floats, axis=1, keepdims=True) + 1e-06)
    normed = (floats * factor * gain_ref[...]).astype(jnp.bfloat16)
    expert = lax.broadcasted_iota(jnp.int32, (LANES, count), 0)
    named = (expert == routes_ref[0:1, :]) | (expert == routes_ref[1:2, :])
    before = lax.broadcasted_iota(jnp.int32, (count, count), 0) < lax.broadcasted_iota(
        jnp.int32, (count, count), 1
    )
    rank = jnp.dot(
        named.astype(jnp.bfloat16),
        before.astype(jnp.bfloat16),
        preferred_element_type=jnp.float32,
    )
    slots = jnp.where(named, rank, -1.0).T.astype(jnp.bfloat16)
    half = count // 2
    for ref, part in ((top_ref, slice(0, half)), (bottom_ref, slice(half, count))):
        ref[:, :width] = normed[part]
        ref[:, width:] = slots[part]


def norm_rows(tokens, norm_gain, routes):
    count, width = tokens.shape
    half = jax.ShapeDtypeStruct((count // 2, width + LANES), jnp.bfloat16)
    return pl.pallas_call(
        norm_kernel, out_shape=[half, half], name="norm_rows"
    )(tokens, norm_gain.reshape(1, -1), routes.T)


def project_kernel(offsets, count, experts, *refs):
    blocks = refs[:count]
    key_ref, value_ref, query_ref, panel_ref, out_ref, pos_ref, picked = refs[count:]
    width = key_ref.shape[0]
    rows = jnp.concatenate([block[:, :width] for block in blocks], axis=0)
    tok_count = rows.shape[0] // len(offsets)

    @pl.when(pl.program_id(0) == 0)
    def _():
        slots = jnp.concatenate([block[:, width:] for block in blocks], axis=0)
        slots = slots.astype(jnp.float32)
        expert = lax.axis_index("ctx") // (lax.axis_size("ctx") // experts)
        lane = lax.broadcasted_iota(jnp.int32, slots.shape, 1)
        slot = jnp.sum(jnp.where(lane == expert, slots, 0.0), axis=1, keepdims=True)
        select = (slot == lane.astype(jnp.float32)).astype(jnp.float32)
        number = lax.broadcasted_iota(jnp.int32, (tok_count, LANES), 0).astype(jnp.bfloat16)
        for g, offset in enumerate(offsets):
            part = slice(g * tok_count, (g + 1) * tok_count)
            chosen = select[part].T[:SLOTS].astype(jnp.bfloat16)
            picked[pl.ds(g * SLOTS, SLOTS), :] = jnp.dot(
                chosen, rows[part], preferred_element_type=jnp.float32
            ).astype(jnp.bfloat16)
            start = (ring_owner(offset) * lax.axis_size("exp") + lax.axis_index("exp")) * tok_count
            pos_ref[g] = jnp.dot(
                chosen, number, preferred_element_type=jnp.float32
            ) + start.astype(jnp.float32)

    panel_ref[0] = jnp.dot(
        rows, key_ref[...], preferred_element_type=jnp.float32
    ).astype(jnp.bfloat16)
    panel_ref[1] = jnp.dot(
        rows, value_ref[...], preferred_element_type=jnp.float32
    ).astype(jnp.bfloat16)
    queries = jnp.dot(picked[...], query_ref[...], preferred_element_type=jnp.float32)
    for g in range(len(offsets)):
        out_ref[g] = queries[g * SLOTS : (g + 1) * SLOTS].astype(jnp.bfloat16)


def project(blocks, offsets, key_weight, value_weight, query_slab):
    row_count = sum(block.shape[0] for block in blocks)
    model_width, width = key_weight.shape
    step = min(width, 256)
    owners = len(offsets)
    weight_spec = pl.BlockSpec((model_width, step), lambda n: (0, n))
    return pl.pallas_call(
        functools.partial(project_kernel, offsets, len(blocks), EXPERTS),
        grid=(width // step,),
        in_specs=[pl.BlockSpec(block.shape, lambda n: (0, 0)) for block in blocks]
        + [weight_spec] * 3,
        out_specs=[
            pl.BlockSpec((2, row_count, step), lambda n: (0, 0, n)),
            pl.BlockSpec((owners, SLOTS, step), lambda n: (0, 0, n)),
            pl.BlockSpec((owners, SLOTS, LANES), lambda n: (0, 0, 0)),
        ],
        out_shape=[
            jax.ShapeDtypeStruct((2, row_count, width), jnp.bfloat16),
            jax.ShapeDtypeStruct((owners, SLOTS, width), jnp.bfloat16),
            jax.ShapeDtypeStruct((owners, SLOTS, LANES), jnp.float32),
        ],
        scratch_shapes=[pltpu.VMEM((owners * SLOTS, model_width), jnp.bfloat16)],
        compiler_params=pltpu.CompilerParams(vmem_limit_bytes=20 * MIB),
        name="project",
    )(*blocks, key_weight, value_weight, query_slab)


def attend_kernel(plan, tok_count, heads, *refs):
    count = len(plan)
    query_refs, pos_refs, own_refs, other_refs = (
        refs[k * count : (k + 1) * count] for k in range(4)
    )
    out_ref, places, queries, keys, values, scores, weights = refs[4 * count :]
    side = lax.axis_index("exp")
    exp_count = 2
    rate = math.log2(math.e) / math.sqrt(HS)
    tile = 2 * MOST
    per_span = 2 * exp_count
    span = per_span * tok_count
    tiles = queries.shape[1] // 2
    group = min(tiles, 4)

    @pl.when(pl.program_id(0) == 0)
    def _():
        for offsets, pos_ref in zip(plan, pos_refs):
            for g, offset in enumerate(offsets):
                places[ring_owner(offset)] = pos_ref[g, :MOST]

    for offsets, query_ref, own_ref, other_ref in zip(plan, query_refs, own_refs, other_refs):
        for g, offset in enumerate(offsets):
            owner = ring_owner(offset)
            part = pl.ds(g * tok_count, tok_count)
            for h in range(heads):
                lanes = pl.ds(h * HS, HS)
                queries[h, owner] = query_ref[g, :, lanes].astype(jnp.float32)[:MOST]
                keys[h, owner * exp_count + side] = own_ref[0, part, lanes]
                values[h, owner * exp_count + side] = own_ref[1, part, lanes]
                keys[h, owner * exp_count + 1 - side] = other_ref[0, part, lanes]
                values[h, owner * exp_count + 1 - side] = other_ref[1, part, lanes]

    for lead in range(0, tiles, group):
        top = lead + group
        base = lead * tile
        for h in range(heads):
            held = queries[h, 2 * lead : 2 * top].reshape(group * tile, HS).astype(jnp.bfloat16)
            for j in range(top):
                skip = max(0, j - lead) * tile
                key_part = keys[h, per_span * j : per_span * (j + 1)].reshape(span, HS)
                scores[h, pl.ds(skip, group * tile - skip), pl.ds(j * span, span)] = (
                    lax.dot_general(
                        held[skip:],
                        key_part,
                        (((1,), (1,)), ((), ())),
                        preferred_element_type=jnp.float32,
                    )
                )
        for h in range(heads):
            for i in range(lead, top):
                reach = (i + 1) * span
                spots = places[2 * i : 2 * i + 2].reshape(tile, LANES)
                for sub in range(0, tile, 16):
                    rows = pl.ds((i - lead) * tile + sub, 16)
                    part = scores[h, rows, pl.ds(0, reach)]
                    last = part[:, reach - span :]
                    key_index = lax.broadcasted_iota(jnp.int32, last.shape, 1) + (reach - span)
                    spot = spots[sub : sub + 16, 0:1]
                    last = jnp.where(key_index.astype(jnp.float32) <= spot, last, MASKED)
                    if i > 0:
                        part = jnp.concatenate([part[:, : reach - span], last], axis=1)
                    else:
                        part = last
                    peak = jnp.max(part, axis=1, keepdims=True)
                    raised = jnp.exp2((part - peak) * rate)
                    total = jnp.sum(raised, axis=1, keepdims=True)
                    weights[h, rows, pl.ds(0, reach)] = (raised * (1.0 / total)).astype(
                        jnp.bfloat16
                    )
        for h in range(heads):
            sums = [None] * group
            for j in range(top):
                skip = max(0, j - lead)
                value_part = values[h, per_span * j : per_span * (j + 1)].reshape(span, HS)
                product = jnp.dot(
                    weights[h, pl.ds(skip * tile, (group - skip) * tile), pl.ds(j * span, span)],
                    value_part,
                    preferred_element_type=jnp.float32,
                )
                for i in range(skip, group):
                    piece = product[(i - skip) * tile : (i - skip + 1) * tile]
                    sums[i] = piece if sums[i] is None else sums[i] + piece
            for i in range(group):
                out_ref[pl.ds(base + i * tile, tile), pl.ds(h * HS, HS)] = sums[i].astype(
                    jnp.bfloat16
                )


def attend(plan, queries, positions, own, other):
    owners = sum(len(offsets) for offsets in plan)
    row_count = owners * MOST
    width = queries[0].shape[-1]
    heads = 2 if owners <= 8 else 1
    step = heads * HS
    tok_count = own[0].shape[1] // len(plan[0])
    length = owners * 2 * tok_count
    group_rows = min(row_count, 8 * MOST)
    query_specs = [pl.BlockSpec((q.shape[0], SLOTS, step), lambda h: (0, 0, h)) for q in queries]
    pos_specs = [pl.BlockSpec(p.shape, lambda h: (0, 0, 0)) for p in positions]
    panel_specs = [pl.BlockSpec((2, p.shape[1], step), lambda h: (0, 0, h)) for p in own]
    scratch = heads * (group_rows * length * 6 + length * HS * 4 + row_count * HS * 4)
    windows = 2 * (length * step * 4 + row_count * step * 4) + 4 * row_count * LANES * 4
    return pl.pallas_call(
        functools.partial(attend_kernel, plan, tok_count, heads),
        grid=(width // step,),
        in_specs=query_specs + pos_specs + panel_specs + panel_specs,
        out_specs=pl.BlockSpec((row_count, step), lambda h: (0, h)),
        out_shape=jax.ShapeDtypeStruct((row_count, width), jnp.bfloat16),
        scratch_shapes=[
            pltpu.VMEM((owners, MOST, LANES), jnp.float32),
            pltpu.VMEM((heads, owners, MOST, HS), jnp.float32),
            pltpu.VMEM((heads, 2 * owners, tok_count, HS), jnp.bfloat16),
            pltpu.VMEM((heads, 2 * owners, tok_count, HS), jnp.bfloat16),
            pltpu.VMEM((heads, group_rows, length), jnp.float32),
            pltpu.VMEM((heads, group_rows, length), jnp.bfloat16),
        ],
        compiler_params=pltpu.CompilerParams(vmem_limit_bytes=scratch + windows + 4 * MIB),
        name="attend",
    )(*queries, *positions, *own, *other)


def per_device(
    tokens, norm_gain, router_weight, routes, key_weight, value_weight, query_weight, output_weight
):
    tok_count, model_width = tokens.shape
    ctx_count = lax.axis_size("ctx")
    exp_count = lax.axis_size("exp")
    quarter_count = ctx_count // EXPERTS
    head_width = query_weight.shape[2]
    ranks = list(range(0, ctx_count, 2)) + list(range(1, ctx_count, 2))[::-1]
    forward = [(ranks[p], ranks[(p + 1) % ctx_count]) for p in range(ctx_count)]
    backward = [(b, a) for a, b in forward]
    sibling = [(e, 1 - e) for e in range(exp_count)]
    query_slab = query_weight[0]
    output_slab = output_weight[0]
    if quarter_count > 1:
        first = (lax.axis_index("ctx") % quarter_count) * head_width
        key_weight = lax.dynamic_slice_in_dim(key_weight, first, head_width, axis=1)
        value_weight = lax.dynamic_slice_in_dim(value_weight, first, head_width, axis=1)

    plan, queries, positions, own, other = [], [], [], [], []

    def serve(blocks, offsets):
        panel, query, position = project(blocks, offsets, key_weight, value_weight, query_slab)
        plan.append(offsets)
        queries.append(query)
        positions.append(position)
        own.append(panel)
        other.append(lax.ppermute(panel, "exp", sibling))

    halves = norm_rows(tokens, norm_gain, routes)
    serve(halves, [0])
    ahead, behind = list(halves), list(halves)
    steps = ctx_count // 2
    for step in range(1, steps):
        ahead = [lax.ppermute(part, "ctx", forward) for part in ahead]
        behind = [lax.ppermute(part, "ctx", backward) for part in behind[::-1]][::-1]
        serve(ahead + behind, [-step, step])
    one = lax.ppermute(ahead[0], "ctx", forward)
    two = lax.ppermute(behind[1], "ctx", backward)
    serve([one, two], [steps])

    attended = attend(plan, queries, positions, own, other)
    pieces = jnp.dot(attended, output_slab, preferred_element_type=jnp.float32).astype(
        jnp.bfloat16
    )
    returned = lax.all_to_all(
        pieces.reshape(ctx_count, MOST, model_width), "ctx", split_axis=0, concat_axis=0, tiled=True
    )

    message = jnp.concatenate(halves, axis=0)
    logits = jnp.dot(
        message[:, :model_width].astype(jnp.float32), router_weight, precision=lax.Precision.HIGHEST
    )
    slots = message[:, model_width : model_width + EXPERTS].astype(jnp.float32)
    gating = jax.nn.softmax(jnp.where(slots >= 0, logits, -jnp.inf), axis=1)
    slot_index = jnp.arange(MOST, dtype=jnp.float32)[None, None, :]
    combine_mat = jnp.where(slots[:, :, None] == slot_index, gating[:, :, None], 0.0)
    combine_mat = combine_mat.reshape(tok_count, EXPERTS * MOST)
    summed = (
        returned.astype(jnp.float32).reshape(EXPERTS, quarter_count, MOST, model_width).sum(axis=1)
    )
    summed = summed.reshape(EXPERTS * MOST, model_width)
    combined = jnp.dot(combine_mat, summed, precision=lax.Precision.HIGHEST)
    return combined.astype(jnp.bfloat16)


def solution(mesh):
    in_specs = (
        P(("groups", "ctx", "exp"), None),
        P(),
        P(),
        P(("groups", "ctx", "exp"), None),
        P(),
        P(),
        P("ctx", None, None),
        P("ctx", None, None),
    )
    out_specs = P(("groups", "ctx", "exp"), None)
    return jax.shard_map(
        per_device, mesh=mesh, in_specs=in_specs, out_specs=out_specs, check_vma=False
    )
```

time: 144 us -> 129 us (0.90)
  blocking collectives: 14 us -> 0 us
  starting transfers between devices: 13.4 us -> 21.1 us
  local copies, waits for them, and re-layouts: 12 us -> 6.73 us
  Pallas kernels: 44.8 us -> 41.4 us
  waiting for transfers between devices: 52.2 us -> 53.9 us
    all_to_all x1 -> x0, blocking collectives: 14 us -> none  [per_device(): lax.all_to_all(send_token, 'ctx', split_axis=0, concat_axis=0, tiled=True)]
    ppermute x8 -> x14, starting transfers between devices: 9.19 us -> 15.5 us  [the longest x6 13 us: per_device(): lax.ppermute(part, 'ctx', backward)]
    pallas_call x7, Pallas kernels: 44.8 us -> 41.4 us  [the longest x5 26.9 us: project(): pl.pallas_call(functools.partial(project_kernel, offsets, len(blocks), EX...]
    gather x5 -> x0, local copies, waits for them, and re-layouts: 1.83 us -> none  [per_device(): gating = jax.nn.softmax(jnp.take_along_axis(logits, routes, axis=1), axis=1)]
    unnamed x31 -> x17, local copies, waits for them, and re-layouts: 8.33 us -> 6.61 us
    all_to_all x1, waiting for transfers between devices: 29.1 us -> 30.6 us  [per_device(): lax.all_to_all(pieces.reshape(ctx_count, MOST, model_width), 'ctx', split...]
    ppermute x5, waiting for transfers between devices: 0.4 us -> 1.88 us  [serve(): other.append(lax.ppermute(panel, 'exp', sibling))]
    ppermute x8 -> x14, waiting for transfers between devices: 22.6 us -> 21.4 us  [the longest x6 17.3 us: per_device(): lax.ppermute(part, 'ctx', backward)]
  transfers between devices with their start and end apart: 14 -> 20, of which waited for: 6 -> 8; matrix products, arithmetic and copies ran while one was open for 4% -> 1% of each run, Pallas kernels for 22% -> 21%
where the time goes in v3:
time: 129 us
  waiting for transfers between devices  53.9 us (42%)
  Pallas kernels  41.4 us (32%)
  starting transfers between devices  21.1 us (16%)
  local copies, waits for them, and re-layouts  6.73 us (5%)
  matrix products  5.11 us (4%)
    all_to_all x1, waiting for transfers between devices, per_device(): lax.all_to_all(pieces.reshape(ctx_count, MOST, model_width), 'ctx', split...  30.6 us
    pallas_call x5, Pallas kernels, project(): pl.pallas_call(functools.partial(project_kernel, offsets, len(blocks), EX...  26.9 us
    ppermute x6, waiting for transfers between devices, per_device(): lax.ppermute(part, 'ctx', backward)  17.3 us
    ppermute x6, starting transfers between devices, per_device(): lax.ppermute(part, 'ctx', backward)  13 us
    pallas_call x1, Pallas kernels, attend(): pl.pallas_call(functools.partial(attend_kernel, plan, tok_count, heads),...  12.4 us
    unnamed x17, local copies, waits for them, and re-layouts  6.61 us
    all_to_all x1, starting transfers between devices, per_device(): lax.all_to_all(pieces.reshape(ctx_count, MOST, model_width), 'ctx', split...  4.82 us
    dot_general x1, matrix products, per_device(): jnp.dot(attended, output_slab, preferred_element_type=jnp.float32)  2.62 us
  transfers between devices with their start and end apart: 20, of which 8 were waited for; matrix products, arithmetic and copies ran while one was open for 1% of the time, Pallas kernels for 21%

profile of v3, /device:TPU:0, one launch (start us, length us, event | category | flops | bytes accessed | tf_op | source)
XLA Modules:
  0.0 128.8 jit_solution(18394544973783416477)
XLA Ops:
  0.0 0.0 copy-start
  0.0 2.1 %norm_rows.1 = (bf16[64,2176]{1,0:T(8,128)(2,1)}, bf16[64,2176]{1,0:T(8,128)(2,1)}) custom-call(bf16[128,2048]{1,0:T(8,128)(2,1)} %tokens_ref.1, f32[1,2048]{1,0:T(1,128)} %bitcast.21, s32[2,128]{1,0:T(2,128)} %bitcast.22), custom_call_target="tpu_custom_call" | custom-call | tf_op jit(solution)/shard_map/norm_rows/pallas_call | solution.py:59
  2.1 3.0 %collective-permute-start.2 = (bf16[64,2176]{1,0:T(8,128)(2,1)}, bf16[64,2176]{1,0:T(8,128)(2,1)S(1)}, u32[]{:S(2)}, u32[]{:S(2)}) collective-permute-start(bf16[64,2176]{1,0:T(8,128)(2,1)} %get-tuple-element.22.refs_0_), channel_id=1, source_target_pairs={{4,0},{8,4},{12,8},{14,12},{10,14},{6,10},{2,6},{0,2},{5,1},{9,5},... | collective-permute-start | bytes 835592 | tf_op jit(solution)/shard_map/ppermute | solution.py:286
  5.1 0.1 collective-permute-start
  5.2 2.0 %collective-permute-start.3 = (bf16[64,2176]{1,0:T(8,128)(2,1)}, bf16[64,2176]{1,0:T(8,128)(2,1)S(1)}, u32[]{:S(2)}, u32[]{:S(2)}) collective-permute-start(bf16[64,2176]{1,0:T(8,128)(2,1)} %get-tuple-element.23.refs_1_), channel_id=1, source_target_pairs={{4,0},{8,4},{12,8},{14,12},{10,14},{6,10},{2,6},{0,2},{5,1},{9,5},... | collective-permute-start | bytes 835592 | tf_op jit(solution)/shard_map/ppermute | solution.py:286
  7.1 0.1 collective-permute-start.1
  7.2 5.7 %collective-permute-done.2.refs_2_ = bf16[64,2176]{1,0:T(8,128)(2,1)S(1)} collective-permute-done((bf16[64,2176]{1,0:T(8,128)(2,1)}, bf16[64,2176]{1,0:T(8,128)(2,1)S(1)}, u32[]{:S(2)}, u32[]{:S(2)}) %collective-permute-start.2) | collective-permute-done | bytes 278560 | tf_op jit(solution)/shard_map/ppermute | solution.py:286
  12.8 2.0 %collective-permute-start.6 = (bf16[64,2176]{1,0:T(8,128)(2,1)S(1)}, bf16[64,2176]{1,0:T(8,128)(2,1)S(1)}, u32[]{:S(2)}, u32[]{:S(2)}) collective-permute-start(bf16[64,2176]{1,0:T(8,128)(2,1)S(1)} %collective-permute-done.2.refs_2_), channel_id=1, source_target_pairs={{4,0},{8,4},{12,8},{14,12},{10,14},{6,10},{2,6},{0,2},{5,1},{9,5},... | collective-permute-start | bytes 835592 | tf_op jit(solution)/shard_map/ppermute | solution.py:286
  14.9 0.0 collective-permute-done.refs_0_
  14.9 0.0 collective-permute-start.4
  14.9 3.9 %collective-permute-done.3.refs_3_ = bf16[64,2176]{1,0:T(8,128)(2,1)S(1)} collective-permute-done((bf16[64,2176]{1,0:T(8,128)(2,1)}, bf16[64,2176]{1,0:T(8,128)(2,1)S(1)}, u32[]{:S(2)}, u32[]{:S(2)}) %collective-permute-start.3) | collective-permute-done | bytes 278560 | tf_op jit(solution)/shard_map/ppermute | solution.py:286
  18.8 2.0 %collective-permute-start.7 = (bf16[64,2176]{1,0:T(8,128)(2,1)S(1)}, bf16[64,2176]{1,0:T(8,128)(2,1)S(1)}, u32[]{:S(2)}, u32[]{:S(2)}) collective-permute-start(bf16[64,2176]{1,0:T(8,128)(2,1)S(1)} %collective-permute-done.3.refs_3_), channel_id=1, source_target_pairs={{4,0},{8,4},{12,8},{14,12},{10,14},{6,10},{2,6},{0,2},{5,1},{9,5},... | collective-permute-start | bytes 835592 | tf_op jit(solution)/shard_map/ppermute | solution.py:286
  20.8 0.0 collective-permute-done.1.refs_1_
  20.9 0.0 collective-permute-start.5
  20.9 3.9 %collective-permute-done.6.refs_2_ = bf16[64,2176]{1,0:T(8,128)(2,1)S(1)} collective-permute-done((bf16[64,2176]{1,0:T(8,128)(2,1)S(1)}, bf16[64,2176]{1,0:T(8,128)(2,1)S(1)}, u32[]{:S(2)}, u32[]{:S(2)}) %collective-permute-start.6) | collective-permute-done | bytes 278560 | tf_op jit(solution)/shard_map/ppermute | solution.py:286
  24.8 2.0 %collective-permute-start.10 = (bf16[64,2176]{1,0:T(8,128)(2,1)S(1)}, bf16[64,2176]{1,0:T(8,128)(2,1)S(1)}, u32[]{:S(2)}, u32[]{:S(2)}) collective-permute-start(bf16[64,2176]{1,0:T(8,128)(2,1)S(1)} %collective-permute-done.6.refs_2_), channel_id=1, source_target_pairs={{4,0},{8,4},{12,8},{14,12},{10,14},{6,10},{2,6},{0,2},{5,1},{9,5},... | collective-permute-start | bytes 835592 | tf_op jit(solution)/shard_map/ppermute | solution.py:286
  26.8 0.0 collective-permute-done.4.refs_0_
  26.8 0.0 collective-permute-start.8
  26.9 3.9 %collective-permute-done.7.refs_3_ = bf16[64,2176]{1,0:T(8,128)(2,1)S(1)} collective-permute-done((bf16[64,2176]{1,0:T(8,128)(2,1)S(1)}, bf16[64,2176]{1,0:T(8,128)(2,1)S(1)}, u32[]{:S(2)}, u32[]{:S(2)}) %collective-permute-start.7) | collective-permute-done | bytes 278560 | tf_op jit(solution)/shard_map/ppermute | solution.py:286
  30.8 2.0 %collective-permute-start.11 = (bf16[64,2176]{1,0:T(8,128)(2,1)S(1)}, bf16[64,2176]{1,0:T(8,128)(2,1)S(1)}, u32[]{:S(2)}, u32[]{:S(2)}) collective-permute-start(bf16[64,2176]{1,0:T(8,128)(2,1)S(1)} %collective-permute-done.7.refs_3_), channel_id=1, source_target_pairs={{4,0},{8,4},{12,8},{14,12},{10,14},{6,10},{2,6},{0,2},{5,1},{9,5},... | collective-permute-start | bytes 835592 | tf_op jit(solution)/shard_map/ppermute | solution.py:286
  32.8 0.0 collective-permute-done.5.refs_1_
  32.8 0.0 collective-permute-start.9
  32.8 2.2 %copy-done.1 = bf16[2048,1024]{1,0:T(8,128)(2,1)S(1)} copy-done((bf16[2048,1024]{1,0:T(8,128)(2,1)S(1)}, bf16[2048,1024]{1,0:T(8,128)(2,1)}, u32[]{:S(2)}) %copy-start.1) | copy-done | bytes 4194328
  35.0 2.2 %copy-done.3 = bf16[2048,1024]{1,0:T(8,128)(2,1)S(1)} copy-done((bf16[2048,1024]{1,0:T(8,128)(2,1)S(1)}, bf16[2048,1024]{1,0:T(8,128)(2,1)}, u32[]{:S(2)}) %copy-start.3) | copy-done | bytes 4194328
  37.2 2.2 %copy-done.4 = bf16[1,2048,1024]{2,1,0:T(8,128)(2,1)S(1)} copy-done((bf16[1,2048,1024]{2,1,0:T(8,128)(2,1)S(1)}, bf16[1,2048,1024]{2,1,0:T(8,128)(2,1)}, u32[]{:S(2)}) %copy-start.4) | copy-done | bytes 4194328
  39.4 5.9 %project.6 = (bf16[2,256,1024]{2,1,0:T(8,128)(2,1)S(1)}, bf16[2,48,1024]{2,1,0:T(8,128)(2,1)S(1)}, f32[2,48,128]{2,1,0:T(8,128)S(1)}) custom-call(bf16[64,2176]{1,0:T(8,128)(2,1)S(1)} %collective-permute-done.refs_0_, bf16[64,2176]{1,0:T(8,128)(2,1)S(1)} %collective-permute-done.1.refs_1_, bf16[64,2176]{1,0:T(8,128)(2,1)S(1)} %collective-permute-done.2.refs_2_, ...), custom_call_target="tpu_custom_call" | custom-call | tf_op jit(solution)/shard_map/project/pallas_call | solution.py:108
  45.3 0.1 collective-permute-start.15
  45.4 5.9 %project.7 = (bf16[2,256,1024]{2,1,0:T(8,128)(2,1)S(1)}, bf16[2,48,1024]{2,1,0:T(8,128)(2,1)S(1)}, f32[2,48,128]{2,1,0:T(8,128)S(1)}) custom-call(bf16[64,2176]{1,0:T(8,128)(2,1)S(1)} %collective-permute-done.4.refs_0_, bf16[64,2176]{1,0:T(8,128)(2,1)S(1)} %collective-permute-done.5.refs_1_, bf16[64,2176]{1,0:T(8,128)(2,1)S(1)} %collective-permute-done.6.refs_2_, ...), custom_call_target="tpu_custom_call" | custom-call | tf_op jit(solution)/shard_map/project/pallas_call | solution.py:108
  51.3 0.0 collective-permute-done.10.refs_2_
  51.3 0.0 copy-start.2
  51.3 0.0 copy-start.5
  51.3 0.0 copy-start.6
  51.3 0.6 collective-permute-start.16
  51.9 0.0 collective-permute-done.8.refs_0_
  51.9 0.0 collective-permute-done.11.refs_3_
  51.9 0.0 collective-permute-done.9.refs_1_
  51.9 5.9 %project.8 = (bf16[2,256,1024]{2,1,0:T(8,128)(2,1)S(1)}, bf16[2,48,1024]{2,1,0:T(8,128)(2,1)S(1)}, f32[2,48,128]{2,1,0:T(8,128)S(1)}) custom-call(bf16[64,2176]{1,0:T(8,128)(2,1)S(1)} %collective-permute-done.8.refs_0_, bf16[64,2176]{1,0:T(8,128)(2,1)S(1)} %collective-permute-done.9.refs_1_, bf16[64,2176]{1,0:T(8,128)(2,1)S(1)} %collective-permute-done.10.refs_2_, ...), custom_call_target="tpu_custom_call" | custom-call | tf_op jit(solution)/shard_map/project/pallas_call | solution.py:108
  57.8 0.1 collective-permute-start.17
  57.9 2.1 %collective-permute-start.12 = (bf16[64,2176]{1,0:T(8,128)(2,1)S(1)}, bf16[64,2176]{1,0:T(8,128)(2,1)S(1)}, u32[]{:S(2)}, u32[]{:S(2)}) collective-permute-start(bf16[64,2176]{1,0:T(8,128)(2,1)S(1)} %collective-permute-done.8.refs_0_), channel_id=1, source_target_pairs={{0,4},{4,8},{8,12},{12,14},{14,10},{10,6},{6,2},{2,0},{1,5},{5,9},... | collective-permute-start | bytes 835592 | tf_op jit(solution)/shard_map/ppermute | solution.py:288
  60.0 0.2 collective-permute-start.13
  60.2 0.0 copy-done.2
  60.2 0.0 copy-done.5
  60.2 0.0 copy-done.6
  60.2 4.6 %project.5 = (bf16[2,128,1024]{2,1,0:T(8,128)(2,1)S(1)}, bf16[1,48,1024]{2,1,0:T(8,128)(2,1)S(1)}, f32[1,48,128]{2,1,0:T(8,128)S(1)}) custom-call(bf16[64,2176]{1,0:T(8,128)(2,1)S(1)} %copy-done.6, bf16[64,2176]{1,0:T(8,128)(2,1)S(1)} %copy-done.5, bf16[2048,1024]{1,0:T(8,128)(2,1)S(1)} %copy-done.2, bf16[2048,1024]{1,0:T(8,128)(2,1)S(1)} %copy-done.3, ...), custom_call_target="tpu_custom_call" | custom-call | tf_op jit(solution)/shard_map/project/pallas_call | solution.py:108
  64.8 2.4 %collective-permute-done.12.refs_0_ = bf16[64,2176]{1,0:T(8,128)(2,1)S(1)} collective-permute-done((bf16[64,2176]{1,0:T(8,128)(2,1)S(1)}, bf16[64,2176]{1,0:T(8,128)(2,1)S(1)}, u32[]{:S(2)}, u32[]{:S(2)}) %collective-permute-start.12) | collective-permute-done | bytes 278560 | tf_op jit(solution)/shard_map/ppermute | solution.py:288
  67.2 0.0 collective-permute-start.14
  67.2 1.5 %collective-permute-done.13.refs_1_ = bf16[64,2176]{1,0:T(8,128)(2,1)S(1)} collective-permute-done((bf16[64,2176]{1,0:T(8,128)(2,1)S(1)}, bf16[64,2176]{1,0:T(8,128)(2,1)S(1)}, u32[]{:S(2)}, u32[]{:S(2)}) %collective-permute-start.13) | collective-permute-done | bytes 278560 | tf_op jit(solution)/shard_map/ppermute | solution.py:289
  68.7 4.6 %project.9 = (bf16[2,128,1024]{2,1,0:T(8,128)(2,1)S(1)}, bf16[1,48,1024]{2,1,0:T(8,128)(2,1)S(1)}, f32[1,48,128]{2,1,0:T(8,128)S(1)}) custom-call(bf16[64,2176]{1,0:T(8,128)(2,1)S(1)} %collective-permute-done.12.refs_0_, bf16[64,2176]{1,0:T(8,128)(2,1)S(1)} %collective-permute-done.13.refs_1_, bf16[2048,1024]{1,0:T(8,128)(2,1)S(1)} %copy-done.2, ...), custom_call_target="tpu_custom_call" | custom-call | tf_op jit(solution)/shard_map/project/pallas_call | solution.py:108
  73.3 0.1 collective-permute-start.18
  73.4 0.0 collective-permute-done.14.refs_15_
  73.4 0.0 collective-permute-done.15.refs_16_
  73.4 0.0 collective-permute-done.16.refs_17_
  73.4 1.9 %collective-permute-done.18.refs_19_ = bf16[2,128,1024]{2,1,0:T(8,128)(2,1)S(1)} collective-permute-done((bf16[2,128,1024]{2,1,0:T(8,128)(2,1)S(1)}, bf16[2,128,1024]{2,1,0:T(8,128)(2,1)S(1)}, u32[]{:S(2)}, u32[]{:S(2)}) %collective-permute-start.18) | collective-permute-done | bytes 524320 | tf_op jit(solution)/shard_map/ppermute | solution.py:278
  75.3 0.0 collective-permute-done.17.refs_18_
  75.3 12.4 %attend.1 = bf16[320,1024]{1,0:T(8,128)(2,1)S(1)} custom-call(bf16[1,48,1024]{2,1,0:T(8,128)(2,1)S(1)} %get-tuple-element.24.refs_0_, bf16[2,48,1024]{2,1,0:T(8,128)(2,1)S(1)} %get-tuple-element.25.refs_1_, bf16[2,48,1024]{2,1,0:T(8,128)(2,1)S(1)} %get-tuple-element.26.refs_2_, bf16[2,48,1024]{2,1,0:T(8,128)(2,1)S(1)} %get-tuple-element.27.refs_3_, ...), custom_call_target="tpu_custom_call" | custom-call | tf_op jit(solution)/shard_map/attend/pallas_call | solution.py:232
  87.7 0.0 copy-done.7
  87.7 2.6 %fusion.2 = bf16[320,2048]{1,0:T(8,128)(2,1)} fusion(bf16[320,1024]{1,0:T(8,128)(2,1)S(1)} %attend.1, bf16[1,1024,2048]{2,1,0:T(8,128)(2,1)S(1)} %copy-done.7), kind=kOutput, calls=%fused_computation.2 | convolution fusion | flops 1342832640 | bytes 6160384 | tf_op jit(solution)/shard_map/dot_general | solution.py:293
  90.3 4.8 %all-to-all-start = ((bf16[8,40,2048]{2,1,0:T(8,128)(2,1)}), bf16[8,40,2048]{2,1,0:T(8,128)(2,1)S(1)}, u32[]{:S(2)}, u32[]{:S(2)}) async-start(bf16[8,40,2048]{2,1,0:T(8,128)(2,1)} %bitcast.4), calls=%async_computation | async-start | bytes 2621440 | tf_op jit(solution)/shard_map/all_to_all | solution.py:296
  95.3 0.0 copy-done
  95.3 0.7 fusion.14
  95.9 0.2 fusion.12
  96.1 0.1 fusion.11
  96.3 30.6 %all-to-all-done = bf16[8,40,2048]{2,1,0:T(8,128)(2,1)S(1)} async-done(((bf16[8,40,2048]{2,1,0:T(8,128)(2,1)}), bf16[8,40,2048]{2,1,0:T(8,128)(2,1)S(1)}, u32[]{:S(2)}, u32[]{:S(2)}) %all-to-all-start) | async-done | bytes 1310752 | tf_op jit(solution)/shard_map/all_to_all | solution.py:296
  126.9 1.8 %fusion.5 = bf16[128,2048]{1,0:T(8,128)(2,1)} fusion(bf16[8,40,2048]{2,1,0:T(8,128)(2,1)S(1)} %all-to-all-done, f32[128,8]{0,1:T(8,128)S(1)} %copy.15, f32[128,8]{0,1:T(8,128)S(1)} %copy.12), kind=kOutput, calls=%fused_computation.4 | convolution fusion | flops 1006977024 | bytes 1843200 | tf_op jit(solution)/shard_map/dot_general | solution.py:313
  (9 shorter events, 0.2 us)
Async XLA Ops:
  0.0 95.3 %copy-start = (f32[2048,8]{0,1:T(8,128)S(1)}, f32[2048,8]{0,1:T(8,128)}, u32[]{:S(2)}) copy-start(f32[2048,8]{0,1:T(8,128)} %param.10) | copy-start | bytes 196612
  2.1 10.7 %collective-permute-start.2 = (bf16[64,2176]{1,0:T(8,128)(2,1)}, bf16[64,2176]{1,0:T(8,128)(2,1)S(1)}, u32[]{:S(2)}, u32[]{:S(2)}) collective-permute-start(bf16[64,2176]{1,0:T(8,128)(2,1)} %get-tuple-element.22.refs_0_), channel_id=1, source_target_pairs={{4,0},{8,4},{12,8},{14,12},{10,14},{6,10},{2,6},{0,2},{5,1},{9,5},... | collective-permute-start | bytes 835592 | tf_op jit(solution)/shard_map/ppermute | solution.py:286
  5.1 9.8 %collective-permute-start = (bf16[64,2176]{1,0:T(8,128)(2,1)}, bf16[64,2176]{1,0:T(8,128)(2,1)S(1)}, u32[]{:S(2)}, u32[]{:S(2)}) collective-permute-start(bf16[64,2176]{1,0:T(8,128)(2,1)} %get-tuple-element.22.refs_0_), channel_id=1, source_target_pairs={{0,4},{4,8},{8,12},{12,14},{14,10},{10,6},{6,2},{2,0},{1,5},{5,9},... | collective-permute-start | bytes 835592 | tf_op jit(solution)/shard_map/ppermute | solution.py:285
  5.2 13.7 %collective-permute-start.3 = (bf16[64,2176]{1,0:T(8,128)(2,1)}, bf16[64,2176]{1,0:T(8,128)(2,1)S(1)}, u32[]{:S(2)}, u32[]{:S(2)}) collective-permute-start(bf16[64,2176]{1,0:T(8,128)(2,1)} %get-tuple-element.23.refs_1_), channel_id=1, source_target_pairs={{4,0},{8,4},{12,8},{14,12},{10,14},{6,10},{2,6},{0,2},{5,1},{9,5},... | collective-permute-start | bytes 835592 | tf_op jit(solution)/shard_map/ppermute | solution.py:286
  7.1 13.7 %collective-permute-start.1 = (bf16[64,2176]{1,0:T(8,128)(2,1)}, bf16[64,2176]{1,0:T(8,128)(2,1)S(1)}, u32[]{:S(2)}, u32[]{:S(2)}) collective-permute-start(bf16[64,2176]{1,0:T(8,128)(2,1)} %get-tuple-element.23.refs_1_), channel_id=1, source_target_pairs={{0,4},{4,8},{8,12},{12,14},{14,10},{10,6},{6,2},{2,0},{1,5},{5,9},... | collective-permute-start | bytes 835592 | tf_op jit(solution)/shard_map/ppermute | solution.py:285
  12.8 11.9 %collective-permute-start.6 = (bf16[64,2176]{1,0:T(8,128)(2,1)S(1)}, bf16[64,2176]{1,0:T(8,128)(2,1)S(1)}, u32[]{:S(2)}, u32[]{:S(2)}) collective-permute-start(bf16[64,2176]{1,0:T(8,128)(2,1)S(1)} %collective-permute-done.2.refs_2_), channel_id=1, source_target_pairs={{4,0},{8,4},{12,8},{14,12},{10,14},{6,10},{2,6},{0,2},{5,1},{9,5},... | collective-permute-start | bytes 835592 | tf_op jit(solution)/shard_map/ppermute | solution.py:286
  14.9 11.9 %collective-permute-start.4 = (bf16[64,2176]{1,0:T(8,128)(2,1)S(1)}, bf16[64,2176]{1,0:T(8,128)(2,1)S(1)}, u32[]{:S(2)}, u32[]{:S(2)}) collective-permute-start(bf16[64,2176]{1,0:T(8,128)(2,1)S(1)} %collective-permute-done.refs_0_), channel_id=1, source_target_pairs={{0,4},{4,8},{8,12},{12,14},{14,10},{10,6},{6,2},{2,0},{1,5},{5,9},... | collective-permute-start | bytes 835592 | tf_op jit(solution)/shard_map/ppermute | solution.py:285
  18.8 11.9 %collective-permute-start.7 = (bf16[64,2176]{1,0:T(8,128)(2,1)S(1)}, bf16[64,2176]{1,0:T(8,128)(2,1)S(1)}, u32[]{:S(2)}, u32[]{:S(2)}) collective-permute-start(bf16[64,2176]{1,0:T(8,128)(2,1)S(1)} %collective-permute-done.3.refs_3_), channel_id=1, source_target_pairs={{4,0},{8,4},{12,8},{14,12},{10,14},{6,10},{2,6},{0,2},{5,1},{9,5},... | collective-permute-start | bytes 835592 | tf_op jit(solution)/shard_map/ppermute | solution.py:286
  20.9 11.9 %collective-permute-start.5 = (bf16[64,2176]{1,0:T(8,128)(2,1)S(1)}, bf16[64,2176]{1,0:T(8,128)(2,1)S(1)}, u32[]{:S(2)}, u32[]{:S(2)}) collective-permute-start(bf16[64,2176]{1,0:T(8,128)(2,1)S(1)} %collective-permute-done.1.refs_1_), channel_id=1, source_target_pairs={{0,4},{4,8},{8,12},{12,14},{14,10},{10,6},{6,2},{2,0},{1,5},{5,9},... | collective-permute-start | bytes 835592 | tf_op jit(solution)/shard_map/ppermute | solution.py:285
  24.8 26.5 %collective-permute-start.10 = (bf16[64,2176]{1,0:T(8,128)(2,1)S(1)}, bf16[64,2176]{1,0:T(8,128)(2,1)S(1)}, u32[]{:S(2)}, u32[]{:S(2)}) collective-permute-start(bf16[64,2176]{1,0:T(8,128)(2,1)S(1)} %collective-permute-done.6.refs_2_), channel_id=1, source_target_pairs={{4,0},{8,4},{12,8},{14,12},{10,14},{6,10},{2,6},{0,2},{5,1},{9,5},... | collective-permute-start | bytes 835592 | tf_op jit(solution)/shard_map/ppermute | solution.py:286
  26.8 25.0 %collective-permute-start.8 = (bf16[64,2176]{1,0:T(8,128)(2,1)S(1)}, bf16[64,2176]{1,0:T(8,128)(2,1)S(1)}, u32[]{:S(2)}, u32[]{:S(2)}) collective-permute-start(bf16[64,2176]{1,0:T(8,128)(2,1)S(1)} %collective-permute-done.4.refs_0_), channel_id=1, source_target_pairs={{0,4},{4,8},{8,12},{12,14},{14,10},{10,6},{6,2},{2,0},{1,5},{5,9},... | collective-permute-start | bytes 835592 | tf_op jit(solution)/shard_map/ppermute | solution.py:285
  30.8 21.1 %collective-permute-start.11 = (bf16[64,2176]{1,0:T(8,128)(2,1)S(1)}, bf16[64,2176]{1,0:T(8,128)(2,1)S(1)}, u32[]{:S(2)}, u32[]{:S(2)}) collective-permute-start(bf16[64,2176]{1,0:T(8,128)(2,1)S(1)} %collective-permute-done.7.refs_3_), channel_id=1, source_target_pairs={{4,0},{8,4},{12,8},{14,12},{10,14},{6,10},{2,6},{0,2},{5,1},{9,5},... | collective-permute-start | bytes 835592 | tf_op jit(solution)/shard_map/ppermute | solution.py:286
  32.8 19.1 %collective-permute-start.9 = (bf16[64,2176]{1,0:T(8,128)(2,1)S(1)}, bf16[64,2176]{1,0:T(8,128)(2,1)S(1)}, u32[]{:S(2)}, u32[]{:S(2)}) collective-permute-start(bf16[64,2176]{1,0:T(8,128)(2,1)S(1)} %collective-permute-done.5.refs_1_), channel_id=1, source_target_pairs={{0,4},{4,8},{8,12},{12,14},{14,10},{10,6},{6,2},{2,0},{1,5},{5,9},... | collective-permute-start | bytes 835592 | tf_op jit(solution)/shard_map/ppermute | solution.py:285
  32.8 2.2 %copy-start.1 = (bf16[2048,1024]{1,0:T(8,128)(2,1)S(1)}, bf16[2048,1024]{1,0:T(8,128)(2,1)}, u32[]{:S(2)}) copy-start(bf16[2048,1024]{1,0:T(8,128)(2,1)} %refs_2_.3) | copy-start | bytes 12582916
  35.0 2.2 %copy-start.3 = (bf16[2048,1024]{1,0:T(8,128)(2,1)S(1)}, bf16[2048,1024]{1,0:T(8,128)(2,1)}, u32[]{:S(2)}) copy-start(bf16[2048,1024]{1,0:T(8,128)(2,1)} %refs_3_.3) | copy-start | bytes 12582916
  37.2 2.2 %copy-start.4 = (bf16[1,2048,1024]{2,1,0:T(8,128)(2,1)S(1)}, bf16[1,2048,1024]{2,1,0:T(8,128)(2,1)}, u32[]{:S(2)}) copy-start(bf16[1,2048,1024]{2,1,0:T(8,128)(2,1)} %param.14) | copy-start | bytes 12582916
  45.3 28.1 %collective-permute-start.15 = (bf16[2,256,1024]{2,1,0:T(8,128)(2,1)S(1)}, bf16[2,256,1024]{2,1,0:T(8,128)(2,1)S(1)}, u32[]{:S(2)}, u32[]{:S(2)}) collective-permute-start(bf16[2,256,1024]{2,1,0:T(8,128)(2,1)S(1)} %get-tuple-element.35.refs_11_), channel_id=1, source_target_pairs={{0,1},{1,0},{2,3},{3,2},{4,5},{5,4},{6,7},{7,6},{8,9},{9,8},{10,11... | collective-permute-start | bytes 3145736 | tf_op jit(solution)/shard_map/ppermute | solution.py:278
  51.3 8.9 %copy-start.2 = (bf16[2048,1024]{1,0:T(8,128)(2,1)S(1)}, bf16[2048,1024]{1,0:T(8,128)(2,1)}, u32[]{:S(2)}) copy-start(bf16[2048,1024]{1,0:T(8,128)(2,1)} %refs_2_.3) | copy-start | bytes 12582916
  51.3 8.9 %copy-start.5 = (bf16[64,2176]{1,0:T(8,128)(2,1)S(1)}, bf16[64,2176]{1,0:T(8,128)(2,1)}, u32[]{:S(2)}) copy-start(bf16[64,2176]{1,0:T(8,128)(2,1)} %get-tuple-element.23.refs_1_) | copy-start | bytes 835588
  51.3 8.9 %copy-start.6 = (bf16[64,2176]{1,0:T(8,128)(2,1)S(1)}, bf16[64,2176]{1,0:T(8,128)(2,1)}, u32[]{:S(2)}) copy-start(bf16[64,2176]{1,0:T(8,128)(2,1)} %get-tuple-element.22.refs_0_) | copy-start | bytes 835588
  51.3 22.1 %collective-permute-start.16 = (bf16[2,256,1024]{2,1,0:T(8,128)(2,1)S(1)}, bf16[2,256,1024]{2,1,0:T(8,128)(2,1)S(1)}, u32[]{:S(2)}, u32[]{:S(2)}) collective-permute-start(bf16[2,256,1024]{2,1,0:T(8,128)(2,1)S(1)} %get-tuple-element.36.refs_12_), channel_id=1, source_target_pairs={{0,1},{1,0},{2,3},{3,2},{4,5},{5,4},{6,7},{7,6},{8,9},{9,8},{10,11... | collective-permute-start | bytes 3145736 | tf_op jit(solution)/shard_map/ppermute | solution.py:278
  57.8 17.5 %collective-permute-start.17 = (bf16[2,256,1024]{2,1,0:T(8,128)(2,1)S(1)}, bf16[2,256,1024]{2,1,0:T(8,128)(2,1)S(1)}, u32[]{:S(2)}, u32[]{:S(2)}) collective-permute-start(bf16[2,256,1024]{2,1,0:T(8,128)(2,1)S(1)} %get-tuple-element.37.refs_13_), channel_id=1, source_target_pairs={{0,1},{1,0},{2,3},{3,2},{4,5},{5,4},{6,7},{7,6},{8,9},{9,8},{10,11... | collective-permute-start | bytes 3145736 | tf_op jit(solution)/shard_map/ppermute | solution.py:278
  57.9 9.3 %collective-permute-start.12 = (bf16[64,2176]{1,0:T(8,128)(2,1)S(1)}, bf16[64,2176]{1,0:T(8,128)(2,1)S(1)}, u32[]{:S(2)}, u32[]{:S(2)}) collective-permute-start(bf16[64,2176]{1,0:T(8,128)(2,1)S(1)} %collective-permute-done.8.refs_0_), channel_id=1, source_target_pairs={{0,4},{4,8},{8,12},{12,14},{14,10},{10,6},{6,2},{2,0},{1,5},{5,9},... | collective-permute-start | bytes 835592 | tf_op jit(solution)/shard_map/ppermute | solution.py:288
  60.0 8.7 %collective-permute-start.13 = (bf16[64,2176]{1,0:T(8,128)(2,1)S(1)}, bf16[64,2176]{1,0:T(8,128)(2,1)S(1)}, u32[]{:S(2)}, u32[]{:S(2)}) collective-permute-start(bf16[64,2176]{1,0:T(8,128)(2,1)S(1)} %collective-permute-done.11.refs_3_), channel_id=1, source_target_pairs={{4,0},{8,4},{12,8},{14,12},{10,14},{6,10},{2,6},{0,2},{5,1},{9,5},... | collective-permute-start | bytes 835592 | tf_op jit(solution)/shard_map/ppermute | solution.py:289
  67.2 6.2 %collective-permute-start.14 = (bf16[2,128,1024]{2,1,0:T(8,128)(2,1)S(1)}, bf16[2,128,1024]{2,1,0:T(8,128)(2,1)S(1)}, u32[]{:S(2)}, u32[]{:S(2)}) collective-permute-start(bf16[2,128,1024]{2,1,0:T(8,128)(2,1)S(1)} %get-tuple-element.34.refs_10_), channel_id=1, source_target_pairs={{0,1},{1,0},{2,3},{3,2},{4,5},{5,4},{6,7},{7,6},{8,9},{9,8},{10,11... | collective-permute-start | bytes 1572872 | tf_op jit(solution)/shard_map/ppermute | solution.py:278
  73.3 2.0 %collective-permute-start.18 = (bf16[2,128,1024]{2,1,0:T(8,128)(2,1)S(1)}, bf16[2,128,1024]{2,1,0:T(8,128)(2,1)S(1)}, u32[]{:S(2)}, u32[]{:S(2)}) collective-permute-start(bf16[2,128,1024]{2,1,0:T(8,128)(2,1)S(1)} %get-tuple-element.38.refs_14_), channel_id=1, source_target_pairs={{0,1},{1,0},{2,3},{3,2},{4,5},{5,4},{6,7},{7,6},{8,9},{9,8},{10,11... | collective-permute-start | bytes 1572872 | tf_op jit(solution)/shard_map/ppermute | solution.py:278
  75.3 12.4 %copy-start.7 = (bf16[1,1024,2048]{2,1,0:T(8,128)(2,1)S(1)}, bf16[1,1024,2048]{2,1,0:T(8,128)(2,1)}, u32[]{:S(2)}) copy-start(bf16[1,1024,2048]{2,1,0:T(8,128)(2,1)} %param.15) | copy-start | bytes 12582916
  90.3 36.6 %all-to-all-start = ((bf16[8,40,2048]{2,1,0:T(8,128)(2,1)}), bf16[8,40,2048]{2,1,0:T(8,128)(2,1)S(1)}, u32[]{:S(2)}, u32[]{:S(2)}) async-start(bf16[8,40,2048]{2,1,0:T(8,128)(2,1)} %bitcast.4), calls=%async_computation | async-start | bytes 2621440 | tf_op jit(solution)/shard_map/all_to_all | solution.py:296

commit v4 on v3

--- a/solution.py
+++ b/solution.py
@@ -277,17 +277,31 @@
         own.append(panel)
         other.append(lax.ppermute(panel, "exp", sibling))
 
+    def after_projection(parts):
+        tied = lax.optimization_barrier((positions[-1], *parts))
+        positions[-1] = tied[0]
+        return list(tied[1:])
+
     halves = norm_rows(tokens, norm_gain, routes)
-    serve(halves, [0])
     ahead, behind = list(halves), list(halves)
     steps = ctx_count // 2
-    for step in range(1, steps):
-        ahead = [lax.ppermute(part, "ctx", forward) for part in ahead]
-        behind = [lax.ppermute(part, "ctx", backward) for part in behind[::-1]][::-1]
-        serve(ahead + behind, [-step, step])
-    one = lax.ppermute(ahead[0], "ctx", forward)
-    two = lax.ppermute(behind[1], "ctx", backward)
-    serve([one, two], [steps])
+    for step in range(1, steps + 1):
+        held = ahead + behind
+        if step > 1:
+            ahead[0], behind[1] = after_projection([ahead[0], behind[1]])
+        if step < steps:
+            ahead = [lax.ppermute(part, "ctx", forward) for part in ahead]
+            behind = [lax.ppermute(part, "ctx", backward) for part in behind[::-1]][::-1]
+        else:
+            last = [
+                lax.ppermute(ahead[0], "ctx", forward),
+                lax.ppermute(behind[1], "ctx", backward),
+            ]
+        if step == 1:
+            serve(held[:2], [0])
+        else:
+            serve(held, [1 - step, step - 1])
+    serve(last, [steps])
 
     attended = attend(plan, queries, positions, own, other)
     pieces = jnp.dot(attended, output_slab, preferred_element_type=jnp.float32).astype(

time: 129 us -> 124 us (0.961)
  waiting for transfers between devices: 53.9 us -> 47.4 us
  local copies, waits for them, and re-layouts: 6.73 us -> 8.65 us
    ppermute x6, waiting for transfers between devices: 17.3 us -> 4.96 us  [per_device(): lax.ppermute(part, 'ctx', backward)]
    ppermute x6, starting transfers between devices: 0.26 us -> 8.55 us  [per_device(): ahead = [lax.ppermute(part, 'ctx', forward) for part in ahead]]
    ppermute x6, starting transfers between devices: 13 us -> 4.71 us  [per_device(): lax.ppermute(part, 'ctx', backward)]
    ppermute x2, waiting for transfers between devices: 3.94 us -> 8.13 us  [the longest x1 6.98 us: per_device(): lax.ppermute(ahead[0], 'ctx', forward)]
    unnamed x17 -> x25, local copies, waits for them, and re-layouts: 6.61 us -> 8.52 us
    ppermute x6, waiting for transfers between devices: 0.16 us -> 1.82 us  [per_device(): ahead = [lax.ppermute(part, 'ctx', forward) for part in ahead]]
  transfers between devices with their start and end apart: 20 -> 20, of which waited for: 8 -> 7; matrix products, arithmetic and copies ran while one was open for 1% -> 1% of each run, Pallas kernels for 21% -> 22%
where the time goes in v4:
time: 124 us
  waiting for transfers between devices  47.4 us (38%)
  Pallas kernels  41.4 us (33%)
  starting transfers between devices  20.9 us (17%)
  local copies, waits for them, and re-layouts  8.65 us (7%)
  matrix products  5.13 us (4%)
    all_to_all x1, waiting for transfers between devices, per_device(): lax.all_to_all(pieces.reshape(ctx_count, MOST, model_width), 'ctx', split...  30.6 us
    pallas_call x5, Pallas kernels, project(): pl.pallas_call(functools.partial(project_kernel, offsets, len(blocks), EX...  26.9 us
    pallas_call x1, Pallas kernels, attend(): pl.pallas_call(functools.partial(attend_kernel, plan, tok_count, heads),...  12.4 us
    ppermute x6, starting transfers between devices, per_device(): ahead = [lax.ppermute(part, 'ctx', forward) for part in ahead]  8.55 us
    unnamed x25, local copies, waits for them, and re-layouts  8.52 us
    ppermute x1, waiting for transfers between devices, per_device(): lax.ppermute(ahead[0], 'ctx', forward)  6.98 us
    ppermute x6, waiting for transfers between devices, per_device(): lax.ppermute(part, 'ctx', backward)  4.96 us
    all_to_all x1, starting transfers between devices, per_device(): lax.all_to_all(pieces.reshape(ctx_count, MOST, model_width), 'ctx', split...  4.82 us
  transfers between devices with their start and end apart: 20, of which 7 were waited for; matrix products, arithmetic and copies ran while one was open for 1% of the time, Pallas kernels for 22%

profile of v4, /device:TPU:0, one launch (start us, length us, event | category | flops | bytes accessed | tf_op | source)
XLA Modules:
  0.0 124.0 jit_solution(8696579178005432724)
XLA Ops:
  0.0 0.0 copy-start
  0.0 2.1 %norm_rows.1 = (bf16[64,2176]{1,0:T(8,128)(2,1)}, bf16[64,2176]{1,0:T(8,128)(2,1)}) custom-call(bf16[128,2048]{1,0:T(8,128)(2,1)} %tokens_ref.1, f32[1,2048]{1,0:T(1,128)} %bitcast.21, s32[2,128]{1,0:T(2,128)} %bitcast.22), custom_call_target="tpu_custom_call" | custom-call | tf_op jit(solution)/shard_map/norm_rows/pallas_call | solution.py:59
  2.1 3.0 %collective-permute-start = (bf16[64,2176]{1,0:T(8,128)(2,1)}, bf16[64,2176]{1,0:T(8,128)(2,1)S(1)}, u32[]{:S(2)}, u32[]{:S(2)}) collective-permute-start(bf16[64,2176]{1,0:T(8,128)(2,1)} %get-tuple-element.31.refs_0_), channel_id=1, source_target_pairs={{0,4},{4,8},{8,12},{12,14},{14,10},{10,6},{6,2},{2,0},{1,5},{5,9},... | collective-permute-start | bytes 835592 | tf_op jit(solution)/shard_map/ppermute | solution.py:293
  5.2 0.0 collective-permute-start.3
  5.2 2.0 %collective-permute-start.2 = (bf16[64,2176]{1,0:T(8,128)(2,1)}, bf16[64,2176]{1,0:T(8,128)(2,1)S(1)}, u32[]{:S(2)}, u32[]{:S(2)}) collective-permute-start(bf16[64,2176]{1,0:T(8,128)(2,1)} %get-tuple-element.31.refs_0_), channel_id=1, source_target_pairs={{4,0},{8,4},{12,8},{14,12},{10,14},{6,10},{2,6},{0,2},{5,1},{9,5},... | collective-permute-start | bytes 835592 | tf_op jit(solution)/shard_map/ppermute | solution.py:294
  7.1 0.1 collective-permute-start.1
  7.2 2.2 %copy-done.1 = bf16[2048,1024]{1,0:T(8,128)(2,1)S(1)} copy-done((bf16[2048,1024]{1,0:T(8,128)(2,1)S(1)}, bf16[2048,1024]{1,0:T(8,128)(2,1)}, u32[]{:S(2)}) %copy-start.1) | copy-done | bytes 4194328
  9.4 2.2 %copy-done.3 = bf16[2048,1024]{1,0:T(8,128)(2,1)S(1)} copy-done((bf16[2048,1024]{1,0:T(8,128)(2,1)S(1)}, bf16[2048,1024]{1,0:T(8,128)(2,1)}, u32[]{:S(2)}) %copy-start.3) | copy-done | bytes 4194328
  11.6 2.2 %copy-done.5 = bf16[1,2048,1024]{2,1,0:T(8,128)(2,1)S(1)} copy-done((bf16[1,2048,1024]{2,1,0:T(8,128)(2,1)S(1)}, bf16[1,2048,1024]{2,1,0:T(8,128)(2,1)}, u32[]{:S(2)}) %copy-start.5) | copy-done | bytes 4194328
  13.8 1.0 copy-done.7
  14.7 1.0 copy-done.9
  15.7 4.6 %project.5 = (bf16[2,128,1024]{2,1,0:T(8,128)(2,1)S(1)}, bf16[1,48,1024]{2,1,0:T(8,128)(2,1)S(1)}, f32[1,48,128]{2,1,0:T(8,128)S(1)}) custom-call(bf16[64,2176]{1,0:T(8,128)(2,1)S(1)} %copy-done.9, bf16[64,2176]{1,0:T(8,128)(2,1)S(1)} %copy-done.7, bf16[2048,1024]{1,0:T(8,128)(2,1)S(1)} %copy-done.1, bf16[2048,1024]{1,0:T(8,128)(2,1)S(1)} %copy-done.3, ...), custom_call_target="tpu_custom_call" | custom-call | tf_op jit(solution)/shard_map/project/pallas_call | solution.py:108
  20.3 0.0 collective-permute-done.refs_0_
  20.4 0.0 collective-permute-done.3.refs_3_
  20.4 2.0 %collective-permute-start.4 = (bf16[64,2176]{1,0:T(8,128)(2,1)S(1)}, bf16[64,2176]{1,0:T(8,128)(2,1)S(1)}, u32[]{:S(2)}, u32[]{:S(2)}) collective-permute-start(bf16[64,2176]{1,0:T(8,128)(2,1)S(1)} %collective-permute-done.refs_0_), channel_id=1, source_target_pairs={{0,4},{4,8},{8,12},{12,14},{14,10},{10,6},{6,2},{2,0},{1,5},{5,9},... | collective-permute-start | bytes 835592 | tf_op jit(solution)/shard_map/ppermute | solution.py:293
  22.4 0.0 collective-permute-start.7
  22.4 0.0 collective-permute-done.2.refs_2_
  22.4 1.9 %collective-permute-start.6 = (bf16[64,2176]{1,0:T(8,128)(2,1)S(1)}, bf16[64,2176]{1,0:T(8,128)(2,1)S(1)}, u32[]{:S(2)}, u32[]{:S(2)}) collective-permute-start(bf16[64,2176]{1,0:T(8,128)(2,1)S(1)} %collective-permute-done.2.refs_2_), channel_id=1, source_target_pairs={{4,0},{8,4},{12,8},{14,12},{10,14},{6,10},{2,6},{0,2},{5,1},{9,5},... | collective-permute-start | bytes 835592 | tf_op jit(solution)/shard_map/ppermute | solution.py:294
  24.4 0.0 collective-permute-done.1.refs_1_
  24.4 0.1 collective-permute-start.5
  24.5 0.0 copy-done.2
  24.5 0.0 copy-done.4
  24.5 0.0 copy-done.6
  24.5 5.9 %project.6 = (bf16[2,256,1024]{2,1,0:T(8,128)(2,1)S(1)}, bf16[2,48,1024]{2,1,0:T(8,128)(2,1)S(1)}, f32[2,48,128]{2,1,0:T(8,128)S(1)}) custom-call(bf16[64,2176]{1,0:T(8,128)(2,1)S(1)} %collective-permute-done.refs_0_, bf16[64,2176]{1,0:T(8,128)(2,1)S(1)} %collective-permute-done.1.refs_1_, bf16[64,2176]{1,0:T(8,128)(2,1)S(1)} %collective-permute-done.2.refs_2_, ...), custom_call_target="tpu_custom_call" | custom-call | tf_op jit(solution)/shard_map/project/pallas_call | solution.py:108
  30.4 0.0 collective-permute-done.4.refs_0_
  30.4 1.6 %collective-permute-done.7.refs_3_ = bf16[64,2176]{1,0:T(8,128)(2,1)S(1)} collective-permute-done((bf16[64,2176]{1,0:T(8,128)(2,1)S(1)}, bf16[64,2176]{1,0:T(8,128)(2,1)S(1)}, u32[]{:S(2)}, u32[]{:S(2)}) %collective-permute-start.7) | collective-permute-done | bytes 278560 | tf_op jit(solution)/shard_map/ppermute | solution.py:294
  32.0 3.4 %collective-permute-done.6.refs_2_ = bf16[64,2176]{1,0:T(8,128)(2,1)S(1)} collective-permute-done((bf16[64,2176]{1,0:T(8,128)(2,1)S(1)}, bf16[64,2176]{1,0:T(8,128)(2,1)S(1)}, u32[]{:S(2)}, u32[]{:S(2)}) %collective-permute-start.6) | collective-permute-done | bytes 278560 | tf_op jit(solution)/shard_map/ppermute | solution.py:294
  35.4 0.3 collective-permute-start.10
  35.7 1.7 %collective-permute-start.8 = (bf16[64,2176]{1,0:T(8,128)(2,1)S(1)}, bf16[64,2176]{1,0:T(8,128)(2,1)S(1)}, u32[]{:S(2)}, u32[]{:S(2)}) collective-permute-start(bf16[64,2176]{1,0:T(8,128)(2,1)S(1)} %collective-permute-done.4.refs_0_), channel_id=1, source_target_pairs={{0,4},{4,8},{8,12},{12,14},{14,10},{10,6},{6,2},{2,0},{1,5},{5,9},... | collective-permute-start | bytes 835592 | tf_op jit(solution)/shard_map/ppermute | solution.py:293
  37.4 0.0 collective-permute-done.5.refs_1_
  37.4 1.6 %collective-permute-start.9 = (bf16[64,2176]{1,0:T(8,128)(2,1)S(1)}, bf16[64,2176]{1,0:T(8,128)(2,1)S(1)}, u32[]{:S(2)}, u32[]{:S(2)}) collective-permute-start(bf16[64,2176]{1,0:T(8,128)(2,1)S(1)} %collective-permute-done.5.refs_1_), channel_id=1, source_target_pairs={{0,4},{4,8},{8,12},{12,14},{14,10},{10,6},{6,2},{2,0},{1,5},{5,9},... | collective-permute-start | bytes 835592 | tf_op jit(solution)/shard_map/ppermute | solution.py:293
  39.0 0.4 collective-permute-start.11
  39.4 0.0 collective-permute-start.15
  39.4 5.9 %project.7 = (bf16[2,256,1024]{2,1,0:T(8,128)(2,1)S(1)}, bf16[2,48,1024]{2,1,0:T(8,128)(2,1)S(1)}, f32[2,48,128]{2,1,0:T(8,128)S(1)}) custom-call(bf16[64,2176]{1,0:T(8,128)(2,1)S(1)} %collective-permute-done.4.refs_0_, bf16[64,2176]{1,0:T(8,128)(2,1)S(1)} %collective-permute-done.5.refs_1_, bf16[64,2176]{1,0:T(8,128)(2,1)S(1)} %collective-permute-done.6.refs_2_, ...), custom_call_target="tpu_custom_call" | custom-call | tf_op jit(solution)/shard_map/project/pallas_call | solution.py:108
  45.3 0.0 collective-permute-done.10.refs_2_
  45.4 0.6 collective-permute-start.16
  45.9 1.8 %collective-permute-done.9.refs_1_ = bf16[64,2176]{1,0:T(8,128)(2,1)S(1)} collective-permute-done((bf16[64,2176]{1,0:T(8,128)(2,1)S(1)}, bf16[64,2176]{1,0:T(8,128)(2,1)S(1)}, u32[]{:S(2)}, u32[]{:S(2)}) %collective-permute-start.9) | collective-permute-done | bytes 278560 | tf_op jit(solution)/shard_map/ppermute | solution.py:293
  47.7 0.0 collective-permute-done.8.refs_0_
  47.7 0.0 collective-permute-done.11.refs_3_
  47.7 5.9 %project.8 = (bf16[2,256,1024]{2,1,0:T(8,128)(2,1)S(1)}, bf16[2,48,1024]{2,1,0:T(8,128)(2,1)S(1)}, f32[2,48,128]{2,1,0:T(8,128)S(1)}) custom-call(bf16[64,2176]{1,0:T(8,128)(2,1)S(1)} %collective-permute-done.8.refs_0_, bf16[64,2176]{1,0:T(8,128)(2,1)S(1)} %collective-permute-done.9.refs_1_, bf16[64,2176]{1,0:T(8,128)(2,1)S(1)} %collective-permute-done.10.refs_2_, ...), custom_call_target="tpu_custom_call" | custom-call | tf_op jit(solution)/shard_map/project/pallas_call | solution.py:108
  53.6 0.1 collective-permute-start.17
  53.7 1.5 %collective-permute-start.12 = (bf16[64,2176]{1,0:T(8,128)(2,1)S(1)}, bf16[64,2176]{1,0:T(8,128)(2,1)S(1)}, u32[]{:S(2)}, u32[]{:S(2)}) collective-permute-start(bf16[64,2176]{1,0:T(8,128)(2,1)S(1)} %collective-permute-done.8.refs_0_), channel_id=1, source_target_pairs={{0,4},{4,8},{8,12},{12,14},{14,10},{10,6},{6,2},{2,0},{1,5},{5,9},... | collective-permute-start | bytes 835592 | tf_op jit(solution)/shard_map/ppermute | solution.py:297
  55.2 0.6 collective-permute-start.13
  55.8 7.0 %collective-permute-done.12.refs_0_ = bf16[64,2176]{1,0:T(8,128)(2,1)S(1)} collective-permute-done((bf16[64,2176]{1,0:T(8,128)(2,1)S(1)}, bf16[64,2176]{1,0:T(8,128)(2,1)S(1)}, u32[]{:S(2)}, u32[]{:S(2)}) %collective-permute-start.12) | collective-permute-done | bytes 278560 | tf_op jit(solution)/shard_map/ppermute | solution.py:297
  62.8 0.0 collective-permute-start.14
  62.8 1.2 collective-permute-done.13.refs_1_
  63.9 4.6 %project.9 = (bf16[2,128,1024]{2,1,0:T(8,128)(2,1)S(1)}, bf16[1,48,1024]{2,1,0:T(8,128)(2,1)S(1)}, f32[1,48,128]{2,1,0:T(8,128)S(1)}) custom-call(bf16[64,2176]{1,0:T(8,128)(2,1)S(1)} %collective-permute-done.12.refs_0_, bf16[64,2176]{1,0:T(8,128)(2,1)S(1)} %collective-permute-done.13.refs_1_, bf16[2048,1024]{1,0:T(8,128)(2,1)S(1)} %copy-done.2, ...), custom_call_target="tpu_custom_call" | custom-call | tf_op jit(solution)/shard_map/project/pallas_call | solution.py:108
  68.5 0.1 collective-permute-start.18
  68.6 0.0 collective-permute-done.14.refs_15_
  68.6 0.0 collective-permute-done.15.refs_16_
  68.6 0.0 collective-permute-done.16.refs_17_
  68.6 1.9 %collective-permute-done.18.refs_19_ = bf16[2,128,1024]{2,1,0:T(8,128)(2,1)S(1)} collective-permute-done((bf16[2,128,1024]{2,1,0:T(8,128)(2,1)S(1)}, bf16[2,128,1024]{2,1,0:T(8,128)(2,1)S(1)}, u32[]{:S(2)}, u32[]{:S(2)}) %collective-permute-start.18) | collective-permute-done | bytes 524320 | tf_op jit(solution)/shard_map/ppermute | solution.py:278
  70.5 0.0 collective-permute-done.17.refs_18_
  70.5 12.4 %attend.1 = bf16[320,1024]{1,0:T(8,128)(2,1)S(1)} custom-call(bf16[1,48,1024]{2,1,0:T(8,128)(2,1)S(1)} %get-tuple-element.33.refs_0_, bf16[2,48,1024]{2,1,0:T(8,128)(2,1)S(1)} %get-tuple-element.34.refs_1_, bf16[2,48,1024]{2,1,0:T(8,128)(2,1)S(1)} %get-tuple-element.38.refs_2_, bf16[2,48,1024]{2,1,0:T(8,128)(2,1)S(1)} %get-tuple-element.42.refs_3_, ...), custom_call_target="tpu_custom_call" | custom-call | tf_op jit(solution)/shard_map/attend/pallas_call | solution.py:232
  82.9 0.0 copy-done.11
  82.9 0.0 copy-start.10
  82.9 0.0 copy-start.8
  82.9 2.6 %fusion.2 = bf16[320,2048]{1,0:T(8,128)(2,1)} fusion(bf16[320,1024]{1,0:T(8,128)(2,1)S(1)} %attend.1, bf16[1,1024,2048]{2,1,0:T(8,128)(2,1)S(1)} %copy-done.11), kind=kOutput, calls=%fused_computation.2 | convolution fusion | flops 1342832640 | bytes 6160384 | tf_op jit(solution)/shard_map/dot_general | solution.py:307
  85.5 4.8 %all-to-all-start = ((bf16[8,40,2048]{2,1,0:T(8,128)(2,1)}), bf16[8,40,2048]{2,1,0:T(8,128)(2,1)S(1)}, u32[]{:S(2)}, u32[]{:S(2)}) async-start(bf16[8,40,2048]{2,1,0:T(8,128)(2,1)} %bitcast.4), calls=%async_computation | async-start | bytes 2621440 | tf_op jit(solution)/shard_map/all_to_all | solution.py:310
  90.5 0.7 fusion.14
  91.2 0.2 fusion.12
  91.4 0.1 fusion.11
  91.5 30.6 %all-to-all-done = bf16[8,40,2048]{2,1,0:T(8,128)(2,1)S(1)} async-done(((bf16[8,40,2048]{2,1,0:T(8,128)(2,1)}), bf16[8,40,2048]{2,1,0:T(8,128)(2,1)S(1)}, u32[]{:S(2)}, u32[]{:S(2)}) %all-to-all-start) | async-done | bytes 1310752 | tf_op jit(solution)/shard_map/all_to_all | solution.py:310
  122.2 1.8 %fusion.5 = bf16[128,2048]{1,0:T(8,128)(2,1)} fusion(bf16[8,40,2048]{2,1,0:T(8,128)(2,1)S(1)} %all-to-all-done, f32[128,8]{0,1:T(8,128)S(1)} %copy.15, f32[128,8]{0,1:T(8,128)S(1)} %copy.12), kind=kOutput, calls=%fused_computation.4 | convolution fusion | flops 1006977024 | bytes 1843200 | tf_op jit(solution)/shard_map/dot_general | solution.py:327
  (17 shorter events, 0.2 us)
Async XLA Ops:
  0.0 90.5 %copy-start = (f32[2048,8]{0,1:T(8,128)S(1)}, f32[2048,8]{0,1:T(8,128)}, u32[]{:S(2)}) copy-start(f32[2048,8]{0,1:T(8,128)} %param.10) | copy-start | bytes 196612
  2.1 18.2 %collective-permute-start = (bf16[64,2176]{1,0:T(8,128)(2,1)}, bf16[64,2176]{1,0:T(8,128)(2,1)S(1)}, u32[]{:S(2)}, u32[]{:S(2)}) collective-permute-start(bf16[64,2176]{1,0:T(8,128)(2,1)} %get-tuple-element.31.refs_0_), channel_id=1, source_target_pairs={{0,4},{4,8},{8,12},{12,14},{14,10},{10,6},{6,2},{2,0},{1,5},{5,9},... | collective-permute-start | bytes 835592 | tf_op jit(solution)/shard_map/ppermute | solution.py:293
  5.2 15.2 %collective-permute-start.3 = (bf16[64,2176]{1,0:T(8,128)(2,1)}, bf16[64,2176]{1,0:T(8,128)(2,1)S(1)}, u32[]{:S(2)}, u32[]{:S(2)}) collective-permute-start(bf16[64,2176]{1,0:T(8,128)(2,1)} %get-tuple-element.32.refs_1_), channel_id=1, source_target_pairs={{4,0},{8,4},{12,8},{14,12},{10,14},{6,10},{2,6},{0,2},{5,1},{9,5},... | collective-permute-start | bytes 835592 | tf_op jit(solution)/shard_map/ppermute | solution.py:294
  5.2 17.3 %collective-permute-start.2 = (bf16[64,2176]{1,0:T(8,128)(2,1)}, bf16[64,2176]{1,0:T(8,128)(2,1)S(1)}, u32[]{:S(2)}, u32[]{:S(2)}) collective-permute-start(bf16[64,2176]{1,0:T(8,128)(2,1)} %get-tuple-element.31.refs_0_), channel_id=1, source_target_pairs={{4,0},{8,4},{12,8},{14,12},{10,14},{6,10},{2,6},{0,2},{5,1},{9,5},... | collective-permute-start | bytes 835592 | tf_op jit(solution)/shard_map/ppermute | solution.py:294
  7.1 17.3 %collective-permute-start.1 = (bf16[64,2176]{1,0:T(8,128)(2,1)}, bf16[64,2176]{1,0:T(8,128)(2,1)S(1)}, u32[]{:S(2)}, u32[]{:S(2)}) collective-permute-start(bf16[64,2176]{1,0:T(8,128)(2,1)} %get-tuple-element.32.refs_1_), channel_id=1, source_target_pairs={{0,4},{4,8},{8,12},{12,14},{14,10},{10,6},{6,2},{2,0},{1,5},{5,9},... | collective-permute-start | bytes 835592 | tf_op jit(solution)/shard_map/ppermute | solution.py:293
  7.2 2.2 %copy-start.1 = (bf16[2048,1024]{1,0:T(8,128)(2,1)S(1)}, bf16[2048,1024]{1,0:T(8,128)(2,1)}, u32[]{:S(2)}) copy-start(bf16[2048,1024]{1,0:T(8,128)(2,1)} %refs_2_.3) | copy-start | bytes 12582916
  9.4 2.2 %copy-start.3 = (bf16[2048,1024]{1,0:T(8,128)(2,1)S(1)}, bf16[2048,1024]{1,0:T(8,128)(2,1)}, u32[]{:S(2)}) copy-start(bf16[2048,1024]{1,0:T(8,128)(2,1)} %refs_3_.3) | copy-start | bytes 12582916
  11.6 2.2 %copy-start.5 = (bf16[1,2048,1024]{2,1,0:T(8,128)(2,1)S(1)}, bf16[1,2048,1024]{2,1,0:T(8,128)(2,1)}, u32[]{:S(2)}) copy-start(bf16[1,2048,1024]{2,1,0:T(8,128)(2,1)} %param.14) | copy-start | bytes 12582916
  13.8 1.0 copy-start.7
  14.7 1.0 copy-start.9
  15.7 8.8 %copy-start.2 = (bf16[2048,1024]{1,0:T(8,128)(2,1)S(1)}, bf16[2048,1024]{1,0:T(8,128)(2,1)}, u32[]{:S(2)}) copy-start(bf16[2048,1024]{1,0:T(8,128)(2,1)} %refs_2_.3) | copy-start | bytes 12582916
  15.7 8.8 %copy-start.4 = (bf16[2048,1024]{1,0:T(8,128)(2,1)S(1)}, bf16[2048,1024]{1,0:T(8,128)(2,1)}, u32[]{:S(2)}) copy-start(bf16[2048,1024]{1,0:T(8,128)(2,1)} %refs_3_.3) | copy-start | bytes 12582916
  15.7 8.8 %copy-start.6 = (bf16[1,2048,1024]{2,1,0:T(8,128)(2,1)S(1)}, bf16[1,2048,1024]{2,1,0:T(8,128)(2,1)}, u32[]{:S(2)}) copy-start(bf16[1,2048,1024]{2,1,0:T(8,128)(2,1)} %param.14) | copy-start | bytes 12582916
  20.4 10.1 %collective-permute-start.4 = (bf16[64,2176]{1,0:T(8,128)(2,1)S(1)}, bf16[64,2176]{1,0:T(8,128)(2,1)S(1)}, u32[]{:S(2)}, u32[]{:S(2)}) collective-permute-start(bf16[64,2176]{1,0:T(8,128)(2,1)S(1)} %collective-permute-done.refs_0_), channel_id=1, source_target_pairs={{0,4},{4,8},{8,12},{12,14},{14,10},{10,6},{6,2},{2,0},{1,5},{5,9},... | collective-permute-start | bytes 835592 | tf_op jit(solution)/shard_map/ppermute | solution.py:293
  22.4 9.6 %collective-permute-start.7 = (bf16[64,2176]{1,0:T(8,128)(2,1)S(1)}, bf16[64,2176]{1,0:T(8,128)(2,1)S(1)}, u32[]{:S(2)}, u32[]{:S(2)}) collective-permute-start(bf16[64,2176]{1,0:T(8,128)(2,1)S(1)} %collective-permute-done.3.refs_3_), channel_id=1, source_target_pairs={{4,0},{8,4},{12,8},{14,12},{10,14},{6,10},{2,6},{0,2},{5,1},{9,5},... | collective-permute-start | bytes 835592 | tf_op jit(solution)/shard_map/ppermute | solution.py:294
  22.4 12.9 %collective-permute-start.6 = (bf16[64,2176]{1,0:T(8,128)(2,1)S(1)}, bf16[64,2176]{1,0:T(8,128)(2,1)S(1)}, u32[]{:S(2)}, u32[]{:S(2)}) collective-permute-start(bf16[64,2176]{1,0:T(8,128)(2,1)S(1)} %collective-permute-done.2.refs_2_), channel_id=1, source_target_pairs={{4,0},{8,4},{12,8},{14,12},{10,14},{6,10},{2,6},{0,2},{5,1},{9,5},... | collective-permute-start | bytes 835592 | tf_op jit(solution)/shard_map/ppermute | solution.py:294
  24.4 13.0 %collective-permute-start.5 = (bf16[64,2176]{1,0:T(8,128)(2,1)S(1)}, bf16[64,2176]{1,0:T(8,128)(2,1)S(1)}, u32[]{:S(2)}, u32[]{:S(2)}) collective-permute-start(bf16[64,2176]{1,0:T(8,128)(2,1)S(1)} %collective-permute-done.1.refs_1_), channel_id=1, source_target_pairs={{0,4},{4,8},{8,12},{12,14},{14,10},{10,6},{6,2},{2,0},{1,5},{5,9},... | collective-permute-start | bytes 835592 | tf_op jit(solution)/shard_map/ppermute | solution.py:293
  35.4 10.0 %collective-permute-start.10 = (bf16[64,2176]{1,0:T(8,128)(2,1)S(1)}, bf16[64,2176]{1,0:T(8,128)(2,1)S(1)}, u32[]{:S(2)}, u32[]{:S(2)}) collective-permute-start(bf16[64,2176]{1,0:T(8,128)(2,1)S(1)} %collective-permute-done.6.refs_2_), channel_id=1, source_target_pairs={{4,0},{8,4},{12,8},{14,12},{10,14},{6,10},{2,6},{0,2},{5,1},{9,5},... | collective-permute-start | bytes 835592 | tf_op jit(solution)/shard_map/ppermute | solution.py:294
  35.7 12.0 %collective-permute-start.8 = (bf16[64,2176]{1,0:T(8,128)(2,1)S(1)}, bf16[64,2176]{1,0:T(8,128)(2,1)S(1)}, u32[]{:S(2)}, u32[]{:S(2)}) collective-permute-start(bf16[64,2176]{1,0:T(8,128)(2,1)S(1)} %collective-permute-done.4.refs_0_), channel_id=1, source_target_pairs={{0,4},{4,8},{8,12},{12,14},{14,10},{10,6},{6,2},{2,0},{1,5},{5,9},... | collective-permute-start | bytes 835592 | tf_op jit(solution)/shard_map/ppermute | solution.py:293
  37.4 10.3 %collective-permute-start.9 = (bf16[64,2176]{1,0:T(8,128)(2,1)S(1)}, bf16[64,2176]{1,0:T(8,128)(2,1)S(1)}, u32[]{:S(2)}, u32[]{:S(2)}) collective-permute-start(bf16[64,2176]{1,0:T(8,128)(2,1)S(1)} %collective-permute-done.5.refs_1_), channel_id=1, source_target_pairs={{0,4},{4,8},{8,12},{12,14},{14,10},{10,6},{6,2},{2,0},{1,5},{5,9},... | collective-permute-start | bytes 835592 | tf_op jit(solution)/shard_map/ppermute | solution.py:293
  39.0 8.7 %collective-permute-start.11 = (bf16[64,2176]{1,0:T(8,128)(2,1)S(1)}, bf16[64,2176]{1,0:T(8,128)(2,1)S(1)}, u32[]{:S(2)}, u32[]{:S(2)}) collective-permute-start(bf16[64,2176]{1,0:T(8,128)(2,1)S(1)} %collective-permute-done.7.refs_3_), channel_id=1, source_target_pairs={{4,0},{8,4},{12,8},{14,12},{10,14},{6,10},{2,6},{0,2},{5,1},{9,5},... | collective-permute-start | bytes 835592 | tf_op jit(solution)/shard_map/ppermute | solution.py:294
  39.4 29.2 %collective-permute-start.15 = (bf16[2,256,1024]{2,1,0:T(8,128)(2,1)S(1)}, bf16[2,256,1024]{2,1,0:T(8,128)(2,1)S(1)}, u32[]{:S(2)}, u32[]{:S(2)}) collective-permute-start(bf16[2,256,1024]{2,1,0:T(8,128)(2,1)S(1)} %get-tuple-element.53.refs_11_), channel_id=1, source_target_pairs={{0,1},{1,0},{2,3},{3,2},{4,5},{5,4},{6,7},{7,6},{8,9},{9,8},{10,11... | collective-permute-start | bytes 3145736 | tf_op jit(solution)/shard_map/ppermute | solution.py:278
  45.4 23.2 %collective-permute-start.16 = (bf16[2,256,1024]{2,1,0:T(8,128)(2,1)S(1)}, bf16[2,256,1024]{2,1,0:T(8,128)(2,1)S(1)}, u32[]{:S(2)}, u32[]{:S(2)}) collective-permute-start(bf16[2,256,1024]{2,1,0:T(8,128)(2,1)S(1)} %get-tuple-element.54.refs_12_), channel_id=1, source_target_pairs={{0,1},{1,0},{2,3},{3,2},{4,5},{5,4},{6,7},{7,6},{8,9},{9,8},{10,11... | collective-permute-start | bytes 3145736 | tf_op jit(solution)/shard_map/ppermute | solution.py:278
  53.6 16.8 %collective-permute-start.17 = (bf16[2,256,1024]{2,1,0:T(8,128)(2,1)S(1)}, bf16[2,256,1024]{2,1,0:T(8,128)(2,1)S(1)}, u32[]{:S(2)}, u32[]{:S(2)}) collective-permute-start(bf16[2,256,1024]{2,1,0:T(8,128)(2,1)S(1)} %get-tuple-element.55.refs_13_), channel_id=1, source_target_pairs={{0,1},{1,0},{2,3},{3,2},{4,5},{5,4},{6,7},{7,6},{8,9},{9,8},{10,11... | collective-permute-start | bytes 3145736 | tf_op jit(solution)/shard_map/ppermute | solution.py:278
  53.7 9.1 %collective-permute-start.12 = (bf16[64,2176]{1,0:T(8,128)(2,1)S(1)}, bf16[64,2176]{1,0:T(8,128)(2,1)S(1)}, u32[]{:S(2)}, u32[]{:S(2)}) collective-permute-start(bf16[64,2176]{1,0:T(8,128)(2,1)S(1)} %collective-permute-done.8.refs_0_), channel_id=1, source_target_pairs={{0,4},{4,8},{8,12},{12,14},{14,10},{10,6},{6,2},{2,0},{1,5},{5,9},... | collective-permute-start | bytes 835592 | tf_op jit(solution)/shard_map/ppermute | solution.py:297
  55.2 8.7 %collective-permute-start.13 = (bf16[64,2176]{1,0:T(8,128)(2,1)S(1)}, bf16[64,2176]{1,0:T(8,128)(2,1)S(1)}, u32[]{:S(2)}, u32[]{:S(2)}) collective-permute-start(bf16[64,2176]{1,0:T(8,128)(2,1)S(1)} %collective-permute-done.11.refs_3_), channel_id=1, source_target_pairs={{4,0},{8,4},{12,8},{14,12},{10,14},{6,10},{2,6},{0,2},{5,1},{9,5},... | collective-permute-start | bytes 835592 | tf_op jit(solution)/shard_map/ppermute | solution.py:298
  62.8 5.8 %collective-permute-start.14 = (bf16[2,128,1024]{2,1,0:T(8,128)(2,1)S(1)}, bf16[2,128,1024]{2,1,0:T(8,128)(2,1)S(1)}, u32[]{:S(2)}, u32[]{:S(2)}) collective-permute-start(bf16[2,128,1024]{2,1,0:T(8,128)(2,1)S(1)} %get-tuple-element.52.refs_10_), channel_id=1, source_target_pairs={{0,1},{1,0},{2,3},{3,2},{4,5},{5,4},{6,7},{7,6},{8,9},{9,8},{10,11... | collective-permute-start | bytes 1572872 | tf_op jit(solution)/shard_map/ppermute | solution.py:278
  68.5 2.0 %collective-permute-start.18 = (bf16[2,128,1024]{2,1,0:T(8,128)(2,1)S(1)}, bf16[2,128,1024]{2,1,0:T(8,128)(2,1)S(1)}, u32[]{:S(2)}, u32[]{:S(2)}) collective-permute-start(bf16[2,128,1024]{2,1,0:T(8,128)(2,1)S(1)} %get-tuple-element.56.refs_14_), channel_id=1, source_target_pairs={{0,1},{1,0},{2,3},{3,2},{4,5},{5,4},{6,7},{7,6},{8,9},{9,8},{10,11... | collective-permute-start | bytes 1572872 | tf_op jit(solution)/shard_map/ppermute | solution.py:278
  70.5 12.4 %copy-start.11 = (bf16[1,1024,2048]{2,1,0:T(8,128)(2,1)S(1)}, bf16[1,1024,2048]{2,1,0:T(8,128)(2,1)}, u32[]{:S(2)}) copy-start(bf16[1,1024,2048]{2,1,0:T(8,128)(2,1)} %param.15) | copy-start | bytes 12582916
  82.9 7.5 %copy-start.10 = (bf16[64,2176]{1,0:T(8,128)(2,1)S(1)}, bf16[64,2176]{1,0:T(8,128)(2,1)}, u32[]{:S(2)}) copy-start(bf16[64,2176]{1,0:T(8,128)(2,1)} %get-tuple-element.31.refs_0_) | copy-start | bytes 835588
  82.9 7.5 %copy-start.8 = (bf16[64,2176]{1,0:T(8,128)(2,1)S(1)}, bf16[64,2176]{1,0:T(8,128)(2,1)}, u32[]{:S(2)}) copy-start(bf16[64,2176]{1,0:T(8,128)(2,1)} %get-tuple-element.32.refs_1_) | copy-start | bytes 835588
  85.5 36.6 %all-to-all-start = ((bf16[8,40,2048]{2,1,0:T(8,128)(2,1)}), bf16[8,40,2048]{2,1,0:T(8,128)(2,1)S(1)}, u32[]{:S(2)}, u32[]{:S(2)}) async-start(bf16[8,40,2048]{2,1,0:T(8,128)(2,1)} %bitcast.4), calls=%async_computation | async-start | bytes 2621440 | tf_op jit(solution)/shard_map/all_to_all | solution.py:310

commit v5 on v3

--- a/solution.py
+++ b/solution.py
@@ -61,10 +61,41 @@
     )(tokens, norm_gain.reshape(1, -1), routes.T)
 
 
-def project_kernel(offsets, count, experts, *refs):
+def keys_kernel(count, *refs):
     blocks = refs[:count]
-    key_ref, value_ref, query_ref, panel_ref, out_ref, pos_ref, picked = refs[count:]
-    width = key_ref.shape[0]
+    weight_ref, out_ref, mark_ref = refs[count:]
+    rows = jnp.concatenate([block[:, : weight_ref.shape[0]] for block in blocks], axis=0)
+    product = jnp.dot(rows, weight_ref[...], preferred_element_type=jnp.float32)
+    out_ref[...] = product.astype(jnp.bfloat16)
+    mark_ref[...] = product[:8, :LANES]
+
+
+def project_keys(blocks, key_weight):
+    row_count = sum(block.shape[0] for block in blocks)
+    model_width, width = key_weight.shape
+    step = min(width, 256)
+    return pl.pallas_call(
+        functools.partial(keys_kernel, len(blocks)),
+        grid=(width // step,),
+        in_specs=[pl.BlockSpec(block.shape, lambda n: (0, 0)) for block in blocks]
+        + [pl.BlockSpec((model_width, step), lambda n: (0, n))],
+        out_specs=[
+            pl.BlockSpec((row_count, step), lambda n: (0, n)),
+            pl.BlockSpec((8, LANES), lambda n: (0, 0)),
+        ],
+        out_shape=[
+            jax.ShapeDtypeStruct((row_count, width), jnp.bfloat16),
+            jax.ShapeDtypeStruct((8, LANES), jnp.float32),
+        ],
+        compiler_params=pltpu.CompilerParams(vmem_limit_bytes=12 * MIB),
+        name="project_keys",
+    )(*blocks, key_weight)
+
+
+def values_kernel(offsets, count, experts, mark_ref, *refs):
+    blocks = refs[:count]
+    value_ref, query_ref, panel_ref, out_ref, pos_ref, picked = refs[count:]
+    width = value_ref.shape[0]
     rows = jnp.concatenate([block[:, :width] for block in blocks], axis=0)
     tok_count = rows.shape[0] // len(offsets)
 
@@ -88,10 +119,7 @@
                 chosen, number, preferred_element_type=jnp.float32
             ) + start.astype(jnp.float32)
 
-    panel_ref[0] = jnp.dot(
-        rows, key_ref[...], preferred_element_type=jnp.float32
-    ).astype(jnp.bfloat16)
-    panel_ref[1] = jnp.dot(
+    panel_ref[...] = jnp.dot(
         rows, value_ref[...], preferred_element_type=jnp.float32
     ).astype(jnp.bfloat16)
     queries = jnp.dot(picked[...], query_ref[...], preferred_element_type=jnp.float32)
@@ -99,47 +127,49 @@
         out_ref[g] = queries[g * SLOTS : (g + 1) * SLOTS].astype(jnp.bfloat16)
 
 
-def project(blocks, offsets, key_weight, value_weight, query_slab):
+def project_values(blocks, offsets, mark, value_weight, query_slab):
     row_count = sum(block.shape[0] for block in blocks)
-    model_width, width = key_weight.shape
+    model_width, width = value_weight.shape
     step = min(width, 256)
     owners = len(offsets)
     weight_spec = pl.BlockSpec((model_width, step), lambda n: (0, n))
     return pl.pallas_call(
-        functools.partial(project_kernel, offsets, len(blocks), EXPERTS),
+        functools.partial(values_kernel, offsets, len(blocks), EXPERTS),
         grid=(width // step,),
-        in_specs=[pl.BlockSpec(block.shape, lambda n: (0, 0)) for block in blocks]
-        + [weight_spec] * 3,
+        in_specs=[pl.BlockSpec(mark.shape, lambda n: (0, 0))]
+        + [pl.BlockSpec(block.shape, lambda n: (0, 0)) for block in blocks]
+        + [weight_spec] * 2,
         out_specs=[
-            pl.BlockSpec((2, row_count, step), lambda n: (0, 0, n)),
+            pl.BlockSpec((row_count, step), lambda n: (0, n)),
             pl.BlockSpec((owners, SLOTS, step), lambda n: (0, 0, n)),
             pl.BlockSpec((owners, SLOTS, LANES), lambda n: (0, 0, 0)),
         ],
         out_shape=[
-            jax.ShapeDtypeStruct((2, row_count, width), jnp.bfloat16),
+            jax.ShapeDtypeStruct((row_count, width), jnp.bfloat16),
             jax.ShapeDtypeStruct((owners, SLOTS, width), jnp.bfloat16),
             jax.ShapeDtypeStruct((owners, SLOTS, LANES), jnp.float32),
         ],
         scratch_shapes=[pltpu.VMEM((owners * SLOTS, model_width), jnp.bfloat16)],
-        compiler_params=pltpu.CompilerParams(vmem_limit_bytes=20 * MIB),
-        name="project",
-    )(*blocks, key_weight, value_weight, query_slab)
-
-
-def attend_kernel(plan, tok_count, heads, *refs):
+        compiler_params=pltpu.CompilerParams(vmem_limit_bytes=16 * MIB),
+        name="project_values",
+    )(mark, *blocks, value_weight, query_slab)
+
+
+def attend_kernel(plan, tok_count, heads, flip, *refs):
     count = len(plan)
-    query_refs, pos_refs, own_refs, other_refs = (
-        refs[k * count : (k + 1) * count] for k in range(4)
-    )
-    out_ref, places, queries, keys, values, scores, weights = refs[4 * count :]
+    query_refs, pos_refs, own_keys, own_values, other_keys, other_values = (
+        refs[k * count : (k + 1) * count] for k in range(6)
+    )
+    out_ref, places, queries, keys, values, scores, weights = refs[6 * count :]
     side = lax.axis_index("exp")
     exp_count = 2
     rate = math.log2(math.e) / math.sqrt(HS)
     tile = 2 * MOST
     per_span = 2 * exp_count
     span = per_span * tok_count
-    tiles = queries.shape[1] // 2
-    group = min(tiles, 4)
+    owners = queries.shape[1]
+    half_tiles = owners // 4
+    group = min(half_tiles, 4)
 
     @pl.when(pl.program_id(0) == 0)
     def _():
@@ -147,21 +177,21 @@
             for g, offset in enumerate(offsets):
                 places[ring_owner(offset)] = pos_ref[g, :MOST]
 
-    for offsets, query_ref, own_ref, other_ref in zip(plan, query_refs, own_refs, other_refs):
+    for p, offsets in enumerate(plan):
         for g, offset in enumerate(offsets):
             owner = ring_owner(offset)
             part = pl.ds(g * tok_count, tok_count)
+            here, there = owner * exp_count + side, owner * exp_count + 1 - side
             for h in range(heads):
                 lanes = pl.ds(h * HS, HS)
-                queries[h, owner] = query_ref[g, :, lanes].astype(jnp.float32)[:MOST]
-                keys[h, owner * exp_count + side] = own_ref[0, part, lanes]
-                values[h, owner * exp_count + side] = own_ref[1, part, lanes]
-                keys[h, owner * exp_count + 1 - side] = other_ref[0, part, lanes]
-                values[h, owner * exp_count + 1 - side] = other_ref[1, part, lanes]
-
-    for lead in range(0, tiles, group):
+                queries[h, owner] = query_refs[p][g, :, lanes].astype(jnp.float32)[:MOST]
+                keys[h, here] = own_keys[p][part, lanes]
+                values[h, here] = own_values[p][part, lanes]
+                keys[h, there] = other_keys[p][part, lanes]
+                values[h, there] = other_values[p][part, lanes]
+
+    def serve(lead, first):
         top = lead + group
-        base = lead * tile
         for h in range(heads):
             held = queries[h, 2 * lead : 2 * top].reshape(group * tile, HS).astype(jnp.bfloat16)
             for j in range(top):
@@ -209,32 +239,46 @@
                 for i in range(skip, group):
                     piece = product[(i - skip) * tile : (i - skip + 1) * tile]
                     sums[i] = piece if sums[i] is None else sums[i] + piece
+            spare = jnp.zeros((SLOTS - MOST, HS), jnp.float32)
             for i in range(group):
-                out_ref[pl.ds(base + i * tile, tile), pl.ds(h * HS, HS)] = sums[i].astype(
-                    jnp.bfloat16
-                )
-
-
-def attend(plan, queries, positions, own, other):
+                for part in range(2):
+                    rows = jnp.concatenate([sums[i][part * MOST : (part + 1) * MOST], spare], axis=0)
+                    place = 2 * (lead - first + i) + part
+                    out_ref[place, :, pl.ds(h * HS, HS)] = rows.astype(jnp.bfloat16)
+
+    late = (lax.axis_index("ctx") >= owners // 2) != flip
+
+    @pl.when(late)
+    def _():
+        for lead in range(half_tiles, 2 * half_tiles, group):
+            serve(lead, half_tiles)
+
+    @pl.when(jnp.logical_not(late))
+    def _():
+        for lead in range(0, half_tiles, group):
+            serve(lead, 0)
+
+
+def attend(flip, plan, queries, positions, own_keys, own_values, other_keys, other_values):
     owners = sum(len(offsets) for offsets in plan)
     row_count = owners * MOST
     width = queries[0].shape[-1]
     heads = 2 if owners <= 8 else 1
     step = heads * HS
-    tok_count = own[0].shape[1] // len(plan[0])
+    tok_count = own_keys[0].shape[0] // len(plan[0])
     length = owners * 2 * tok_count
-    group_rows = min(row_count, 8 * MOST)
+    group_rows = min(row_count // 2, 8 * MOST)
     query_specs = [pl.BlockSpec((q.shape[0], SLOTS, step), lambda h: (0, 0, h)) for q in queries]
     pos_specs = [pl.BlockSpec(p.shape, lambda h: (0, 0, 0)) for p in positions]
-    panel_specs = [pl.BlockSpec((2, p.shape[1], step), lambda h: (0, 0, h)) for p in own]
+    panel_specs = [pl.BlockSpec((p.shape[0], step), lambda h: (0, h)) for p in own_keys]
     scratch = heads * (group_rows * length * 6 + length * HS * 4 + row_count * HS * 4)
-    windows = 2 * (length * step * 4 + row_count * step * 4) + 4 * row_count * LANES * 4
-    return pl.pallas_call(
-        functools.partial(attend_kernel, plan, tok_count, heads),
+    windows = 2 * (length * step * 4 + row_count * step * 5) + 5 * row_count * LANES * 4
+    return pl.pallas_call(
+        functools.partial(attend_kernel, plan, tok_count, heads, flip),
         grid=(width // step,),
-        in_specs=query_specs + pos_specs + panel_specs + panel_specs,
-        out_specs=pl.BlockSpec((row_count, step), lambda h: (0, h)),
-        out_shape=jax.ShapeDtypeStruct((row_count, width), jnp.bfloat16),
+        in_specs=query_specs + pos_specs + panel_specs * 4,
+        out_specs=pl.BlockSpec((owners // 2, SLOTS, step), lambda h: (0, 0, h)),
+        out_shape=jax.ShapeDtypeStruct((owners // 2, SLOTS, width), jnp.bfloat16),
         scratch_shapes=[
             pltpu.VMEM((owners, MOST, LANES), jnp.float32),
             pltpu.VMEM((heads, owners, MOST, HS), jnp.float32),
@@ -243,9 +287,93 @@
             pltpu.VMEM((heads, group_rows, length), jnp.float32),
             pltpu.VMEM((heads, group_rows, length), jnp.bfloat16),
         ],
-        compiler_params=pltpu.CompilerParams(vmem_limit_bytes=scratch + windows + 4 * MIB),
+        compiler_params=pltpu.CompilerParams(vmem_limit_bytes=scratch + windows * 5 // 4 + 4 * MIB),
         name="attend",
-    )(*queries, *positions, *own, *other)
+    )(*queries, *positions, *own_keys, *own_values, *other_keys, *other_values)
+
+
+def output_kernel(attended_ref, weight_ref, *refs):
+    outs, pieces = refs[:-1], refs[-1]
+    count, _, width = attended_ref.shape
+    rows = attended_ref[...].reshape(count * SLOTS, width)
+    product = jnp.dot(rows, weight_ref[...], preferred_element_type=jnp.float32)
+    for b in range(count):
+        pieces[b] = product[b * SLOTS : b * SLOTS + MOST]
+    own = lax.rem(lax.axis_index("ctx"), count)
+    for r, out_ref in enumerate(outs):
+        out_ref[...] = pieces[own ^ r].astype(jnp.bfloat16)
+
+
+def project_output(attended, output_slab):
+    count, _, width = attended.shape
+    model_width = output_slab.shape[1]
+    step = 512
+    return pl.pallas_call(
+        output_kernel,
+        grid=(model_width // step,),
+        in_specs=[
+            pl.BlockSpec(attended.shape, lambda n: (0, 0, 0)),
+            pl.BlockSpec((width, step), lambda n: (0, n)),
+        ],
+        out_specs=[pl.BlockSpec((MOST, step), lambda n: (0, n))] * count,
+        out_shape=[jax.ShapeDtypeStruct((MOST, model_width), jnp.bfloat16)] * count,
+        scratch_shapes=[pltpu.VMEM((count, MOST, step), jnp.float32)],
+        compiler_params=pltpu.CompilerParams(vmem_limit_bytes=12 * MIB),
+        name="project_output",
+    )(attended, output_slab)
+
+
+def combine_kernel(quarter_count, slots_ref, gates_ref, *refs):
+    pieces, out_ref, mix = refs[:-2], refs[-2], refs[-1]
+    tok_count = slots_ref.shape[0]
+
+    @pl.when(pl.program_id(0) == 0)
+    def _():
+        slots = slots_ref[...].astype(jnp.float32)
+        gates = gates_ref[...]
+        lane = lax.broadcasted_iota(jnp.int32, slots.shape, 1)
+        wide = lax.broadcasted_iota(jnp.int32, (tok_count, len(pieces) * SLOTS), 1).astype(
+            jnp.float32
+        )
+        total = jnp.zeros_like(wide)
+        for k in range(len(pieces)):
+            mine = lane == (lax.axis_index("ctx") ^ k) // quarter_count
+            slot = jnp.sum(jnp.where(mine, slots, 0.0), axis=1, keepdims=True)
+            gate = jnp.sum(jnp.where(mine, gates, 0.0), axis=1, keepdims=True)
+            spot = jnp.where(slot >= 0, slot + float(k * SLOTS), -1.0)
+            total = total + jnp.where(wide == spot, gate, 0.0)
+        for part in range(3):
+            term = total.astype(jnp.bfloat16)
+            mix[pl.ds(part * tok_count, tok_count), :] = term
+            total = total - term.astype(jnp.float32)
+
+    spare = jnp.zeros((SLOTS - MOST, out_ref.shape[1]), jnp.float32)
+    rows = []
+    for piece in pieces:
+        rows += [piece[...].astype(jnp.float32), spare]
+    rows = jnp.concatenate(rows, axis=0).astype(jnp.bfloat16)
+    product = jnp.dot(mix[...], rows, preferred_element_type=jnp.float32)
+    total = product[:tok_count] + (
+        product[tok_count : 2 * tok_count] + product[2 * tok_count :]
+    )
+    out_ref[...] = total.astype(jnp.bfloat16)
+
+
+def combine(quarter_count, slots, gates, pieces):
+    tok_count = slots.shape[0]
+    model_width = pieces[0].shape[1]
+    step = 512
+    return pl.pallas_call(
+        functools.partial(combine_kernel, quarter_count),
+        grid=(model_width // step,),
+        in_specs=[pl.BlockSpec((tok_count, LANES), lambda n: (0, 0))] * 2
+        + [pl.BlockSpec((MOST, step), lambda n: (0, n))] * len(pieces),
+        out_specs=pl.BlockSpec((tok_count, step), lambda n: (0, n)),
+        out_shape=jax.ShapeDtypeStruct((tok_count, model_width), jnp.bfloat16),
+        scratch_shapes=[pltpu.VMEM((3 * tok_count, len(pieces) * SLOTS), jnp.bfloat16)],
+        compiler_params=pltpu.CompilerParams(vmem_limit_bytes=24 * MIB),
+        name="combine",
+    )(slots, gates, *pieces)
 
 
 def per_device(
@@ -267,51 +395,89 @@
         key_weight = lax.dynamic_slice_in_dim(key_weight, first, head_width, axis=1)
         value_weight = lax.dynamic_slice_in_dim(value_weight, first, head_width, axis=1)
 
-    plan, queries, positions, own, other = [], [], [], [], []
-
-    def serve(blocks, offsets):
-        panel, query, position = project(blocks, offsets, key_weight, value_weight, query_slab)
-        plan.append(offsets)
+    halves = norm_rows(tokens, norm_gain, routes)
+    steps = ctx_count // 2
+    plan = [[0]] + [[-step, step] for step in range(1, steps)] + [[steps]]
+    arrived = {0: list(halves)}
+    own_keys, own_values, queries, positions = [], [], [], []
+    lead = [halves[0], halves[1]]
+    rest = [halves[1], halves[0]]
+    for step in range(1, steps + 1):
+        done = step - 1
+        blocks = arrived[done]
+        if done == 0:
+            lead = [lax.ppermute(lead[0], "ctx", forward), lax.ppermute(lead[1], "ctx", backward)]
+            rest = [lax.ppermute(rest[0], "ctx", forward), lax.ppermute(rest[1], "ctx", backward)]
+        keys, mark = project_keys(blocks, key_weight)
+        if step < steps:
+            mark, *lead_next = lax.optimization_barrier((mark, *lead))
+        else:
+            lead_next = lead
+        values, query, position = project_values(
+            blocks, plan[done], mark, value_weight, query_slab
+        )
+        if step < steps:
+            position, *rest_next = lax.optimization_barrier((position, *rest))
+            arrived[step] = [lead[0], rest[0], rest[1], lead[1]]
+            lead = [
+                lax.ppermute(lead_next[0], "ctx", forward),
+                lax.ppermute(lead_next[1], "ctx", backward),
+            ]
+            if step < steps - 1:
+                rest = [
+                    lax.ppermute(rest_next[0], "ctx", forward),
+                    lax.ppermute(rest_next[1], "ctx", backward),
+                ]
+        else:
+            arrived[step] = [lead[0], lead[1]]
+        own_keys.append(keys)
+        own_values.append(values)
         queries.append(query)
         positions.append(position)
-        own.append(panel)
-        other.append(lax.ppermute(panel, "exp", sibling))
-
-    halves = norm_rows(tokens, norm_gain, routes)
-    serve(halves, [0])
-    ahead, behind = list(halves), list(halves)
-    steps = ctx_count // 2
-    for step in range(1, steps):
-        ahead = [lax.ppermute(part, "ctx", forward) for part in ahead]
-        behind = [lax.ppermute(part, "ctx", backward) for part in behind[::-1]][::-1]
-        serve(ahead + behind, [-step, step])
-    one = lax.ppermute(ahead[0], "ctx", forward)
-    two = lax.ppermute(behind[1], "ctx", backward)
-    serve([one, two], [steps])
-
-    attended = attend(plan, queries, positions, own, other)
-    pieces = jnp.dot(attended, output_slab, preferred_element_type=jnp.float32).astype(
-        jnp.bfloat16
-    )
-    returned = lax.all_to_all(
-        pieces.reshape(ctx_count, MOST, model_width), "ctx", split_axis=0, concat_axis=0, tiled=True
-    )
+
+    def hand_over(panel):
+        return lax.ppermute(panel, "exp", sibling)
+
+    other_keys = [hand_over(panel) for panel in own_keys[:-1]]
+    other_values = [hand_over(panel) for panel in own_values[:-1]]
+    late_keys, late_values, *last = lax.optimization_barrier(
+        (own_keys[-1], own_values[-1], *arrived[steps])
+    )
+    other_keys.append(hand_over(late_keys))
+    other_values.append(hand_over(late_values))
+    keys, mark = project_keys(last, key_weight)
+    values, query, position = project_values(last, plan[-1], mark, value_weight, query_slab)
+    own_keys.append(keys)
+    own_values.append(values)
+    queries.append(query)
+    positions.append(position)
+    other_keys.append(hand_over(keys))
+    other_values.append(hand_over(values))
+
+    panels = (own_keys, own_values, other_keys, other_values)
+    attended = attend(True, plan, queries, positions, *panels)
+    far = project_output(attended, output_slab)
+    positions[0], *far = lax.optimization_barrier((positions[0], *far))
+    half = ctx_count // 2
+
+    def swap(piece, k):
+        return lax.ppermute(piece, "ctx", [(c, c ^ k) for c in range(ctx_count)])
+
+    far = [swap(piece, half + r) for r, piece in enumerate(far)]
+    attended = attend(False, plan, queries, positions, *panels)
+    near = project_output(attended, output_slab)
+    tied = lax.optimization_barrier((*near, *far))
+    near, far = tied[:half], list(tied[half:])
+    near = [near[0]] + [swap(near[r], r) for r in range(1, half)]
 
     message = jnp.concatenate(halves, axis=0)
     logits = jnp.dot(
         message[:, :model_width].astype(jnp.float32), router_weight, precision=lax.Precision.HIGHEST
     )
-    slots = message[:, model_width : model_width + EXPERTS].astype(jnp.float32)
-    gating = jax.nn.softmax(jnp.where(slots >= 0, logits, -jnp.inf), axis=1)
-    slot_index = jnp.arange(MOST, dtype=jnp.float32)[None, None, :]
-    combine_mat = jnp.where(slots[:, :, None] == slot_index, gating[:, :, None], 0.0)
-    combine_mat = combine_mat.reshape(tok_count, EXPERTS * MOST)
-    summed = (
-        returned.astype(jnp.float32).reshape(EXPERTS, quarter_count, MOST, model_width).sum(axis=1)
-    )
-    summed = summed.reshape(EXPERTS * MOST, model_width)
-    combined = jnp.dot(combine_mat, summed, precision=lax.Precision.HIGHEST)
-    return combined.astype(jnp.bfloat16)
+    slots = message[:, model_width:]
+    gating = jax.nn.softmax(jnp.where(slots[:, :EXPERTS] >= 0, logits, -jnp.inf), axis=1)
+    gates = jnp.pad(gating, ((0, 0), (0, LANES - EXPERTS)))
+    return combine(quarter_count, slots, gates, near + far)
 
 
 def solution(mesh):

time: 129 us -> 124 us (0.961)
  waiting for transfers between devices: 53.9 us -> 27.4 us
  Pallas kernels: 41.4 us -> 55.5 us
  starting transfers between devices: 21.1 us -> 33.2 us
  matrix products: 5.11 us -> 0.64 us
    all_to_all x1 -> x0, waiting for transfers between devices: 30.6 us -> none  [per_device(): lax.all_to_all(pieces.reshape(ctx_count, MOST, model_width), 'ctx', split...]
    ppermute x19 -> x31, starting transfers between devices: 16.3 us -> 33.2 us  [the longest x7 16.2 us: swap(): return lax.ppermute(piece, 'ctx', [(c, c ^ k) for c in range(ctx_count)])]
    pallas_call x6 -> x15, Pallas kernels: 39.3 us -> 53.4 us  [the longest x5 19.6 us: project_values(): pl.pallas_call(functools.partial(values_kernel, offsets, len(blocks), EXP...]
    all_to_all x1 -> x0, starting transfers between devices: 4.82 us -> none  [per_device(): lax.all_to_all(pieces.reshape(ctx_count, MOST, model_width), 'ctx', split...]
    dot_general x2 -> x0, matrix products: 4.45 us -> none  [the longest x1 2.62 us: per_device(): jnp.dot(attended, output_slab, preferred_element_type=jnp.float32)]
    ppermute x19 -> x31, waiting for transfers between devices: 23.3 us -> 27.4 us  [the longest x7 15.1 us: swap(): return lax.ppermute(piece, 'ctx', [(c, c ^ k) for c in range(ctx_count)])]
    unnamed x17 -> x23, local copies, waits for them, and re-layouts: 6.61 us -> 6.33 us
  transfers between devices with their start and end apart: 20 -> 31, of which waited for: 8 -> 13; matrix products, arithmetic and copies ran while one was open for 1% -> 1% of each run, Pallas kernels for 21% -> 32%
where the time goes in v5:
time: 124 us
  Pallas kernels  55.5 us (45%)
  starting transfers between devices  33.2 us (27%)
  waiting for transfers between devices  27.4 us (22%)
  local copies, waits for them, and re-layouts  6.37 us (5%)
    pallas_call x5, Pallas kernels, project_values(): pl.pallas_call(functools.partial(values_kernel, offsets, len(blocks), EXP...  19.6 us
    ppermute x7, starting transfers between devices, swap(): return lax.ppermute(piece, 'ctx', [(c, c ^ k) for c in range(ctx_count)])  16.2 us
    pallas_call x2, Pallas kernels, attend(): pl.pallas_call(functools.partial(attend_kernel, plan, tok_count, heads, f...  15.5 us
    ppermute x7, waiting for transfers between devices, swap(): return lax.ppermute(piece, 'ctx', [(c, c ^ k) for c in range(ctx_count)])  15.1 us
    pallas_call x5, Pallas kernels, project_keys(): pl.pallas_call(functools.partial(keys_kernel, len(blocks)), grid=(width /...  11.1 us
    unnamed x23, local copies, waits for them, and re-layouts  6.33 us
    ppermute x3, starting transfers between devices, per_device(): lax.ppermute(lead_next[0], 'ctx', forward)  4.8 us
    pallas_call x2, Pallas kernels, project_output(): pl.pallas_call(output_kernel, grid=(model_width // step,), in_specs=[pl.B...  4.13 us
  transfers between devices with their start and end apart: 31, of which 13 were waited for; matrix products, arithmetic and copies ran while one was open for 1% of the time, Pallas kernels for 32%

profile of v5, /device:TPU:0, one launch (start us, length us, event | category | flops | bytes accessed | tf_op | source)
XLA Modules:
  0.0 123.7 jit_solution(15407629853600046062)
XLA Ops:
  0.0 2.1 %norm_rows.1 = (bf16[64,2176]{1,0:T(8,128)(2,1)}, bf16[64,2176]{1,0:T(8,128)(2,1)}) custom-call(bf16[128,2048]{1,0:T(8,128)(2,1)} %tokens_ref.1, f32[1,2048]{1,0:T(1,128)} %bitcast.12, s32[2,128]{1,0:T(2,128)} %bitcast.13), custom_call_target="tpu_custom_call" | custom-call | tf_op jit(solution)/shard_map/norm_rows/pallas_call | solution.py:59
  2.1 3.0 %collective-permute-start = (bf16[64,2176]{1,0:T(8,128)(2,1)}, bf16[64,2176]{1,0:T(8,128)(2,1)S(1)}, u32[]{:S(2)}, u32[]{:S(2)}) collective-permute-start(bf16[64,2176]{1,0:T(8,128)(2,1)} %get-tuple-element.73.refs_0_), channel_id=1, source_target_pairs={{0,4},{4,8},{8,12},{12,14},{14,10},{10,6},{6,2},{2,0},{1,5},{5,9},... | collective-permute-start | bytes 835592 | tf_op jit(solution)/shard_map/ppermute | solution.py:409
  5.2 0.0 collective-permute-start.1
  5.2 2.0 %collective-permute-start.3 = (bf16[64,2176]{1,0:T(8,128)(2,1)}, bf16[64,2176]{1,0:T(8,128)(2,1)S(1)}, u32[]{:S(2)}, u32[]{:S(2)}) collective-permute-start(bf16[64,2176]{1,0:T(8,128)(2,1)} %get-tuple-element.73.refs_0_), channel_id=1, source_target_pairs={{4,0},{8,4},{12,8},{14,12},{10,14},{6,10},{2,6},{0,2},{5,1},{9,5},... | collective-permute-start | bytes 835592 | tf_op jit(solution)/shard_map/ppermute | solution.py:410
  7.1 0.1 collective-permute-start.2
  7.2 2.2 %copy-done.1 = bf16[2048,1024]{1,0:T(8,128)(2,1)S(1)} copy-done((bf16[2048,1024]{1,0:T(8,128)(2,1)S(1)}, bf16[2048,1024]{1,0:T(8,128)(2,1)}, u32[]{:S(2)}) %copy-start.1) | copy-done | bytes 4194328
  9.4 1.0 copy-done.7
  10.4 1.0 copy-done.9
  11.3 1.9 %project_keys.5 = (bf16[128,1024]{1,0:T(8,128)(2,1)S(1)}, f32[8,128]{1,0:T(8,128)S(1)}) custom-call(bf16[64,2176]{1,0:T(8,128)(2,1)S(1)} %copy-done.9, bf16[64,2176]{1,0:T(8,128)(2,1)S(1)} %copy-done.7, bf16[2048,1024]{1,0:T(8,128)(2,1)S(1)} %copy-done.1), custom_call_target="tpu_custom_call" | custom-call | tf_op jit(solution)/shard_map/project_keys/pallas_call | solution.py:77
  13.2 1.7 %collective-permute-done.1.refs_3_ = bf16[64,2176]{1,0:T(8,128)(2,1)S(1)} collective-permute-done((bf16[64,2176]{1,0:T(8,128)(2,1)}, bf16[64,2176]{1,0:T(8,128)(2,1)S(1)}, u32[]{:S(2)}, u32[]{:S(2)}) %collective-permute-start.1) | collective-permute-done | bytes 278560 | tf_op jit(solution)/shard_map/ppermute | solution.py:409
  14.9 1.6 %collective-permute-start.4 = (bf16[64,2176]{1,0:T(8,128)(2,1)S(1)}, bf16[64,2176]{1,0:T(8,128)(2,1)S(1)}, u32[]{:S(2)}, u32[]{:S(2)}) collective-permute-start(bf16[64,2176]{1,0:T(8,128)(2,1)S(1)} %collective-permute-done.refs_0_), channel_id=1, source_target_pairs={{0,4},{4,8},{8,12},{12,14},{14,10},{10,6},{6,2},{2,0},{1,5},{5,9},... | collective-permute-start | bytes 835592 | tf_op jit(solution)/shard_map/ppermute | solution.py:423
  16.5 0.4 collective-permute-start.5
  17.0 2.2 %copy-done.4 = bf16[1,2048,1024]{2,1,0:T(8,128)(2,1)S(1)} copy-done((bf16[1,2048,1024]{2,1,0:T(8,128)(2,1)S(1)}, bf16[1,2048,1024]{2,1,0:T(8,128)(2,1)}, u32[]{:S(2)}) %copy-start.4) | copy-done | bytes 4194328
  19.2 3.5 %project_values.5 = (bf16[128,1024]{1,0:T(8,128)(2,1)S(1)}, bf16[1,48,1024]{2,1,0:T(8,128)(2,1)S(1)}, f32[1,48,128]{2,1,0:T(8,128)S(1)}) custom-call(f32[8,128]{1,0:T(8,128)S(1)} %get-tuple-element.76.mark_ref, bf16[64,2176]{1,0:T(8,128)(2,1)S(1)} %copy-done.10, bf16[64,2176]{1,0:T(8,128)(2,1)S(1)} %copy-done.8, bf16[2048,1024]{1,0:T(8,128)(2,1)S(1)} %copy-done.3, ...), custom_call_target="tpu_custom_call" | custom-call | tf_op jit(solution)/shard_map/project_values/pallas_call | solution.py:136
  22.6 0.0 copy-start.5
  22.7 1.6 %collective-permute-start.6 = (bf16[64,2176]{1,0:T(8,128)(2,1)S(1)}, bf16[64,2176]{1,0:T(8,128)(2,1)S(1)}, u32[]{:S(2)}, u32[]{:S(2)}) collective-permute-start(bf16[64,2176]{1,0:T(8,128)(2,1)S(1)} %collective-permute-done.2.refs_1_), channel_id=1, source_target_pairs={{0,4},{4,8},{8,12},{12,14},{14,10},{10,6},{6,2},{2,0},{1,5},{5,9},... | collective-permute-start | bytes 835592 | tf_op jit(solution)/shard_map/ppermute | solution.py:428
  24.3 0.4 collective-permute-start.7
  24.8 2.4 %project_keys.6 = (bf16[256,1024]{1,0:T(8,128)(2,1)S(1)}, f32[8,128]{1,0:T(8,128)S(1)}) custom-call(bf16[64,2176]{1,0:T(8,128)(2,1)S(1)} %collective-permute-done.refs_0_, bf16[64,2176]{1,0:T(8,128)(2,1)S(1)} %collective-permute-done.2.refs_1_, bf16[64,2176]{1,0:T(8,128)(2,1)S(1)} %collective-permute-done.3.refs_2_, ...), custom_call_target="tpu_custom_call" | custom-call | tf_op jit(solution)/shard_map/project_keys/pallas_call | solution.py:77
  27.2 1.6 %collective-permute-start.8 = (bf16[64,2176]{1,0:T(8,128)(2,1)S(1)}, bf16[64,2176]{1,0:T(8,128)(2,1)S(1)}, u32[]{:S(2)}, u32[]{:S(2)}) collective-permute-start(bf16[64,2176]{1,0:T(8,128)(2,1)S(1)} %collective-permute-done.4.refs_0_), channel_id=1, source_target_pairs={{0,4},{4,8},{8,12},{12,14},{14,10},{10,6},{6,2},{2,0},{1,5},{5,9},... | collective-permute-start | bytes 835592 | tf_op jit(solution)/shard_map/ppermute | solution.py:423
  28.9 0.4 collective-permute-start.9
  29.3 4.2 %project_values.6 = (bf16[256,1024]{1,0:T(8,128)(2,1)S(1)}, bf16[2,48,1024]{2,1,0:T(8,128)(2,1)S(1)}, f32[2,48,128]{2,1,0:T(8,128)S(1)}) custom-call(f32[8,128]{1,0:T(8,128)S(1)} %get-tuple-element.81.mark_ref, bf16[64,2176]{1,0:T(8,128)(2,1)S(1)} %collective-permute-done.refs_0_, bf16[64,2176]{1,0:T(8,128)(2,1)S(1)} %collective-permute-done.2.refs_1_, ...), custom_call_target="tpu_custom_call" | custom-call | tf_op jit(solution)/shard_map/project_values/pallas_call | solution.py:136
  33.5 0.4 collective-permute-done.7.refs_2_
  33.9 1.6 %collective-permute-start.10 = (bf16[64,2176]{1,0:T(8,128)(2,1)S(1)}, bf16[64,2176]{1,0:T(8,128)(2,1)S(1)}, u32[]{:S(2)}, u32[]{:S(2)}) collective-permute-start(bf16[64,2176]{1,0:T(8,128)(2,1)S(1)} %collective-permute-done.6.refs_1_), channel_id=1, source_target_pairs={{0,4},{4,8},{8,12},{12,14},{14,10},{10,6},{6,2},{2,0},{1,5},{5,9},... | collective-permute-start | bytes 835592 | tf_op jit(solution)/shard_map/ppermute | solution.py:428
  35.5 0.4 collective-permute-start.11
  36.0 2.4 %project_keys.7 = (bf16[256,1024]{1,0:T(8,128)(2,1)S(1)}, f32[8,128]{1,0:T(8,128)S(1)}) custom-call(bf16[64,2176]{1,0:T(8,128)(2,1)S(1)} %collective-permute-done.4.refs_0_, bf16[64,2176]{1,0:T(8,128)(2,1)S(1)} %collective-permute-done.6.refs_1_, bf16[64,2176]{1,0:T(8,128)(2,1)S(1)} %collective-permute-done.7.refs_2_, ...), custom_call_target="tpu_custom_call" | custom-call | tf_op jit(solution)/shard_map/project_keys/pallas_call | solution.py:77
  38.4 0.0 collective-permute-done.8.refs_0_
  38.4 1.5 %collective-permute-done.9.refs_3_ = bf16[64,2176]{1,0:T(8,128)(2,1)S(1)} collective-permute-done((bf16[64,2176]{1,0:T(8,128)(2,1)S(1)}, bf16[64,2176]{1,0:T(8,128)(2,1)S(1)}, u32[]{:S(2)}, u32[]{:S(2)}) %collective-permute-start.9) | collective-permute-done | bytes 278560 | tf_op jit(solution)/shard_map/ppermute | solution.py:424
  39.9 1.6 %collective-permute-start.12 = (bf16[64,2176]{1,0:T(8,128)(2,1)S(1)}, bf16[64,2176]{1,0:T(8,128)(2,1)S(1)}, u32[]{:S(2)}, u32[]{:S(2)}) collective-permute-start(bf16[64,2176]{1,0:T(8,128)(2,1)S(1)} %collective-permute-done.8.refs_0_), channel_id=1, source_target_pairs={{0,4},{4,8},{8,12},{12,14},{14,10},{10,6},{6,2},{2,0},{1,5},{5,9},... | collective-permute-start | bytes 835592 | tf_op jit(solution)/shard_map/ppermute | solution.py:423
  41.5 0.5 collective-permute-start.13
  41.9 0.1 collective-permute-done.10.refs_1_
  42.0 1.7 %collective-permute-done.11.refs_2_ = bf16[64,2176]{1,0:T(8,128)(2,1)S(1)} collective-permute-done((bf16[64,2176]{1,0:T(8,128)(2,1)S(1)}, bf16[64,2176]{1,0:T(8,128)(2,1)S(1)}, u32[]{:S(2)}, u32[]{:S(2)}) %collective-permute-start.11) | collective-permute-done | bytes 278560 | tf_op jit(solution)/shard_map/ppermute | solution.py:429
  43.7 4.0 %collective-permute-done.12.refs_0_ = bf16[64,2176]{1,0:T(8,128)(2,1)S(1)} collective-permute-done((bf16[64,2176]{1,0:T(8,128)(2,1)S(1)}, bf16[64,2176]{1,0:T(8,128)(2,1)S(1)}, u32[]{:S(2)}, u32[]{:S(2)}) %collective-permute-start.12) | collective-permute-done | bytes 278560 | tf_op jit(solution)/shard_map/ppermute | solution.py:423
  47.8 1.5 %collective-permute-done.13.refs_1_ = bf16[64,2176]{1,0:T(8,128)(2,1)S(1)} collective-permute-done((bf16[64,2176]{1,0:T(8,128)(2,1)S(1)}, bf16[64,2176]{1,0:T(8,128)(2,1)S(1)}, u32[]{:S(2)}, u32[]{:S(2)}) %collective-permute-start.13) | collective-permute-done | bytes 278560 | tf_op jit(solution)/shard_map/ppermute | solution.py:424
  49.3 4.2 %project_values.7 = (bf16[256,1024]{1,0:T(8,128)(2,1)S(1)}, bf16[2,48,1024]{2,1,0:T(8,128)(2,1)S(1)}, f32[2,48,128]{2,1,0:T(8,128)S(1)}) custom-call(f32[8,128]{1,0:T(8,128)S(1)} %get-tuple-element.89.mark_ref, bf16[64,2176]{1,0:T(8,128)(2,1)S(1)} %collective-permute-done.4.refs_0_, bf16[64,2176]{1,0:T(8,128)(2,1)S(1)} %collective-permute-done.6.refs_1_, ...), custom_call_target="tpu_custom_call" | custom-call | tf_op jit(solution)/shard_map/project_values/pallas_call | solution.py:136
  53.5 2.5 %project_keys.8 = (bf16[256,1024]{1,0:T(8,128)(2,1)S(1)}, f32[8,128]{1,0:T(8,128)S(1)}) custom-call(bf16[64,2176]{1,0:T(8,128)(2,1)S(1)} %collective-permute-done.8.refs_0_, bf16[64,2176]{1,0:T(8,128)(2,1)S(1)} %collective-permute-done.10.refs_1_, bf16[64,2176]{1,0:T(8,128)(2,1)S(1)} %collective-permute-done.11.refs_2_, ...), custom_call_target="tpu_custom_call" | custom-call | tf_op jit(solution)/shard_map/project_keys/pallas_call | solution.py:77
  56.0 4.2 %project_values.8 = (bf16[256,1024]{1,0:T(8,128)(2,1)S(1)}, bf16[2,48,1024]{2,1,0:T(8,128)(2,1)S(1)}, f32[2,48,128]{2,1,0:T(8,128)S(1)}) custom-call(f32[8,128]{1,0:T(8,128)S(1)} %get-tuple-element.94.mark_ref, bf16[64,2176]{1,0:T(8,128)(2,1)S(1)} %collective-permute-done.8.refs_0_, bf16[64,2176]{1,0:T(8,128)(2,1)S(1)} %collective-permute-done.10.refs_1_, ...), custom_call_target="tpu_custom_call" | custom-call | tf_op jit(solution)/shard_map/project_values/pallas_call | solution.py:136
  60.2 0.6 collective-permute-start.21
  60.8 0.1 collective-permute-start.17
  60.9 0.4 collective-permute-start.22
  61.4 1.9 %project_keys.9 = (bf16[128,1024]{1,0:T(8,128)(2,1)S(1)}, f32[8,128]{1,0:T(8,128)S(1)}) custom-call(bf16[64,2176]{1,0:T(8,128)(2,1)S(1)} %collective-permute-done.12.refs_0_, bf16[64,2176]{1,0:T(8,128)(2,1)S(1)} %collective-permute-done.13.refs_1_, bf16[2048,1024]{1,0:T(8,128)(2,1)S(1)} %copy-done.2), custom_call_target="tpu_custom_call" | custom-call | tf_op jit(solution)/shard_map/project_keys/pallas_call | solution.py:77
  63.3 3.5 %project_values.9 = (bf16[128,1024]{1,0:T(8,128)(2,1)S(1)}, bf16[1,48,1024]{2,1,0:T(8,128)(2,1)S(1)}, f32[1,48,128]{2,1,0:T(8,128)S(1)}) custom-call(f32[8,128]{1,0:T(8,128)S(1)} %get-tuple-element.102.mark_ref, bf16[64,2176]{1,0:T(8,128)(2,1)S(1)} %collective-permute-done.12.refs_0_, bf16[64,2176]{1,0:T(8,128)(2,1)S(1)} %collective-permute-done.13.refs_1_, ...), custom_call_target="tpu_custom_call" | custom-call | tf_op jit(solution)/shard_map/project_values/pallas_call | solution.py:136
  66.8 0.1 collective-permute-start.23
  66.9 0.5 collective-permute-start.18
  67.4 1.0 collective-permute-done.23.refs_29_
  68.4 0.4 collective-permute-done.18.refs_24_
  68.8 8.8 %attend.2.attended_ref = bf16[4,48,1024]{2,1,0:T(8,128)(2,1)S(1)} custom-call(bf16[1,48,1024]{2,1,0:T(8,128)(2,1)S(1)} %get-tuple-element.77.refs_0_, bf16[2,48,1024]{2,1,0:T(8,128)(2,1)S(1)} %get-tuple-element.82.refs_1_, bf16[2,48,1024]{2,1,0:T(8,128)(2,1)S(1)} %get-tuple-element.90.refs_2_, bf16[2,48,1024]{2,1,0:T(8,128)(2,1)S(1)} %get-tuple-element.95.refs_3_, ...), custom_call_target="tpu_custom_call" | custom-call | tf_op jit(solution)/shard_map/attend/pallas_call | solution.py:276
  77.6 2.1 %project_output.2 = (bf16[40,2048]{1,0:T(8,128)(2,1)S(1)}, bf16[40,2048]{1,0:T(8,128)(2,1)S(1)}, bf16[40,2048]{1,0:T(8,128)(2,1)S(1)}, bf16[40,2048]{1,0:T(8,128)(2,1)S(1)}) custom-call(bf16[4,48,1024]{2,1,0:T(8,128)(2,1)S(1)} %attend.2.attended_ref, bf16[1024,2048]{1,0:T(8,128)(2,1)S(1)} %bitcast.10), custom_call_target="tpu_custom_call" | custom-call | tf_op jit(solution)/shard_map/project_output/pallas_call | solution.py:311
  79.7 0.6 collective-permute-start.24
  80.2 2.3 %collective-permute-start.25 = (bf16[40,2048]{1,0:T(8,128)(2,1)S(1)}, bf16[40,2048]{1,0:T(8,128)(2,1)S(1)}, u32[]{:S(2)}, u32[]{:S(2)}) collective-permute-start(bf16[40,2048]{1,0:T(8,128)(2,1)S(1)} %get-tuple-element.130), channel_id=1, source_target_pairs={{0,10},{2,8},{4,14},{6,12},{8,2},{10,0},{12,6},{14,4},{1,11},{3,9}... | collective-permute-start | bytes 491528 | tf_op jit(solution)/shard_map/ppermute | solution.py:464
  82.5 1.5 %collective-permute-start.26 = (bf16[40,2048]{1,0:T(8,128)(2,1)S(1)}, bf16[40,2048]{1,0:T(8,128)(2,1)S(1)}, u32[]{:S(2)}, u32[]{:S(2)}) collective-permute-start(bf16[40,2048]{1,0:T(8,128)(2,1)S(1)} %get-tuple-element.131), channel_id=1, source_target_pairs={{0,12},{2,14},{4,8},{6,10},{8,4},{10,6},{12,0},{14,2},{1,13},{3,15... | collective-permute-start | bytes 491528 | tf_op jit(solution)/shard_map/ppermute | solution.py:464
  84.0 3.4 %collective-permute-start.27 = (bf16[40,2048]{1,0:T(8,128)(2,1)S(1)}, bf16[40,2048]{1,0:T(8,128)(2,1)S(1)}, u32[]{:S(2)}, u32[]{:S(2)}) collective-permute-start(bf16[40,2048]{1,0:T(8,128)(2,1)S(1)} %get-tuple-element.132), channel_id=1, source_target_pairs={{0,14},{2,12},{4,10},{6,8},{8,6},{10,4},{12,2},{14,0},{1,15},{3,13... | collective-permute-start | bytes 491528 | tf_op jit(solution)/shard_map/ppermute | solution.py:464
  87.4 0.6 fusion.3
  88.0 0.2 fusion.2
  88.2 6.7 %attend.3.attended_ref = bf16[4,48,1024]{2,1,0:T(8,128)(2,1)S(1)} custom-call(bf16[1,48,1024]{2,1,0:T(8,128)(2,1)S(1)} %get-tuple-element.77.refs_0_, bf16[2,48,1024]{2,1,0:T(8,128)(2,1)S(1)} %get-tuple-element.82.refs_1_, bf16[2,48,1024]{2,1,0:T(8,128)(2,1)S(1)} %get-tuple-element.90.refs_2_, bf16[2,48,1024]{2,1,0:T(8,128)(2,1)S(1)} %get-tuple-element.95.refs_3_, ...), custom_call_target="tpu_custom_call" | custom-call | tf_op jit(solution)/shard_map/attend/pallas_call | solution.py:276
  94.9 2.1 %project_output.3 = (bf16[40,2048]{1,0:T(8,128)(2,1)S(1)}, bf16[40,2048]{1,0:T(8,128)(2,1)S(1)}, bf16[40,2048]{1,0:T(8,128)(2,1)S(1)}, bf16[40,2048]{1,0:T(8,128)(2,1)S(1)}) custom-call(bf16[4,48,1024]{2,1,0:T(8,128)(2,1)S(1)} %attend.3.attended_ref, bf16[1024,2048]{1,0:T(8,128)(2,1)S(1)} %bitcast.11), custom_call_target="tpu_custom_call" | custom-call | tf_op jit(solution)/shard_map/project_output/pallas_call | solution.py:311
  97.0 4.8 %collective-permute-done.24.refs_4_ = bf16[40,2048]{1,0:T(8,128)(2,1)S(1)} collective-permute-done((bf16[40,2048]{1,0:T(8,128)(2,1)S(1)}, bf16[40,2048]{1,0:T(8,128)(2,1)S(1)}, u32[]{:S(2)}, u32[]{:S(2)}) %collective-permute-start.24) | collective-permute-done | bytes 163872 | tf_op jit(solution)/shard_map/ppermute | solution.py:464
  101.7 3.3 %collective-permute-done.25.refs_5_ = bf16[40,2048]{1,0:T(8,128)(2,1)S(1)} collective-permute-done((bf16[40,2048]{1,0:T(8,128)(2,1)S(1)}, bf16[40,2048]{1,0:T(8,128)(2,1)S(1)}, u32[]{:S(2)}, u32[]{:S(2)}) %collective-permute-start.25) | collective-permute-done | bytes 163872 | tf_op jit(solution)/shard_map/ppermute | solution.py:464
  105.0 1.7 %collective-permute-start.28 = (bf16[40,2048]{1,0:T(8,128)(2,1)S(1)}, bf16[40,2048]{1,0:T(8,128)(2,1)S(1)}, u32[]{:S(2)}, u32[]{:S(2)}) collective-permute-start(bf16[40,2048]{1,0:T(8,128)(2,1)S(1)} %get-tuple-element.134), channel_id=1, source_target_pairs={{0,2},{2,0},{4,6},{6,4},{8,10},{10,8},{12,14},{14,12},{1,3},{3,1},... | collective-permute-start | bytes 491528 | tf_op jit(solution)/shard_map/ppermute | solution.py:464
  106.7 6.8 %collective-permute-start.29 = (bf16[40,2048]{1,0:T(8,128)(2,1)S(1)}, bf16[40,2048]{1,0:T(8,128)(2,1)S(1)}, u32[]{:S(2)}, u32[]{:S(2)}) collective-permute-start(bf16[40,2048]{1,0:T(8,128)(2,1)S(1)} %get-tuple-element.135), channel_id=1, source_target_pairs={{0,4},{2,6},{4,0},{6,2},{8,12},{10,14},{12,8},{14,10},{1,5},{3,7},... | collective-permute-start | bytes 491528 | tf_op jit(solution)/shard_map/ppermute | solution.py:464
  113.5 0.0 collective-permute-start.30
  113.5 0.1 fusion.1
  113.7 4.9 %collective-permute-done.29.refs_2_ = bf16[40,2048]{1,0:T(8,128)(2,1)S(1)} collective-permute-done((bf16[40,2048]{1,0:T(8,128)(2,1)S(1)}, bf16[40,2048]{1,0:T(8,128)(2,1)S(1)}, u32[]{:S(2)}, u32[]{:S(2)}) %collective-permute-start.29) | collective-permute-done | bytes 163872 | tf_op jit(solution)/shard_map/ppermute | solution.py:464
  118.6 2.1 %collective-permute-done.30.refs_3_ = bf16[40,2048]{1,0:T(8,128)(2,1)S(1)} collective-permute-done((bf16[40,2048]{1,0:T(8,128)(2,1)S(1)}, bf16[40,2048]{1,0:T(8,128)(2,1)S(1)}, u32[]{:S(2)}, u32[]{:S(2)}) %collective-permute-start.30) | collective-permute-done | bytes 163872 | tf_op jit(solution)/shard_map/ppermute | solution.py:464
  120.7 3.1 %combine.1 = bf16[128,2048]{1,0:T(8,128)(2,1)} custom-call(bf16[128,128]{1,0:T(8,128)(2,1)S(1)} %slice.13.slots_ref, f32[128,128]{1,0:T(8,128)S(1)} %pad.4.gates_ref, bf16[40,2048]{1,0:T(8,128)(2,1)S(1)} %get-tuple-element.133.refs_0_, bf16[40,2048]{1,0:T(8,128)(2,1)S(1)} %collective-permute-done.28.refs_1_, ...), custom_call_target="tpu_custom_call" | custom-call | tf_op jit(solution)/shard_map/combine/pallas_call | solution.py:366
  (43 shorter events, 0.1 us)
Async XLA Ops:
  0.0 87.4 %copy-start = (f32[2048,8]{0,1:T(8,128)S(1)}, f32[2048,8]{0,1:T(8,128)}, u32[]{:S(2)}) copy-start(f32[2048,8]{0,1:T(8,128)} %param.10) | copy-start | bytes 196612
  2.1 11.1 %collective-permute-start = (bf16[64,2176]{1,0:T(8,128)(2,1)}, bf16[64,2176]{1,0:T(8,128)(2,1)S(1)}, u32[]{:S(2)}, u32[]{:S(2)}) collective-permute-start(bf16[64,2176]{1,0:T(8,128)(2,1)} %get-tuple-element.73.refs_0_), channel_id=1, source_target_pairs={{0,4},{4,8},{8,12},{12,14},{14,10},{10,6},{6,2},{2,0},{1,5},{5,9},... | collective-permute-start | bytes 835592 | tf_op jit(solution)/shard_map/ppermute | solution.py:409
  5.2 9.8 %collective-permute-start.1 = (bf16[64,2176]{1,0:T(8,128)(2,1)}, bf16[64,2176]{1,0:T(8,128)(2,1)S(1)}, u32[]{:S(2)}, u32[]{:S(2)}) collective-permute-start(bf16[64,2176]{1,0:T(8,128)(2,1)} %get-tuple-element.74.refs_1_), channel_id=1, source_target_pairs={{4,0},{8,4},{12,8},{14,12},{10,14},{6,10},{2,6},{0,2},{5,1},{9,5},... | collective-permute-start | bytes 835592 | tf_op jit(solution)/shard_map/ppermute | solution.py:409
  5.2 17.5 %collective-permute-start.3 = (bf16[64,2176]{1,0:T(8,128)(2,1)}, bf16[64,2176]{1,0:T(8,128)(2,1)S(1)}, u32[]{:S(2)}, u32[]{:S(2)}) collective-permute-start(bf16[64,2176]{1,0:T(8,128)(2,1)} %get-tuple-element.73.refs_0_), channel_id=1, source_target_pairs={{4,0},{8,4},{12,8},{14,12},{10,14},{6,10},{2,6},{0,2},{5,1},{9,5},... | collective-permute-start | bytes 835592 | tf_op jit(solution)/shard_map/ppermute | solution.py:410
  7.1 15.6 %collective-permute-start.2 = (bf16[64,2176]{1,0:T(8,128)(2,1)}, bf16[64,2176]{1,0:T(8,128)(2,1)S(1)}, u32[]{:S(2)}, u32[]{:S(2)}) collective-permute-start(bf16[64,2176]{1,0:T(8,128)(2,1)} %get-tuple-element.74.refs_1_), channel_id=1, source_target_pairs={{0,4},{4,8},{8,12},{12,14},{14,10},{10,6},{6,2},{2,0},{1,5},{5,9},... | collective-permute-start | bytes 835592 | tf_op jit(solution)/shard_map/ppermute | solution.py:410
  7.2 2.2 %copy-start.1 = (bf16[2048,1024]{1,0:T(8,128)(2,1)S(1)}, bf16[2048,1024]{1,0:T(8,128)(2,1)}, u32[]{:S(2)}) copy-start(bf16[2048,1024]{1,0:T(8,128)(2,1)} %refs_2_.6) | copy-start | bytes 12582916
  9.4 1.0 copy-start.7
  10.4 1.0 copy-start.9
  11.3 5.7 %copy-start.3 = (bf16[2048,1024]{1,0:T(8,128)(2,1)S(1)}, bf16[2048,1024]{1,0:T(8,128)(2,1)}, u32[]{:S(2)}) copy-start(bf16[2048,1024]{1,0:T(8,128)(2,1)} %refs_2_.7) | copy-start | bytes 12582916
  11.3 5.7 %copy-start.8 = (bf16[64,2176]{1,0:T(8,128)(2,1)S(1)}, bf16[64,2176]{1,0:T(8,128)(2,1)}, u32[]{:S(2)}) copy-start(bf16[64,2176]{1,0:T(8,128)(2,1)} %get-tuple-element.74.refs_1_) | copy-start | bytes 835588
  11.3 5.7 %copy-start.10 = (bf16[64,2176]{1,0:T(8,128)(2,1)S(1)}, bf16[64,2176]{1,0:T(8,128)(2,1)}, u32[]{:S(2)}) copy-start(bf16[64,2176]{1,0:T(8,128)(2,1)} %get-tuple-element.73.refs_0_) | copy-start | bytes 835588
  14.9 12.2 %collective-permute-start.4 = (bf16[64,2176]{1,0:T(8,128)(2,1)S(1)}, bf16[64,2176]{1,0:T(8,128)(2,1)S(1)}, u32[]{:S(2)}, u32[]{:S(2)}) collective-permute-start(bf16[64,2176]{1,0:T(8,128)(2,1)S(1)} %collective-permute-done.refs_0_), channel_id=1, source_target_pairs={{0,4},{4,8},{8,12},{12,14},{14,10},{10,6},{6,2},{2,0},{1,5},{5,9},... | collective-permute-start | bytes 835592 | tf_op jit(solution)/shard_map/ppermute | solution.py:423
  16.5 10.7 %collective-permute-start.5 = (bf16[64,2176]{1,0:T(8,128)(2,1)S(1)}, bf16[64,2176]{1,0:T(8,128)(2,1)S(1)}, u32[]{:S(2)}, u32[]{:S(2)}) collective-permute-start(bf16[64,2176]{1,0:T(8,128)(2,1)S(1)} %collective-permute-done.1.refs_3_), channel_id=1, source_target_pairs={{4,0},{8,4},{12,8},{14,12},{10,14},{6,10},{2,6},{0,2},{5,1},{9,5},... | collective-permute-start | bytes 835592 | tf_op jit(solution)/shard_map/ppermute | solution.py:424
  17.0 2.2 %copy-start.4 = (bf16[1,2048,1024]{2,1,0:T(8,128)(2,1)S(1)}, bf16[1,2048,1024]{2,1,0:T(8,128)(2,1)}, u32[]{:S(2)}) copy-start(bf16[1,2048,1024]{2,1,0:T(8,128)(2,1)} %param.14) | copy-start | bytes 12582916
  19.2 5.6 %copy-start.2 = (bf16[2048,1024]{1,0:T(8,128)(2,1)S(1)}, bf16[2048,1024]{1,0:T(8,128)(2,1)}, u32[]{:S(2)}) copy-start(bf16[2048,1024]{1,0:T(8,128)(2,1)} %refs_2_.6) | copy-start | bytes 12582916
  22.6 6.6 %copy-start.5 = (bf16[1,2048,1024]{2,1,0:T(8,128)(2,1)S(1)}, bf16[1,2048,1024]{2,1,0:T(8,128)(2,1)}, u32[]{:S(2)}) copy-start(bf16[1,2048,1024]{2,1,0:T(8,128)(2,1)} %param.14) | copy-start | bytes 12582916
  22.7 10.8 %collective-permute-start.6 = (bf16[64,2176]{1,0:T(8,128)(2,1)S(1)}, bf16[64,2176]{1,0:T(8,128)(2,1)S(1)}, u32[]{:S(2)}, u32[]{:S(2)}) collective-permute-start(bf16[64,2176]{1,0:T(8,128)(2,1)S(1)} %collective-permute-done.2.refs_1_), channel_id=1, source_target_pairs={{0,4},{4,8},{8,12},{12,14},{14,10},{10,6},{6,2},{2,0},{1,5},{5,9},... | collective-permute-start | bytes 835592 | tf_op jit(solution)/shard_map/ppermute | solution.py:428
  24.3 9.6 %collective-permute-start.7 = (bf16[64,2176]{1,0:T(8,128)(2,1)S(1)}, bf16[64,2176]{1,0:T(8,128)(2,1)S(1)}, u32[]{:S(2)}, u32[]{:S(2)}) collective-permute-start(bf16[64,2176]{1,0:T(8,128)(2,1)S(1)} %collective-permute-done.3.refs_2_), channel_id=1, source_target_pairs={{4,0},{8,4},{12,8},{14,12},{10,14},{6,10},{2,6},{0,2},{5,1},{9,5},... | collective-permute-start | bytes 835592 | tf_op jit(solution)/shard_map/ppermute | solution.py:429
  27.2 11.2 %collective-permute-start.8 = (bf16[64,2176]{1,0:T(8,128)(2,1)S(1)}, bf16[64,2176]{1,0:T(8,128)(2,1)S(1)}, u32[]{:S(2)}, u32[]{:S(2)}) collective-permute-start(bf16[64,2176]{1,0:T(8,128)(2,1)S(1)} %collective-permute-done.4.refs_0_), channel_id=1, source_target_pairs={{0,4},{4,8},{8,12},{12,14},{14,10},{10,6},{6,2},{2,0},{1,5},{5,9},... | collective-permute-start | bytes 835592 | tf_op jit(solution)/shard_map/ppermute | solution.py:423
  28.9 11.0 %collective-permute-start.9 = (bf16[64,2176]{1,0:T(8,128)(2,1)S(1)}, bf16[64,2176]{1,0:T(8,128)(2,1)S(1)}, u32[]{:S(2)}, u32[]{:S(2)}) collective-permute-start(bf16[64,2176]{1,0:T(8,128)(2,1)S(1)} %collective-permute-done.5.refs_3_), channel_id=1, source_target_pairs={{4,0},{8,4},{12,8},{14,12},{10,14},{6,10},{2,6},{0,2},{5,1},{9,5},... | collective-permute-start | bytes 835592 | tf_op jit(solution)/shard_map/ppermute | solution.py:424
  33.9 8.1 %collective-permute-start.10 = (bf16[64,2176]{1,0:T(8,128)(2,1)S(1)}, bf16[64,2176]{1,0:T(8,128)(2,1)S(1)}, u32[]{:S(2)}, u32[]{:S(2)}) collective-permute-start(bf16[64,2176]{1,0:T(8,128)(2,1)S(1)} %collective-permute-done.6.refs_1_), channel_id=1, source_target_pairs={{0,4},{4,8},{8,12},{12,14},{14,10},{10,6},{6,2},{2,0},{1,5},{5,9},... | collective-permute-start | bytes 835592 | tf_op jit(solution)/shard_map/ppermute | solution.py:428
  35.5 8.2 %collective-permute-start.11 = (bf16[64,2176]{1,0:T(8,128)(2,1)S(1)}, bf16[64,2176]{1,0:T(8,128)(2,1)S(1)}, u32[]{:S(2)}, u32[]{:S(2)}) collective-permute-start(bf16[64,2176]{1,0:T(8,128)(2,1)S(1)} %collective-permute-done.7.refs_2_), channel_id=1, source_target_pairs={{4,0},{8,4},{12,8},{14,12},{10,14},{6,10},{2,6},{0,2},{5,1},{9,5},... | collective-permute-start | bytes 835592 | tf_op jit(solution)/shard_map/ppermute | solution.py:429
  36.0 25.0 %collective-permute-start.15 = (bf16[256,1024]{1,0:T(8,128)(2,1)S(1)}, bf16[256,1024]{1,0:T(8,128)(2,1)S(1)}, u32[]{:S(2)}, u32[]{:S(2)}) collective-permute-start(bf16[256,1024]{1,0:T(8,128)(2,1)S(1)} %get-tuple-element.111.refs_11_), channel_id=1, source_target_pairs={{0,1},{1,0},{2,3},{3,2},{4,5},{5,4},{6,7},{7,6},{8,9},{9,8},{10,11... | collective-permute-start | bytes 1572872 | tf_op jit(solution)/shard_map/ppermute | solution.py:439
  39.9 7.9 %collective-permute-start.12 = (bf16[64,2176]{1,0:T(8,128)(2,1)S(1)}, bf16[64,2176]{1,0:T(8,128)(2,1)S(1)}, u32[]{:S(2)}, u32[]{:S(2)}) collective-permute-start(bf16[64,2176]{1,0:T(8,128)(2,1)S(1)} %collective-permute-done.8.refs_0_), channel_id=1, source_target_pairs={{0,4},{4,8},{8,12},{12,14},{14,10},{10,6},{6,2},{2,0},{1,5},{5,9},... | collective-permute-start | bytes 835592 | tf_op jit(solution)/shard_map/ppermute | solution.py:423
  41.5 7.8 %collective-permute-start.13 = (bf16[64,2176]{1,0:T(8,128)(2,1)S(1)}, bf16[64,2176]{1,0:T(8,128)(2,1)S(1)}, u32[]{:S(2)}, u32[]{:S(2)}) collective-permute-start(bf16[64,2176]{1,0:T(8,128)(2,1)S(1)} %collective-permute-done.9.refs_3_), channel_id=1, source_target_pairs={{4,0},{8,4},{12,8},{14,12},{10,14},{6,10},{2,6},{0,2},{5,1},{9,5},... | collective-permute-start | bytes 835592 | tf_op jit(solution)/shard_map/ppermute | solution.py:424
  42.0 18.3 %collective-permute-start.14 = (bf16[128,1024]{1,0:T(8,128)(2,1)S(1)}, bf16[128,1024]{1,0:T(8,128)(2,1)S(1)}, u32[]{:S(2)}, u32[]{:S(2)}) collective-permute-start(bf16[128,1024]{1,0:T(8,128)(2,1)S(1)} %get-tuple-element.110.refs_10_), channel_id=1, source_target_pairs={{0,1},{1,0},{2,3},{3,2},{4,5},{5,4},{6,7},{7,6},{8,9},{9,8},{10,11... | collective-permute-start | bytes 786440 | tf_op jit(solution)/shard_map/ppermute | solution.py:439
  43.7 17.1 %collective-permute-start.19 = (bf16[128,1024]{1,0:T(8,128)(2,1)S(1)}, bf16[128,1024]{1,0:T(8,128)(2,1)S(1)}, u32[]{:S(2)}, u32[]{:S(2)}) collective-permute-start(bf16[128,1024]{1,0:T(8,128)(2,1)S(1)} %get-tuple-element.114.refs_15_), channel_id=1, source_target_pairs={{0,1},{1,0},{2,3},{3,2},{4,5},{5,4},{6,7},{7,6},{8,9},{9,8},{10,11... | collective-permute-start | bytes 786440 | tf_op jit(solution)/shard_map/ppermute | solution.py:439
  47.8 19.0 %collective-permute-start.20 = (bf16[256,1024]{1,0:T(8,128)(2,1)S(1)}, bf16[256,1024]{1,0:T(8,128)(2,1)S(1)}, u32[]{:S(2)}, u32[]{:S(2)}) collective-permute-start(bf16[256,1024]{1,0:T(8,128)(2,1)S(1)} %get-tuple-element.115.refs_16_), channel_id=1, source_target_pairs={{0,1},{1,0},{2,3},{3,2},{4,5},{5,4},{6,7},{7,6},{8,9},{9,8},{10,11... | collective-permute-start | bytes 1572872 | tf_op jit(solution)/shard_map/ppermute | solution.py:439
  49.3 17.6 %collective-permute-start.16 = (bf16[256,1024]{1,0:T(8,128)(2,1)S(1)}, bf16[256,1024]{1,0:T(8,128)(2,1)S(1)}, u32[]{:S(2)}, u32[]{:S(2)}) collective-permute-start(bf16[256,1024]{1,0:T(8,128)(2,1)S(1)} %get-tuple-element.112.refs_12_), channel_id=1, source_target_pairs={{0,1},{1,0},{2,3},{3,2},{4,5},{5,4},{6,7},{7,6},{8,9},{9,8},{10,11... | collective-permute-start | bytes 1572872 | tf_op jit(solution)/shard_map/ppermute | solution.py:439
  60.2 7.2 %collective-permute-start.21 = (bf16[256,1024]{1,0:T(8,128)(2,1)S(1)}, bf16[256,1024]{1,0:T(8,128)(2,1)S(1)}, u32[]{:S(2)}, u32[]{:S(2)}) collective-permute-start(bf16[256,1024]{1,0:T(8,128)(2,1)S(1)} %get-tuple-element.116.refs_17_), channel_id=1, source_target_pairs={{0,1},{1,0},{2,3},{3,2},{4,5},{5,4},{6,7},{7,6},{8,9},{9,8},{10,11... | collective-permute-start | bytes 1572872 | tf_op jit(solution)/shard_map/ppermute | solution.py:439
  60.8 7.9 %collective-permute-start.17 = (bf16[256,1024]{1,0:T(8,128)(2,1)S(1)}, bf16[256,1024]{1,0:T(8,128)(2,1)S(1)}, u32[]{:S(2)}, u32[]{:S(2)}) collective-permute-start(bf16[256,1024]{1,0:T(8,128)(2,1)S(1)} %get-tuple-element.118.refs_13_), channel_id=1, source_target_pairs={{0,1},{1,0},{2,3},{3,2},{4,5},{5,4},{6,7},{7,6},{8,9},{9,8},{10,11... | collective-permute-start | bytes 1572872 | tf_op jit(solution)/shard_map/ppermute | solution.py:439
  60.9 7.9 %collective-permute-start.22 = (bf16[256,1024]{1,0:T(8,128)(2,1)S(1)}, bf16[256,1024]{1,0:T(8,128)(2,1)S(1)}, u32[]{:S(2)}, u32[]{:S(2)}) collective-permute-start(bf16[256,1024]{1,0:T(8,128)(2,1)S(1)} %get-tuple-element.119.refs_18_), channel_id=1, source_target_pairs={{0,1},{1,0},{2,3},{3,2},{4,5},{5,4},{6,7},{7,6},{8,9},{9,8},{10,11... | collective-permute-start | bytes 1572872 | tf_op jit(solution)/shard_map/ppermute | solution.py:439
  66.8 1.6 %collective-permute-start.23 = (bf16[128,1024]{1,0:T(8,128)(2,1)S(1)}, bf16[128,1024]{1,0:T(8,128)(2,1)S(1)}, u32[]{:S(2)}, u32[]{:S(2)}) collective-permute-start(bf16[128,1024]{1,0:T(8,128)(2,1)S(1)} %get-tuple-element.117.refs_19_), channel_id=1, source_target_pairs={{0,1},{1,0},{2,3},{3,2},{4,5},{5,4},{6,7},{7,6},{8,9},{9,8},{10,11... | collective-permute-start | bytes 786440 | tf_op jit(solution)/shard_map/ppermute | solution.py:439
  66.9 1.9 %collective-permute-start.18 = (bf16[128,1024]{1,0:T(8,128)(2,1)S(1)}, bf16[128,1024]{1,0:T(8,128)(2,1)S(1)}, u32[]{:S(2)}, u32[]{:S(2)}) collective-permute-start(bf16[128,1024]{1,0:T(8,128)(2,1)S(1)} %get-tuple-element.113.refs_14_), channel_id=1, source_target_pairs={{0,1},{1,0},{2,3},{3,2},{4,5},{5,4},{6,7},{7,6},{8,9},{9,8},{10,11... | collective-permute-start | bytes 786440 | tf_op jit(solution)/shard_map/ppermute | solution.py:439
  68.8 8.8 %copy-start.6 = (bf16[1,1024,2048]{2,1,0:T(8,128)(2,1)S(1)}, bf16[1,1024,2048]{2,1,0:T(8,128)(2,1)}, u32[]{:S(2)}) copy-start(bf16[1,1024,2048]{2,1,0:T(8,128)(2,1)} %param.15) | copy-start | bytes 12582916
  79.7 22.1 %collective-permute-start.24 = (bf16[40,2048]{1,0:T(8,128)(2,1)S(1)}, bf16[40,2048]{1,0:T(8,128)(2,1)S(1)}, u32[]{:S(2)}, u32[]{:S(2)}) collective-permute-start(bf16[40,2048]{1,0:T(8,128)(2,1)S(1)} %get-tuple-element.129), channel_id=1, source_target_pairs={{0,8},{2,10},{4,12},{6,14},{8,0},{10,2},{12,4},{14,6},{1,9},{3,11}... | collective-permute-start | bytes 491528 | tf_op jit(solution)/shard_map/ppermute | solution.py:464
  80.2 24.8 %collective-permute-start.25 = (bf16[40,2048]{1,0:T(8,128)(2,1)S(1)}, bf16[40,2048]{1,0:T(8,128)(2,1)S(1)}, u32[]{:S(2)}, u32[]{:S(2)}) collective-permute-start(bf16[40,2048]{1,0:T(8,128)(2,1)S(1)} %get-tuple-element.130), channel_id=1, source_target_pairs={{0,10},{2,8},{4,14},{6,12},{8,2},{10,0},{12,6},{14,4},{1,11},{3,9}... | collective-permute-start | bytes 491528 | tf_op jit(solution)/shard_map/ppermute | solution.py:464
  82.5 22.5 %collective-permute-start.26 = (bf16[40,2048]{1,0:T(8,128)(2,1)S(1)}, bf16[40,2048]{1,0:T(8,128)(2,1)S(1)}, u32[]{:S(2)}, u32[]{:S(2)}) collective-permute-start(bf16[40,2048]{1,0:T(8,128)(2,1)S(1)} %get-tuple-element.131), channel_id=1, source_target_pairs={{0,12},{2,14},{4,8},{6,10},{8,4},{10,6},{12,0},{14,2},{1,13},{3,15... | collective-permute-start | bytes 491528 | tf_op jit(solution)/shard_map/ppermute | solution.py:464
  84.0 21.0 %collective-permute-start.27 = (bf16[40,2048]{1,0:T(8,128)(2,1)S(1)}, bf16[40,2048]{1,0:T(8,128)(2,1)S(1)}, u32[]{:S(2)}, u32[]{:S(2)}) collective-permute-start(bf16[40,2048]{1,0:T(8,128)(2,1)S(1)} %get-tuple-element.132), channel_id=1, source_target_pairs={{0,14},{2,12},{4,10},{6,8},{8,6},{10,4},{12,2},{14,0},{1,15},{3,13... | collective-permute-start | bytes 491528 | tf_op jit(solution)/shard_map/ppermute | solution.py:464
  105.0 8.6 %collective-permute-start.28 = (bf16[40,2048]{1,0:T(8,128)(2,1)S(1)}, bf16[40,2048]{1,0:T(8,128)(2,1)S(1)}, u32[]{:S(2)}, u32[]{:S(2)}) collective-permute-start(bf16[40,2048]{1,0:T(8,128)(2,1)S(1)} %get-tuple-element.134), channel_id=1, source_target_pairs={{0,2},{2,0},{4,6},{6,4},{8,10},{10,8},{12,14},{14,12},{1,3},{3,1},... | collective-permute-start | bytes 491528 | tf_op jit(solution)/shard_map/ppermute | solution.py:464
  106.7 11.9 %collective-permute-start.29 = (bf16[40,2048]{1,0:T(8,128)(2,1)S(1)}, bf16[40,2048]{1,0:T(8,128)(2,1)S(1)}, u32[]{:S(2)}, u32[]{:S(2)}) collective-permute-start(bf16[40,2048]{1,0:T(8,128)(2,1)S(1)} %get-tuple-element.135), channel_id=1, source_target_pairs={{0,4},{2,6},{4,0},{6,2},{8,12},{10,14},{12,8},{14,10},{1,5},{3,7},... | collective-permute-start | bytes 491528 | tf_op jit(solution)/shard_map/ppermute | solution.py:464
  113.5 7.2 %collective-permute-start.30 = (bf16[40,2048]{1,0:T(8,128)(2,1)S(1)}, bf16[40,2048]{1,0:T(8,128)(2,1)S(1)}, u32[]{:S(2)}, u32[]{:S(2)}) collective-permute-start(bf16[40,2048]{1,0:T(8,128)(2,1)S(1)} %get-tuple-element.136), channel_id=1, source_target_pairs={{0,6},{2,4},{4,2},{6,0},{8,14},{10,12},{12,10},{14,8},{1,7},{3,5},... | collective-permute-start | bytes 491528 | tf_op jit(solution)/shard_map/ppermute | solution.py:464

commit v6 on v5

--- a/solution.py
+++ b/solution.py
@@ -63,10 +63,10 @@
 
 def keys_kernel(count, *refs):
     blocks = refs[:count]
-    weight_ref, out_ref, mark_ref = refs[count:]
+    weight_ref, panel_ref, mark_ref = refs[count:]
     rows = jnp.concatenate([block[:, : weight_ref.shape[0]] for block in blocks], axis=0)
     product = jnp.dot(rows, weight_ref[...], preferred_element_type=jnp.float32)
-    out_ref[...] = product.astype(jnp.bfloat16)
+    panel_ref[0] = product.astype(jnp.bfloat16)
     mark_ref[...] = product[:8, :LANES]
 
 
@@ -80,11 +80,11 @@
         in_specs=[pl.BlockSpec(block.shape, lambda n: (0, 0)) for block in blocks]
         + [pl.BlockSpec((model_width, step), lambda n: (0, n))],
         out_specs=[
-            pl.BlockSpec((row_count, step), lambda n: (0, n)),
+            pl.BlockSpec((1, row_count, step), lambda n: (0, 0, n)),
             pl.BlockSpec((8, LANES), lambda n: (0, 0)),
         ],
         out_shape=[
-            jax.ShapeDtypeStruct((row_count, width), jnp.bfloat16),
+            jax.ShapeDtypeStruct((2, row_count, width), jnp.bfloat16),
             jax.ShapeDtypeStruct((8, LANES), jnp.float32),
         ],
         compiler_params=pltpu.CompilerParams(vmem_limit_bytes=12 * MIB),
@@ -92,9 +92,9 @@
     )(*blocks, key_weight)
 
 
-def values_kernel(offsets, count, experts, mark_ref, *refs):
+def values_kernel(offsets, count, experts, mark_ref, half_panel_ref, *refs):
     blocks = refs[:count]
-    value_ref, query_ref, panel_ref, out_ref, pos_ref, picked = refs[count:]
+    value_ref, panel_ref, picked_ref, pos_ref = refs[count:]
     width = value_ref.shape[0]
     rows = jnp.concatenate([block[:, :width] for block in blocks], axis=0)
     tok_count = rows.shape[0] // len(offsets)
@@ -111,7 +111,7 @@
         for g, offset in enumerate(offsets):
             part = slice(g * tok_count, (g + 1) * tok_count)
             chosen = select[part].T[:SLOTS].astype(jnp.bfloat16)
-            picked[pl.ds(g * SLOTS, SLOTS), :] = jnp.dot(
+            picked_ref[g] = jnp.dot(
                 chosen, rows[part], preferred_element_type=jnp.float32
             ).astype(jnp.bfloat16)
             start = (ring_owner(offset) * lax.axis_size("exp") + lax.axis_index("exp")) * tok_count
@@ -119,48 +119,74 @@
                 chosen, number, preferred_element_type=jnp.float32
             ) + start.astype(jnp.float32)
 
-    panel_ref[...] = jnp.dot(
+    panel_ref[0] = jnp.dot(
         rows, value_ref[...], preferred_element_type=jnp.float32
     ).astype(jnp.bfloat16)
-    queries = jnp.dot(picked[...], query_ref[...], preferred_element_type=jnp.float32)
-    for g in range(len(offsets)):
-        out_ref[g] = queries[g * SLOTS : (g + 1) * SLOTS].astype(jnp.bfloat16)
-
-
-def project_values(blocks, offsets, mark, value_weight, query_slab):
+
+
+def project_values(blocks, offsets, mark, panel, value_weight):
     row_count = sum(block.shape[0] for block in blocks)
     model_width, width = value_weight.shape
     step = min(width, 256)
     owners = len(offsets)
-    weight_spec = pl.BlockSpec((model_width, step), lambda n: (0, n))
     return pl.pallas_call(
         functools.partial(values_kernel, offsets, len(blocks), EXPERTS),
         grid=(width // step,),
-        in_specs=[pl.BlockSpec(mark.shape, lambda n: (0, 0))]
+        in_specs=[
+            pl.BlockSpec(mark.shape, lambda n: (0, 0)),
+            pl.BlockSpec(memory_space=pl.ANY),
+        ]
         + [pl.BlockSpec(block.shape, lambda n: (0, 0)) for block in blocks]
-        + [weight_spec] * 2,
+        + [pl.BlockSpec((model_width, step), lambda n: (0, n))],
         out_specs=[
-            pl.BlockSpec((row_count, step), lambda n: (0, n)),
-            pl.BlockSpec((owners, SLOTS, step), lambda n: (0, 0, n)),
+            pl.BlockSpec((1, row_count, step), lambda n: (1, 0, n)),
+            pl.BlockSpec((owners, SLOTS, model_width), lambda n: (0, 0, 0)),
             pl.BlockSpec((owners, SLOTS, LANES), lambda n: (0, 0, 0)),
         ],
         out_shape=[
-            jax.ShapeDtypeStruct((row_count, width), jnp.bfloat16),
-            jax.ShapeDtypeStruct((owners, SLOTS, width), jnp.bfloat16),
+            jax.ShapeDtypeStruct((2, row_count, width), jnp.bfloat16),
+            jax.ShapeDtypeStruct((owners, SLOTS, model_width), jnp.bfloat16),
             jax.ShapeDtypeStruct((owners, SLOTS, LANES), jnp.float32),
         ],
-        scratch_shapes=[pltpu.VMEM((owners * SLOTS, model_width), jnp.bfloat16)],
-        compiler_params=pltpu.CompilerParams(vmem_limit_bytes=16 * MIB),
+        input_output_aliases={1: 0},
+        compiler_params=pltpu.CompilerParams(vmem_limit_bytes=12 * MIB),
         name="project_values",
-    )(mark, *blocks, value_weight, query_slab)
-
-
-def attend_kernel(plan, tok_count, heads, flip, *refs):
+    )(mark, panel, *blocks, value_weight)
+
+
+def queries_kernel(*refs):
+    *picked, weight_ref, out_ref = refs
+    rows = [ref[g] for ref in picked for g in range(ref.shape[0])]
+    product = jnp.dot(
+        jnp.concatenate(rows, axis=0), weight_ref[...], preferred_element_type=jnp.float32
+    )
+    for g in range(len(rows)):
+        out_ref[g] = product[g * SLOTS : (g + 1) * SLOTS].astype(jnp.bfloat16)
+
+
+def project_queries(picked, query_slab):
+    model_width, width = query_slab.shape
+    step = min(width, 256)
+    owners = sum(rows.shape[0] for rows in picked)
+    held = owners * SLOTS * (4 * model_width + 12 * step) * 2
+    return pl.pallas_call(
+        queries_kernel,
+        grid=(width // step,),
+        in_specs=[pl.BlockSpec(rows.shape, lambda n: (0, 0, 0)) for rows in picked]
+        + [pl.BlockSpec((model_width, step), lambda n: (0, n))],
+        out_specs=pl.BlockSpec((owners, SLOTS, step), lambda n: (0, 0, n)),
+        out_shape=jax.ShapeDtypeStruct((owners, SLOTS, width), jnp.bfloat16),
+        compiler_params=pltpu.CompilerParams(vmem_limit_bytes=held + 6 * MIB),
+        name="project_queries",
+    )(*picked, query_slab)
+
+
+def attend_kernel(plan, tok_count, heads, flip, query_count, *refs):
     count = len(plan)
-    query_refs, pos_refs, own_keys, own_values, other_keys, other_values = (
-        refs[k * count : (k + 1) * count] for k in range(6)
-    )
-    out_ref, places, queries, keys, values, scores, weights = refs[6 * count :]
+    query_refs, refs = refs[:query_count], refs[query_count:]
+    pos_refs, own_refs, other_refs = (refs[k * count : (k + 1) * count] for k in range(3))
+    out_ref, places, queries, keys, values, scores, weights = refs[3 * count :]
+    query_parts = [(ref, g) for ref in query_refs for g in range(ref.shape[0])]
     side = lax.axis_index("exp")
     exp_count = 2
     rate = math.log2(math.e) / math.sqrt(HS)
@@ -177,18 +203,19 @@
             for g, offset in enumerate(offsets):
                 places[ring_owner(offset)] = pos_ref[g, :MOST]
 
-    for p, offsets in enumerate(plan):
+    for offsets, own_ref, other_ref in zip(plan, own_refs, other_refs):
         for g, offset in enumerate(offsets):
             owner = ring_owner(offset)
+            query_ref, place = query_parts.pop(0)
             part = pl.ds(g * tok_count, tok_count)
             here, there = owner * exp_count + side, owner * exp_count + 1 - side
             for h in range(heads):
                 lanes = pl.ds(h * HS, HS)
-                queries[h, owner] = query_refs[p][g, :, lanes].astype(jnp.float32)[:MOST]
-                keys[h, here] = own_keys[p][part, lanes]
-                values[h, here] = own_values[p][part, lanes]
-                keys[h, there] = other_keys[p][part, lanes]
-                values[h, there] = other_values[p][part, lanes]
+                queries[h, owner] = query_ref[place, :, lanes].astype(jnp.float32)[:MOST]
+                keys[h, here] = own_ref[0, part, lanes]
+                values[h, here] = own_ref[1, part, lanes]
+                keys[h, there] = other_ref[0, part, lanes]
+                values[h, there] = other_ref[1, part, lanes]
 
     def serve(lead, first):
         top = lead + group
@@ -259,24 +286,24 @@
             serve(lead, 0)
 
 
-def attend(flip, plan, queries, positions, own_keys, own_values, other_keys, other_values):
+def attend(flip, plan, queries, positions, own, other):
     owners = sum(len(offsets) for offsets in plan)
     row_count = owners * MOST
     width = queries[0].shape[-1]
     heads = 2 if owners <= 8 else 1
     step = heads * HS
-    tok_count = own_keys[0].shape[0] // len(plan[0])
+    tok_count = own[0].shape[1] // len(plan[0])
     length = owners * 2 * tok_count
     group_rows = min(row_count // 2, 8 * MOST)
     query_specs = [pl.BlockSpec((q.shape[0], SLOTS, step), lambda h: (0, 0, h)) for q in queries]
     pos_specs = [pl.BlockSpec(p.shape, lambda h: (0, 0, 0)) for p in positions]
-    panel_specs = [pl.BlockSpec((p.shape[0], step), lambda h: (0, h)) for p in own_keys]
+    panel_specs = [pl.BlockSpec((2, p.shape[1], step), lambda h: (0, 0, h)) for p in own]
     scratch = heads * (group_rows * length * 6 + length * HS * 4 + row_count * HS * 4)
     windows = 2 * (length * step * 4 + row_count * step * 5) + 5 * row_count * LANES * 4
     return pl.pallas_call(
-        functools.partial(attend_kernel, plan, tok_count, heads, flip),
+        functools.partial(attend_kernel, plan, tok_count, heads, flip, len(queries)),
         grid=(width // step,),
-        in_specs=query_specs + pos_specs + panel_specs * 4,
+        in_specs=query_specs + pos_specs + panel_specs * 2,
         out_specs=pl.BlockSpec((owners // 2, SLOTS, step), lambda h: (0, 0, h)),
         out_shape=jax.ShapeDtypeStruct((owners // 2, SLOTS, width), jnp.bfloat16),
         scratch_shapes=[
@@ -289,7 +316,7 @@
         ],
         compiler_params=pltpu.CompilerParams(vmem_limit_bytes=scratch + windows * 5 // 4 + 4 * MIB),
         name="attend",
-    )(*queries, *positions, *own_keys, *own_values, *other_keys, *other_values)
+    )(*queries, *positions, *own, *other)
 
 
 def output_kernel(attended_ref, weight_ref, *refs):
@@ -323,57 +350,73 @@
     )(attended, output_slab)
 
 
-def combine_kernel(quarter_count, slots_ref, gates_ref, *refs):
-    pieces, out_ref, mix = refs[:-2], refs[-2], refs[-1]
-    tok_count = slots_ref.shape[0]
-
-    @pl.when(pl.program_id(0) == 0)
-    def _():
-        slots = slots_ref[...].astype(jnp.float32)
-        gates = gates_ref[...]
-        lane = lax.broadcasted_iota(jnp.int32, slots.shape, 1)
-        wide = lax.broadcasted_iota(jnp.int32, (tok_count, len(pieces) * SLOTS), 1).astype(
-            jnp.float32
-        )
-        total = jnp.zeros_like(wide)
-        for k in range(len(pieces)):
-            mine = lane == (lax.axis_index("ctx") ^ k) // quarter_count
-            slot = jnp.sum(jnp.where(mine, slots, 0.0), axis=1, keepdims=True)
-            gate = jnp.sum(jnp.where(mine, gates, 0.0), axis=1, keepdims=True)
-            spot = jnp.where(slot >= 0, slot + float(k * SLOTS), -1.0)
-            total = total + jnp.where(wide == spot, gate, 0.0)
-        for part in range(3):
-            term = total.astype(jnp.bfloat16)
-            mix[pl.ds(part * tok_count, tok_count), :] = term
-            total = total - term.astype(jnp.float32)
-
+def mix_kernel(quarter_count, top_ref, bottom_ref, logits_ref, mix_ref):
+    slots = jnp.concatenate([top_ref[...], bottom_ref[...]], axis=0).astype(jnp.float32)
+    tok_count = slots.shape[0]
+    logits = jnp.where(slots >= 0, logits_ref[...], -jnp.inf)
+    raised = jnp.exp(logits - jnp.max(logits, axis=1, keepdims=True))
+    gates = raised / jnp.sum(raised, axis=1, keepdims=True)
+    lane = lax.broadcasted_iota(jnp.int32, slots.shape, 1)
+    count = mix_ref.shape[1] // SLOTS
+    wide = lax.broadcasted_iota(jnp.int32, (tok_count, count * SLOTS), 1).astype(jnp.float32)
+    total = jnp.zeros_like(wide)
+    for k in range(count):
+        mine = lane == (lax.axis_index("ctx") ^ k) // quarter_count
+        slot = jnp.sum(jnp.where(mine, slots, 0.0), axis=1, keepdims=True)
+        gate = jnp.sum(jnp.where(mine, gates, 0.0), axis=1, keepdims=True)
+        spot = jnp.where(slot >= 0, slot + float(k * SLOTS), -1.0)
+        total = total + jnp.where(wide == spot, gate, 0.0)
+    for part in range(3):
+        term = total.astype(jnp.bfloat16)
+        mix_ref[pl.ds(part * tok_count, tok_count), :] = term
+        total = total - term.astype(jnp.float32)
+
+
+def gate_mix(quarter_count, halves, logits, count):
+    half, width = halves[0].shape
+    tok_count = 2 * half
+    lanes = width // LANES - 1
+    return pl.pallas_call(
+        functools.partial(mix_kernel, quarter_count),
+        grid=(1,),
+        in_specs=[pl.BlockSpec((half, LANES), lambda n: (0, lanes))] * 2
+        + [pl.BlockSpec((tok_count, LANES), lambda n: (0, 0))],
+        out_specs=pl.BlockSpec((3 * tok_count, count * SLOTS), lambda n: (0, 0)),
+        out_shape=jax.ShapeDtypeStruct((3 * tok_count, count * SLOTS), jnp.bfloat16),
+        compiler_params=pltpu.CompilerParams(vmem_limit_bytes=16 * MIB),
+        name="gate_mix",
+    )(*halves, logits)
+
+
+def combine_kernel(mix_ref, *refs):
+    pieces, out_ref = refs[:-1], refs[-1]
+    tok_count = out_ref.shape[0]
     spare = jnp.zeros((SLOTS - MOST, out_ref.shape[1]), jnp.float32)
     rows = []
     for piece in pieces:
         rows += [piece[...].astype(jnp.float32), spare]
     rows = jnp.concatenate(rows, axis=0).astype(jnp.bfloat16)
-    product = jnp.dot(mix[...], rows, preferred_element_type=jnp.float32)
+    product = jnp.dot(mix_ref[...], rows, preferred_element_type=jnp.float32)
     total = product[:tok_count] + (
         product[tok_count : 2 * tok_count] + product[2 * tok_count :]
     )
     out_ref[...] = total.astype(jnp.bfloat16)
 
 
-def combine(quarter_count, slots, gates, pieces):
-    tok_count = slots.shape[0]
+def combine(mix, pieces):
+    tok_count = mix.shape[0] // 3
     model_width = pieces[0].shape[1]
     step = 512
     return pl.pallas_call(
-        functools.partial(combine_kernel, quarter_count),
+        combine_kernel,
         grid=(model_width // step,),
-        in_specs=[pl.BlockSpec((tok_count, LANES), lambda n: (0, 0))] * 2
+        in_specs=[pl.BlockSpec(mix.shape, lambda n: (0, 0))]
         + [pl.BlockSpec((MOST, step), lambda n: (0, n))] * len(pieces),
         out_specs=pl.BlockSpec((tok_count, step), lambda n: (0, n)),
         out_shape=jax.ShapeDtypeStruct((tok_count, model_width), jnp.bfloat16),
-        scratch_shapes=[pltpu.VMEM((3 * tok_count, len(pieces) * SLOTS), jnp.bfloat16)],
         compiler_params=pltpu.CompilerParams(vmem_limit_bytes=24 * MIB),
         name="combine",
-    )(slots, gates, *pieces)
+    )(mix, *pieces)
 
 
 def per_device(
@@ -398,86 +441,71 @@
     halves = norm_rows(tokens, norm_gain, routes)
     steps = ctx_count // 2
     plan = [[0]] + [[-step, step] for step in range(1, steps)] + [[steps]]
-    arrived = {0: list(halves)}
-    own_keys, own_values, queries, positions = [], [], [], []
-    lead = [halves[0], halves[1]]
-    rest = [halves[1], halves[0]]
-    for step in range(1, steps + 1):
-        done = step - 1
-        blocks = arrived[done]
-        if done == 0:
-            lead = [lax.ppermute(lead[0], "ctx", forward), lax.ppermute(lead[1], "ctx", backward)]
-            rest = [lax.ppermute(rest[0], "ctx", forward), lax.ppermute(rest[1], "ctx", backward)]
-        keys, mark = project_keys(blocks, key_weight)
-        if step < steps:
-            mark, *lead_next = lax.optimization_barrier((mark, *lead))
-        else:
-            lead_next = lead
-        values, query, position = project_values(
-            blocks, plan[done], mark, value_weight, query_slab
-        )
-        if step < steps:
-            position, *rest_next = lax.optimization_barrier((position, *rest))
-            arrived[step] = [lead[0], rest[0], rest[1], lead[1]]
-            lead = [
-                lax.ppermute(lead_next[0], "ctx", forward),
-                lax.ppermute(lead_next[1], "ctx", backward),
-            ]
-            if step < steps - 1:
-                rest = [
-                    lax.ppermute(rest_next[0], "ctx", forward),
-                    lax.ppermute(rest_next[1], "ctx", backward),
-                ]
-        else:
-            arrived[step] = [lead[0], lead[1]]
-        own_keys.append(keys)
-        own_values.append(values)
-        queries.append(query)
-        positions.append(position)
+    own, other, picked, queries, positions = [], [], [], [], []
+
+    def send(parts):
+        return [lax.ppermute(parts[0], "ctx", forward), lax.ppermute(parts[1], "ctx", backward)]
 
     def hand_over(panel):
         return lax.ppermute(panel, "exp", sibling)
 
-    other_keys = [hand_over(panel) for panel in own_keys[:-1]]
-    other_values = [hand_over(panel) for panel in own_values[:-1]]
-    late_keys, late_values, *last = lax.optimization_barrier(
-        (own_keys[-1], own_values[-1], *arrived[steps])
-    )
-    other_keys.append(hand_over(late_keys))
-    other_values.append(hand_over(late_values))
-    keys, mark = project_keys(last, key_weight)
-    values, query, position = project_values(last, plan[-1], mark, value_weight, query_slab)
-    own_keys.append(keys)
-    own_values.append(values)
-    queries.append(query)
+    def tie(*arrays):
+        return lax.optimization_barrier(arrays)
+
+    blocks = halves
+    lead = send([halves[0], halves[1]])
+    rest = send([halves[1], halves[0]])
+    for step in range(steps):
+        panel, mark = project_keys(blocks, key_weight)
+        following = [lead[0], rest[0], rest[1], lead[1]]
+        if step == steps - 2:
+            queries.append(project_queries(picked, query_slab))
+            picked = []
+        if step < steps - 1:
+            mark, *lead_next = tie(mark, *lead, *queries)
+            if queries:
+                queries = lead_next[-1:]
+            lead = send(lead_next[:2])
+        panel, rows, position = project_values(blocks, plan[step], mark, panel, value_weight)
+        if step < steps - 2:
+            position, *rest_next = tie(position, *rest)
+            rest = send(rest_next)
+        own.append(panel)
+        picked.append(rows)
+        positions.append(position)
+        if step < steps - 1:
+            other.append(hand_over(panel))
+        blocks = following
+    own[-1], last_one, last_two = tie(own[-1], *lead)
+    other.append(hand_over(own[-1]))
+    blocks = [last_one, last_two]
+    panel, mark = project_keys(blocks, key_weight)
+    panel, rows, position = project_values(blocks, plan[-1], mark, panel, value_weight)
+    own.append(panel)
+    other.append(hand_over(panel))
     positions.append(position)
-    other_keys.append(hand_over(keys))
-    other_values.append(hand_over(values))
-
-    panels = (own_keys, own_values, other_keys, other_values)
-    attended = attend(True, plan, queries, positions, *panels)
+    queries.append(project_queries(picked + [rows], query_slab))
+
+    attended = attend(True, plan, queries, positions, own, other)
     far = project_output(attended, output_slab)
-    positions[0], *far = lax.optimization_barrier((positions[0], *far))
+    positions[0], *far = tie(positions[0], *far)
     half = ctx_count // 2
 
     def swap(piece, k):
         return lax.ppermute(piece, "ctx", [(c, c ^ k) for c in range(ctx_count)])
 
     far = [swap(piece, half + r) for r, piece in enumerate(far)]
-    attended = attend(False, plan, queries, positions, *panels)
+    attended = attend(False, plan, queries, positions, own, other)
     near = project_output(attended, output_slab)
-    tied = lax.optimization_barrier((*near, *far))
-    near, far = tied[:half], list(tied[half:])
+    tied = tie(*near, *far[: half // 2])
+    near, far = tied[:half], list(tied[half:]) + far[half // 2 :]
     near = [near[0]] + [swap(near[r], r) for r in range(1, half)]
 
-    message = jnp.concatenate(halves, axis=0)
-    logits = jnp.dot(
-        message[:, :model_width].astype(jnp.float32), router_weight, precision=lax.Precision.HIGHEST
-    )
-    slots = message[:, model_width:]
-    gating = jax.nn.softmax(jnp.where(slots[:, :EXPERTS] >= 0, logits, -jnp.inf), axis=1)
-    gates = jnp.pad(gating, ((0, 0), (0, LANES - EXPERTS)))
-    return combine(quarter_count, slots, gates, near + far)
+    normed = jnp.concatenate([part[:, :model_width] for part in halves], axis=0)
+    logits = jnp.dot(normed.astype(jnp.float32), router_weight, precision=lax.Precision.HIGHEST)
+    logits = jnp.pad(logits, ((0, 0), (0, LANES - EXPERTS)))
+    mix = gate_mix(quarter_count, halves, logits, ctx_count)
+    return combine(mix, near + far)
 
 
 def solution(mesh):

time: 124 us -> 107 us (0.86)
  waiting for transfers between devices: 27.4 us -> 17.7 us
  starting transfers between devices: 33.2 us -> 27.9 us
  Pallas kernels: 55.5 us -> 53.9 us
    ppermute x14, waiting for transfers between devices: 11 us -> 3.3 us  [the longest x7 3.28 us: send(): lax.ppermute(parts[1], 'ctx', backward)]
    pallas_call x5, Pallas kernels: 19.6 us -> 14.1 us  [project_values(): pl.pallas_call(functools.partial(values_kernel, offsets, len(blocks), EXP...]
    ppermute x7, starting transfers between devices: 16.2 us -> 11.3 us  [swap(): return lax.ppermute(piece, 'ctx', [(c, c ^ k) for c in range(ctx_count)])]
    pallas_call x1 -> x4, Pallas kernels: 3.06 us -> 7.4 us  [the longest x2 4.33 us: project_queries(): pl.pallas_call(queries_kernel, grid=(width // step,), in_specs=[pl.BlockS...]
    ppermute x10 -> x5, waiting for transfers between devices: 1.38 us -> 0.01 us  [hand_over(): return lax.ppermute(panel, 'exp', sibling)]
    unnamed x23 -> x22, local copies, waits for them, and re-layouts: 6.33 us -> 6.32 us
  transfers between devices with their start and end apart: 31 -> 26, of which waited for: 13 -> 8; matrix products, arithmetic and copies ran while one was open for 1% -> 1% of each run, Pallas kernels for 32% -> 36%
where the time goes in v6:
time: 107 us
  Pallas kernels  53.9 us (50%)
  starting transfers between devices  27.9 us (26%)
  waiting for transfers between devices  17.7 us (17%)
  local copies, waits for them, and re-layouts  6.37 us (6%)
    pallas_call x2, Pallas kernels, attend(): pl.pallas_call(functools.partial(attend_kernel, plan, tok_count, heads, f...  15 us
    ppermute x7, waiting for transfers between devices, swap(): return lax.ppermute(piece, 'ctx', [(c, c ^ k) for c in range(ctx_count)])  14.4 us
    pallas_call x5, Pallas kernels, project_values(): pl.pallas_call(functools.partial(values_kernel, offsets, len(blocks), EXP...  14.1 us
    ppermute x7, starting transfers between devices, swap(): return lax.ppermute(piece, 'ctx', [(c, c ^ k) for c in range(ctx_count)])  11.3 us
    ppermute x7, starting transfers between devices, send(): lax.ppermute(parts[0], 'ctx', forward)  11.1 us
    pallas_call x5, Pallas kernels, project_keys(): pl.pallas_call(functools.partial(keys_kernel, len(blocks)), grid=(width /...  11.1 us
    unnamed x22, local copies, waits for them, and re-layouts  6.32 us
    pallas_call x2, Pallas kernels, project_queries(): pl.pallas_call(queries_kernel, grid=(width // step,), in_specs=[pl.BlockS...  4.33 us
  transfers between devices with their start and end apart: 26, of which 8 were waited for; matrix products, arithmetic and copies ran while one was open for 1% of the time, Pallas kernels for 36%

profile of v6, /device:TPU:0, one launch (start us, length us, event | category | flops | bytes accessed | tf_op | source)
XLA Modules:
  0.0 106.8 jit_solution(14695077404868901706)
XLA Ops:
  0.0 2.1 %norm_rows.1 = (bf16[64,2176]{1,0:T(8,128)(2,1)}, bf16[64,2176]{1,0:T(8,128)(2,1)}) custom-call(bf16[128,2048]{1,0:T(8,128)(2,1)} %tokens_ref.1, f32[1,2048]{1,0:T(1,128)} %bitcast.9, s32[2,128]{1,0:T(2,128)} %bitcast.10), custom_call_target="tpu_custom_call" | custom-call | tf_op jit(solution)/shard_map/norm_rows/pallas_call | solution.py:59
  2.1 3.0 %collective-permute-start = (bf16[64,2176]{1,0:T(8,128)(2,1)}, bf16[64,2176]{1,0:T(8,128)(2,1)S(1)}, u32[]{:S(2)}, u32[]{:S(2)}) collective-permute-start(bf16[64,2176]{1,0:T(8,128)(2,1)} %get-tuple-element.70.top_ref.refs_0_), channel_id=1, source_target_pairs={{0,4},{4,8},{8,12},{12,14},{14,10},{10,6},{6,2},{2,0},{1,5},{5,9},... | collective-permute-start | bytes 835592 | tf_op jit(solution)/shard_map/ppermute | solution.py:447
  5.2 0.0 collective-permute-start.1
  5.2 2.0 %collective-permute-start.4 = (bf16[64,2176]{1,0:T(8,128)(2,1)}, bf16[64,2176]{1,0:T(8,128)(2,1)S(1)}, u32[]{:S(2)}, u32[]{:S(2)}) collective-permute-start(bf16[64,2176]{1,0:T(8,128)(2,1)} %get-tuple-element.70.top_ref.refs_0_), channel_id=1, source_target_pairs={{4,0},{8,4},{12,8},{14,12},{10,14},{6,10},{2,6},{0,2},{5,1},{9,5},... | collective-permute-start | bytes 835592 | tf_op jit(solution)/shard_map/ppermute | solution.py:447
  7.1 0.1 collective-permute-start.3
  7.2 2.2 %copy-done.1 = bf16[2048,1024]{1,0:T(8,128)(2,1)S(1)} copy-done((bf16[2048,1024]{1,0:T(8,128)(2,1)S(1)}, bf16[2048,1024]{1,0:T(8,128)(2,1)}, u32[]{:S(2)}) %copy-start.1) | copy-done | bytes 4194328
  9.4 1.0 copy-done.7
  10.4 1.0 copy-done.9
  11.3 1.9 %project_keys.5 = (bf16[2,128,1024]{2,1,0:T(8,128)(2,1)S(1)}, f32[8,128]{1,0:T(8,128)S(1)}) custom-call(bf16[64,2176]{1,0:T(8,128)(2,1)S(1)} %copy-done.7, bf16[64,2176]{1,0:T(8,128)(2,1)S(1)} %copy-done.9, bf16[2048,1024]{1,0:T(8,128)(2,1)S(1)} %copy-done.1), custom_call_target="tpu_custom_call" | custom-call | tf_op jit(solution)/shard_map/project_keys/pallas_call | solution.py:77
  13.2 0.0 collective-permute-done.refs_0_
  13.2 1.7 %collective-permute-done.1.refs_3_ = bf16[64,2176]{1,0:T(8,128)(2,1)S(1)} collective-permute-done((bf16[64,2176]{1,0:T(8,128)(2,1)}, bf16[64,2176]{1,0:T(8,128)(2,1)S(1)}, u32[]{:S(2)}, u32[]{:S(2)}) %collective-permute-start.1) | collective-permute-done | bytes 278560 | tf_op jit(solution)/shard_map/ppermute | solution.py:447
  15.0 1.6 %collective-permute-start.2 = (bf16[64,2176]{1,0:T(8,128)(2,1)S(1)}, bf16[64,2176]{1,0:T(8,128)(2,1)S(1)}, u32[]{:S(2)}, u32[]{:S(2)}) collective-permute-start(bf16[64,2176]{1,0:T(8,128)(2,1)S(1)} %collective-permute-done.refs_0_), channel_id=1, source_target_pairs={{0,4},{4,8},{8,12},{12,14},{14,10},{10,6},{6,2},{2,0},{1,5},{5,9},... | collective-permute-start | bytes 835592 | tf_op jit(solution)/shard_map/ppermute | solution.py:447
  16.5 0.4 collective-permute-start.7
  17.0 2.2 %copy-done.3 = bf16[2048,1024]{1,0:T(8,128)(2,1)S(1)} copy-done((bf16[2048,1024]{1,0:T(8,128)(2,1)S(1)}, bf16[2048,1024]{1,0:T(8,128)(2,1)}, u32[]{:S(2)}) %copy-start.3) | copy-done | bytes 4194328
  19.2 2.4 %project_values.5 = (bf16[2,128,1024]{2,1,0:T(8,128)(2,1)S(1)}, bf16[1,48,2048]{2,1,0:T(8,128)(2,1)S(1)}, f32[1,48,128]{2,1,0:T(8,128)S(1)}) custom-call(f32[8,128]{1,0:T(8,128)S(1)} %get-tuple-element.74.mark_ref, bf16[2,128,1024]{2,1,0:T(8,128)(2,1)S(1)} %get-tuple-element.75.half_panel_ref, ...), custom_call_target="tpu_custom_call", output_to_operand_aliasing={{0}: (1, {})} | custom-call | tf_op jit(solution)/shard_map/project_values/pallas_call | solution.py:132
  21.6 0.0 collective-permute-done.4.refs_2_
  21.6 0.0 collective-permute-done.3.refs_1_
  21.6 1.6 %collective-permute-start.5 = (bf16[64,2176]{1,0:T(8,128)(2,1)S(1)}, bf16[64,2176]{1,0:T(8,128)(2,1)S(1)}, u32[]{:S(2)}, u32[]{:S(2)}) collective-permute-start(bf16[64,2176]{1,0:T(8,128)(2,1)S(1)} %collective-permute-done.3.refs_1_), channel_id=1, source_target_pairs={{0,4},{4,8},{8,12},{12,14},{14,10},{10,6},{6,2},{2,0},{1,5},{5,9},... | collective-permute-start | bytes 835592 | tf_op jit(solution)/shard_map/ppermute | solution.py:447
  23.2 0.4 collective-permute-start.6
  23.7 2.4 %project_keys.7 = (bf16[2,256,1024]{2,1,0:T(8,128)(2,1)S(1)}, f32[8,128]{1,0:T(8,128)S(1)}) custom-call(bf16[64,2176]{1,0:T(8,128)(2,1)S(1)} %collective-permute-done.refs_0_, bf16[64,2176]{1,0:T(8,128)(2,1)S(1)} %collective-permute-done.3.refs_1_, bf16[64,2176]{1,0:T(8,128)(2,1)S(1)} %collective-permute-done.4.refs_2_, ...), custom_call_target="tpu_custom_call" | custom-call | tf_op jit(solution)/shard_map/project_keys/pallas_call | solution.py:77
  26.1 0.0 copy-start.5
  26.1 0.8 collective-permute-done.7.refs_3_
  26.9 1.6 %collective-permute-start.8 = (bf16[64,2176]{1,0:T(8,128)(2,1)S(1)}, bf16[64,2176]{1,0:T(8,128)(2,1)S(1)}, u32[]{:S(2)}, u32[]{:S(2)}) collective-permute-start(bf16[64,2176]{1,0:T(8,128)(2,1)S(1)} %collective-permute-done.2.refs_0_), channel_id=1, source_target_pairs={{0,4},{4,8},{8,12},{12,14},{14,10},{10,6},{6,2},{2,0},{1,5},{5,9},... | collective-permute-start | bytes 835592 | tf_op jit(solution)/shard_map/ppermute | solution.py:447
  28.5 0.4 collective-permute-start.9
  28.9 3.1 %project_values.6 = (bf16[2,256,1024]{2,1,0:T(8,128)(2,1)S(1)}, bf16[2,48,2048]{2,1,0:T(8,128)(2,1)S(1)}, f32[2,48,128]{2,1,0:T(8,128)S(1)}) custom-call(f32[8,128]{1,0:T(8,128)S(1)} %get-tuple-element.85.mark_ref, bf16[2,256,1024]{2,1,0:T(8,128)(2,1)S(1)} %get-tuple-element.86.half_panel_ref, ...), custom_call_target="tpu_custom_call", output_to_operand_aliasing={{0}: (1, {})} | custom-call | tf_op jit(solution)/shard_map/project_values/pallas_call | solution.py:132
  32.1 0.0 collective-permute-done.5.refs_1_
  32.1 0.8 collective-permute-done.6.refs_2_
  32.9 1.6 %collective-permute-start.10 = (bf16[64,2176]{1,0:T(8,128)(2,1)S(1)}, bf16[64,2176]{1,0:T(8,128)(2,1)S(1)}, u32[]{:S(2)}, u32[]{:S(2)}) collective-permute-start(bf16[64,2176]{1,0:T(8,128)(2,1)S(1)} %collective-permute-done.5.refs_1_), channel_id=1, source_target_pairs={{0,4},{4,8},{8,12},{12,14},{14,10},{10,6},{6,2},{2,0},{1,5},{5,9},... | collective-permute-start | bytes 835592 | tf_op jit(solution)/shard_map/ppermute | solution.py:447
  34.4 0.4 collective-permute-start.11
  34.9 2.0 %project_queries.2.refs_0_ = bf16[3,48,1024]{2,1,0:T(8,128)(2,1)S(1)} custom-call(bf16[1,48,2048]{2,1,0:T(8,128)(2,1)S(1)} %get-tuple-element.84.refs_0_, bf16[2,48,2048]{2,1,0:T(8,128)(2,1)S(1)} %get-tuple-element.87.refs_1_, bf16[2048,1024]{1,0:T(8,128)(2,1)S(1)} %bitcast.5), custom_call_target="tpu_custom_call" | custom-call | tf_op jit(solution)/shard_map/project_queries/pallas_call | solution.py:172
  36.9 2.4 %project_keys.6 = (bf16[2,256,1024]{2,1,0:T(8,128)(2,1)S(1)}, f32[8,128]{1,0:T(8,128)S(1)}) custom-call(bf16[64,2176]{1,0:T(8,128)(2,1)S(1)} %collective-permute-done.2.refs_0_, bf16[64,2176]{1,0:T(8,128)(2,1)S(1)} %collective-permute-done.5.refs_1_, bf16[64,2176]{1,0:T(8,128)(2,1)S(1)} %collective-permute-done.6.refs_2_, ...), custom_call_target="tpu_custom_call" | custom-call | tf_op jit(solution)/shard_map/project_keys/pallas_call | solution.py:77
  39.3 0.0 collective-permute-done.9.refs_3_
  39.3 1.6 %collective-permute-start.12 = (bf16[64,2176]{1,0:T(8,128)(2,1)S(1)}, bf16[64,2176]{1,0:T(8,128)(2,1)S(1)}, u32[]{:S(2)}, u32[]{:S(2)}) collective-permute-start(bf16[64,2176]{1,0:T(8,128)(2,1)S(1)} %collective-permute-done.8.refs_0_), channel_id=1, source_target_pairs={{0,4},{4,8},{8,12},{12,14},{14,10},{10,6},{6,2},{2,0},{1,5},{5,9},... | collective-permute-start | bytes 835592 | tf_op jit(solution)/shard_map/ppermute | solution.py:447
  41.0 0.4 collective-permute-start.13
  41.4 3.1 %project_values.7 = (bf16[2,256,1024]{2,1,0:T(8,128)(2,1)S(1)}, bf16[2,48,2048]{2,1,0:T(8,128)(2,1)S(1)}, f32[2,48,128]{2,1,0:T(8,128)S(1)}) custom-call(f32[8,128]{1,0:T(8,128)S(1)} %get-tuple-element.89.mark_ref, bf16[2,256,1024]{2,1,0:T(8,128)(2,1)S(1)} %get-tuple-element.90.half_panel_ref, ...), custom_call_target="tpu_custom_call", output_to_operand_aliasing={{0}: (1, {})} | custom-call | tf_op jit(solution)/shard_map/project_values/pallas_call | solution.py:132
  44.5 0.6 collective-permute-start.16
  45.1 2.4 %project_keys.8 = (bf16[2,256,1024]{2,1,0:T(8,128)(2,1)S(1)}, f32[8,128]{1,0:T(8,128)S(1)}) custom-call(bf16[64,2176]{1,0:T(8,128)(2,1)S(1)} %collective-permute-done.8.refs_0_, bf16[64,2176]{1,0:T(8,128)(2,1)S(1)} %collective-permute-done.10.refs_1_, bf16[64,2176]{1,0:T(8,128)(2,1)S(1)} %collective-permute-done.11.refs_2_, ...), custom_call_target="tpu_custom_call" | custom-call | tf_op jit(solution)/shard_map/project_keys/pallas_call | solution.py:77
  47.5 3.1 %project_values.8 = (bf16[2,256,1024]{2,1,0:T(8,128)(2,1)S(1)}, bf16[2,48,2048]{2,1,0:T(8,128)(2,1)S(1)}, f32[2,48,128]{2,1,0:T(8,128)S(1)}) custom-call(f32[8,128]{1,0:T(8,128)S(1)} %get-tuple-element.95.mark_ref, bf16[2,256,1024]{2,1,0:T(8,128)(2,1)S(1)} %get-tuple-element.96.half_panel_ref, ...), custom_call_target="tpu_custom_call", output_to_operand_aliasing={{0}: (1, {})} | custom-call | tf_op jit(solution)/shard_map/project_values/pallas_call | solution.py:132
  50.7 0.1 collective-permute-start.17
  50.8 0.5 collective-permute-start.14
  51.3 1.9 %project_keys.9 = (bf16[2,128,1024]{2,1,0:T(8,128)(2,1)S(1)}, f32[8,128]{1,0:T(8,128)S(1)}) custom-call(bf16[64,2176]{1,0:T(8,128)(2,1)S(1)} %collective-permute-done.12.refs_0_, bf16[64,2176]{1,0:T(8,128)(2,1)S(1)} %collective-permute-done.13.refs_1_, bf16[2048,1024]{1,0:T(8,128)(2,1)S(1)} %copy-done.2), custom_call_target="tpu_custom_call" | custom-call | tf_op jit(solution)/shard_map/project_keys/pallas_call | solution.py:77
  53.2 2.4 %project_values.9 = (bf16[2,128,1024]{2,1,0:T(8,128)(2,1)S(1)}, bf16[1,48,2048]{2,1,0:T(8,128)(2,1)S(1)}, f32[1,48,128]{2,1,0:T(8,128)S(1)}) custom-call(f32[8,128]{1,0:T(8,128)S(1)} %get-tuple-element.103.mark_ref, bf16[2,128,1024]{2,1,0:T(8,128)(2,1)S(1)} %get-tuple-element.104.half_panel_ref, ...), custom_call_target="tpu_custom_call", output_to_operand_aliasing={{0}: (1, {})} | custom-call | tf_op jit(solution)/shard_map/project_values/pallas_call | solution.py:132
  55.6 0.1 collective-permute-start.18
  55.7 2.4 %project_queries.3.refs_1_ = bf16[5,48,1024]{2,1,0:T(8,128)(2,1)S(1)} custom-call(bf16[2,48,2048]{2,1,0:T(8,128)(2,1)S(1)} %get-tuple-element.91.refs_0_, bf16[2,48,2048]{2,1,0:T(8,128)(2,1)S(1)} %get-tuple-element.97.refs_1_, bf16[1,48,2048]{2,1,0:T(8,128)(2,1)S(1)} %get-tuple-element.105.refs_2_, bf16[2048,1024]{1,0:T(8,128)(2,1)S(1)} %bitcast.6), custom_call_target="tpu_custom_call" | custom-call | tf_op jit(solution)/shard_map/project_queries/pallas_call | solution.py:172
  58.2 0.0 copy-start.6
  58.2 8.6 %attend.2.attended_ref = bf16[4,48,1024]{2,1,0:T(8,128)(2,1)S(1)} custom-call(bf16[3,48,1024]{2,1,0:T(8,128)(2,1)S(1)} %project_queries.2.refs_0_, bf16[5,48,1024]{2,1,0:T(8,128)(2,1)S(1)} %project_queries.3.refs_1_, f32[1,48,128]{2,1,0:T(8,128)S(1)} %get-tuple-element.120.refs_2_, f32[2,48,128]{2,1,0:T(8,128)S(1)} %get-tuple-element.107.refs_3_, ...), custom_call_target="tpu_custom_call" | custom-call | tf_op jit(solution)/shard_map/attend/pallas_call | solution.py:303
  66.8 0.0 copy-start.8
  66.8 2.1 %project_output.2 = (bf16[40,2048]{1,0:T(8,128)(2,1)S(1)}, bf16[40,2048]{1,0:T(8,128)(2,1)S(1)}, bf16[40,2048]{1,0:T(8,128)(2,1)S(1)}, bf16[40,2048]{1,0:T(8,128)(2,1)S(1)}) custom-call(bf16[4,48,1024]{2,1,0:T(8,128)(2,1)S(1)} %attend.2.attended_ref, bf16[1024,2048]{1,0:T(8,128)(2,1)S(1)} %bitcast.7), custom_call_target="tpu_custom_call" | custom-call | tf_op jit(solution)/shard_map/project_output/pallas_call | solution.py:338
  68.9 0.5 collective-permute-start.19
  69.4 2.3 %collective-permute-start.20 = (bf16[40,2048]{1,0:T(8,128)(2,1)S(1)}, bf16[40,2048]{1,0:T(8,128)(2,1)S(1)}, u32[]{:S(2)}, u32[]{:S(2)}) collective-permute-start(bf16[40,2048]{1,0:T(8,128)(2,1)S(1)} %get-tuple-element.126), channel_id=1, source_target_pairs={{0,10},{2,8},{4,14},{6,12},{8,2},{10,0},{12,6},{14,4},{1,11},{3,9}... | collective-permute-start | bytes 491528 | tf_op jit(solution)/shard_map/ppermute | solution.py:495
  71.8 1.6 %collective-permute-start.24 = (bf16[40,2048]{1,0:T(8,128)(2,1)S(1)}, bf16[40,2048]{1,0:T(8,128)(2,1)S(1)}, u32[]{:S(2)}, u32[]{:S(2)}) collective-permute-start(bf16[40,2048]{1,0:T(8,128)(2,1)S(1)} %get-tuple-element.133), channel_id=1, source_target_pairs={{0,12},{2,14},{4,8},{6,10},{8,4},{10,6},{12,0},{14,2},{1,13},{3,15... | collective-permute-start | bytes 491528 | tf_op jit(solution)/shard_map/ppermute | solution.py:495
  73.3 3.4 %collective-permute-start.25 = (bf16[40,2048]{1,0:T(8,128)(2,1)S(1)}, bf16[40,2048]{1,0:T(8,128)(2,1)S(1)}, u32[]{:S(2)}, u32[]{:S(2)}) collective-permute-start(bf16[40,2048]{1,0:T(8,128)(2,1)S(1)} %get-tuple-element.134), channel_id=1, source_target_pairs={{0,14},{2,12},{4,10},{6,8},{8,6},{10,4},{12,2},{14,0},{1,15},{3,13... | collective-permute-start | bytes 491528 | tf_op jit(solution)/shard_map/ppermute | solution.py:495
  76.7 6.4 %attend.3.attended_ref = bf16[4,48,1024]{2,1,0:T(8,128)(2,1)S(1)} custom-call(bf16[3,48,1024]{2,1,0:T(8,128)(2,1)S(1)} %project_queries.2.refs_0_, bf16[5,48,1024]{2,1,0:T(8,128)(2,1)S(1)} %project_queries.3.refs_1_, f32[1,48,128]{2,1,0:T(8,128)S(1)} %get-tuple-element.120.refs_2_, f32[2,48,128]{2,1,0:T(8,128)S(1)} %get-tuple-element.107.refs_3_, ...), custom_call_target="tpu_custom_call" | custom-call | tf_op jit(solution)/shard_map/attend/pallas_call | solution.py:303
  83.1 2.1 %project_output.3 = (bf16[40,2048]{1,0:T(8,128)(2,1)S(1)}, bf16[40,2048]{1,0:T(8,128)(2,1)S(1)}, bf16[40,2048]{1,0:T(8,128)(2,1)S(1)}, bf16[40,2048]{1,0:T(8,128)(2,1)S(1)}) custom-call(bf16[4,48,1024]{2,1,0:T(8,128)(2,1)S(1)} %attend.3.attended_ref, bf16[1024,2048]{1,0:T(8,128)(2,1)S(1)} %bitcast.8), custom_call_target="tpu_custom_call" | custom-call | tf_op jit(solution)/shard_map/project_output/pallas_call | solution.py:338
  85.2 5.7 %collective-permute-done.19.refs_4_ = bf16[40,2048]{1,0:T(8,128)(2,1)S(1)} collective-permute-done((bf16[40,2048]{1,0:T(8,128)(2,1)S(1)}, bf16[40,2048]{1,0:T(8,128)(2,1)S(1)}, u32[]{:S(2)}, u32[]{:S(2)}) %collective-permute-start.19) | collective-permute-done | bytes 163872 | tf_op jit(solution)/shard_map/ppermute | solution.py:495
  90.9 3.3 %collective-permute-done.20.refs_5_ = bf16[40,2048]{1,0:T(8,128)(2,1)S(1)} collective-permute-done((bf16[40,2048]{1,0:T(8,128)(2,1)S(1)}, bf16[40,2048]{1,0:T(8,128)(2,1)S(1)}, u32[]{:S(2)}, u32[]{:S(2)}) %collective-permute-start.20) | collective-permute-done | bytes 163872 | tf_op jit(solution)/shard_map/ppermute | solution.py:495
  94.2 1.6 %collective-permute-start.21 = (bf16[40,2048]{1,0:T(8,128)(2,1)S(1)}, bf16[40,2048]{1,0:T(8,128)(2,1)S(1)}, u32[]{:S(2)}, u32[]{:S(2)}) collective-permute-start(bf16[40,2048]{1,0:T(8,128)(2,1)S(1)} %get-tuple-element.128), channel_id=1, source_target_pairs={{0,2},{2,0},{4,6},{6,4},{8,10},{10,8},{12,14},{14,12},{1,3},{3,1},... | collective-permute-start | bytes 491528 | tf_op jit(solution)/shard_map/ppermute | solution.py:495
  95.9 1.8 %collective-permute-start.23 = (bf16[40,2048]{1,0:T(8,128)(2,1)S(1)}, bf16[40,2048]{1,0:T(8,128)(2,1)S(1)}, u32[]{:S(2)}, u32[]{:S(2)}) collective-permute-start(bf16[40,2048]{1,0:T(8,128)(2,1)S(1)} %get-tuple-element.130), channel_id=1, source_target_pairs={{0,6},{2,4},{4,2},{6,0},{8,14},{10,12},{12,10},{14,8},{1,7},{3,5},... | collective-permute-start | bytes 491528 | tf_op jit(solution)/shard_map/ppermute | solution.py:495
  97.7 0.5 fusion
  98.3 0.5 gate_mix.1.mix_ref
  98.8 1.6 %collective-permute-done.21.refs_1_ = bf16[40,2048]{1,0:T(8,128)(2,1)S(1)} collective-permute-done((bf16[40,2048]{1,0:T(8,128)(2,1)S(1)}, bf16[40,2048]{1,0:T(8,128)(2,1)S(1)}, u32[]{:S(2)}, u32[]{:S(2)}) %collective-permute-start.21) | collective-permute-done | bytes 163872 | tf_op jit(solution)/shard_map/ppermute | solution.py:495
  100.5 2.2 %collective-permute-done.22.refs_2_ = bf16[40,2048]{1,0:T(8,128)(2,1)S(1)} collective-permute-done((bf16[40,2048]{1,0:T(8,128)(2,1)S(1)}, bf16[40,2048]{1,0:T(8,128)(2,1)S(1)}, u32[]{:S(2)}, u32[]{:S(2)}) %collective-permute-start.22) | collective-permute-done | bytes 163872 | tf_op jit(solution)/shard_map/ppermute | solution.py:495
  102.6 1.6 %collective-permute-done.23.refs_3_ = bf16[40,2048]{1,0:T(8,128)(2,1)S(1)} collective-permute-done((bf16[40,2048]{1,0:T(8,128)(2,1)S(1)}, bf16[40,2048]{1,0:T(8,128)(2,1)S(1)}, u32[]{:S(2)}, u32[]{:S(2)}) %collective-permute-start.23) | collective-permute-done | bytes 163872 | tf_op jit(solution)/shard_map/ppermute | solution.py:495
  104.2 2.5 %combine.1 = bf16[128,2048]{1,0:T(8,128)(2,1)} custom-call(bf16[384,384]{1,0:T(8,128)(2,1)S(1)} %gate_mix.1.mix_ref, bf16[40,2048]{1,0:T(8,128)(2,1)S(1)} %get-tuple-element.127.refs_0_, bf16[40,2048]{1,0:T(8,128)(2,1)S(1)} %collective-permute-done.21.refs_1_, bf16[40,2048]{1,0:T(8,128)(2,1)S(1)} %collective-permute-done.22.refs_2_, ...), custom_call_target="tpu_custom_call" | custom-call | tf_op jit(solution)/shard_map/combine/pallas_call | solution.py:410
  (33 shorter events, 0.1 us)
Async XLA Ops:
  0.0 97.7 %copy-start = (f32[2048,8]{0,1:T(8,128)S(1)}, f32[2048,8]{0,1:T(8,128)}, u32[]{:S(2)}) copy-start(f32[2048,8]{0,1:T(8,128)} %param.10) | copy-start | bytes 196612
  2.1 11.1 %collective-permute-start = (bf16[64,2176]{1,0:T(8,128)(2,1)}, bf16[64,2176]{1,0:T(8,128)(2,1)S(1)}, u32[]{:S(2)}, u32[]{:S(2)}) collective-permute-start(bf16[64,2176]{1,0:T(8,128)(2,1)} %get-tuple-element.70.top_ref.refs_0_), channel_id=1, source_target_pairs={{0,4},{4,8},{8,12},{12,14},{14,10},{10,6},{6,2},{2,0},{1,5},{5,9},... | collective-permute-start | bytes 835592 | tf_op jit(solution)/shard_map/ppermute | solution.py:447
  5.2 9.8 %collective-permute-start.1 = (bf16[64,2176]{1,0:T(8,128)(2,1)}, bf16[64,2176]{1,0:T(8,128)(2,1)S(1)}, u32[]{:S(2)}, u32[]{:S(2)}) collective-permute-start(bf16[64,2176]{1,0:T(8,128)(2,1)} %get-tuple-element.71.bottom_ref.refs_1_), channel_id=1, source_target_pairs={{4,0},{8,4},{12,8},{14,12},{10,14},{6,10},{2,6},{0,2},{5,1},{9,5},... | collective-permute-start | bytes 835592 | tf_op jit(solution)/shard_map/ppermute | solution.py:447
  5.2 16.4 %collective-permute-start.4 = (bf16[64,2176]{1,0:T(8,128)(2,1)}, bf16[64,2176]{1,0:T(8,128)(2,1)S(1)}, u32[]{:S(2)}, u32[]{:S(2)}) collective-permute-start(bf16[64,2176]{1,0:T(8,128)(2,1)} %get-tuple-element.70.top_ref.refs_0_), channel_id=1, source_target_pairs={{4,0},{8,4},{12,8},{14,12},{10,14},{6,10},{2,6},{0,2},{5,1},{9,5},... | collective-permute-start | bytes 835592 | tf_op jit(solution)/shard_map/ppermute | solution.py:447
  7.1 14.4 %collective-permute-start.3 = (bf16[64,2176]{1,0:T(8,128)(2,1)}, bf16[64,2176]{1,0:T(8,128)(2,1)S(1)}, u32[]{:S(2)}, u32[]{:S(2)}) collective-permute-start(bf16[64,2176]{1,0:T(8,128)(2,1)} %get-tuple-element.71.bottom_ref.refs_1_), channel_id=1, source_target_pairs={{0,4},{4,8},{8,12},{12,14},{14,10},{10,6},{6,2},{2,0},{1,5},{5,9},... | collective-permute-start | bytes 835592 | tf_op jit(solution)/shard_map/ppermute | solution.py:447
  7.2 2.2 %copy-start.1 = (bf16[2048,1024]{1,0:T(8,128)(2,1)S(1)}, bf16[2048,1024]{1,0:T(8,128)(2,1)}, u32[]{:S(2)}) copy-start(bf16[2048,1024]{1,0:T(8,128)(2,1)} %refs_2_.6) | copy-start | bytes 12582916
  9.4 1.0 copy-start.7
  10.4 1.0 copy-start.9
  11.3 12.3 %copy-start.2 = (bf16[2048,1024]{1,0:T(8,128)(2,1)S(1)}, bf16[2048,1024]{1,0:T(8,128)(2,1)}, u32[]{:S(2)}) copy-start(bf16[2048,1024]{1,0:T(8,128)(2,1)} %refs_2_.6) | copy-start | bytes 12582916
  15.0 11.2 %collective-permute-start.2 = (bf16[64,2176]{1,0:T(8,128)(2,1)S(1)}, bf16[64,2176]{1,0:T(8,128)(2,1)S(1)}, u32[]{:S(2)}, u32[]{:S(2)}) collective-permute-start(bf16[64,2176]{1,0:T(8,128)(2,1)S(1)} %collective-permute-done.refs_0_), channel_id=1, source_target_pairs={{0,4},{4,8},{8,12},{12,14},{14,10},{10,6},{6,2},{2,0},{1,5},{5,9},... | collective-permute-start | bytes 835592 | tf_op jit(solution)/shard_map/ppermute | solution.py:447
  16.5 10.4 %collective-permute-start.7 = (bf16[64,2176]{1,0:T(8,128)(2,1)S(1)}, bf16[64,2176]{1,0:T(8,128)(2,1)S(1)}, u32[]{:S(2)}, u32[]{:S(2)}) collective-permute-start(bf16[64,2176]{1,0:T(8,128)(2,1)S(1)} %collective-permute-done.1.refs_3_), channel_id=1, source_target_pairs={{4,0},{8,4},{12,8},{14,12},{10,14},{6,10},{2,6},{0,2},{5,1},{9,5},... | collective-permute-start | bytes 835592 | tf_op jit(solution)/shard_map/ppermute | solution.py:447
  17.0 2.2 %copy-start.3 = (bf16[2048,1024]{1,0:T(8,128)(2,1)S(1)}, bf16[2048,1024]{1,0:T(8,128)(2,1)}, u32[]{:S(2)}) copy-start(bf16[2048,1024]{1,0:T(8,128)(2,1)} %refs_2_.7) | copy-start | bytes 12582916
  19.2 9.8 %copy-start.4 = (bf16[2048,1024]{1,0:T(8,128)(2,1)S(1)}, bf16[2048,1024]{1,0:T(8,128)(2,1)}, u32[]{:S(2)}) copy-start(bf16[2048,1024]{1,0:T(8,128)(2,1)} %refs_2_.7) | copy-start | bytes 12582916
  21.6 10.5 %collective-permute-start.5 = (bf16[64,2176]{1,0:T(8,128)(2,1)S(1)}, bf16[64,2176]{1,0:T(8,128)(2,1)S(1)}, u32[]{:S(2)}, u32[]{:S(2)}) collective-permute-start(bf16[64,2176]{1,0:T(8,128)(2,1)S(1)} %collective-permute-done.3.refs_1_), channel_id=1, source_target_pairs={{0,4},{4,8},{8,12},{12,14},{14,10},{10,6},{6,2},{2,0},{1,5},{5,9},... | collective-permute-start | bytes 835592 | tf_op jit(solution)/shard_map/ppermute | solution.py:447
  23.2 9.6 %collective-permute-start.6 = (bf16[64,2176]{1,0:T(8,128)(2,1)S(1)}, bf16[64,2176]{1,0:T(8,128)(2,1)S(1)}, u32[]{:S(2)}, u32[]{:S(2)}) collective-permute-start(bf16[64,2176]{1,0:T(8,128)(2,1)S(1)} %collective-permute-done.4.refs_2_), channel_id=1, source_target_pairs={{4,0},{8,4},{12,8},{14,12},{10,14},{6,10},{2,6},{0,2},{5,1},{9,5},... | collective-permute-start | bytes 835592 | tf_op jit(solution)/shard_map/ppermute | solution.py:447
  26.1 8.8 %copy-start.5 = (bf16[1,2048,1024]{2,1,0:T(8,128)(2,1)S(1)}, bf16[1,2048,1024]{2,1,0:T(8,128)(2,1)}, u32[]{:S(2)}) copy-start(bf16[1,2048,1024]{2,1,0:T(8,128)(2,1)} %param.14) | copy-start | bytes 12582916
  26.9 12.4 %collective-permute-start.8 = (bf16[64,2176]{1,0:T(8,128)(2,1)S(1)}, bf16[64,2176]{1,0:T(8,128)(2,1)S(1)}, u32[]{:S(2)}, u32[]{:S(2)}) collective-permute-start(bf16[64,2176]{1,0:T(8,128)(2,1)S(1)} %collective-permute-done.2.refs_0_), channel_id=1, source_target_pairs={{0,4},{4,8},{8,12},{12,14},{14,10},{10,6},{6,2},{2,0},{1,5},{5,9},... | collective-permute-start | bytes 835592 | tf_op jit(solution)/shard_map/ppermute | solution.py:447
  28.5 10.9 %collective-permute-start.9 = (bf16[64,2176]{1,0:T(8,128)(2,1)S(1)}, bf16[64,2176]{1,0:T(8,128)(2,1)S(1)}, u32[]{:S(2)}, u32[]{:S(2)}) collective-permute-start(bf16[64,2176]{1,0:T(8,128)(2,1)S(1)} %collective-permute-done.7.refs_3_), channel_id=1, source_target_pairs={{4,0},{8,4},{12,8},{14,12},{10,14},{6,10},{2,6},{0,2},{5,1},{9,5},... | collective-permute-start | bytes 835592 | tf_op jit(solution)/shard_map/ppermute | solution.py:447
  32.9 11.7 %collective-permute-start.10 = (bf16[64,2176]{1,0:T(8,128)(2,1)S(1)}, bf16[64,2176]{1,0:T(8,128)(2,1)S(1)}, u32[]{:S(2)}, u32[]{:S(2)}) collective-permute-start(bf16[64,2176]{1,0:T(8,128)(2,1)S(1)} %collective-permute-done.5.refs_1_), channel_id=1, source_target_pairs={{0,4},{4,8},{8,12},{12,14},{14,10},{10,6},{6,2},{2,0},{1,5},{5,9},... | collective-permute-start | bytes 835592 | tf_op jit(solution)/shard_map/ppermute | solution.py:447
  34.4 10.7 %collective-permute-start.11 = (bf16[64,2176]{1,0:T(8,128)(2,1)S(1)}, bf16[64,2176]{1,0:T(8,128)(2,1)S(1)}, u32[]{:S(2)}, u32[]{:S(2)}) collective-permute-start(bf16[64,2176]{1,0:T(8,128)(2,1)S(1)} %collective-permute-done.6.refs_2_), channel_id=1, source_target_pairs={{4,0},{8,4},{12,8},{14,12},{10,14},{6,10},{2,6},{0,2},{5,1},{9,5},... | collective-permute-start | bytes 835592 | tf_op jit(solution)/shard_map/ppermute | solution.py:447
  39.3 11.4 %collective-permute-start.12 = (bf16[64,2176]{1,0:T(8,128)(2,1)S(1)}, bf16[64,2176]{1,0:T(8,128)(2,1)S(1)}, u32[]{:S(2)}, u32[]{:S(2)}) collective-permute-start(bf16[64,2176]{1,0:T(8,128)(2,1)S(1)} %collective-permute-done.8.refs_0_), channel_id=1, source_target_pairs={{0,4},{4,8},{8,12},{12,14},{14,10},{10,6},{6,2},{2,0},{1,5},{5,9},... | collective-permute-start | bytes 835592 | tf_op jit(solution)/shard_map/ppermute | solution.py:447
  41.0 9.7 %collective-permute-start.13 = (bf16[64,2176]{1,0:T(8,128)(2,1)S(1)}, bf16[64,2176]{1,0:T(8,128)(2,1)S(1)}, u32[]{:S(2)}, u32[]{:S(2)}) collective-permute-start(bf16[64,2176]{1,0:T(8,128)(2,1)S(1)} %collective-permute-done.9.refs_3_), channel_id=1, source_target_pairs={{4,0},{8,4},{12,8},{14,12},{10,14},{6,10},{2,6},{0,2},{5,1},{9,5},... | collective-permute-start | bytes 835592 | tf_op jit(solution)/shard_map/ppermute | solution.py:447
  41.4 16.7 %collective-permute-start.15 = (bf16[2,256,1024]{2,1,0:T(8,128)(2,1)S(1)}, bf16[2,256,1024]{2,1,0:T(8,128)(2,1)S(1)}, u32[]{:S(2)}, u32[]{:S(2)}) collective-permute-start(bf16[2,256,1024]{2,1,0:T(8,128)(2,1)S(1)} %get-tuple-element.112.refs_8_), channel_id=1, source_target_pairs={{0,1},{1,0},{2,3},{3,2},{4,5},{5,4},{6,7},{7,6},{8,9},{9,8},{10,11... | collective-permute-start | bytes 3145736 | tf_op jit(solution)/shard_map/ppermute | solution.py:450
  44.5 13.6 %collective-permute-start.16 = (bf16[2,256,1024]{2,1,0:T(8,128)(2,1)S(1)}, bf16[2,256,1024]{2,1,0:T(8,128)(2,1)S(1)}, u32[]{:S(2)}, u32[]{:S(2)}) collective-permute-start(bf16[2,256,1024]{2,1,0:T(8,128)(2,1)S(1)} %get-tuple-element.113.refs_9_), channel_id=1, source_target_pairs={{0,1},{1,0},{2,3},{3,2},{4,5},{5,4},{6,7},{7,6},{8,9},{9,8},{10,11... | collective-permute-start | bytes 3145736 | tf_op jit(solution)/shard_map/ppermute | solution.py:450
  50.7 7.5 %collective-permute-start.17 = (bf16[2,256,1024]{2,1,0:T(8,128)(2,1)S(1)}, bf16[2,256,1024]{2,1,0:T(8,128)(2,1)S(1)}, u32[]{:S(2)}, u32[]{:S(2)}) collective-permute-start(bf16[2,256,1024]{2,1,0:T(8,128)(2,1)S(1)} %get-tuple-element.114.refs_10_), channel_id=1, source_target_pairs={{0,1},{1,0},{2,3},{3,2},{4,5},{5,4},{6,7},{7,6},{8,9},{9,8},{10,11... | collective-permute-start | bytes 3145736 | tf_op jit(solution)/shard_map/ppermute | solution.py:450
  50.8 7.3 %collective-permute-start.14 = (bf16[2,128,1024]{2,1,0:T(8,128)(2,1)S(1)}, bf16[2,128,1024]{2,1,0:T(8,128)(2,1)S(1)}, u32[]{:S(2)}, u32[]{:S(2)}) collective-permute-start(bf16[2,128,1024]{2,1,0:T(8,128)(2,1)S(1)} %get-tuple-element.111.refs_7_), channel_id=1, source_target_pairs={{0,1},{1,0},{2,3},{3,2},{4,5},{5,4},{6,7},{7,6},{8,9},{9,8},{10,11... | collective-permute-start | bytes 1572872 | tf_op jit(solution)/shard_map/ppermute | solution.py:450
  55.6 2.5 %collective-permute-start.18 = (bf16[2,128,1024]{2,1,0:T(8,128)(2,1)S(1)}, bf16[2,128,1024]{2,1,0:T(8,128)(2,1)S(1)}, u32[]{:S(2)}, u32[]{:S(2)}) collective-permute-start(bf16[2,128,1024]{2,1,0:T(8,128)(2,1)S(1)} %get-tuple-element.115.refs_11_), channel_id=1, source_target_pairs={{0,1},{1,0},{2,3},{3,2},{4,5},{5,4},{6,7},{7,6},{8,9},{9,8},{10,11... | collective-permute-start | bytes 1572872 | tf_op jit(solution)/shard_map/ppermute | solution.py:450
  58.2 8.6 %copy-start.6 = (bf16[1,1024,2048]{2,1,0:T(8,128)(2,1)S(1)}, bf16[1,1024,2048]{2,1,0:T(8,128)(2,1)}, u32[]{:S(2)}) copy-start(bf16[1,1024,2048]{2,1,0:T(8,128)(2,1)} %param.15) | copy-start | bytes 12582916
  66.8 4.9 %copy-start.8 = (bf16[64,2176]{1,0:T(8,128)(2,1)S(1)}, bf16[64,2176]{1,0:T(8,128)(2,1)}, u32[]{:S(2)}) copy-start(bf16[64,2176]{1,0:T(8,128)(2,1)} %get-tuple-element.70.top_ref.refs_0_) | copy-start | bytes 835588
  66.8 4.9 %copy-start.10 = (bf16[64,2176]{1,0:T(8,128)(2,1)S(1)}, bf16[64,2176]{1,0:T(8,128)(2,1)}, u32[]{:S(2)}) copy-start(bf16[64,2176]{1,0:T(8,128)(2,1)} %get-tuple-element.71.bottom_ref.refs_1_) | copy-start | bytes 835588
  68.9 22.0 %collective-permute-start.19 = (bf16[40,2048]{1,0:T(8,128)(2,1)S(1)}, bf16[40,2048]{1,0:T(8,128)(2,1)S(1)}, u32[]{:S(2)}, u32[]{:S(2)}) collective-permute-start(bf16[40,2048]{1,0:T(8,128)(2,1)S(1)} %get-tuple-element.125), channel_id=1, source_target_pairs={{0,8},{2,10},{4,12},{6,14},{8,0},{10,2},{12,4},{14,6},{1,9},{3,11}... | collective-permute-start | bytes 491528 | tf_op jit(solution)/shard_map/ppermute | solution.py:495
  69.4 24.8 %collective-permute-start.20 = (bf16[40,2048]{1,0:T(8,128)(2,1)S(1)}, bf16[40,2048]{1,0:T(8,128)(2,1)S(1)}, u32[]{:S(2)}, u32[]{:S(2)}) collective-permute-start(bf16[40,2048]{1,0:T(8,128)(2,1)S(1)} %get-tuple-element.126), channel_id=1, source_target_pairs={{0,10},{2,8},{4,14},{6,12},{8,2},{10,0},{12,6},{14,4},{1,11},{3,9}... | collective-permute-start | bytes 491528 | tf_op jit(solution)/shard_map/ppermute | solution.py:495
  71.8 27.1 %collective-permute-start.24 = (bf16[40,2048]{1,0:T(8,128)(2,1)S(1)}, bf16[40,2048]{1,0:T(8,128)(2,1)S(1)}, u32[]{:S(2)}, u32[]{:S(2)}) collective-permute-start(bf16[40,2048]{1,0:T(8,128)(2,1)S(1)} %get-tuple-element.133), channel_id=1, source_target_pairs={{0,12},{2,14},{4,8},{6,10},{8,4},{10,6},{12,0},{14,2},{1,13},{3,15... | collective-permute-start | bytes 491528 | tf_op jit(solution)/shard_map/ppermute | solution.py:495
  73.3 25.5 %collective-permute-start.25 = (bf16[40,2048]{1,0:T(8,128)(2,1)S(1)}, bf16[40,2048]{1,0:T(8,128)(2,1)S(1)}, u32[]{:S(2)}, u32[]{:S(2)}) collective-permute-start(bf16[40,2048]{1,0:T(8,128)(2,1)S(1)} %get-tuple-element.134), channel_id=1, source_target_pairs={{0,14},{2,12},{4,10},{6,8},{8,6},{10,4},{12,2},{14,0},{1,15},{3,13... | collective-permute-start | bytes 491528 | tf_op jit(solution)/shard_map/ppermute | solution.py:495
  94.2 6.2 %collective-permute-start.21 = (bf16[40,2048]{1,0:T(8,128)(2,1)S(1)}, bf16[40,2048]{1,0:T(8,128)(2,1)S(1)}, u32[]{:S(2)}, u32[]{:S(2)}) collective-permute-start(bf16[40,2048]{1,0:T(8,128)(2,1)S(1)} %get-tuple-element.128), channel_id=1, source_target_pairs={{0,2},{2,0},{4,6},{6,4},{8,10},{10,8},{12,14},{14,12},{1,3},{3,1},... | collective-permute-start | bytes 491528 | tf_op jit(solution)/shard_map/ppermute | solution.py:495
  95.9 6.8 %collective-permute-start.22 = (bf16[40,2048]{1,0:T(8,128)(2,1)S(1)}, bf16[40,2048]{1,0:T(8,128)(2,1)S(1)}, u32[]{:S(2)}, u32[]{:S(2)}) collective-permute-start(bf16[40,2048]{1,0:T(8,128)(2,1)S(1)} %get-tuple-element.129), channel_id=1, source_target_pairs={{0,4},{2,6},{4,0},{6,2},{8,12},{10,14},{12,8},{14,10},{1,5},{3,7},... | collective-permute-start | bytes 491528 | tf_op jit(solution)/shard_map/ppermute | solution.py:495
  95.9 8.4 %collective-permute-start.23 = (bf16[40,2048]{1,0:T(8,128)(2,1)S(1)}, bf16[40,2048]{1,0:T(8,128)(2,1)S(1)}, u32[]{:S(2)}, u32[]{:S(2)}) collective-permute-start(bf16[40,2048]{1,0:T(8,128)(2,1)S(1)} %get-tuple-element.130), channel_id=1, source_target_pairs={{0,6},{2,4},{4,2},{6,0},{8,14},{10,12},{12,10},{14,8},{1,7},{3,5},... | collective-permute-start | bytes 491528 | tf_op jit(solution)/shard_map/ppermute | solution.py:495

commit v7 on v6

--- a/solution.py
+++ b/solution.py
@@ -57,34 +57,40 @@
     count, width = tokens.shape
     half = jax.ShapeDtypeStruct((count // 2, width + LANES), jnp.bfloat16)
     return pl.pallas_call(
-        norm_kernel, out_shape=[half, half], name="norm_rows"
+        norm_kernel,
+        out_shape=[half, half],
+        compiler_params=pltpu.CompilerParams(vmem_limit_bytes=8 * MIB),
+        name="norm_rows",
     )(tokens, norm_gain.reshape(1, -1), routes.T)
+
+
+def column_parts(ref):
+    step = min(ref.shape[1], 256)
+    return [pl.ds(start, step) for start in range(0, ref.shape[1], step)]
+
+
+WHOLE = pl.BlockSpec(memory_space=pltpu.VMEM)
 
 
 def keys_kernel(count, *refs):
     blocks = refs[:count]
     weight_ref, panel_ref, mark_ref = refs[count:]
     rows = jnp.concatenate([block[:, : weight_ref.shape[0]] for block in blocks], axis=0)
-    product = jnp.dot(rows, weight_ref[...], preferred_element_type=jnp.float32)
-    panel_ref[0] = product.astype(jnp.bfloat16)
+    for cols in column_parts(weight_ref):
+        product = jnp.dot(rows, weight_ref[:, cols], preferred_element_type=jnp.float32)
+        panel_ref[:, cols] = product.astype(jnp.bfloat16)
     mark_ref[...] = product[:8, :LANES]
 
 
 def project_keys(blocks, key_weight):
     row_count = sum(block.shape[0] for block in blocks)
-    model_width, width = key_weight.shape
-    step = min(width, 256)
+    width = key_weight.shape[1]
     return pl.pallas_call(
         functools.partial(keys_kernel, len(blocks)),
-        grid=(width // step,),
-        in_specs=[pl.BlockSpec(block.shape, lambda n: (0, 0)) for block in blocks]
-        + [pl.BlockSpec((model_width, step), lambda n: (0, n))],
-        out_specs=[
-            pl.BlockSpec((1, row_count, step), lambda n: (0, 0, n)),
-            pl.BlockSpec((8, LANES), lambda n: (0, 0)),
-        ],
+        in_specs=[WHOLE] * (len(blocks) + 1),
+        out_specs=[WHOLE] * 2,
         out_shape=[
-            jax.ShapeDtypeStruct((2, row_count, width), jnp.bfloat16),
+            jax.ShapeDtypeStruct((row_count, width), jnp.bfloat16),
             jax.ShapeDtypeStruct((8, LANES), jnp.float32),
         ],
         compiler_params=pltpu.CompilerParams(vmem_limit_bytes=12 * MIB),
@@ -92,89 +98,74 @@
     )(*blocks, key_weight)
 
 
-def values_kernel(offsets, count, experts, mark_ref, half_panel_ref, *refs):
+def values_kernel(offsets, count, experts, mark_ref, keys_ref, *refs):
     blocks = refs[:count]
     value_ref, panel_ref, picked_ref, pos_ref = refs[count:]
     width = value_ref.shape[0]
     rows = jnp.concatenate([block[:, :width] for block in blocks], axis=0)
     tok_count = rows.shape[0] // len(offsets)
 
-    @pl.when(pl.program_id(0) == 0)
-    def _():
-        slots = jnp.concatenate([block[:, width:] for block in blocks], axis=0)
-        slots = slots.astype(jnp.float32)
-        expert = lax.axis_index("ctx") // (lax.axis_size("ctx") // experts)
-        lane = lax.broadcasted_iota(jnp.int32, slots.shape, 1)
-        slot = jnp.sum(jnp.where(lane == expert, slots, 0.0), axis=1, keepdims=True)
-        select = (slot == lane.astype(jnp.float32)).astype(jnp.float32)
-        number = lax.broadcasted_iota(jnp.int32, (tok_count, LANES), 0).astype(jnp.bfloat16)
-        for g, offset in enumerate(offsets):
-            part = slice(g * tok_count, (g + 1) * tok_count)
-            chosen = select[part].T[:SLOTS].astype(jnp.bfloat16)
-            picked_ref[g] = jnp.dot(
-                chosen, rows[part], preferred_element_type=jnp.float32
-            ).astype(jnp.bfloat16)
-            start = (ring_owner(offset) * lax.axis_size("exp") + lax.axis_index("exp")) * tok_count
-            pos_ref[g] = jnp.dot(
-                chosen, number, preferred_element_type=jnp.float32
-            ) + start.astype(jnp.float32)
-
-    panel_ref[0] = jnp.dot(
-        rows, value_ref[...], preferred_element_type=jnp.float32
-    ).astype(jnp.bfloat16)
-
-
-def project_values(blocks, offsets, mark, panel, value_weight):
+    slots = jnp.concatenate([block[:, width:] for block in blocks], axis=0)
+    slots = slots.astype(jnp.float32)
+    expert = lax.axis_index("ctx") // (lax.axis_size("ctx") // experts)
+    lane = lax.broadcasted_iota(jnp.int32, slots.shape, 1)
+    slot = jnp.sum(jnp.where(lane == expert, slots, 0.0), axis=1, keepdims=True)
+    select = (slot == lane.astype(jnp.float32)).astype(jnp.float32)
+    number = lax.broadcasted_iota(jnp.int32, (tok_count, LANES), 0).astype(jnp.bfloat16)
+    for g, offset in enumerate(offsets):
+        part = slice(g * tok_count, (g + 1) * tok_count)
+        chosen = select[part].T[:SLOTS].astype(jnp.bfloat16)
+        picked_ref[g] = jnp.dot(
+            chosen, rows[part], preferred_element_type=jnp.float32
+        ).astype(jnp.bfloat16)
+        start = (ring_owner(offset) * lax.axis_size("exp") + lax.axis_index("exp")) * tok_count
+        pos_ref[g] = jnp.dot(
+            chosen, number, preferred_element_type=jnp.float32
+        ) + start.astype(jnp.float32)
+    panel_ref[0] = keys_ref[...]
+    for cols in column_parts(value_ref):
+        panel_ref[1, :, cols] = jnp.dot(
+            rows, value_ref[:, cols], preferred_element_type=jnp.float32
+        ).astype(jnp.bfloat16)
+
+
+def project_values(blocks, offsets, mark, keys, value_weight):
     row_count = sum(block.shape[0] for block in blocks)
     model_width, width = value_weight.shape
-    step = min(width, 256)
     owners = len(offsets)
     return pl.pallas_call(
         functools.partial(values_kernel, offsets, len(blocks), EXPERTS),
-        grid=(width // step,),
-        in_specs=[
-            pl.BlockSpec(mark.shape, lambda n: (0, 0)),
-            pl.BlockSpec(memory_space=pl.ANY),
-        ]
-        + [pl.BlockSpec(block.shape, lambda n: (0, 0)) for block in blocks]
-        + [pl.BlockSpec((model_width, step), lambda n: (0, n))],
-        out_specs=[
-            pl.BlockSpec((1, row_count, step), lambda n: (1, 0, n)),
-            pl.BlockSpec((owners, SLOTS, model_width), lambda n: (0, 0, 0)),
-            pl.BlockSpec((owners, SLOTS, LANES), lambda n: (0, 0, 0)),
-        ],
+        in_specs=[WHOLE] * (len(blocks) + 3),
+        out_specs=[WHOLE] * 3,
         out_shape=[
             jax.ShapeDtypeStruct((2, row_count, width), jnp.bfloat16),
             jax.ShapeDtypeStruct((owners, SLOTS, model_width), jnp.bfloat16),
             jax.ShapeDtypeStruct((owners, SLOTS, LANES), jnp.float32),
         ],
-        input_output_aliases={1: 0},
         compiler_params=pltpu.CompilerParams(vmem_limit_bytes=12 * MIB),
         name="project_values",
-    )(mark, panel, *blocks, value_weight)
+    )(mark, keys, *blocks, value_weight)
 
 
 def queries_kernel(*refs):
     *picked, weight_ref, out_ref = refs
     rows = [ref[g] for ref in picked for g in range(ref.shape[0])]
-    product = jnp.dot(
-        jnp.concatenate(rows, axis=0), weight_ref[...], preferred_element_type=jnp.float32
-    )
-    for g in range(len(rows)):
-        out_ref[g] = product[g * SLOTS : (g + 1) * SLOTS].astype(jnp.bfloat16)
+    count = len(rows)
+    rows = jnp.concatenate(rows, axis=0)
+    for cols in column_parts(weight_ref):
+        product = jnp.dot(rows, weight_ref[:, cols], preferred_element_type=jnp.float32)
+        for g in range(count):
+            out_ref[g, :, cols] = product[g * SLOTS : (g + 1) * SLOTS].astype(jnp.bfloat16)
 
 
 def project_queries(picked, query_slab):
     model_width, width = query_slab.shape
-    step = min(width, 256)
     owners = sum(rows.shape[0] for rows in picked)
-    held = owners * SLOTS * (4 * model_width + 12 * step) * 2
+    held = 2 * model_width * width + owners * SLOTS * (4 * model_width + 4 * width)
     return pl.pallas_call(
         queries_kernel,
-        grid=(width // step,),
-        in_specs=[pl.BlockSpec(rows.shape, lambda n: (0, 0, 0)) for rows in picked]
-        + [pl.BlockSpec((model_width, step), lambda n: (0, n))],
-        out_specs=pl.BlockSpec((owners, SLOTS, step), lambda n: (0, 0, n)),
+        in_specs=[WHOLE] * (len(picked) + 1),
+        out_specs=WHOLE,
         out_shape=jax.ShapeDtypeStruct((owners, SLOTS, width), jnp.bfloat16),
         compiler_params=pltpu.CompilerParams(vmem_limit_bytes=held + 6 * MIB),
         name="project_queries",
@@ -185,7 +176,7 @@
     count = len(plan)
     query_refs, refs = refs[:query_count], refs[query_count:]
     pos_refs, own_refs, other_refs = (refs[k * count : (k + 1) * count] for k in range(3))
-    out_ref, places, queries, keys, values, scores, weights = refs[3 * count :]
+    out_ref, places, queries, panel, scores, weights, arrivals = refs[3 * count :]
     query_parts = [(ref, g) for ref in query_refs for g in range(ref.shape[0])]
     side = lax.axis_index("exp")
     exp_count = 2
@@ -197,25 +188,42 @@
     half_tiles = owners // 4
     group = min(half_tiles, 4)
 
-    @pl.when(pl.program_id(0) == 0)
+    step = heads * HS
+    steps = panel.shape[-1] // step
+    now = pl.program_id(0)
+
+    @pl.when(now == 0)
     def _():
+        for s in range(steps):
+            lanes = pl.ds(s * step, step)
+            for offsets, own_ref, other_ref in zip(plan, own_refs, other_refs):
+                for g, offset in enumerate(offsets):
+                    block = ring_owner(offset) * exp_count
+                    part = pl.ds(g * tok_count, tok_count)
+                    for ref, place in ((own_ref, block + side), (other_ref, block + 1 - side)):
+                        pltpu.make_async_copy(
+                            ref.at[:, part, lanes], panel.at[:, place, :, lanes], arrivals.at[s]
+                        ).start()
         for offsets, pos_ref in zip(plan, pos_refs):
             for g, offset in enumerate(offsets):
                 places[ring_owner(offset)] = pos_ref[g, :MOST]
 
-    for offsets, own_ref, other_ref in zip(plan, own_refs, other_refs):
-        for g, offset in enumerate(offsets):
-            owner = ring_owner(offset)
+    for offsets in plan:
+        for offset in offsets:
             query_ref, place = query_parts.pop(0)
-            part = pl.ds(g * tok_count, tok_count)
-            here, there = owner * exp_count + side, owner * exp_count + 1 - side
             for h in range(heads):
-                lanes = pl.ds(h * HS, HS)
-                queries[h, owner] = query_ref[place, :, lanes].astype(jnp.float32)[:MOST]
-                keys[h, here] = own_ref[0, part, lanes]
-                values[h, here] = own_ref[1, part, lanes]
-                keys[h, there] = other_ref[0, part, lanes]
-                values[h, there] = other_ref[1, part, lanes]
+                queries[h, ring_owner(offset)] = query_ref[
+                    place, :, pl.ds(h * HS, HS)
+                ].astype(jnp.float32)[:MOST]
+
+    first_lane = pl.multiple_of(now * step, step)
+    lanes_now = pl.ds(first_lane, step)
+    held_now = panel.at[:, :, :, lanes_now]
+    pltpu.make_async_copy(held_now, held_now, arrivals.at[now]).wait()
+
+    def panel_part(which, h, j):
+        lanes = pl.ds(pl.multiple_of(now * step + h * HS, HS), HS)
+        return panel[which, per_span * j : per_span * (j + 1), :, lanes].reshape(span, HS)
 
     def serve(lead, first):
         top = lead + group
@@ -223,7 +231,7 @@
             held = queries[h, 2 * lead : 2 * top].reshape(group * tile, HS).astype(jnp.bfloat16)
             for j in range(top):
                 skip = max(0, j - lead) * tile
-                key_part = keys[h, per_span * j : per_span * (j + 1)].reshape(span, HS)
+                key_part = panel_part(0, h, j)
                 scores[h, pl.ds(skip, group * tile - skip), pl.ds(j * span, span)] = (
                     lax.dot_general(
                         held[skip:],
@@ -257,7 +265,7 @@
             sums = [None] * group
             for j in range(top):
                 skip = max(0, j - lead)
-                value_part = values[h, per_span * j : per_span * (j + 1)].reshape(span, HS)
+                value_part = panel_part(1, h, j)
                 product = jnp.dot(
                     weights[h, pl.ds(skip * tile, (group - skip) * tile), pl.ds(j * span, span)],
                     value_part,
@@ -297,9 +305,9 @@
     group_rows = min(row_count // 2, 8 * MOST)
     query_specs = [pl.BlockSpec((q.shape[0], SLOTS, step), lambda h: (0, 0, h)) for q in queries]
     pos_specs = [pl.BlockSpec(p.shape, lambda h: (0, 0, 0)) for p in positions]
-    panel_specs = [pl.BlockSpec((2, p.shape[1], step), lambda h: (0, 0, h)) for p in own]
-    scratch = heads * (group_rows * length * 6 + length * HS * 4 + row_count * HS * 4)
-    windows = 2 * (length * step * 4 + row_count * step * 5) + 5 * row_count * LANES * 4
+    panel_specs = [pl.BlockSpec(memory_space=pl.ANY)] * len(own)
+    scratch = heads * (group_rows * length * 6 + row_count * HS * 4) + length * width * 4
+    windows = 2 * row_count * step * 5 + 5 * row_count * LANES * 4
     return pl.pallas_call(
         functools.partial(attend_kernel, plan, tok_count, heads, flip, len(queries)),
         grid=(width // step,),
@@ -309,12 +317,12 @@
         scratch_shapes=[
             pltpu.VMEM((owners, MOST, LANES), jnp.float32),
             pltpu.VMEM((heads, owners, MOST, HS), jnp.float32),
-            pltpu.VMEM((heads, 2 * owners, tok_count, HS), jnp.bfloat16),
-            pltpu.VMEM((heads, 2 * owners, tok_count, HS), jnp.bfloat16),
+            pltpu.VMEM((2, 2 * owners, tok_count, width), jnp.bfloat16),
             pltpu.VMEM((heads, group_rows, length), jnp.float32),
             pltpu.VMEM((heads, group_rows, length), jnp.bfloat16),
+            pltpu.SemaphoreType.DMA((width // step,)),
         ],
-        compiler_params=pltpu.CompilerParams(vmem_limit_bytes=scratch + windows * 5 // 4 + 4 * MIB),
+        compiler_params=pltpu.CompilerParams(vmem_limit_bytes=(scratch + windows) * 5 // 4 + 3 * MIB),
         name="attend",
     )(*queries, *positions, *own, *other)
 
@@ -406,7 +414,7 @@
 def combine(mix, pieces):
     tok_count = mix.shape[0] // 3
     model_width = pieces[0].shape[1]
-    step = 512
+    step = 1024
     return pl.pallas_call(
         combine_kernel,
         grid=(model_width // step,),
@@ -456,7 +464,7 @@
     lead = send([halves[0], halves[1]])
     rest = send([halves[1], halves[0]])
     for step in range(steps):
-        panel, mark = project_keys(blocks, key_weight)
+        keys, mark = project_keys(blocks, key_weight)
         following = [lead[0], rest[0], rest[1], lead[1]]
         if step == steps - 2:
             queries.append(project_queries(picked, query_slab))
@@ -466,7 +474,7 @@
             if queries:
                 queries = lead_next[-1:]
             lead = send(lead_next[:2])
-        panel, rows, position = project_values(blocks, plan[step], mark, panel, value_weight)
+        panel, rows, position = project_values(blocks, plan[step], mark, keys, value_weight)
         if step < steps - 2:
             position, *rest_next = tie(position, *rest)
             rest = send(rest_next)
@@ -479,8 +487,8 @@
     own[-1], last_one, last_two = tie(own[-1], *lead)
     other.append(hand_over(own[-1]))
     blocks = [last_one, last_two]
-    panel, mark = project_keys(blocks, key_weight)
-    panel, rows, position = project_values(blocks, plan[-1], mark, panel, value_weight)
+    keys, mark = project_keys(blocks, key_weight)
+    panel, rows, position = project_values(blocks, plan[-1], mark, keys, value_weight)
     own.append(panel)
     other.append(hand_over(panel))
     positions.append(position)
@@ -494,11 +502,14 @@
     def swap(piece, k):
         return lax.ppermute(piece, "ctx", [(c, c ^ k) for c in range(ctx_count)])
 
-    far = [swap(piece, half + r) for r, piece in enumerate(far)]
+    first_lot = [swap(far[r], half + r) for r in range(half // 2)]
     attended = attend(False, plan, queries, positions, own, other)
     near = project_output(attended, output_slab)
-    tied = tie(*near, *far[: half // 2])
-    near, far = tied[:half], list(tied[half:]) + far[half // 2 :]
+    tied = tie(*near, *first_lot, *far[half // 2 :])
+    near, first_lot, second_lot = (
+        tied[:half], tied[half : half + half // 2], tied[half + half // 2 :]
+    )
+    far = list(first_lot) + [swap(p, half + half // 2 + r) for r, p in enumerate(second_lot)]
     near = [near[0]] + [swap(near[r], r) for r in range(1, half)]
 
     normed = jnp.concatenate([part[:, :model_width] for part in halves], axis=0)

time: 107 us -> 102 us (0.953)
  Pallas kernels: 53.9 us -> 34.4 us
  waiting for transfers between devices: 17.7 us -> 31.7 us
    pallas_call x8, Pallas kernels: 17.6 us -> 7.51 us  [the longest x5 5.28 us: project_keys(): pl.pallas_call(functools.partial(keys_kernel, len(blocks)), in_specs=[WHO...]
    ppermute x7, waiting for transfers between devices: 3.28 us -> 12.3 us  [send(): lax.ppermute(parts[1], 'ctx', backward)]
    pallas_call x5, Pallas kernels: 14.1 us -> 6.84 us  [project_values(): pl.pallas_call(functools.partial(values_kernel, offsets, len(blocks), EXP...]
    ppermute x7, waiting for transfers between devices: 0.02 us -> 3.31 us  [send(): lax.ppermute(parts[0], 'ctx', forward)]
    pallas_call x2, Pallas kernels: 15 us -> 13.4 us  [attend(): pl.pallas_call(functools.partial(attend_kernel, plan, tok_count, heads, f...]
    unnamed x22 -> x20, local copies, waits for them, and re-layouts: 6.32 us -> 6.84 us
  transfers between devices with their start and end apart: 26 -> 26, of which waited for: 8 -> 17; matrix products, arithmetic and copies ran while one was open for 1% -> 1% of each run, Pallas kernels for 36% -> 22%
where the time goes in v7:
time: 102 us; the launch traced here: 101 us
  Pallas kernels  34.4 us (34%)
  waiting for transfers between devices  31.7 us (31%)
  starting transfers between devices  27.5 us (27%)
  local copies, waits for them, and re-layouts  6.89 us (7%)
    ppermute x7, waiting for transfers between devices, swap(): return lax.ppermute(piece, 'ctx', [(c, c ^ k) for c in range(ctx_count)])  15.4 us
    pallas_call x2, Pallas kernels, attend(): pl.pallas_call(functools.partial(attend_kernel, plan, tok_count, heads, f...  13.4 us
    ppermute x7, waiting for transfers between devices, send(): lax.ppermute(parts[1], 'ctx', backward)  12.3 us
    ppermute x7, starting transfers between devices, swap(): return lax.ppermute(piece, 'ctx', [(c, c ^ k) for c in range(ctx_count)])  11.2 us
    ppermute x7, starting transfers between devices, send(): lax.ppermute(parts[0], 'ctx', forward)  11.1 us
    unnamed x20, local copies, waits for them, and re-layouts  6.84 us
    pallas_call x5, Pallas kernels, project_values(): pl.pallas_call(functools.partial(values_kernel, offsets, len(blocks), EXP...  6.84 us
    pallas_call x5, Pallas kernels, project_keys(): pl.pallas_call(functools.partial(keys_kernel, len(blocks)), in_specs=[WHO...  5.28 us
  transfers between devices with their start and end apart: 26, of which 17 were waited for; matrix products, arithmetic and copies ran while one was open for 1% of the time, Pallas kernels for 22%

profile of v7, /device:TPU:0, one launch (start us, length us, event | category | flops | bytes accessed | tf_op | source)
XLA Modules:
  0.0 101.3 jit_solution(6459957598159901755)
XLA Ops:
  0.0 1.1 %copy-done.7 = bf16[128,2048]{1,0:T(8,128)(2,1)S(1)} copy-done((bf16[128,2048]{1,0:T(8,128)(2,1)S(1)}, bf16[128,2048]{1,0:T(8,128)(2,1)}, u32[]{:S(2)}) %copy-start.7) | copy-done | bytes 524312
  1.1 0.7 copy-done.8
  1.8 0.7 copy-done.9
  2.5 0.3 norm_rows.1
  2.7 3.1 %collective-permute-start = (bf16[64,2176]{1,0:T(8,128)(2,1)S(1)}, bf16[64,2176]{1,0:T(8,128)(2,1)S(1)}, u32[]{:S(2)}, u32[]{:S(2)}) collective-permute-start(bf16[64,2176]{1,0:T(8,128)(2,1)S(1)} %get-tuple-element.72.top_ref.refs_0_), channel_id=1, source_target_pairs={{0,4},{4,8},{8,12},{12,14},{14,10},{10,6},{6,2},{2,0},{1,5},{5,9},... | collective-permute-start | bytes 835592 | tf_op jit(solution)/shard_map/ppermute | solution.py:455
  5.8 2.0 %collective-permute-start.4 = (bf16[64,2176]{1,0:T(8,128)(2,1)S(1)}, bf16[64,2176]{1,0:T(8,128)(2,1)S(1)}, u32[]{:S(2)}, u32[]{:S(2)}) collective-permute-start(bf16[64,2176]{1,0:T(8,128)(2,1)S(1)} %get-tuple-element.72.top_ref.refs_0_), channel_id=1, source_target_pairs={{4,0},{8,4},{12,8},{14,12},{10,14},{6,10},{2,6},{0,2},{5,1},{9,5},... | collective-permute-start | bytes 835592 | tf_op jit(solution)/shard_map/ppermute | solution.py:455
  7.8 0.1 collective-permute-start.3
  7.9 2.2 %copy-done.1 = bf16[2048,1024]{1,0:T(8,128)(2,1)S(1)} copy-done((bf16[2048,1024]{1,0:T(8,128)(2,1)S(1)}, bf16[2048,1024]{1,0:T(8,128)(2,1)}, u32[]{:S(2)}) %copy-start.1) | copy-done | bytes 4194328
  10.0 0.7 project_keys.5
  10.8 2.4 %collective-permute-done.refs_0_ = bf16[64,2176]{1,0:T(8,128)(2,1)S(1)} collective-permute-done((bf16[64,2176]{1,0:T(8,128)(2,1)S(1)}, bf16[64,2176]{1,0:T(8,128)(2,1)S(1)}, u32[]{:S(2)}, u32[]{:S(2)}) %collective-permute-start) | collective-permute-done | bytes 278560 | tf_op jit(solution)/shard_map/ppermute | solution.py:455
  13.2 2.2 %collective-permute-done.1.refs_3_ = bf16[64,2176]{1,0:T(8,128)(2,1)S(1)} collective-permute-done((bf16[64,2176]{1,0:T(8,128)(2,1)S(1)}, bf16[64,2176]{1,0:T(8,128)(2,1)S(1)}, u32[]{:S(2)}, u32[]{:S(2)}) %collective-permute-start.1) | collective-permute-done | bytes 278560 | tf_op jit(solution)/shard_map/ppermute | solution.py:455
  15.4 1.6 %collective-permute-start.2 = (bf16[64,2176]{1,0:T(8,128)(2,1)S(1)}, bf16[64,2176]{1,0:T(8,128)(2,1)S(1)}, u32[]{:S(2)}, u32[]{:S(2)}) collective-permute-start(bf16[64,2176]{1,0:T(8,128)(2,1)S(1)} %collective-permute-done.refs_0_), channel_id=1, source_target_pairs={{0,4},{4,8},{8,12},{12,14},{14,10},{10,6},{6,2},{2,0},{1,5},{5,9},... | collective-permute-start | bytes 835592 | tf_op jit(solution)/shard_map/ppermute | solution.py:455
  17.0 0.4 collective-permute-start.7
  17.4 2.2 %copy-done.3 = bf16[2048,1024]{1,0:T(8,128)(2,1)S(1)} copy-done((bf16[2048,1024]{1,0:T(8,128)(2,1)S(1)}, bf16[2048,1024]{1,0:T(8,128)(2,1)}, u32[]{:S(2)}) %copy-start.3) | copy-done | bytes 4194328
  19.6 1.0 project_values.5
  20.6 0.7 collective-permute-done.4.refs_2_
  21.3 1.6 %collective-permute-start.5 = (bf16[64,2176]{1,0:T(8,128)(2,1)S(1)}, bf16[64,2176]{1,0:T(8,128)(2,1)S(1)}, u32[]{:S(2)}, u32[]{:S(2)}) collective-permute-start(bf16[64,2176]{1,0:T(8,128)(2,1)S(1)} %collective-permute-done.3.refs_1_), channel_id=1, source_target_pairs={{0,4},{4,8},{8,12},{12,14},{14,10},{10,6},{6,2},{2,0},{1,5},{5,9},... | collective-permute-start | bytes 835592 | tf_op jit(solution)/shard_map/ppermute | solution.py:455
  22.9 0.4 collective-permute-start.6
  23.4 1.3 %project_keys.7 = (bf16[256,1024]{1,0:T(8,128)(2,1)S(1)}, f32[8,128]{1,0:T(8,128)S(1)}) custom-call(bf16[64,2176]{1,0:T(8,128)(2,1)S(1)} %collective-permute-done.refs_0_, bf16[64,2176]{1,0:T(8,128)(2,1)S(1)} %collective-permute-done.3.refs_1_, bf16[64,2176]{1,0:T(8,128)(2,1)S(1)} %collective-permute-done.4.refs_2_, ...), custom_call_target="tpu_custom_call" | custom-call | tf_op jit(solution)/shard_map/project_keys/pallas_call | solution.py:88
  24.7 0.5 collective-permute-done.2.refs_0_
  25.2 2.2 %collective-permute-done.7.refs_3_ = bf16[64,2176]{1,0:T(8,128)(2,1)S(1)} collective-permute-done((bf16[64,2176]{1,0:T(8,128)(2,1)S(1)}, bf16[64,2176]{1,0:T(8,128)(2,1)S(1)}, u32[]{:S(2)}, u32[]{:S(2)}) %collective-permute-start.7) | collective-permute-done | bytes 278560 | tf_op jit(solution)/shard_map/ppermute | solution.py:455
  27.3 1.6 %collective-permute-start.8 = (bf16[64,2176]{1,0:T(8,128)(2,1)S(1)}, bf16[64,2176]{1,0:T(8,128)(2,1)S(1)}, u32[]{:S(2)}, u32[]{:S(2)}) collective-permute-start(bf16[64,2176]{1,0:T(8,128)(2,1)S(1)} %collective-permute-done.2.refs_0_), channel_id=1, source_target_pairs={{0,4},{4,8},{8,12},{12,14},{14,10},{10,6},{6,2},{2,0},{1,5},{5,9},... | collective-permute-start | bytes 835592 | tf_op jit(solution)/shard_map/ppermute | solution.py:455
  28.9 0.4 collective-permute-start.9
  29.3 1.6 %project_values.6 = (bf16[2,256,1024]{2,1,0:T(8,128)(2,1)S(1)}, bf16[2,48,2048]{2,1,0:T(8,128)(2,1)S(1)}, f32[2,48,128]{2,1,0:T(8,128)S(1)}) custom-call(f32[8,128]{1,0:T(8,128)S(1)} %get-tuple-element.87.mark_ref, bf16[256,1024]{1,0:T(8,128)(2,1)S(1)} %get-tuple-element.88.keys_ref, bf16[64,2176]{1,0:T(8,128)(2,1)S(1)} %collective-permute-done.refs_0_, ...), custom_call_target="tpu_custom_call" | custom-call | tf_op jit(solution)/shard_map/project_values/pallas_call | solution.py:136
  31.0 0.2 collective-permute-done.5.refs_1_
  31.1 2.2 %collective-permute-done.6.refs_2_ = bf16[64,2176]{1,0:T(8,128)(2,1)S(1)} collective-permute-done((bf16[64,2176]{1,0:T(8,128)(2,1)S(1)}, bf16[64,2176]{1,0:T(8,128)(2,1)S(1)}, u32[]{:S(2)}, u32[]{:S(2)}) %collective-permute-start.6) | collective-permute-done | bytes 278560 | tf_op jit(solution)/shard_map/ppermute | solution.py:455
  33.3 1.6 %collective-permute-start.10 = (bf16[64,2176]{1,0:T(8,128)(2,1)S(1)}, bf16[64,2176]{1,0:T(8,128)(2,1)S(1)}, u32[]{:S(2)}, u32[]{:S(2)}) collective-permute-start(bf16[64,2176]{1,0:T(8,128)(2,1)S(1)} %collective-permute-done.5.refs_1_), channel_id=1, source_target_pairs={{0,4},{4,8},{8,12},{12,14},{14,10},{10,6},{6,2},{2,0},{1,5},{5,9},... | collective-permute-start | bytes 835592 | tf_op jit(solution)/shard_map/ppermute | solution.py:455
  34.9 0.4 collective-permute-start.11
  35.3 0.8 project_queries.2.refs_0_
  36.1 1.3 %project_keys.6 = (bf16[256,1024]{1,0:T(8,128)(2,1)S(1)}, f32[8,128]{1,0:T(8,128)S(1)}) custom-call(bf16[64,2176]{1,0:T(8,128)(2,1)S(1)} %collective-permute-done.2.refs_0_, bf16[64,2176]{1,0:T(8,128)(2,1)S(1)} %collective-permute-done.5.refs_1_, bf16[64,2176]{1,0:T(8,128)(2,1)S(1)} %collective-permute-done.6.refs_2_, ...), custom_call_target="tpu_custom_call" | custom-call | tf_op jit(solution)/shard_map/project_keys/pallas_call | solution.py:88
  37.4 1.8 %collective-permute-done.9.refs_3_ = bf16[64,2176]{1,0:T(8,128)(2,1)S(1)} collective-permute-done((bf16[64,2176]{1,0:T(8,128)(2,1)S(1)}, bf16[64,2176]{1,0:T(8,128)(2,1)S(1)}, u32[]{:S(2)}, u32[]{:S(2)}) %collective-permute-start.9) | collective-permute-done | bytes 278560 | tf_op jit(solution)/shard_map/ppermute | solution.py:455
  39.2 1.6 %collective-permute-start.12 = (bf16[64,2176]{1,0:T(8,128)(2,1)S(1)}, bf16[64,2176]{1,0:T(8,128)(2,1)S(1)}, u32[]{:S(2)}, u32[]{:S(2)}) collective-permute-start(bf16[64,2176]{1,0:T(8,128)(2,1)S(1)} %collective-permute-done.8.refs_0_), channel_id=1, source_target_pairs={{0,4},{4,8},{8,12},{12,14},{14,10},{10,6},{6,2},{2,0},{1,5},{5,9},... | collective-permute-start | bytes 835592 | tf_op jit(solution)/shard_map/ppermute | solution.py:455
  40.8 0.4 collective-permute-start.13
  41.3 1.6 %project_values.7 = (bf16[2,256,1024]{2,1,0:T(8,128)(2,1)S(1)}, bf16[2,48,2048]{2,1,0:T(8,128)(2,1)S(1)}, f32[2,48,128]{2,1,0:T(8,128)S(1)}) custom-call(f32[8,128]{1,0:T(8,128)S(1)} %get-tuple-element.91.mark_ref, bf16[256,1024]{1,0:T(8,128)(2,1)S(1)} %get-tuple-element.92.keys_ref, bf16[64,2176]{1,0:T(8,128)(2,1)S(1)} %collective-permute-done.2.refs_0_, ...), custom_call_target="tpu_custom_call" | custom-call | tf_op jit(solution)/shard_map/project_values/pallas_call | solution.py:136
  42.9 0.1 collective-permute-done.10.refs_1_
  43.1 0.4 collective-permute-start.16
  43.5 1.7 %collective-permute-done.11.refs_2_ = bf16[64,2176]{1,0:T(8,128)(2,1)S(1)} collective-permute-done((bf16[64,2176]{1,0:T(8,128)(2,1)S(1)}, bf16[64,2176]{1,0:T(8,128)(2,1)S(1)}, u32[]{:S(2)}, u32[]{:S(2)}) %collective-permute-start.11) | collective-permute-done | bytes 278560 | tf_op jit(solution)/shard_map/ppermute | solution.py:455
  45.2 1.3 %project_keys.8 = (bf16[256,1024]{1,0:T(8,128)(2,1)S(1)}, f32[8,128]{1,0:T(8,128)S(1)}) custom-call(bf16[64,2176]{1,0:T(8,128)(2,1)S(1)} %collective-permute-done.8.refs_0_, bf16[64,2176]{1,0:T(8,128)(2,1)S(1)} %collective-permute-done.10.refs_1_, bf16[64,2176]{1,0:T(8,128)(2,1)S(1)} %collective-permute-done.11.refs_2_, ...), custom_call_target="tpu_custom_call" | custom-call | tf_op jit(solution)/shard_map/project_keys/pallas_call | solution.py:88
  46.5 1.6 %project_values.8 = (bf16[2,256,1024]{2,1,0:T(8,128)(2,1)S(1)}, bf16[2,48,2048]{2,1,0:T(8,128)(2,1)S(1)}, f32[2,48,128]{2,1,0:T(8,128)S(1)}) custom-call(f32[8,128]{1,0:T(8,128)S(1)} %get-tuple-element.97.mark_ref, bf16[256,1024]{1,0:T(8,128)(2,1)S(1)} %get-tuple-element.98.keys_ref, bf16[64,2176]{1,0:T(8,128)(2,1)S(1)} %collective-permute-done.8.refs_0_, ...), custom_call_target="tpu_custom_call" | custom-call | tf_op jit(solution)/shard_map/project_values/pallas_call | solution.py:136
  48.2 1.5 %collective-permute-done.13.refs_1_ = bf16[64,2176]{1,0:T(8,128)(2,1)S(1)} collective-permute-done((bf16[64,2176]{1,0:T(8,128)(2,1)S(1)}, bf16[64,2176]{1,0:T(8,128)(2,1)S(1)}, u32[]{:S(2)}, u32[]{:S(2)}) %collective-permute-start.13) | collective-permute-done | bytes 278560 | tf_op jit(solution)/shard_map/ppermute | solution.py:455
  49.7 0.5 collective-permute-start.14
  50.2 0.7 project_keys.9
  51.0 1.0 project_values.9
  51.9 0.1 collective-permute-start.18
  52.0 1.2 %project_queries.3.refs_1_ = bf16[5,48,1024]{2,1,0:T(8,128)(2,1)S(1)} custom-call(bf16[2,48,2048]{2,1,0:T(8,128)(2,1)S(1)} %get-tuple-element.93.refs_0_, bf16[2,48,2048]{2,1,0:T(8,128)(2,1)S(1)} %get-tuple-element.99.refs_1_, bf16[1,48,2048]{2,1,0:T(8,128)(2,1)S(1)} %get-tuple-element.107.refs_2_, bf16[2048,1024]{1,0:T(8,128)(2,1)S(1)} %bitcast.6), custom_call_target="tpu_custom_call" | custom-call | tf_op jit(solution)/shard_map/project_queries/pallas_call | solution.py:165
  53.2 0.7 collective-permute-done.18.refs_16_
  53.9 8.1 %attend.2.attended_ref = bf16[4,48,1024]{2,1,0:T(8,128)(2,1)S(1)} custom-call(bf16[3,48,1024]{2,1,0:T(8,128)(2,1)S(1)} %project_queries.2.refs_0_, bf16[5,48,1024]{2,1,0:T(8,128)(2,1)S(1)} %project_queries.3.refs_1_, f32[1,48,128]{2,1,0:T(8,128)S(1)} %get-tuple-element.122.refs_2_, f32[2,48,128]{2,1,0:T(8,128)S(1)} %get-tuple-element.109.refs_3_, ...), custom_call_target="tpu_custom_call" | custom-call | tf_op jit(solution)/shard_map/attend/pallas_call | solution.py:311
  62.0 2.1 %project_output.2 = (bf16[40,2048]{1,0:T(8,128)(2,1)S(1)}, bf16[40,2048]{1,0:T(8,128)(2,1)S(1)}, bf16[40,2048]{1,0:T(8,128)(2,1)S(1)}, bf16[40,2048]{1,0:T(8,128)(2,1)S(1)}) custom-call(bf16[4,48,1024]{2,1,0:T(8,128)(2,1)S(1)} %attend.2.attended_ref, bf16[1024,2048]{1,0:T(8,128)(2,1)S(1)} %bitcast.7), custom_call_target="tpu_custom_call" | custom-call | tf_op jit(solution)/shard_map/project_output/pallas_call | solution.py:346
  64.1 0.1 collective-permute-start.19
  64.2 2.6 %collective-permute-start.20 = (bf16[40,2048]{1,0:T(8,128)(2,1)S(1)}, bf16[40,2048]{1,0:T(8,128)(2,1)S(1)}, u32[]{:S(2)}, u32[]{:S(2)}) collective-permute-start(bf16[40,2048]{1,0:T(8,128)(2,1)S(1)} %get-tuple-element.128), channel_id=1, source_target_pairs={{0,10},{2,8},{4,14},{6,12},{8,2},{10,0},{12,6},{14,4},{1,11},{3,9}... | collective-permute-start | bytes 491528 | tf_op jit(solution)/shard_map/ppermute | solution.py:503
  66.8 5.3 %attend.3.attended_ref = bf16[4,48,1024]{2,1,0:T(8,128)(2,1)S(1)} custom-call(bf16[3,48,1024]{2,1,0:T(8,128)(2,1)S(1)} %project_queries.2.refs_0_, bf16[5,48,1024]{2,1,0:T(8,128)(2,1)S(1)} %project_queries.3.refs_1_, f32[1,48,128]{2,1,0:T(8,128)S(1)} %get-tuple-element.122.refs_2_, f32[2,48,128]{2,1,0:T(8,128)S(1)} %get-tuple-element.109.refs_3_, ...), custom_call_target="tpu_custom_call" | custom-call | tf_op jit(solution)/shard_map/attend/pallas_call | solution.py:311
  72.2 2.1 %project_output.3 = (bf16[40,2048]{1,0:T(8,128)(2,1)S(1)}, bf16[40,2048]{1,0:T(8,128)(2,1)S(1)}, bf16[40,2048]{1,0:T(8,128)(2,1)S(1)}, bf16[40,2048]{1,0:T(8,128)(2,1)S(1)}) custom-call(bf16[4,48,1024]{2,1,0:T(8,128)(2,1)S(1)} %attend.3.attended_ref, bf16[1024,2048]{1,0:T(8,128)(2,1)S(1)} %bitcast.8), custom_call_target="tpu_custom_call" | custom-call | tf_op jit(solution)/shard_map/project_output/pallas_call | solution.py:346
  74.2 4.9 %collective-permute-done.19.refs_4_ = bf16[40,2048]{1,0:T(8,128)(2,1)S(1)} collective-permute-done((bf16[40,2048]{1,0:T(8,128)(2,1)S(1)}, bf16[40,2048]{1,0:T(8,128)(2,1)S(1)}, u32[]{:S(2)}, u32[]{:S(2)}) %collective-permute-start.19) | collective-permute-done | bytes 163872 | tf_op jit(solution)/shard_map/ppermute | solution.py:503
  79.1 2.4 %collective-permute-done.20.refs_5_ = bf16[40,2048]{1,0:T(8,128)(2,1)S(1)} collective-permute-done((bf16[40,2048]{1,0:T(8,128)(2,1)S(1)}, bf16[40,2048]{1,0:T(8,128)(2,1)S(1)}, u32[]{:S(2)}, u32[]{:S(2)}) %collective-permute-start.20) | collective-permute-done | bytes 163872 | tf_op jit(solution)/shard_map/ppermute | solution.py:503
  81.5 1.7 %collective-permute-start.21 = (bf16[40,2048]{1,0:T(8,128)(2,1)S(1)}, bf16[40,2048]{1,0:T(8,128)(2,1)S(1)}, u32[]{:S(2)}, u32[]{:S(2)}) collective-permute-start(bf16[40,2048]{1,0:T(8,128)(2,1)S(1)} %get-tuple-element.132), channel_id=1, source_target_pairs={{0,2},{2,0},{4,6},{6,4},{8,10},{10,8},{12,14},{14,12},{1,3},{3,1},... | collective-permute-start | bytes 491528 | tf_op jit(solution)/shard_map/ppermute | solution.py:503
  83.3 1.7 %collective-permute-start.23 = (bf16[40,2048]{1,0:T(8,128)(2,1)S(1)}, bf16[40,2048]{1,0:T(8,128)(2,1)S(1)}, u32[]{:S(2)}, u32[]{:S(2)}) collective-permute-start(bf16[40,2048]{1,0:T(8,128)(2,1)S(1)} %get-tuple-element.134), channel_id=1, source_target_pairs={{0,6},{2,4},{4,2},{6,0},{8,14},{10,12},{12,10},{14,8},{1,7},{3,5},... | collective-permute-start | bytes 491528 | tf_op jit(solution)/shard_map/ppermute | solution.py:503
  85.0 1.2 %collective-permute-start.24 = (bf16[40,2048]{1,0:T(8,128)(2,1)S(1)}, bf16[40,2048]{1,0:T(8,128)(2,1)S(1)}, u32[]{:S(2)}, u32[]{:S(2)}) collective-permute-start(bf16[40,2048]{1,0:T(8,128)(2,1)S(1)} %get-tuple-element.137), channel_id=1, source_target_pairs={{0,12},{2,14},{4,8},{6,10},{8,4},{10,6},{12,0},{14,2},{1,13},{3,15... | collective-permute-start | bytes 491528 | tf_op jit(solution)/shard_map/ppermute | solution.py:503
  86.2 3.8 %collective-permute-start.25 = (bf16[40,2048]{1,0:T(8,128)(2,1)S(1)}, bf16[40,2048]{1,0:T(8,128)(2,1)S(1)}, u32[]{:S(2)}, u32[]{:S(2)}) collective-permute-start(bf16[40,2048]{1,0:T(8,128)(2,1)S(1)} %get-tuple-element.138), channel_id=1, source_target_pairs={{0,14},{2,12},{4,10},{6,8},{8,6},{10,4},{12,2},{14,0},{1,15},{3,13... | collective-permute-start | bytes 491528 | tf_op jit(solution)/shard_map/ppermute | solution.py:503
  90.0 0.5 fusion
  90.6 0.5 gate_mix.1.mix_ref
  91.2 0.8 collective-permute-done.23.refs_3_
  92.0 5.0 %collective-permute-done.24.refs_6_ = bf16[40,2048]{1,0:T(8,128)(2,1)S(1)} collective-permute-done((bf16[40,2048]{1,0:T(8,128)(2,1)S(1)}, bf16[40,2048]{1,0:T(8,128)(2,1)S(1)}, u32[]{:S(2)}, u32[]{:S(2)}) %collective-permute-start.24) | collective-permute-done | bytes 163872 | tf_op jit(solution)/shard_map/ppermute | solution.py:503
  97.0 2.3 %collective-permute-done.25.refs_7_ = bf16[40,2048]{1,0:T(8,128)(2,1)S(1)} collective-permute-done((bf16[40,2048]{1,0:T(8,128)(2,1)S(1)}, bf16[40,2048]{1,0:T(8,128)(2,1)S(1)}, u32[]{:S(2)}, u32[]{:S(2)}) %collective-permute-start.25) | collective-permute-done | bytes 163872 | tf_op jit(solution)/shard_map/ppermute | solution.py:503
  99.2 2.0 %combine.1 = bf16[128,2048]{1,0:T(8,128)(2,1)} custom-call(bf16[384,384]{1,0:T(8,128)(2,1)S(1)} %gate_mix.1.mix_ref, bf16[40,2048]{1,0:T(8,128)(2,1)S(1)} %get-tuple-element.131.refs_0_, bf16[40,2048]{1,0:T(8,128)(2,1)S(1)} %collective-permute-done.21.refs_1_, bf16[40,2048]{1,0:T(8,128)(2,1)S(1)} %collective-permute-done.22.refs_2_, ...), custom_call_target="tpu_custom_call" | custom-call | tf_op jit(solution)/shard_map/combine/pallas_call | solution.py:418
  (31 shorter events, 0.2 us)
Async XLA Ops:
  0.0 90.0 %copy-start = (f32[2048,8]{0,1:T(8,128)S(1)}, f32[2048,8]{0,1:T(8,128)}, u32[]{:S(2)}) copy-start(f32[2048,8]{0,1:T(8,128)} %param.10) | copy-start | bytes 196612
  0.0 1.1 %copy-start.7 = (bf16[128,2048]{1,0:T(8,128)(2,1)S(1)}, bf16[128,2048]{1,0:T(8,128)(2,1)}, u32[]{:S(2)}) copy-start(bf16[128,2048]{1,0:T(8,128)(2,1)} %tokens_ref.1) | copy-start | bytes 1572868
  1.1 0.7 copy-start.8
  1.8 0.7 copy-start.9
  2.7 10.5 %collective-permute-start = (bf16[64,2176]{1,0:T(8,128)(2,1)S(1)}, bf16[64,2176]{1,0:T(8,128)(2,1)S(1)}, u32[]{:S(2)}, u32[]{:S(2)}) collective-permute-start(bf16[64,2176]{1,0:T(8,128)(2,1)S(1)} %get-tuple-element.72.top_ref.refs_0_), channel_id=1, source_target_pairs={{0,4},{4,8},{8,12},{12,14},{14,10},{10,6},{6,2},{2,0},{1,5},{5,9},... | collective-permute-start | bytes 835592 | tf_op jit(solution)/shard_map/ppermute | solution.py:455
  5.8 9.6 %collective-permute-start.1 = (bf16[64,2176]{1,0:T(8,128)(2,1)S(1)}, bf16[64,2176]{1,0:T(8,128)(2,1)S(1)}, u32[]{:S(2)}, u32[]{:S(2)}) collective-permute-start(bf16[64,2176]{1,0:T(8,128)(2,1)S(1)} %get-tuple-element.73.bottom_ref.refs_1_), channel_id=1, source_target_pairs={{4,0},{8,4},{12,8},{14,12},{10,14},{6,10},{2,6},{0,2},{5,1},{9,5},... | collective-permute-start | bytes 835592 | tf_op jit(solution)/shard_map/ppermute | solution.py:455
  5.8 15.5 %collective-permute-start.4 = (bf16[64,2176]{1,0:T(8,128)(2,1)S(1)}, bf16[64,2176]{1,0:T(8,128)(2,1)S(1)}, u32[]{:S(2)}, u32[]{:S(2)}) collective-permute-start(bf16[64,2176]{1,0:T(8,128)(2,1)S(1)} %get-tuple-element.72.top_ref.refs_0_), channel_id=1, source_target_pairs={{4,0},{8,4},{12,8},{14,12},{10,14},{6,10},{2,6},{0,2},{5,1},{9,5},... | collective-permute-start | bytes 835592 | tf_op jit(solution)/shard_map/ppermute | solution.py:455
  7.8 13.6 %collective-permute-start.3 = (bf16[64,2176]{1,0:T(8,128)(2,1)S(1)}, bf16[64,2176]{1,0:T(8,128)(2,1)S(1)}, u32[]{:S(2)}, u32[]{:S(2)}) collective-permute-start(bf16[64,2176]{1,0:T(8,128)(2,1)S(1)} %get-tuple-element.73.bottom_ref.refs_1_), channel_id=1, source_target_pairs={{0,4},{4,8},{8,12},{12,14},{14,10},{10,6},{6,2},{2,0},{1,5},{5,9},... | collective-permute-start | bytes 835592 | tf_op jit(solution)/shard_map/ppermute | solution.py:455
  7.9 2.2 %copy-start.1 = (bf16[2048,1024]{1,0:T(8,128)(2,1)S(1)}, bf16[2048,1024]{1,0:T(8,128)(2,1)}, u32[]{:S(2)}) copy-start(bf16[2048,1024]{1,0:T(8,128)(2,1)} %refs_2_.6) | copy-start | bytes 12582916
  10.0 13.3 %copy-start.2 = (bf16[2048,1024]{1,0:T(8,128)(2,1)S(1)}, bf16[2048,1024]{1,0:T(8,128)(2,1)}, u32[]{:S(2)}) copy-start(bf16[2048,1024]{1,0:T(8,128)(2,1)} %refs_2_.6) | copy-start | bytes 12582916
  15.4 9.8 %collective-permute-start.2 = (bf16[64,2176]{1,0:T(8,128)(2,1)S(1)}, bf16[64,2176]{1,0:T(8,128)(2,1)S(1)}, u32[]{:S(2)}, u32[]{:S(2)}) collective-permute-start(bf16[64,2176]{1,0:T(8,128)(2,1)S(1)} %collective-permute-done.refs_0_), channel_id=1, source_target_pairs={{0,4},{4,8},{8,12},{12,14},{14,10},{10,6},{6,2},{2,0},{1,5},{5,9},... | collective-permute-start | bytes 835592 | tf_op jit(solution)/shard_map/ppermute | solution.py:455
  17.0 10.4 %collective-permute-start.7 = (bf16[64,2176]{1,0:T(8,128)(2,1)S(1)}, bf16[64,2176]{1,0:T(8,128)(2,1)S(1)}, u32[]{:S(2)}, u32[]{:S(2)}) collective-permute-start(bf16[64,2176]{1,0:T(8,128)(2,1)S(1)} %collective-permute-done.1.refs_3_), channel_id=1, source_target_pairs={{4,0},{8,4},{12,8},{14,12},{10,14},{6,10},{2,6},{0,2},{5,1},{9,5},... | collective-permute-start | bytes 835592 | tf_op jit(solution)/shard_map/ppermute | solution.py:455
  17.4 2.2 %copy-start.3 = (bf16[2048,1024]{1,0:T(8,128)(2,1)S(1)}, bf16[2048,1024]{1,0:T(8,128)(2,1)}, u32[]{:S(2)}) copy-start(bf16[2048,1024]{1,0:T(8,128)(2,1)} %refs_2_.7) | copy-start | bytes 12582916
  19.6 9.8 %copy-start.4 = (bf16[2048,1024]{1,0:T(8,128)(2,1)S(1)}, bf16[2048,1024]{1,0:T(8,128)(2,1)}, u32[]{:S(2)}) copy-start(bf16[2048,1024]{1,0:T(8,128)(2,1)} %refs_2_.7) | copy-start | bytes 12582916
  21.3 9.8 %collective-permute-start.5 = (bf16[64,2176]{1,0:T(8,128)(2,1)S(1)}, bf16[64,2176]{1,0:T(8,128)(2,1)S(1)}, u32[]{:S(2)}, u32[]{:S(2)}) collective-permute-start(bf16[64,2176]{1,0:T(8,128)(2,1)S(1)} %collective-permute-done.3.refs_1_), channel_id=1, source_target_pairs={{0,4},{4,8},{8,12},{12,14},{14,10},{10,6},{6,2},{2,0},{1,5},{5,9},... | collective-permute-start | bytes 835592 | tf_op jit(solution)/shard_map/ppermute | solution.py:455
  22.9 10.4 %collective-permute-start.6 = (bf16[64,2176]{1,0:T(8,128)(2,1)S(1)}, bf16[64,2176]{1,0:T(8,128)(2,1)S(1)}, u32[]{:S(2)}, u32[]{:S(2)}) collective-permute-start(bf16[64,2176]{1,0:T(8,128)(2,1)S(1)} %collective-permute-done.4.refs_2_), channel_id=1, source_target_pairs={{4,0},{8,4},{12,8},{14,12},{10,14},{6,10},{2,6},{0,2},{5,1},{9,5},... | collective-permute-start | bytes 835592 | tf_op jit(solution)/shard_map/ppermute | solution.py:455
  24.6 10.7 %copy-start.5 = (bf16[1,2048,1024]{2,1,0:T(8,128)(2,1)S(1)}, bf16[1,2048,1024]{2,1,0:T(8,128)(2,1)}, u32[]{:S(2)}) copy-start(bf16[1,2048,1024]{2,1,0:T(8,128)(2,1)} %param.14) | copy-start | bytes 12582916
  27.3 10.1 %collective-permute-start.8 = (bf16[64,2176]{1,0:T(8,128)(2,1)S(1)}, bf16[64,2176]{1,0:T(8,128)(2,1)S(1)}, u32[]{:S(2)}, u32[]{:S(2)}) collective-permute-start(bf16[64,2176]{1,0:T(8,128)(2,1)S(1)} %collective-permute-done.2.refs_0_), channel_id=1, source_target_pairs={{0,4},{4,8},{8,12},{12,14},{14,10},{10,6},{6,2},{2,0},{1,5},{5,9},... | collective-permute-start | bytes 835592 | tf_op jit(solution)/shard_map/ppermute | solution.py:455
  28.9 10.4 %collective-permute-start.9 = (bf16[64,2176]{1,0:T(8,128)(2,1)S(1)}, bf16[64,2176]{1,0:T(8,128)(2,1)S(1)}, u32[]{:S(2)}, u32[]{:S(2)}) collective-permute-start(bf16[64,2176]{1,0:T(8,128)(2,1)S(1)} %collective-permute-done.7.refs_3_), channel_id=1, source_target_pairs={{4,0},{8,4},{12,8},{14,12},{10,14},{6,10},{2,6},{0,2},{5,1},{9,5},... | collective-permute-start | bytes 835592 | tf_op jit(solution)/shard_map/ppermute | solution.py:455
  33.3 9.8 %collective-permute-start.10 = (bf16[64,2176]{1,0:T(8,128)(2,1)S(1)}, bf16[64,2176]{1,0:T(8,128)(2,1)S(1)}, u32[]{:S(2)}, u32[]{:S(2)}) collective-permute-start(bf16[64,2176]{1,0:T(8,128)(2,1)S(1)} %collective-permute-done.5.refs_1_), channel_id=1, source_target_pairs={{0,4},{4,8},{8,12},{12,14},{14,10},{10,6},{6,2},{2,0},{1,5},{5,9},... | collective-permute-start | bytes 835592 | tf_op jit(solution)/shard_map/ppermute | solution.py:455
  34.9 10.4 %collective-permute-start.11 = (bf16[64,2176]{1,0:T(8,128)(2,1)S(1)}, bf16[64,2176]{1,0:T(8,128)(2,1)S(1)}, u32[]{:S(2)}, u32[]{:S(2)}) collective-permute-start(bf16[64,2176]{1,0:T(8,128)(2,1)S(1)} %collective-permute-done.6.refs_2_), channel_id=1, source_target_pairs={{4,0},{8,4},{12,8},{14,12},{10,14},{6,10},{2,6},{0,2},{5,1},{9,5},... | collective-permute-start | bytes 835592 | tf_op jit(solution)/shard_map/ppermute | solution.py:455
  39.2 9.0 %collective-permute-start.12 = (bf16[64,2176]{1,0:T(8,128)(2,1)S(1)}, bf16[64,2176]{1,0:T(8,128)(2,1)S(1)}, u32[]{:S(2)}, u32[]{:S(2)}) collective-permute-start(bf16[64,2176]{1,0:T(8,128)(2,1)S(1)} %collective-permute-done.8.refs_0_), channel_id=1, source_target_pairs={{0,4},{4,8},{8,12},{12,14},{14,10},{10,6},{6,2},{2,0},{1,5},{5,9},... | collective-permute-start | bytes 835592 | tf_op jit(solution)/shard_map/ppermute | solution.py:455
  40.8 8.9 %collective-permute-start.13 = (bf16[64,2176]{1,0:T(8,128)(2,1)S(1)}, bf16[64,2176]{1,0:T(8,128)(2,1)S(1)}, u32[]{:S(2)}, u32[]{:S(2)}) collective-permute-start(bf16[64,2176]{1,0:T(8,128)(2,1)S(1)} %collective-permute-done.9.refs_3_), channel_id=1, source_target_pairs={{4,0},{8,4},{12,8},{14,12},{10,14},{6,10},{2,6},{0,2},{5,1},{9,5},... | collective-permute-start | bytes 835592 | tf_op jit(solution)/shard_map/ppermute | solution.py:455
  41.3 11.9 %collective-permute-start.15 = (bf16[2,256,1024]{2,1,0:T(8,128)(2,1)S(1)}, bf16[2,256,1024]{2,1,0:T(8,128)(2,1)S(1)}, u32[]{:S(2)}, u32[]{:S(2)}) collective-permute-start(bf16[2,256,1024]{2,1,0:T(8,128)(2,1)S(1)} %get-tuple-element.114.refs_8_), channel_id=1, source_target_pairs={{0,1},{1,0},{2,3},{3,2},{4,5},{5,4},{6,7},{7,6},{8,9},{9,8},{10,11... | collective-permute-start | bytes 3145736 | tf_op jit(solution)/shard_map/ppermute | solution.py:458
  43.1 10.8 %collective-permute-start.16 = (bf16[2,256,1024]{2,1,0:T(8,128)(2,1)S(1)}, bf16[2,256,1024]{2,1,0:T(8,128)(2,1)S(1)}, u32[]{:S(2)}, u32[]{:S(2)}) collective-permute-start(bf16[2,256,1024]{2,1,0:T(8,128)(2,1)S(1)} %get-tuple-element.115.refs_9_), channel_id=1, source_target_pairs={{0,1},{1,0},{2,3},{3,2},{4,5},{5,4},{6,7},{7,6},{8,9},{9,8},{10,11... | collective-permute-start | bytes 3145736 | tf_op jit(solution)/shard_map/ppermute | solution.py:458
  49.7 4.2 %collective-permute-start.17 = (bf16[2,256,1024]{2,1,0:T(8,128)(2,1)S(1)}, bf16[2,256,1024]{2,1,0:T(8,128)(2,1)S(1)}, u32[]{:S(2)}, u32[]{:S(2)}) collective-permute-start(bf16[2,256,1024]{2,1,0:T(8,128)(2,1)S(1)} %get-tuple-element.116.refs_10_), channel_id=1, source_target_pairs={{0,1},{1,0},{2,3},{3,2},{4,5},{5,4},{6,7},{7,6},{8,9},{9,8},{10,11... | collective-permute-start | bytes 3145736 | tf_op jit(solution)/shard_map/ppermute | solution.py:458
  49.7 3.5 %collective-permute-start.14 = (bf16[2,128,1024]{2,1,0:T(8,128)(2,1)S(1)}, bf16[2,128,1024]{2,1,0:T(8,128)(2,1)S(1)}, u32[]{:S(2)}, u32[]{:S(2)}) collective-permute-start(bf16[2,128,1024]{2,1,0:T(8,128)(2,1)S(1)} %get-tuple-element.113.refs_7_), channel_id=1, source_target_pairs={{0,1},{1,0},{2,3},{3,2},{4,5},{5,4},{6,7},{7,6},{8,9},{9,8},{10,11... | collective-permute-start | bytes 1572872 | tf_op jit(solution)/shard_map/ppermute | solution.py:458
  51.9 2.0 %collective-permute-start.18 = (bf16[2,128,1024]{2,1,0:T(8,128)(2,1)S(1)}, bf16[2,128,1024]{2,1,0:T(8,128)(2,1)S(1)}, u32[]{:S(2)}, u32[]{:S(2)}) collective-permute-start(bf16[2,128,1024]{2,1,0:T(8,128)(2,1)S(1)} %get-tuple-element.117.refs_11_), channel_id=1, source_target_pairs={{0,1},{1,0},{2,3},{3,2},{4,5},{5,4},{6,7},{7,6},{8,9},{9,8},{10,11... | collective-permute-start | bytes 1572872 | tf_op jit(solution)/shard_map/ppermute | solution.py:458
  53.9 8.1 %copy-start.6 = (bf16[1,1024,2048]{2,1,0:T(8,128)(2,1)S(1)}, bf16[1,1024,2048]{2,1,0:T(8,128)(2,1)}, u32[]{:S(2)}) copy-start(bf16[1,1024,2048]{2,1,0:T(8,128)(2,1)} %param.15) | copy-start | bytes 12582916
  64.1 15.0 %collective-permute-start.19 = (bf16[40,2048]{1,0:T(8,128)(2,1)S(1)}, bf16[40,2048]{1,0:T(8,128)(2,1)S(1)}, u32[]{:S(2)}, u32[]{:S(2)}) collective-permute-start(bf16[40,2048]{1,0:T(8,128)(2,1)S(1)} %get-tuple-element.127), channel_id=1, source_target_pairs={{0,8},{2,10},{4,12},{6,14},{8,0},{10,2},{12,4},{14,6},{1,9},{3,11}... | collective-permute-start | bytes 491528 | tf_op jit(solution)/shard_map/ppermute | solution.py:503
  64.2 17.4 %collective-permute-start.20 = (bf16[40,2048]{1,0:T(8,128)(2,1)S(1)}, bf16[40,2048]{1,0:T(8,128)(2,1)S(1)}, u32[]{:S(2)}, u32[]{:S(2)}) collective-permute-start(bf16[40,2048]{1,0:T(8,128)(2,1)S(1)} %get-tuple-element.128), channel_id=1, source_target_pairs={{0,10},{2,8},{4,14},{6,12},{8,2},{10,0},{12,6},{14,4},{1,11},{3,9}... | collective-permute-start | bytes 491528 | tf_op jit(solution)/shard_map/ppermute | solution.py:503
  81.5 9.6 %collective-permute-start.21 = (bf16[40,2048]{1,0:T(8,128)(2,1)S(1)}, bf16[40,2048]{1,0:T(8,128)(2,1)S(1)}, u32[]{:S(2)}, u32[]{:S(2)}) collective-permute-start(bf16[40,2048]{1,0:T(8,128)(2,1)S(1)} %get-tuple-element.132), channel_id=1, source_target_pairs={{0,2},{2,0},{4,6},{6,4},{8,10},{10,8},{12,14},{14,12},{1,3},{3,1},... | collective-permute-start | bytes 491528 | tf_op jit(solution)/shard_map/ppermute | solution.py:503
  83.3 7.9 %collective-permute-start.22 = (bf16[40,2048]{1,0:T(8,128)(2,1)S(1)}, bf16[40,2048]{1,0:T(8,128)(2,1)S(1)}, u32[]{:S(2)}, u32[]{:S(2)}) collective-permute-start(bf16[40,2048]{1,0:T(8,128)(2,1)S(1)} %get-tuple-element.133), channel_id=1, source_target_pairs={{0,4},{2,6},{4,0},{6,2},{8,12},{10,14},{12,8},{14,10},{1,5},{3,7},... | collective-permute-start | bytes 491528 | tf_op jit(solution)/shard_map/ppermute | solution.py:503
  83.3 8.7 %collective-permute-start.23 = (bf16[40,2048]{1,0:T(8,128)(2,1)S(1)}, bf16[40,2048]{1,0:T(8,128)(2,1)S(1)}, u32[]{:S(2)}, u32[]{:S(2)}) collective-permute-start(bf16[40,2048]{1,0:T(8,128)(2,1)S(1)} %get-tuple-element.134), channel_id=1, source_target_pairs={{0,6},{2,4},{4,2},{6,0},{8,14},{10,12},{12,10},{14,8},{1,7},{3,5},... | collective-permute-start | bytes 491528 | tf_op jit(solution)/shard_map/ppermute | solution.py:503
  85.0 11.9 %collective-permute-start.24 = (bf16[40,2048]{1,0:T(8,128)(2,1)S(1)}, bf16[40,2048]{1,0:T(8,128)(2,1)S(1)}, u32[]{:S(2)}, u32[]{:S(2)}) collective-permute-start(bf16[40,2048]{1,0:T(8,128)(2,1)S(1)} %get-tuple-element.137), channel_id=1, source_target_pairs={{0,12},{2,14},{4,8},{6,10},{8,4},{10,6},{12,0},{14,2},{1,13},{3,15... | collective-permute-start | bytes 491528 | tf_op jit(solution)/shard_map/ppermute | solution.py:503
  86.2 13.0 %collective-permute-start.25 = (bf16[40,2048]{1,0:T(8,128)(2,1)S(1)}, bf16[40,2048]{1,0:T(8,128)(2,1)S(1)}, u32[]{:S(2)}, u32[]{:S(2)}) collective-permute-start(bf16[40,2048]{1,0:T(8,128)(2,1)S(1)} %get-tuple-element.138), channel_id=1, source_target_pairs={{0,14},{2,12},{4,10},{6,8},{8,6},{10,4},{12,2},{14,0},{1,15},{3,13... | collective-permute-start | bytes 491528 | tf_op jit(solution)/shard_map/ppermute | solution.py:503

commit v8 on v7

v8 whole, which is shorter than its diff:
```python
import functools
import math

import jax
import jax.numpy as jnp
from jax import lax
from jax.experimental import pallas as pl
from jax.experimental.pallas import tpu as pltpu
from jax.sharding import PartitionSpec as P

HS = 128
EXPERTS = 8
MOST = 40
SLOTS = 48
MASKED = -1e30
LANES = 128
MIB = 1 << 20
WHOLE = pl.BlockSpec(memory_space=pltpu.VMEM)


def ring_rank(place, count):
    place = lax.rem(place + 2 * count, count)
    return jnp.where(place < count // 2, 2 * place, 2 * (count - 1 - place) + 1)


def ring_place(rank, count):
    return jnp.where(rank % 2 == 0, rank // 2, count - 1 - rank // 2)


def ring_owner(offset):
    count = lax.axis_size("ctx")
    return ring_rank(ring_place(lax.axis_index("ctx"), count) + offset, count)


def norm_kernel(*refs):
    sources, top_ref, bottom_ref, *held, arrivals = refs[:3], *refs[3:]
    copies = [
        pltpu.make_async_copy(source, target, arrivals.at[i])
        for i, (source, target) in enumerate(zip(sources, held))
    ]
    for copy in copies:
        copy.start()
    for copy in copies:
        copy.wait()
    tokens_ref, gain_ref, routes_ref = held
    floats = tokens_ref[...].astype(jnp.float32)
    count, width = floats.shape
    factor = lax.rsqrt(jnp.mean(floats * floats, axis=1, keepdims=True) + 1e-06)
    normed = (floats * factor * gain_ref[...]).astype(jnp.bfloat16)
    expert = lax.broadcasted_iota(jnp.int32, (LANES, count), 0)
    named = (expert == routes_ref[0:1, :]) | (expert == routes_ref[1:2, :])
    before = lax.broadcasted_iota(jnp.int32, (count, count), 0) < lax.broadcasted_iota(
        jnp.int32, (count, count), 1
    )
    rank = jnp.dot(
        named.astype(jnp.bfloat16),
        before.astype(jnp.bfloat16),
        preferred_element_type=jnp.float32,
    )
    slots = jnp.where(named, rank, -1.0).T.astype(jnp.bfloat16)
    half = count // 2
    for ref, part in ((top_ref, slice(0, half)), (bottom_ref, slice(half, count))):
        ref[:, :width] = normed[part]
        ref[:, width:] = slots[part]


def norm_rows(tokens, norm_gain, routes):
    count, width = tokens.shape
    half = jax.ShapeDtypeStruct((count // 2, width + LANES), jnp.bfloat16)
    operands = (tokens, norm_gain.reshape(1, -1), routes.T)
    return pl.pallas_call(
        norm_kernel,
        in_specs=[pl.BlockSpec(memory_space=pl.ANY)] * 3,
        out_specs=[WHOLE] * 2,
        out_shape=[half, half],
        scratch_shapes=[pltpu.VMEM(x.shape, x.dtype) for x in operands]
        + [pltpu.SemaphoreType.DMA((3,))],
        compiler_params=pltpu.CompilerParams(vmem_limit_bytes=8 * MIB),
        name="norm_rows",
    )(*operands)


def column_parts(ref):
    step = min(ref.shape[1], 256)
    return [pl.ds(start, step) for start in range(0, ref.shape[1], step)]


def keys_kernel(count, *refs):
    blocks = refs[:count]
    weight_ref, panel_ref, mark_ref = refs[count:]
    rows = jnp.concatenate([block[:, : weight_ref.shape[0]] for block in blocks], axis=0)
    for cols in column_parts(weight_ref):
        product = jnp.dot(rows, weight_ref[:, cols], preferred_element_type=jnp.float32)
        panel_ref[:, cols] = product.astype(jnp.bfloat16)
    mark_ref[...] = product[:8, :LANES]


def project_keys(blocks, key_weight):
    row_count = sum(block.shape[0] for block in blocks)
    width = key_weight.shape[1]
    return pl.pallas_call(
        functools.partial(keys_kernel, len(blocks)),
        in_specs=[WHOLE] * (len(blocks) + 1),
        out_specs=[WHOLE] * 2,
        out_shape=[
            jax.ShapeDtypeStruct((row_count, width), jnp.bfloat16),
            jax.ShapeDtypeStruct((8, LANES), jnp.float32),
        ],
        compiler_params=pltpu.CompilerParams(vmem_limit_bytes=12 * MIB),
        name="project_keys",
    )(*blocks, key_weight)


def values_kernel(offsets, count, experts, mark_ref, keys_ref, *refs):
    blocks = refs[:count]
    value_ref, panel_ref, picked_ref, pos_ref = refs[count:]
    width = value_ref.shape[0]
    rows = jnp.concatenate([block[:, :width] for block in blocks], axis=0)
    tok_count = rows.shape[0] // len(offsets)

    slots = jnp.concatenate([block[:, width:] for block in blocks], axis=0)
    slots = slots.astype(jnp.float32)
    expert = lax.axis_index("ctx") // (lax.axis_size("ctx") // experts)
    lane = lax.broadcasted_iota(jnp.int32, slots.shape, 1)
    slot = jnp.sum(jnp.where(lane == expert, slots, 0.0), axis=1, keepdims=True)
    select = (slot == lane.astype(jnp.float32)).astype(jnp.float32)
    number = lax.broadcasted_iota(jnp.int32, (tok_count, LANES), 0).astype(jnp.bfloat16)
    for g, offset in enumerate(offsets):
        part = slice(g * tok_count, (g + 1) * tok_count)
        chosen = select[part].T[:SLOTS].astype(jnp.bfloat16)
        picked_ref[g] = jnp.dot(
            chosen, rows[part], preferred_element_type=jnp.float32
        ).astype(jnp.bfloat16)
        start = (ring_owner(offset) * lax.axis_size("exp") + lax.axis_index("exp")) * tok_count
        pos_ref[g] = jnp.dot(
            chosen, number, preferred_element_type=jnp.float32
        ) + start.astype(jnp.float32)
    panel_ref[0] = keys_ref[...]
    for cols in column_parts(value_ref):
        panel_ref[1, :, cols] = jnp.dot(
            rows, value_ref[:, cols], preferred_element_type=jnp.float32
        ).astype(jnp.bfloat16)


def project_values(blocks, offsets, mark, keys, value_weight):
    row_count = sum(block.shape[0] for block in blocks)
    model_width, width = value_weight.shape
    owners = len(offsets)
    return pl.pallas_call(
        functools.partial(values_kernel, offsets, len(blocks), EXPERTS),
        in_specs=[WHOLE] * (len(blocks) + 3),
        out_specs=[WHOLE] * 3,
        out_shape=[
            jax.ShapeDtypeStruct((2, row_count, width), jnp.bfloat16),
            jax.ShapeDtypeStruct((owners, SLOTS, model_width), jnp.bfloat16),
            jax.ShapeDtypeStruct((owners, SLOTS, LANES), jnp.float32),
        ],
        compiler_params=pltpu.CompilerParams(vmem_limit_bytes=12 * MIB),
        name="project_values",
    )(mark, keys, *blocks, value_weight)


def queries_kernel(*refs):
    count = len(refs) // 2
    picked, weight_ref, outs = refs[:count], refs[count], refs[count + 1 :]
    rows = jnp.concatenate([ref[g] for ref in picked for g in range(ref.shape[0])], axis=0)
    places = [(ref, g) for ref in outs for g in range(ref.shape[0])]
    for cols in column_parts(weight_ref):
        product = jnp.dot(rows, weight_ref[:, cols], preferred_element_type=jnp.float32)
        for i, (ref, g) in enumerate(places):
            ref[g, :, cols] = product[i * SLOTS : (i + 1) * SLOTS].astype(jnp.bfloat16)


def project_queries(picked, query_slab):
    model_width, width = query_slab.shape
    owners = sum(rows.shape[0] for rows in picked)
    held = 2 * model_width * width + owners * SLOTS * (4 * model_width + 4 * width)
    return pl.pallas_call(
        queries_kernel,
        in_specs=[WHOLE] * (len(picked) + 1),
        out_specs=[WHOLE] * len(picked),
        out_shape=[
            jax.ShapeDtypeStruct((rows.shape[0], SLOTS, width), jnp.bfloat16) for rows in picked
        ],
        compiler_params=pltpu.CompilerParams(vmem_limit_bytes=held + 6 * MIB),
        name="project_queries",
    )(*picked, query_slab)


def arrange_kernel(plan, *refs):
    count = len(plan)
    own_refs, other_refs, query_refs, pos_refs = (refs[k * count : (k + 1) * count] for k in range(4))
    panel_ref, queries_ref, places_ref = refs[4 * count :]
    exp_count = 2
    side = lax.axis_index("exp")
    tok_count = panel_ref.shape[2]
    for offsets, own_ref, other_ref, query_ref, pos_ref in zip(
        plan, own_refs, other_refs, query_refs, pos_refs
    ):
        for g, offset in enumerate(offsets):
            owner = ring_owner(offset)
            part = pl.ds(g * tok_count, tok_count)
            for which in range(2):
                panel_ref[which, owner * exp_count + side] = own_ref[which, part]
                panel_ref[which, owner * exp_count + 1 - side] = other_ref[which, part]
            queries_ref[owner] = query_ref[g]
            places_ref[owner] = pos_ref[g]


def arrange(owners, plan, own, other, queries, positions):
    width = own[0].shape[2]
    tok_count = own[0].shape[1] // len(plan[0])
    shapes = [
        jax.ShapeDtypeStruct((2, 2 * owners, tok_count, width), jnp.bfloat16),
        jax.ShapeDtypeStruct((owners, SLOTS, width), jnp.bfloat16),
        jax.ShapeDtypeStruct((owners, SLOTS, LANES), jnp.float32),
    ]
    operands = (*own, *other, *queries, *positions)
    return pl.pallas_call(
        functools.partial(arrange_kernel, plan),
        in_specs=[WHOLE] * len(operands),
        out_specs=[WHOLE] * 3,
        out_shape=shapes,
        compiler_params=pltpu.CompilerParams(
            vmem_limit_bytes=owners * tok_count * width * 24 + 4 * MIB
        ),
        name="arrange",
    )(*operands)


def attend_kernel(lots, heads, panel_ref, queries_ref, places_ref, weight_ref, *refs):
    outs, (attended, scores, weights) = refs[:-3], refs[-3:]
    first, count = lots
    blocks, tok_count, width = panel_ref.shape[1:]
    rate = math.log2(math.e) / math.sqrt(HS)
    rank = lax.axis_index("ctx")
    tiles = blocks // 4
    tile = 2 * SLOTS
    parts = 4
    span = blocks * tok_count // parts
    per_span = blocks // parts
    passes = width // (heads * HS)

    def serve(part_id, number, lot, lanes):
        reach = (part_id + 1) * span
        pair = pl.ds(2 * number, 2)
        spots = places_ref[pair].reshape(tile, LANES)
        for h in range(heads):
            held = queries_ref[pair, :, lanes[h]].reshape(tile, HS)
            for j in range(part_id + 1):
                key_part = panel_ref[0, per_span * j : per_span * (j + 1), :, lanes[h]]
                scores[h, :, pl.ds(j * span, span)] = lax.dot_general(
                    held,
                    key_part.reshape(span, HS),
                    (((1,), (1,)), ((), ())),
                    preferred_element_type=jnp.float32,
                )
        for h in range(heads):
            for sub in range(0, tile, 16):
                rows = pl.ds(sub, 16)
                part = scores[h, rows, pl.ds(0, reach)]
                last = part[:, reach - span :]
                key_index = lax.broadcasted_iota(jnp.int32, last.shape, 1) + (reach - span)
                spot = spots[sub : sub + 16, 0:1]
                last = jnp.where(key_index.astype(jnp.float32) <= spot, last, MASKED)
                if part_id > 0:
                    part = jnp.concatenate([part[:, : reach - span], last], axis=1)
                else:
                    part = last
                peak = jnp.max(part, axis=1, keepdims=True)
                raised = jnp.exp2((part - peak) * rate)
                total = jnp.sum(raised, axis=1, keepdims=True)
                weights[h, rows, pl.ds(0, reach)] = (raised * (1.0 / total)).astype(jnp.bfloat16)
        for h in range(heads):
            total = None
            for j in range(part_id + 1):
                value_part = panel_ref[1, per_span * j : per_span * (j + 1), :, lanes[h]]
                product = jnp.dot(
                    weights[h, :, pl.ds(j * span, span)],
                    value_part.reshape(span, HS),
                    preferred_element_type=jnp.float32,
                )
                total = product if total is None else total + product
            total = total.astype(jnp.bfloat16)
            for side in range(2):
                attended[2 * lot + (side ^ (rank % 2)), :, lanes[h]] = total[
                    side * SLOTS : (side + 1) * SLOTS
                ]

    def one(at, carry):
        lot, now = at // passes, at % passes
        number = (rank // 2) ^ (first + lot)
        lanes = [pl.ds(pl.multiple_of((now * heads + h) * HS, HS), HS) for h in range(heads)]
        for part_id in range(parts):
            pl.when(number // (tiles // parts) == part_id)(
                functools.partial(serve, part_id, number, lot, lanes)
            )
        return carry

    lax.fori_loop(0, count * passes, one, 0)
    rows = attended[...].reshape(2 * count * SLOTS, width)
    for cols in column_parts(weight_ref):
        product = jnp.dot(rows, weight_ref[:, cols], preferred_element_type=jnp.float32)
        for k, out_ref in enumerate(outs):
            out_ref[:, cols] = product[k * SLOTS : k * SLOTS + MOST].astype(jnp.bfloat16)


def attend(lots, panel, queries, places, output_slab):
    first, count = lots
    _, blocks, tok_count, width = panel.shape
    length = blocks * tok_count
    heads = min(4, width // HS) if blocks <= 16 else 1
    model_width = output_slab.shape[1]
    held = heads * 2 * SLOTS * length * 6 + 2 * length * width * 2 + width * model_width * 2
    held += 2 * count * SLOTS * (model_width * 8 + width * 2)
    return pl.pallas_call(
        functools.partial(attend_kernel, lots, heads),
        in_specs=[WHOLE] * 4,
        out_specs=[WHOLE] * (2 * count),
        out_shape=[jax.ShapeDtypeStruct((MOST, model_width), jnp.bfloat16)] * (2 * count),
        scratch_shapes=[
            pltpu.VMEM((2 * count, SLOTS, width), jnp.bfloat16),
            pltpu.VMEM((heads, 2 * SLOTS, length), jnp.float32),
            pltpu.VMEM((heads, 2 * SLOTS, length), jnp.bfloat16),
        ],
        compiler_params=pltpu.CompilerParams(vmem_limit_bytes=held * 9 // 8 + 4 * MIB),
        cost_estimate=pl.CostEstimate(
            flops=count * 2 * SLOTS * width * (4 * length + 2 * model_width),
            bytes_accessed=4 * length * width,
            transcendentals=count * 2 * SLOTS * length * width // HS,
        ),
        name="attend",
    )(panel, queries, places, output_slab)


def mix_kernel(quarter_count, top_ref, bottom_ref, logits_ref, mix_ref):
    slots = jnp.concatenate([top_ref[...], bottom_ref[...]], axis=0).astype(jnp.float32)
    tok_count = slots.shape[0]
    logits = jnp.where(slots >= 0, logits_ref[...], -jnp.inf)
    raised = jnp.exp(logits - jnp.max(logits, axis=1, keepdims=True))
    gates = raised / jnp.sum(raised, axis=1, keepdims=True)
    lane = lax.broadcasted_iota(jnp.int32, slots.shape, 1)
    count = mix_ref.shape[1] // SLOTS
    wide = lax.broadcasted_iota(jnp.int32, (tok_count, count * SLOTS), 1).astype(jnp.float32)
    total = jnp.zeros_like(wide)
    for k in range(count):
        mine = lane == (lax.axis_index("ctx") ^ k) // quarter_count
        slot = jnp.sum(jnp.where(mine, slots, 0.0), axis=1, keepdims=True)
        gate = jnp.sum(jnp.where(mine, gates, 0.0), axis=1, keepdims=True)
        spot = jnp.where(slot >= 0, slot + float(k * SLOTS), -1.0)
        total = total + jnp.where(wide == spot, gate, 0.0)
    for part in range(3):
        term = total.astype(jnp.bfloat16)
        mix_ref[pl.ds(part * tok_count, tok_count), :] = term
        total = total - term.astype(jnp.float32)


def gate_mix(quarter_count, halves, logits, count):
    half, width = halves[0].shape
    tok_count = 2 * half
    lanes = width // LANES - 1
    return pl.pallas_call(
        functools.partial(mix_kernel, quarter_count),
        grid=(1,),
        in_specs=[pl.BlockSpec((half, LANES), lambda n: (0, lanes))] * 2
        + [pl.BlockSpec((tok_count, LANES), lambda n: (0, 0))],
        out_specs=pl.BlockSpec((3 * tok_count, count * SLOTS), lambda n: (0, 0)),
        out_shape=jax.ShapeDtypeStruct((3 * tok_count, count * SLOTS), jnp.bfloat16),
        compiler_params=pltpu.CompilerParams(vmem_limit_bytes=16 * MIB),
        name="gate_mix",
    )(*halves, logits)


def combine_kernel(mix_ref, *refs):
    pieces, out_ref = refs[:-1], refs[-1]
    tok_count, model_width = out_ref.shape
    step = min(model_width, 512)
    spare = jnp.zeros((SLOTS - MOST, step), jnp.float32)
    for start in range(0, model_width, step):
        cols = pl.ds(start, step)
        rows = []
        for piece in pieces:
            rows += [piece[:, cols].astype(jnp.float32), spare]
        rows = jnp.concatenate(rows, axis=0).astype(jnp.bfloat16)
        product = jnp.dot(mix_ref[...], rows, preferred_element_type=jnp.float32)
        total = product[:tok_count] + (
            product[tok_count : 2 * tok_count] + product[2 * tok_count :]
        )
        out_ref[:, cols] = total.astype(jnp.bfloat16)


def combine(mix, pieces):
    tok_count = mix.shape[0] // 3
    model_width = pieces[0].shape[1]
    return pl.pallas_call(
        combine_kernel,
        in_specs=[WHOLE] * (1 + len(pieces)),
        out_specs=WHOLE,
        out_shape=jax.ShapeDtypeStruct((tok_count, model_width), jnp.bfloat16),
        compiler_params=pltpu.CompilerParams(vmem_limit_bytes=24 * MIB),
        name="combine",
    )(mix, *pieces)


def per_device(
    tokens, norm_gain, router_weight, routes, key_weight, value_weight, query_weight, output_weight
):
    tok_count, model_width = tokens.shape
    ctx_count = lax.axis_size("ctx")
    exp_count = lax.axis_size("exp")
    quarter_count = ctx_count // EXPERTS
    head_width = query_weight.shape[2]
    ranks = list(range(0, ctx_count, 2)) + list(range(1, ctx_count, 2))[::-1]
    forward = [(ranks[p], ranks[(p + 1) % ctx_count]) for p in range(ctx_count)]
    backward = [(b, a) for a, b in forward]
    sibling = [(e, 1 - e) for e in range(exp_count)]
    query_slab = query_weight[0]
    output_slab = output_weight[0]
    if quarter_count > 1:
        first = (lax.axis_index("ctx") % quarter_count) * head_width
        key_weight = lax.dynamic_slice_in_dim(key_weight, first, head_width, axis=1)
        value_weight = lax.dynamic_slice_in_dim(value_weight, first, head_width, axis=1)

    halves = norm_rows(tokens, norm_gain, routes)
    steps = ctx_count // 2
    plan = [[0]] + [[-step, step] for step in range(1, steps)] + [[steps]]
    own, other, picked, queries, positions = [], [], [], [], []

    def send(parts):
        return [lax.ppermute(parts[0], "ctx", forward), lax.ppermute(parts[1], "ctx", backward)]

    def hand_over(panel):
        return lax.ppermute(panel, "exp", sibling)

    def tie(*arrays):
        return lax.optimization_barrier(arrays)

    blocks = halves
    lead = send([halves[0], halves[1]])
    rest = send([halves[1], halves[0]])
    for step in range(steps):
        keys, mark = project_keys(blocks, key_weight)
        following = [lead[0], rest[0], rest[1], lead[1]]
        if step == steps - 2:
            queries = project_queries(picked, query_slab)
            picked = []
        if step < steps - 1:
            mark, *lead_next = tie(mark, *lead, *queries)
            queries = lead_next[2:]
            lead = send(lead_next[:2])
        panel, rows, position = project_values(blocks, plan[step], mark, keys, value_weight)
        if step < steps - 2:
            position, *rest_next = tie(position, *rest)
            rest = send(rest_next)
        own.append(panel)
        picked.append(rows)
        positions.append(position)
        if step < steps - 1:
            other.append(hand_over(panel))
        blocks = following
    own[-1], *blocks = tie(own[-1], *lead)
    other.append(hand_over(own[-1]))
    keys, mark = project_keys(blocks, key_weight)
    panel, rows, position = project_values(blocks, plan[-1], mark, keys, value_weight)
    own.append(panel)
    other.append(hand_over(panel))
    positions.append(position)
    queries = [*queries, *project_queries(picked + [rows], query_slab)]
    held = arrange(ctx_count, plan, own, other, queries, positions)

    def swap(piece, k):
        return lax.ppermute(piece, "ctx", [(c, c ^ k) for c in range(ctx_count)])

    half, quarter = ctx_count // 2, ctx_count // 4
    far, mine = [], []
    for start, count in ((half, quarter), (half + quarter, quarter), (0, half)):
        pieces = attend((start // 2, count // 2), *held, output_slab)
        if start > 0:
            places, *pieces = tie(held[2], *pieces)
            held = [*held[:2], places]
            far.append([swap(piece, start + r) for r, piece in enumerate(pieces)])
        else:
            near = pieces
    tied = tie(*near, *far[0])
    near, far[0] = tied[:half], tied[half:]
    near = [near[0]] + [swap(near[r], r) for r in range(1, half)]

    normed = jnp.concatenate([part[:, :model_width] for part in halves], axis=0)
    logits = jnp.dot(normed.astype(jnp.float32), router_weight, precision=lax.Precision.HIGHEST)
    logits = jnp.pad(logits, ((0, 0), (0, LANES - EXPERTS)))
    mix = gate_mix(quarter_count, halves, logits, ctx_count)
    return combine(mix, [*near, *far[0], *far[1]])


def solution(mesh):
    in_specs = (
        P(("groups", "ctx", "exp"), None),
        P(),
        P(),
        P(("groups", "ctx", "exp"), None),
        P(),
        P(),
        P("ctx", None, None),
        P("ctx", None, None),
    )
    out_specs = P(("groups", "ctx", "exp"), None)
    return jax.shard_map(
        per_device, mesh=mesh, in_specs=in_specs, out_specs=out_specs, check_vma=False
    )
```

time: 102 us -> 97.4 us (0.955)
  waiting for transfers between devices: 31.7 us -> 28.2 us
  Pallas kernels: 34.4 us -> 32.2 us
  local copies, waits for them, and re-layouts: 6.89 us -> 8.38 us
    ppermute x7, waiting for transfers between devices: 15.4 us -> 12 us  [swap(): return lax.ppermute(piece, 'ctx', [(c, c ^ k) for c in range(ctx_count)])]
    pallas_call x6, Pallas kernels: 19.8 us -> 17.4 us  [the longest x3 14.6 us: attend(): pl.pallas_call(functools.partial(attend_kernel, lots, heads), in_specs=[W...]
    unnamed x20, local copies, waits for them, and re-layouts: 6.84 us -> 8.33 us
  transfers between devices with their start and end apart: 26 -> 26, of which waited for: 17 -> 17; matrix products, arithmetic and copies ran while one was open for 1% -> 1% of each run, Pallas kernels for 22% -> 26%
where the time goes in v8:
time: 97.4 us; the launch traced here: 97.1 us
  Pallas kernels  32.2 us (33%)
  waiting for transfers between devices  28.2 us (29%)
  starting transfers between devices  27.6 us (28%)
  local copies, waits for them, and re-layouts  8.38 us (9%)
    pallas_call x3, Pallas kernels, attend(): pl.pallas_call(functools.partial(attend_kernel, lots, heads), in_specs=[W...  14.6 us
    ppermute x7, waiting for transfers between devices, send(): lax.ppermute(parts[1], 'ctx', backward)  12.3 us
    ppermute x7, waiting for transfers between devices, swap(): return lax.ppermute(piece, 'ctx', [(c, c ^ k) for c in range(ctx_count)])  12 us
    ppermute x7, starting transfers between devices, swap(): return lax.ppermute(piece, 'ctx', [(c, c ^ k) for c in range(ctx_count)])  11.3 us
    ppermute x7, starting transfers between devices, send(): lax.ppermute(parts[0], 'ctx', forward)  11.1 us
    unnamed x20, local copies, waits for them, and re-layouts  8.33 us
    pallas_call x5, Pallas kernels, project_values(): pl.pallas_call(functools.partial(values_kernel, offsets, len(blocks), EXP...  6.86 us
    pallas_call x5, Pallas kernels, project_keys(): pl.pallas_call(functools.partial(keys_kernel, len(blocks)), in_specs=[WHO...  5.34 us
  transfers between devices with their start and end apart: 26, of which 17 were waited for; matrix products, arithmetic and copies ran while one was open for 1% of the time, Pallas kernels for 26%

profile of v8, /device:TPU:0, one launch (start us, length us, event | category | flops | bytes accessed | tf_op | source)
XLA Modules:
  0.0 97.1 jit_solution(3423677003391798646)
XLA Ops:
  0.0 1.1 %copy-done.7 = bf16[128,2048]{1,0:T(8,128)(2,1)S(1)} copy-done((bf16[128,2048]{1,0:T(8,128)(2,1)S(1)}, bf16[128,2048]{1,0:T(8,128)(2,1)}, u32[]{:S(2)}) %copy-start.7) | copy-done | bytes 524312
  1.1 0.7 copy-done.8
  1.8 0.7 copy-done.9
  2.5 0.3 norm_rows.1
  2.8 3.1 %collective-permute-start = (bf16[64,2176]{1,0:T(8,128)(2,1)S(1)}, bf16[64,2176]{1,0:T(8,128)(2,1)S(1)}, u32[]{:S(2)}, u32[]{:S(2)}) collective-permute-start(bf16[64,2176]{1,0:T(8,128)(2,1)S(1)} %get-tuple-element.80.top_ref.refs_0_), channel_id=1, source_target_pairs={{0,4},{4,8},{8,12},{12,14},{14,10},{10,6},{6,2},{2,0},{1,5},{5,9},... | collective-permute-start | bytes 835592 | tf_op jit(solution)/shard_map/ppermute | solution.py:430
  5.9 2.0 %collective-permute-start.3 = (bf16[64,2176]{1,0:T(8,128)(2,1)S(1)}, bf16[64,2176]{1,0:T(8,128)(2,1)S(1)}, u32[]{:S(2)}, u32[]{:S(2)}) collective-permute-start(bf16[64,2176]{1,0:T(8,128)(2,1)S(1)} %get-tuple-element.80.top_ref.refs_0_), channel_id=1, source_target_pairs={{4,0},{8,4},{12,8},{14,12},{10,14},{6,10},{2,6},{0,2},{5,1},{9,5},... | collective-permute-start | bytes 835592 | tf_op jit(solution)/shard_map/ppermute | solution.py:430
  7.8 0.1 collective-permute-start.2
  7.9 2.2 %copy-done.1 = bf16[2048,1024]{1,0:T(8,128)(2,1)S(1)} copy-done((bf16[2048,1024]{1,0:T(8,128)(2,1)S(1)}, bf16[2048,1024]{1,0:T(8,128)(2,1)}, u32[]{:S(2)}) %copy-start.1) | copy-done | bytes 4194328
  10.1 0.7 project_keys.5
  10.9 2.4 %collective-permute-done.refs_0_ = bf16[64,2176]{1,0:T(8,128)(2,1)S(1)} collective-permute-done((bf16[64,2176]{1,0:T(8,128)(2,1)S(1)}, bf16[64,2176]{1,0:T(8,128)(2,1)S(1)}, u32[]{:S(2)}, u32[]{:S(2)}) %collective-permute-start) | collective-permute-done | bytes 278560 | tf_op jit(solution)/shard_map/ppermute | solution.py:430
  13.3 2.2 %collective-permute-done.1.refs_3_ = bf16[64,2176]{1,0:T(8,128)(2,1)S(1)} collective-permute-done((bf16[64,2176]{1,0:T(8,128)(2,1)S(1)}, bf16[64,2176]{1,0:T(8,128)(2,1)S(1)}, u32[]{:S(2)}, u32[]{:S(2)}) %collective-permute-start.1) | collective-permute-done | bytes 278560 | tf_op jit(solution)/shard_map/ppermute | solution.py:430
  15.5 1.6 %collective-permute-start.4 = (bf16[64,2176]{1,0:T(8,128)(2,1)S(1)}, bf16[64,2176]{1,0:T(8,128)(2,1)S(1)}, u32[]{:S(2)}, u32[]{:S(2)}) collective-permute-start(bf16[64,2176]{1,0:T(8,128)(2,1)S(1)} %collective-permute-done.refs_0_), channel_id=1, source_target_pairs={{0,4},{4,8},{8,12},{12,14},{14,10},{10,6},{6,2},{2,0},{1,5},{5,9},... | collective-permute-start | bytes 835592 | tf_op jit(solution)/shard_map/ppermute | solution.py:430
  17.0 0.4 collective-permute-start.5
  17.5 2.2 %copy-done.3 = bf16[2048,1024]{1,0:T(8,128)(2,1)S(1)} copy-done((bf16[2048,1024]{1,0:T(8,128)(2,1)S(1)}, bf16[2048,1024]{1,0:T(8,128)(2,1)}, u32[]{:S(2)}) %copy-start.3) | copy-done | bytes 4194328
  19.7 1.0 %project_values.5 = (bf16[2,128,1024]{2,1,0:T(8,128)(2,1)S(1)}, bf16[1,48,2048]{2,1,0:T(8,128)(2,1)S(1)}, f32[1,48,128]{2,1,0:T(8,128)S(1)}) custom-call(f32[8,128]{1,0:T(8,128)S(1)} %get-tuple-element.83.mark_ref, bf16[128,1024]{1,0:T(8,128)(2,1)S(1)} %get-tuple-element.84.keys_ref, bf16[64,2176]{1,0:T(8,128)(2,1)S(1)} %get-tuple-element.80.top_ref.refs_0_, ...), custom_call_target="tpu_custom_call" | custom-call | tf_op jit(solution)/shard_map/project_values/pallas_call | solution.py:149
  20.7 0.8 collective-permute-done.3.refs_2_
  21.4 1.6 %collective-permute-start.6 = (bf16[64,2176]{1,0:T(8,128)(2,1)S(1)}, bf16[64,2176]{1,0:T(8,128)(2,1)S(1)}, u32[]{:S(2)}, u32[]{:S(2)}) collective-permute-start(bf16[64,2176]{1,0:T(8,128)(2,1)S(1)} %collective-permute-done.2.refs_1_), channel_id=1, source_target_pairs={{0,4},{4,8},{8,12},{12,14},{14,10},{10,6},{6,2},{2,0},{1,5},{5,9},... | collective-permute-start | bytes 835592 | tf_op jit(solution)/shard_map/ppermute | solution.py:430
  23.0 0.4 collective-permute-start.7
  23.5 1.3 %project_keys.6 = (bf16[256,1024]{1,0:T(8,128)(2,1)S(1)}, f32[8,128]{1,0:T(8,128)S(1)}) custom-call(bf16[64,2176]{1,0:T(8,128)(2,1)S(1)} %collective-permute-done.refs_0_, bf16[64,2176]{1,0:T(8,128)(2,1)S(1)} %collective-permute-done.2.refs_1_, bf16[64,2176]{1,0:T(8,128)(2,1)S(1)} %collective-permute-done.3.refs_2_, ...), custom_call_target="tpu_custom_call" | custom-call | tf_op jit(solution)/shard_map/project_keys/pallas_call | solution.py:101
  24.7 0.5 collective-permute-done.4.refs_0_
  25.2 2.2 %collective-permute-done.5.refs_3_ = bf16[64,2176]{1,0:T(8,128)(2,1)S(1)} collective-permute-done((bf16[64,2176]{1,0:T(8,128)(2,1)S(1)}, bf16[64,2176]{1,0:T(8,128)(2,1)S(1)}, u32[]{:S(2)}, u32[]{:S(2)}) %collective-permute-start.5) | collective-permute-done | bytes 278560 | tf_op jit(solution)/shard_map/ppermute | solution.py:430
  27.4 1.6 %collective-permute-start.8 = (bf16[64,2176]{1,0:T(8,128)(2,1)S(1)}, bf16[64,2176]{1,0:T(8,128)(2,1)S(1)}, u32[]{:S(2)}, u32[]{:S(2)}) collective-permute-start(bf16[64,2176]{1,0:T(8,128)(2,1)S(1)} %collective-permute-done.4.refs_0_), channel_id=1, source_target_pairs={{0,4},{4,8},{8,12},{12,14},{14,10},{10,6},{6,2},{2,0},{1,5},{5,9},... | collective-permute-start | bytes 835592 | tf_op jit(solution)/shard_map/ppermute | solution.py:430
  29.0 0.4 collective-permute-start.9
  29.4 1.6 %project_values.6 = (bf16[2,256,1024]{2,1,0:T(8,128)(2,1)S(1)}, bf16[2,48,2048]{2,1,0:T(8,128)(2,1)S(1)}, f32[2,48,128]{2,1,0:T(8,128)S(1)}) custom-call(f32[8,128]{1,0:T(8,128)S(1)} %get-tuple-element.89.mark_ref, bf16[256,1024]{1,0:T(8,128)(2,1)S(1)} %get-tuple-element.90.keys_ref, bf16[64,2176]{1,0:T(8,128)(2,1)S(1)} %collective-permute-done.refs_0_, ...), custom_call_target="tpu_custom_call" | custom-call | tf_op jit(solution)/shard_map/project_values/pallas_call | solution.py:149
  31.0 0.2 collective-permute-done.6.refs_1_
  31.2 2.2 %collective-permute-done.7.refs_2_ = bf16[64,2176]{1,0:T(8,128)(2,1)S(1)} collective-permute-done((bf16[64,2176]{1,0:T(8,128)(2,1)S(1)}, bf16[64,2176]{1,0:T(8,128)(2,1)S(1)}, u32[]{:S(2)}, u32[]{:S(2)}) %collective-permute-start.7) | collective-permute-done | bytes 278560 | tf_op jit(solution)/shard_map/ppermute | solution.py:430
  33.4 1.6 %collective-permute-start.10 = (bf16[64,2176]{1,0:T(8,128)(2,1)S(1)}, bf16[64,2176]{1,0:T(8,128)(2,1)S(1)}, u32[]{:S(2)}, u32[]{:S(2)}) collective-permute-start(bf16[64,2176]{1,0:T(8,128)(2,1)S(1)} %collective-permute-done.6.refs_1_), channel_id=1, source_target_pairs={{0,4},{4,8},{8,12},{12,14},{14,10},{10,6},{6,2},{2,0},{1,5},{5,9},... | collective-permute-start | bytes 835592 | tf_op jit(solution)/shard_map/ppermute | solution.py:430
  34.9 0.4 collective-permute-start.11
  35.4 0.8 project_queries.2
  36.2 1.3 %project_keys.7 = (bf16[256,1024]{1,0:T(8,128)(2,1)S(1)}, f32[8,128]{1,0:T(8,128)S(1)}) custom-call(bf16[64,2176]{1,0:T(8,128)(2,1)S(1)} %collective-permute-done.4.refs_0_, bf16[64,2176]{1,0:T(8,128)(2,1)S(1)} %collective-permute-done.6.refs_1_, bf16[64,2176]{1,0:T(8,128)(2,1)S(1)} %collective-permute-done.7.refs_2_, ...), custom_call_target="tpu_custom_call" | custom-call | tf_op jit(solution)/shard_map/project_keys/pallas_call | solution.py:101
  37.5 1.8 %collective-permute-done.9.refs_3_ = bf16[64,2176]{1,0:T(8,128)(2,1)S(1)} collective-permute-done((bf16[64,2176]{1,0:T(8,128)(2,1)S(1)}, bf16[64,2176]{1,0:T(8,128)(2,1)S(1)}, u32[]{:S(2)}, u32[]{:S(2)}) %collective-permute-start.9) | collective-permute-done | bytes 278560 | tf_op jit(solution)/shard_map/ppermute | solution.py:430
  39.3 1.6 %collective-permute-start.12 = (bf16[64,2176]{1,0:T(8,128)(2,1)S(1)}, bf16[64,2176]{1,0:T(8,128)(2,1)S(1)}, u32[]{:S(2)}, u32[]{:S(2)}) collective-permute-start(bf16[64,2176]{1,0:T(8,128)(2,1)S(1)} %collective-permute-done.8.refs_0_), channel_id=1, source_target_pairs={{0,4},{4,8},{8,12},{12,14},{14,10},{10,6},{6,2},{2,0},{1,5},{5,9},... | collective-permute-start | bytes 835592 | tf_op jit(solution)/shard_map/ppermute | solution.py:430
  40.9 0.4 collective-permute-start.13
  41.4 1.6 %project_values.7 = (bf16[2,256,1024]{2,1,0:T(8,128)(2,1)S(1)}, bf16[2,48,2048]{2,1,0:T(8,128)(2,1)S(1)}, f32[2,48,128]{2,1,0:T(8,128)S(1)}) custom-call(f32[8,128]{1,0:T(8,128)S(1)} %get-tuple-element.102.mark_ref, bf16[256,1024]{1,0:T(8,128)(2,1)S(1)} %get-tuple-element.103.keys_ref, bf16[64,2176]{1,0:T(8,128)(2,1)S(1)} %collective-permute-done.4.refs_0_, ...), custom_call_target="tpu_custom_call" | custom-call | tf_op jit(solution)/shard_map/project_values/pallas_call | solution.py:149
  43.0 0.1 collective-permute-done.10.refs_1_
  43.1 0.4 collective-permute-start.16
  43.6 1.7 %collective-permute-done.11.refs_2_ = bf16[64,2176]{1,0:T(8,128)(2,1)S(1)} collective-permute-done((bf16[64,2176]{1,0:T(8,128)(2,1)S(1)}, bf16[64,2176]{1,0:T(8,128)(2,1)S(1)}, u32[]{:S(2)}, u32[]{:S(2)}) %collective-permute-start.11) | collective-permute-done | bytes 278560 | tf_op jit(solution)/shard_map/ppermute | solution.py:430
  45.3 1.3 %project_keys.8 = (bf16[256,1024]{1,0:T(8,128)(2,1)S(1)}, f32[8,128]{1,0:T(8,128)S(1)}) custom-call(bf16[64,2176]{1,0:T(8,128)(2,1)S(1)} %collective-permute-done.8.refs_0_, bf16[64,2176]{1,0:T(8,128)(2,1)S(1)} %collective-permute-done.10.refs_1_, bf16[64,2176]{1,0:T(8,128)(2,1)S(1)} %collective-permute-done.11.refs_2_, ...), custom_call_target="tpu_custom_call" | custom-call | tf_op jit(solution)/shard_map/project_keys/pallas_call | solution.py:101
  46.6 1.6 %project_values.8 = (bf16[2,256,1024]{2,1,0:T(8,128)(2,1)S(1)}, bf16[2,48,2048]{2,1,0:T(8,128)(2,1)S(1)}, f32[2,48,128]{2,1,0:T(8,128)S(1)}) custom-call(f32[8,128]{1,0:T(8,128)S(1)} %get-tuple-element.108.mark_ref, bf16[256,1024]{1,0:T(8,128)(2,1)S(1)} %get-tuple-element.109.keys_ref, bf16[64,2176]{1,0:T(8,128)(2,1)S(1)} %collective-permute-done.8.refs_0_, ...), custom_call_target="tpu_custom_call" | custom-call | tf_op jit(solution)/shard_map/project_values/pallas_call | solution.py:149
  48.3 1.5 %collective-permute-done.13.refs_1_ = bf16[64,2176]{1,0:T(8,128)(2,1)S(1)} collective-permute-done((bf16[64,2176]{1,0:T(8,128)(2,1)S(1)}, bf16[64,2176]{1,0:T(8,128)(2,1)S(1)}, u32[]{:S(2)}, u32[]{:S(2)}) %collective-permute-start.13) | collective-permute-done | bytes 278560 | tf_op jit(solution)/shard_map/ppermute | solution.py:430
  49.8 0.5 collective-permute-start.14
  50.3 0.8 project_keys.9
  51.1 1.0 %project_values.9 = (bf16[2,128,1024]{2,1,0:T(8,128)(2,1)S(1)}, bf16[1,48,2048]{2,1,0:T(8,128)(2,1)S(1)}, f32[1,48,128]{2,1,0:T(8,128)S(1)}) custom-call(f32[8,128]{1,0:T(8,128)S(1)} %get-tuple-element.116.mark_ref, bf16[128,1024]{1,0:T(8,128)(2,1)S(1)} %get-tuple-element.117.keys_ref, bf16[64,2176]{1,0:T(8,128)(2,1)S(1)} %collective-permute-done.12.refs_0_, ...), custom_call_target="tpu_custom_call" | custom-call | tf_op jit(solution)/shard_map/project_values/pallas_call | solution.py:149
  52.1 0.1 collective-permute-start.18
  52.2 1.2 %project_queries.3 = (bf16[2,48,1024]{2,1,0:T(8,128)(2,1)S(1)}, bf16[2,48,1024]{2,1,0:T(8,128)(2,1)S(1)}, bf16[1,48,1024]{2,1,0:T(8,128)(2,1)S(1)}) custom-call(bf16[2,48,2048]{2,1,0:T(8,128)(2,1)S(1)} %get-tuple-element.121.refs_0_, bf16[2,48,2048]{2,1,0:T(8,128)(2,1)S(1)} %get-tuple-element.122.refs_1_, ...), custom_call_target="tpu_custom_call" | custom-call | tf_op jit(solution)/shard_map/project_queries/pallas_call | solution.py:178
  53.4 0.6 collective-permute-done.18.refs_9_
  54.1 0.7 arrange.1
  54.8 1.5 %copy-done.5 = bf16[1,1024,2048]{2,1,0:T(8,128)(2,1)S(1)} copy-done((bf16[1,1024,2048]{2,1,0:T(8,128)(2,1)S(1)}, bf16[1,1024,2048]{2,1,0:T(8,128)(2,1)}, u32[]{:S(2)}) %copy-start.5) | copy-done | bytes 4194328
  56.2 4.5 %attend.3 = (bf16[40,2048]{1,0:T(8,128)(2,1)S(1)}, bf16[40,2048]{1,0:T(8,128)(2,1)S(1)}) custom-call(bf16[2,16,128,1024]{3,2,1,0:T(8,128)(2,1)S(1)} %get-tuple-element.132.panel_ref, bf16[8,48,1024]{2,1,0:T(8,128)(2,1)S(1)} %get-tuple-element.133.queries_ref, f32[8,48,128]{2,1,0:T(8,128)S(1)} %get-tuple-element.140.places_ref, bf16[1024,2048]{1,0:T(8,128)(2,1)S(1)} %bitcast.5), custom_call_target="tpu_custom_call" | custom-call | flops 1207959552 | bytes 8388608 | tf_op jit(solution)/shard_map/attend/pallas_call | solution.py:316
  60.7 0.6 collective-permute-start.19
  61.3 2.2 %collective-permute-start.20 = (bf16[40,2048]{1,0:T(8,128)(2,1)S(1)}, bf16[40,2048]{1,0:T(8,128)(2,1)S(1)}, u32[]{:S(2)}, u32[]{:S(2)}) collective-permute-start(bf16[40,2048]{1,0:T(8,128)(2,1)S(1)} %get-tuple-element.146), channel_id=1, source_target_pairs={{0,10},{2,8},{4,14},{6,12},{8,2},{10,0},{12,6},{14,4},{1,11},{3,9}... | collective-permute-start | bytes 491528 | tf_op jit(solution)/shard_map/ppermute | solution.py:472
  63.4 5.3 %attend.4 = (bf16[40,2048]{1,0:T(8,128)(2,1)S(1)}, bf16[40,2048]{1,0:T(8,128)(2,1)S(1)}) custom-call(bf16[2,16,128,1024]{3,2,1,0:T(8,128)(2,1)S(1)} %get-tuple-element.132.panel_ref, bf16[8,48,1024]{2,1,0:T(8,128)(2,1)S(1)} %get-tuple-element.133.queries_ref, f32[8,48,128]{2,1,0:T(8,128)S(1)} %get-tuple-element.140.places_ref, bf16[1024,2048]{1,0:T(8,128)(2,1)S(1)} %bitcast.6), custom_call_target="tpu_custom_call" | custom-call | flops 1207959552 | bytes 8388608 | tf_op jit(solution)/shard_map/attend/pallas_call | solution.py:316
  68.8 5.0 %collective-permute-start.25 = (bf16[40,2048]{1,0:T(8,128)(2,1)S(1)}, bf16[40,2048]{1,0:T(8,128)(2,1)S(1)}, u32[]{:S(2)}, u32[]{:S(2)}) collective-permute-start(bf16[40,2048]{1,0:T(8,128)(2,1)S(1)} %get-tuple-element.154), channel_id=1, source_target_pairs={{0,14},{2,12},{4,10},{6,8},{8,6},{10,4},{12,2},{14,0},{1,15},{3,13... | collective-permute-start | bytes 491528 | tf_op jit(solution)/shard_map/ppermute | solution.py:472
  73.8 4.9 %attend.5 = (bf16[40,2048]{1,0:T(8,128)(2,1)S(1)}, bf16[40,2048]{1,0:T(8,128)(2,1)S(1)}, bf16[40,2048]{1,0:T(8,128)(2,1)S(1)}, bf16[40,2048]{1,0:T(8,128)(2,1)S(1)}) custom-call(bf16[2,16,128,1024]{3,2,1,0:T(8,128)(2,1)S(1)} %get-tuple-element.132.panel_ref, bf16[8,48,1024]{2,1,0:T(8,128)(2,1)S(1)} %get-tuple-element.133.queries_ref, ...), custom_call_target="tpu_custom_call" | custom-call | flops 2415919104 | bytes 8388608 | tf_op jit(solution)/shard_map/attend/pallas_call | solution.py:316
  78.7 4.1 %collective-permute-done.19.refs_4_ = bf16[40,2048]{1,0:T(8,128)(2,1)S(1)} collective-permute-done((bf16[40,2048]{1,0:T(8,128)(2,1)S(1)}, bf16[40,2048]{1,0:T(8,128)(2,1)S(1)}, u32[]{:S(2)}, u32[]{:S(2)}) %collective-permute-start.19) | collective-permute-done | bytes 163872 | tf_op jit(solution)/shard_map/ppermute | solution.py:472
  82.8 3.2 %collective-permute-done.20.refs_5_ = bf16[40,2048]{1,0:T(8,128)(2,1)S(1)} collective-permute-done((bf16[40,2048]{1,0:T(8,128)(2,1)S(1)}, bf16[40,2048]{1,0:T(8,128)(2,1)S(1)}, u32[]{:S(2)}, u32[]{:S(2)}) %collective-permute-start.20) | collective-permute-done | bytes 163872 | tf_op jit(solution)/shard_map/ppermute | solution.py:472
  86.0 1.7 %collective-permute-start.21 = (bf16[40,2048]{1,0:T(8,128)(2,1)S(1)}, bf16[40,2048]{1,0:T(8,128)(2,1)S(1)}, u32[]{:S(2)}, u32[]{:S(2)}) collective-permute-start(bf16[40,2048]{1,0:T(8,128)(2,1)S(1)} %get-tuple-element.148), channel_id=1, source_target_pairs={{0,2},{2,0},{4,6},{6,4},{8,10},{10,8},{12,14},{14,12},{1,3},{3,1},... | collective-permute-start | bytes 491528 | tf_op jit(solution)/shard_map/ppermute | solution.py:472
  87.7 1.7 %collective-permute-start.23 = (bf16[40,2048]{1,0:T(8,128)(2,1)S(1)}, bf16[40,2048]{1,0:T(8,128)(2,1)S(1)}, u32[]{:S(2)}, u32[]{:S(2)}) collective-permute-start(bf16[40,2048]{1,0:T(8,128)(2,1)S(1)} %get-tuple-element.150), channel_id=1, source_target_pairs={{0,6},{2,4},{4,2},{6,0},{8,14},{10,12},{12,10},{14,8},{1,7},{3,5},... | collective-permute-start | bytes 491528 | tf_op jit(solution)/shard_map/ppermute | solution.py:472
  89.5 0.5 fusion
  90.1 0.5 gate_mix.1.mix_ref
  90.6 2.5 %collective-permute-done.21.refs_1_ = bf16[40,2048]{1,0:T(8,128)(2,1)S(1)} collective-permute-done((bf16[40,2048]{1,0:T(8,128)(2,1)S(1)}, bf16[40,2048]{1,0:T(8,128)(2,1)S(1)}, u32[]{:S(2)}, u32[]{:S(2)}) %collective-permute-start.21) | collective-permute-done | bytes 163872 | tf_op jit(solution)/shard_map/ppermute | solution.py:472
  93.1 0.8 collective-permute-done.22.refs_2_
  93.9 1.5 %collective-permute-done.23.refs_3_ = bf16[40,2048]{1,0:T(8,128)(2,1)S(1)} collective-permute-done((bf16[40,2048]{1,0:T(8,128)(2,1)S(1)}, bf16[40,2048]{1,0:T(8,128)(2,1)S(1)}, u32[]{:S(2)}, u32[]{:S(2)}) %collective-permute-start.23) | collective-permute-done | bytes 163872 | tf_op jit(solution)/shard_map/ppermute | solution.py:472
  95.3 1.8 %combine.1 = bf16[128,2048]{1,0:T(8,128)(2,1)} custom-call(bf16[384,384]{1,0:T(8,128)(2,1)S(1)} %gate_mix.1.mix_ref, bf16[40,2048]{1,0:T(8,128)(2,1)S(1)} %get-tuple-element.147.refs_0_, bf16[40,2048]{1,0:T(8,128)(2,1)S(1)} %collective-permute-done.21.refs_1_, bf16[40,2048]{1,0:T(8,128)(2,1)S(1)} %collective-permute-done.22.refs_2_, ...), custom_call_target="tpu_custom_call" | custom-call | tf_op jit(solution)/shard_map/combine/pallas_call | solution.py:395
  (31 shorter events, 0.2 us)
Async XLA Ops:
  0.0 89.5 %copy-start = (f32[2048,8]{0,1:T(8,128)S(1)}, f32[2048,8]{0,1:T(8,128)}, u32[]{:S(2)}) copy-start(f32[2048,8]{0,1:T(8,128)} %param.10) | copy-start | bytes 196612
  0.0 1.1 %copy-start.7 = (bf16[128,2048]{1,0:T(8,128)(2,1)S(1)}, bf16[128,2048]{1,0:T(8,128)(2,1)}, u32[]{:S(2)}) copy-start(bf16[128,2048]{1,0:T(8,128)(2,1)} %refs_0_.1) | copy-start | bytes 1572868
  1.1 0.7 copy-start.8
  1.8 0.7 copy-start.9
  2.8 10.5 %collective-permute-start = (bf16[64,2176]{1,0:T(8,128)(2,1)S(1)}, bf16[64,2176]{1,0:T(8,128)(2,1)S(1)}, u32[]{:S(2)}, u32[]{:S(2)}) collective-permute-start(bf16[64,2176]{1,0:T(8,128)(2,1)S(1)} %get-tuple-element.80.top_ref.refs_0_), channel_id=1, source_target_pairs={{0,4},{4,8},{8,12},{12,14},{14,10},{10,6},{6,2},{2,0},{1,5},{5,9},... | collective-permute-start | bytes 835592 | tf_op jit(solution)/shard_map/ppermute | solution.py:430
  5.9 9.6 %collective-permute-start.1 = (bf16[64,2176]{1,0:T(8,128)(2,1)S(1)}, bf16[64,2176]{1,0:T(8,128)(2,1)S(1)}, u32[]{:S(2)}, u32[]{:S(2)}) collective-permute-start(bf16[64,2176]{1,0:T(8,128)(2,1)S(1)} %get-tuple-element.81.bottom_ref.refs_1_), channel_id=1, source_target_pairs={{4,0},{8,4},{12,8},{14,12},{10,14},{6,10},{2,6},{0,2},{5,1},{9,5},... | collective-permute-start | bytes 835592 | tf_op jit(solution)/shard_map/ppermute | solution.py:430
  5.9 15.5 %collective-permute-start.3 = (bf16[64,2176]{1,0:T(8,128)(2,1)S(1)}, bf16[64,2176]{1,0:T(8,128)(2,1)S(1)}, u32[]{:S(2)}, u32[]{:S(2)}) collective-permute-start(bf16[64,2176]{1,0:T(8,128)(2,1)S(1)} %get-tuple-element.80.top_ref.refs_0_), channel_id=1, source_target_pairs={{4,0},{8,4},{12,8},{14,12},{10,14},{6,10},{2,6},{0,2},{5,1},{9,5},... | collective-permute-start | bytes 835592 | tf_op jit(solution)/shard_map/ppermute | solution.py:430
  7.8 13.6 %collective-permute-start.2 = (bf16[64,2176]{1,0:T(8,128)(2,1)S(1)}, bf16[64,2176]{1,0:T(8,128)(2,1)S(1)}, u32[]{:S(2)}, u32[]{:S(2)}) collective-permute-start(bf16[64,2176]{1,0:T(8,128)(2,1)S(1)} %get-tuple-element.81.bottom_ref.refs_1_), channel_id=1, source_target_pairs={{0,4},{4,8},{8,12},{12,14},{14,10},{10,6},{6,2},{2,0},{1,5},{5,9},... | collective-permute-start | bytes 835592 | tf_op jit(solution)/shard_map/ppermute | solution.py:430
  7.9 2.2 %copy-start.1 = (bf16[2048,1024]{1,0:T(8,128)(2,1)S(1)}, bf16[2048,1024]{1,0:T(8,128)(2,1)}, u32[]{:S(2)}) copy-start(bf16[2048,1024]{1,0:T(8,128)(2,1)} %refs_2_.6) | copy-start | bytes 12582916
  10.1 13.3 %copy-start.2 = (bf16[2048,1024]{1,0:T(8,128)(2,1)S(1)}, bf16[2048,1024]{1,0:T(8,128)(2,1)}, u32[]{:S(2)}) copy-start(bf16[2048,1024]{1,0:T(8,128)(2,1)} %refs_2_.6) | copy-start | bytes 12582916
  15.5 9.8 %collective-permute-start.4 = (bf16[64,2176]{1,0:T(8,128)(2,1)S(1)}, bf16[64,2176]{1,0:T(8,128)(2,1)S(1)}, u32[]{:S(2)}, u32[]{:S(2)}) collective-permute-start(bf16[64,2176]{1,0:T(8,128)(2,1)S(1)} %collective-permute-done.refs_0_), channel_id=1, source_target_pairs={{0,4},{4,8},{8,12},{12,14},{14,10},{10,6},{6,2},{2,0},{1,5},{5,9},... | collective-permute-start | bytes 835592 | tf_op jit(solution)/shard_map/ppermute | solution.py:430
  17.0 10.4 %collective-permute-start.5 = (bf16[64,2176]{1,0:T(8,128)(2,1)S(1)}, bf16[64,2176]{1,0:T(8,128)(2,1)S(1)}, u32[]{:S(2)}, u32[]{:S(2)}) collective-permute-start(bf16[64,2176]{1,0:T(8,128)(2,1)S(1)} %collective-permute-done.1.refs_3_), channel_id=1, source_target_pairs={{4,0},{8,4},{12,8},{14,12},{10,14},{6,10},{2,6},{0,2},{5,1},{9,5},... | collective-permute-start | bytes 835592 | tf_op jit(solution)/shard_map/ppermute | solution.py:430
  17.5 2.2 %copy-start.3 = (bf16[2048,1024]{1,0:T(8,128)(2,1)S(1)}, bf16[2048,1024]{1,0:T(8,128)(2,1)}, u32[]{:S(2)}) copy-start(bf16[2048,1024]{1,0:T(8,128)(2,1)} %refs_2_.7) | copy-start | bytes 12582916
  19.7 9.8 %copy-start.4 = (bf16[2048,1024]{1,0:T(8,128)(2,1)S(1)}, bf16[2048,1024]{1,0:T(8,128)(2,1)}, u32[]{:S(2)}) copy-start(bf16[2048,1024]{1,0:T(8,128)(2,1)} %refs_2_.7) | copy-start | bytes 12582916
  21.4 9.8 %collective-permute-start.6 = (bf16[64,2176]{1,0:T(8,128)(2,1)S(1)}, bf16[64,2176]{1,0:T(8,128)(2,1)S(1)}, u32[]{:S(2)}, u32[]{:S(2)}) collective-permute-start(bf16[64,2176]{1,0:T(8,128)(2,1)S(1)} %collective-permute-done.2.refs_1_), channel_id=1, source_target_pairs={{0,4},{4,8},{8,12},{12,14},{14,10},{10,6},{6,2},{2,0},{1,5},{5,9},... | collective-permute-start | bytes 835592 | tf_op jit(solution)/shard_map/ppermute | solution.py:430
  23.0 10.4 %collective-permute-start.7 = (bf16[64,2176]{1,0:T(8,128)(2,1)S(1)}, bf16[64,2176]{1,0:T(8,128)(2,1)S(1)}, u32[]{:S(2)}, u32[]{:S(2)}) collective-permute-start(bf16[64,2176]{1,0:T(8,128)(2,1)S(1)} %collective-permute-done.3.refs_2_), channel_id=1, source_target_pairs={{4,0},{8,4},{12,8},{14,12},{10,14},{6,10},{2,6},{0,2},{5,1},{9,5},... | collective-permute-start | bytes 835592 | tf_op jit(solution)/shard_map/ppermute | solution.py:430
  24.7 10.7 %copy-start.6 = (bf16[1,2048,1024]{2,1,0:T(8,128)(2,1)S(1)}, bf16[1,2048,1024]{2,1,0:T(8,128)(2,1)}, u32[]{:S(2)}) copy-start(bf16[1,2048,1024]{2,1,0:T(8,128)(2,1)} %param.14) | copy-start | bytes 12582916
  27.4 10.1 %collective-permute-start.8 = (bf16[64,2176]{1,0:T(8,128)(2,1)S(1)}, bf16[64,2176]{1,0:T(8,128)(2,1)S(1)}, u32[]{:S(2)}, u32[]{:S(2)}) collective-permute-start(bf16[64,2176]{1,0:T(8,128)(2,1)S(1)} %collective-permute-done.4.refs_0_), channel_id=1, source_target_pairs={{0,4},{4,8},{8,12},{12,14},{14,10},{10,6},{6,2},{2,0},{1,5},{5,9},... | collective-permute-start | bytes 835592 | tf_op jit(solution)/shard_map/ppermute | solution.py:430
  29.0 10.4 %collective-permute-start.9 = (bf16[64,2176]{1,0:T(8,128)(2,1)S(1)}, bf16[64,2176]{1,0:T(8,128)(2,1)S(1)}, u32[]{:S(2)}, u32[]{:S(2)}) collective-permute-start(bf16[64,2176]{1,0:T(8,128)(2,1)S(1)} %collective-permute-done.5.refs_3_), channel_id=1, source_target_pairs={{4,0},{8,4},{12,8},{14,12},{10,14},{6,10},{2,6},{0,2},{5,1},{9,5},... | collective-permute-start | bytes 835592 | tf_op jit(solution)/shard_map/ppermute | solution.py:430
  33.4 9.8 %collective-permute-start.10 = (bf16[64,2176]{1,0:T(8,128)(2,1)S(1)}, bf16[64,2176]{1,0:T(8,128)(2,1)S(1)}, u32[]{:S(2)}, u32[]{:S(2)}) collective-permute-start(bf16[64,2176]{1,0:T(8,128)(2,1)S(1)} %collective-permute-done.6.refs_1_), channel_id=1, source_target_pairs={{0,4},{4,8},{8,12},{12,14},{14,10},{10,6},{6,2},{2,0},{1,5},{5,9},... | collective-permute-start | bytes 835592 | tf_op jit(solution)/shard_map/ppermute | solution.py:430
  34.9 10.4 %collective-permute-start.11 = (bf16[64,2176]{1,0:T(8,128)(2,1)S(1)}, bf16[64,2176]{1,0:T(8,128)(2,1)S(1)}, u32[]{:S(2)}, u32[]{:S(2)}) collective-permute-start(bf16[64,2176]{1,0:T(8,128)(2,1)S(1)} %collective-permute-done.7.refs_2_), channel_id=1, source_target_pairs={{4,0},{8,4},{12,8},{14,12},{10,14},{6,10},{2,6},{0,2},{5,1},{9,5},... | collective-permute-start | bytes 835592 | tf_op jit(solution)/shard_map/ppermute | solution.py:430
  39.3 8.9 %collective-permute-start.12 = (bf16[64,2176]{1,0:T(8,128)(2,1)S(1)}, bf16[64,2176]{1,0:T(8,128)(2,1)S(1)}, u32[]{:S(2)}, u32[]{:S(2)}) collective-permute-start(bf16[64,2176]{1,0:T(8,128)(2,1)S(1)} %collective-permute-done.8.refs_0_), channel_id=1, source_target_pairs={{0,4},{4,8},{8,12},{12,14},{14,10},{10,6},{6,2},{2,0},{1,5},{5,9},... | collective-permute-start | bytes 835592 | tf_op jit(solution)/shard_map/ppermute | solution.py:430
  40.9 8.9 %collective-permute-start.13 = (bf16[64,2176]{1,0:T(8,128)(2,1)S(1)}, bf16[64,2176]{1,0:T(8,128)(2,1)S(1)}, u32[]{:S(2)}, u32[]{:S(2)}) collective-permute-start(bf16[64,2176]{1,0:T(8,128)(2,1)S(1)} %collective-permute-done.9.refs_3_), channel_id=1, source_target_pairs={{4,0},{8,4},{12,8},{14,12},{10,14},{6,10},{2,6},{0,2},{5,1},{9,5},... | collective-permute-start | bytes 835592 | tf_op jit(solution)/shard_map/ppermute | solution.py:430
  41.4 12.1 %collective-permute-start.15 = (bf16[2,256,1024]{2,1,0:T(8,128)(2,1)S(1)}, bf16[2,256,1024]{2,1,0:T(8,128)(2,1)S(1)}, u32[]{:S(2)}, u32[]{:S(2)}) collective-permute-start(bf16[2,256,1024]{2,1,0:T(8,128)(2,1)S(1)} %get-tuple-element.91.refs_1_), channel_id=1, source_target_pairs={{0,1},{1,0},{2,3},{3,2},{4,5},{5,4},{6,7},{7,6},{8,9},{9,8},{10,11... | collective-permute-start | bytes 3145736 | tf_op jit(solution)/shard_map/ppermute | solution.py:433
  43.1 10.9 %collective-permute-start.16 = (bf16[2,256,1024]{2,1,0:T(8,128)(2,1)S(1)}, bf16[2,256,1024]{2,1,0:T(8,128)(2,1)S(1)}, u32[]{:S(2)}, u32[]{:S(2)}) collective-permute-start(bf16[2,256,1024]{2,1,0:T(8,128)(2,1)S(1)} %get-tuple-element.104.refs_2_), channel_id=1, source_target_pairs={{0,1},{1,0},{2,3},{3,2},{4,5},{5,4},{6,7},{7,6},{8,9},{9,8},{10,11... | collective-permute-start | bytes 3145736 | tf_op jit(solution)/shard_map/ppermute | solution.py:433
  49.8 4.3 %collective-permute-start.17 = (bf16[2,256,1024]{2,1,0:T(8,128)(2,1)S(1)}, bf16[2,256,1024]{2,1,0:T(8,128)(2,1)S(1)}, u32[]{:S(2)}, u32[]{:S(2)}) collective-permute-start(bf16[2,256,1024]{2,1,0:T(8,128)(2,1)S(1)} %get-tuple-element.113.refs_3_), channel_id=1, source_target_pairs={{0,1},{1,0},{2,3},{3,2},{4,5},{5,4},{6,7},{7,6},{8,9},{9,8},{10,11... | collective-permute-start | bytes 3145736 | tf_op jit(solution)/shard_map/ppermute | solution.py:433
  49.8 3.6 %collective-permute-start.14 = (bf16[2,128,1024]{2,1,0:T(8,128)(2,1)S(1)}, bf16[2,128,1024]{2,1,0:T(8,128)(2,1)S(1)}, u32[]{:S(2)}, u32[]{:S(2)}) collective-permute-start(bf16[2,128,1024]{2,1,0:T(8,128)(2,1)S(1)} %get-tuple-element.85.refs_0_), channel_id=1, source_target_pairs={{0,1},{1,0},{2,3},{3,2},{4,5},{5,4},{6,7},{7,6},{8,9},{9,8},{10,11... | collective-permute-start | bytes 1572872 | tf_op jit(solution)/shard_map/ppermute | solution.py:433
  52.1 2.0 %collective-permute-start.18 = (bf16[2,128,1024]{2,1,0:T(8,128)(2,1)S(1)}, bf16[2,128,1024]{2,1,0:T(8,128)(2,1)S(1)}, u32[]{:S(2)}, u32[]{:S(2)}) collective-permute-start(bf16[2,128,1024]{2,1,0:T(8,128)(2,1)S(1)} %get-tuple-element.118.refs_4_), channel_id=1, source_target_pairs={{0,1},{1,0},{2,3},{3,2},{4,5},{5,4},{6,7},{7,6},{8,9},{9,8},{10,11... | collective-permute-start | bytes 1572872 | tf_op jit(solution)/shard_map/ppermute | solution.py:433
  54.1 2.2 %copy-start.5 = (bf16[1,1024,2048]{2,1,0:T(8,128)(2,1)S(1)}, bf16[1,1024,2048]{2,1,0:T(8,128)(2,1)}, u32[]{:S(2)}) copy-start(bf16[1,1024,2048]{2,1,0:T(8,128)(2,1)} %param.15) | copy-start | bytes 12582916
  60.7 22.1 %collective-permute-start.19 = (bf16[40,2048]{1,0:T(8,128)(2,1)S(1)}, bf16[40,2048]{1,0:T(8,128)(2,1)S(1)}, u32[]{:S(2)}, u32[]{:S(2)}) collective-permute-start(bf16[40,2048]{1,0:T(8,128)(2,1)S(1)} %get-tuple-element.145), channel_id=1, source_target_pairs={{0,8},{2,10},{4,12},{6,14},{8,0},{10,2},{12,4},{14,6},{1,9},{3,11}... | collective-permute-start | bytes 491528 | tf_op jit(solution)/shard_map/ppermute | solution.py:472
  61.3 24.7 %collective-permute-start.20 = (bf16[40,2048]{1,0:T(8,128)(2,1)S(1)}, bf16[40,2048]{1,0:T(8,128)(2,1)S(1)}, u32[]{:S(2)}, u32[]{:S(2)}) collective-permute-start(bf16[40,2048]{1,0:T(8,128)(2,1)S(1)} %get-tuple-element.146), channel_id=1, source_target_pairs={{0,10},{2,8},{4,14},{6,12},{8,2},{10,0},{12,6},{14,4},{1,11},{3,9}... | collective-permute-start | bytes 491528 | tf_op jit(solution)/shard_map/ppermute | solution.py:472
  68.7 21.9 %collective-permute-start.24 = (bf16[40,2048]{1,0:T(8,128)(2,1)S(1)}, bf16[40,2048]{1,0:T(8,128)(2,1)S(1)}, u32[]{:S(2)}, u32[]{:S(2)}) collective-permute-start(bf16[40,2048]{1,0:T(8,128)(2,1)S(1)} %get-tuple-element.153), channel_id=1, source_target_pairs={{0,12},{2,14},{4,8},{6,10},{8,4},{10,6},{12,0},{14,2},{1,13},{3,15... | collective-permute-start | bytes 491528 | tf_op jit(solution)/shard_map/ppermute | solution.py:472
  68.8 21.8 %collective-permute-start.25 = (bf16[40,2048]{1,0:T(8,128)(2,1)S(1)}, bf16[40,2048]{1,0:T(8,128)(2,1)S(1)}, u32[]{:S(2)}, u32[]{:S(2)}) collective-permute-start(bf16[40,2048]{1,0:T(8,128)(2,1)S(1)} %get-tuple-element.154), channel_id=1, source_target_pairs={{0,14},{2,12},{4,10},{6,8},{8,6},{10,4},{12,2},{14,0},{1,15},{3,13... | collective-permute-start | bytes 491528 | tf_op jit(solution)/shard_map/ppermute | solution.py:472
  86.0 7.1 %collective-permute-start.21 = (bf16[40,2048]{1,0:T(8,128)(2,1)S(1)}, bf16[40,2048]{1,0:T(8,128)(2,1)S(1)}, u32[]{:S(2)}, u32[]{:S(2)}) collective-permute-start(bf16[40,2048]{1,0:T(8,128)(2,1)S(1)} %get-tuple-element.148), channel_id=1, source_target_pairs={{0,2},{2,0},{4,6},{6,4},{8,10},{10,8},{12,14},{14,12},{1,3},{3,1},... | collective-permute-start | bytes 491528 | tf_op jit(solution)/shard_map/ppermute | solution.py:472
  87.7 6.1 %collective-permute-start.22 = (bf16[40,2048]{1,0:T(8,128)(2,1)S(1)}, bf16[40,2048]{1,0:T(8,128)(2,1)S(1)}, u32[]{:S(2)}, u32[]{:S(2)}) collective-permute-start(bf16[40,2048]{1,0:T(8,128)(2,1)S(1)} %get-tuple-element.149), channel_id=1, source_target_pairs={{0,4},{2,6},{4,0},{6,2},{8,12},{10,14},{12,8},{14,10},{1,5},{3,7},... | collective-permute-start | bytes 491528 | tf_op jit(solution)/shard_map/ppermute | solution.py:472
  87.7 7.6 %collective-permute-start.23 = (bf16[40,2048]{1,0:T(8,128)(2,1)S(1)}, bf16[40,2048]{1,0:T(8,128)(2,1)S(1)}, u32[]{:S(2)}, u32[]{:S(2)}) collective-permute-start(bf16[40,2048]{1,0:T(8,128)(2,1)S(1)} %get-tuple-element.150), channel_id=1, source_target_pairs={{0,6},{2,4},{4,2},{6,0},{8,14},{10,12},{12,10},{14,8},{1,7},{3,5},... | collective-permute-start | bytes 491528 | tf_op jit(solution)/shard_map/ppermute | solution.py:472

commit v9 on v8

--- a/solution.py
+++ b/solution.py
@@ -14,6 +14,8 @@
 SLOTS = 48
 MASKED = -1e30
 LANES = 128
+CODES = 16
+TERMS = 3
 MIB = 1 << 20
 WHOLE = pl.BlockSpec(memory_space=pltpu.VMEM)
 
@@ -47,7 +49,7 @@
     count, width = floats.shape
     factor = lax.rsqrt(jnp.mean(floats * floats, axis=1, keepdims=True) + 1e-06)
     normed = (floats * factor * gain_ref[...]).astype(jnp.bfloat16)
-    expert = lax.broadcasted_iota(jnp.int32, (LANES, count), 0)
+    expert = lax.broadcasted_iota(jnp.int32, (CODES, count), 0)
     named = (expert == routes_ref[0:1, :]) | (expert == routes_ref[1:2, :])
     before = lax.broadcasted_iota(jnp.int32, (count, count), 0) < lax.broadcasted_iota(
         jnp.int32, (count, count), 1
@@ -57,20 +59,32 @@
         before.astype(jnp.bfloat16),
         preferred_element_type=jnp.float32,
     )
-    slots = jnp.where(named, rank, -1.0).T.astype(jnp.bfloat16)
+    codes = jnp.where(named, rank, -1.0).astype(jnp.bfloat16)
     half = count // 2
-    for ref, part in ((top_ref, slice(0, half)), (bottom_ref, slice(half, count))):
-        ref[:, :width] = normed[part]
-        ref[:, width:] = slots[part]
+    for ref, first in ((top_ref, 0), (bottom_ref, half)):
+        for c in range(width // LANES):
+            ref[pl.ds(c * half, half), :] = normed[
+                first : first + half, c * LANES : (c + 1) * LANES
+            ]
+        ref[pl.ds(width // LANES * half, CODES), :] = codes
+
+
+def message_rows(ref, half):
+    tiles = (ref.shape[0] - CODES) // half
+    return jnp.concatenate([ref[pl.ds(c * half, half), :] for c in range(tiles)], axis=1)
+
+
+def message_codes(ref):
+    return ref[pl.ds(ref.shape[0] - CODES, CODES), :].astype(jnp.float32)
 
 
 def norm_rows(tokens, norm_gain, routes):
     count, width = tokens.shape
-    half = jax.ShapeDtypeStruct((count // 2, width + LANES), jnp.bfloat16)
+    half = jax.ShapeDtypeStruct((width // LANES * (count // 2) + CODES, LANES), jnp.bfloat16)
     operands = (tokens, norm_gain.reshape(1, -1), routes.T)
     return pl.pallas_call(
         norm_kernel,
-        in_specs=[pl.BlockSpec(memory_space=pl.ANY)] * 3,
+        in_specs=[pl.BlockSpec(memory_space=pltpu.HBM)] * 3,
         out_specs=[WHOLE] * 2,
         out_shape=[half, half],
         scratch_shapes=[pltpu.VMEM(x.shape, x.dtype) for x in operands]
@@ -85,21 +99,21 @@
     return [pl.ds(start, step) for start in range(0, ref.shape[1], step)]
 
 
-def keys_kernel(count, *refs):
+def keys_kernel(half, count, *refs):
     blocks = refs[:count]
     weight_ref, panel_ref, mark_ref = refs[count:]
-    rows = jnp.concatenate([block[:, : weight_ref.shape[0]] for block in blocks], axis=0)
+    rows = jnp.concatenate([message_rows(block, half) for block in blocks], axis=0)
     for cols in column_parts(weight_ref):
         product = jnp.dot(rows, weight_ref[:, cols], preferred_element_type=jnp.float32)
         panel_ref[:, cols] = product.astype(jnp.bfloat16)
     mark_ref[...] = product[:8, :LANES]
 
 
-def project_keys(blocks, key_weight):
-    row_count = sum(block.shape[0] for block in blocks)
+def project_keys(half, blocks, key_weight):
+    row_count = half * len(blocks)
     width = key_weight.shape[1]
     return pl.pallas_call(
-        functools.partial(keys_kernel, len(blocks)),
+        functools.partial(keys_kernel, half, len(blocks)),
         in_specs=[WHOLE] * (len(blocks) + 1),
         out_specs=[WHOLE] * 2,
         out_shape=[
@@ -111,23 +125,20 @@
     )(*blocks, key_weight)
 
 
-def values_kernel(offsets, count, experts, mark_ref, keys_ref, *refs):
+def values_kernel(half, offsets, count, experts, mark_ref, keys_ref, *refs):
     blocks = refs[:count]
     value_ref, panel_ref, picked_ref, pos_ref = refs[count:]
-    width = value_ref.shape[0]
-    rows = jnp.concatenate([block[:, :width] for block in blocks], axis=0)
-    tok_count = rows.shape[0] // len(offsets)
-
-    slots = jnp.concatenate([block[:, width:] for block in blocks], axis=0)
-    slots = slots.astype(jnp.float32)
+    rows = jnp.concatenate([message_rows(block, half) for block in blocks], axis=0)
+    tok_count = 2 * half
     expert = lax.axis_index("ctx") // (lax.axis_size("ctx") // experts)
-    lane = lax.broadcasted_iota(jnp.int32, slots.shape, 1)
-    slot = jnp.sum(jnp.where(lane == expert, slots, 0.0), axis=1, keepdims=True)
-    select = (slot == lane.astype(jnp.float32)).astype(jnp.float32)
     number = lax.broadcasted_iota(jnp.int32, (tok_count, LANES), 0).astype(jnp.bfloat16)
     for g, offset in enumerate(offsets):
         part = slice(g * tok_count, (g + 1) * tok_count)
-        chosen = select[part].T[:SLOTS].astype(jnp.bfloat16)
+        codes = message_codes(blocks[2 * g])
+        mine = lax.broadcasted_iota(jnp.int32, codes.shape, 0) == expert
+        slot = jnp.sum(jnp.where(mine, codes, 0.0), axis=0, keepdims=True)
+        order = lax.broadcasted_iota(jnp.int32, (SLOTS, tok_count), 0).astype(jnp.float32)
+        chosen = (order == slot).astype(jnp.bfloat16)
         picked_ref[g] = jnp.dot(
             chosen, rows[part], preferred_element_type=jnp.float32
         ).astype(jnp.bfloat16)
@@ -142,12 +153,12 @@
         ).astype(jnp.bfloat16)
 
 
-def project_values(blocks, offsets, mark, keys, value_weight):
-    row_count = sum(block.shape[0] for block in blocks)
+def project_values(half, blocks, offsets, mark, keys, value_weight):
+    row_count = half * len(blocks)
     model_width, width = value_weight.shape
     owners = len(offsets)
     return pl.pallas_call(
-        functools.partial(values_kernel, offsets, len(blocks), EXPERTS),
+        functools.partial(values_kernel, half, offsets, len(blocks), EXPERTS),
         in_specs=[WHOLE] * (len(blocks) + 3),
         out_specs=[WHOLE] * 3,
         out_shape=[
@@ -222,7 +233,7 @@
         out_specs=[WHOLE] * 3,
         out_shape=shapes,
         compiler_params=pltpu.CompilerParams(
-            vmem_limit_bytes=owners * tok_count * width * 24 + 4 * MIB
+            vmem_limit_bytes=8 * MIB
         ),
         name="arrange",
     )(*operands)
@@ -333,42 +344,51 @@
     )(panel, queries, places, output_slab)
 
 
-def mix_kernel(quarter_count, top_ref, bottom_ref, logits_ref, mix_ref):
-    slots = jnp.concatenate([top_ref[...], bottom_ref[...]], axis=0).astype(jnp.float32)
-    tok_count = slots.shape[0]
-    logits = jnp.where(slots >= 0, logits_ref[...], -jnp.inf)
-    raised = jnp.exp(logits - jnp.max(logits, axis=1, keepdims=True))
-    gates = raised / jnp.sum(raised, axis=1, keepdims=True)
-    lane = lax.broadcasted_iota(jnp.int32, slots.shape, 1)
-    count = mix_ref.shape[1] // SLOTS
-    wide = lax.broadcasted_iota(jnp.int32, (tok_count, count * SLOTS), 1).astype(jnp.float32)
-    total = jnp.zeros_like(wide)
-    for k in range(count):
-        mine = lane == (lax.axis_index("ctx") ^ k) // quarter_count
-        slot = jnp.sum(jnp.where(mine, slots, 0.0), axis=1, keepdims=True)
-        gate = jnp.sum(jnp.where(mine, gates, 0.0), axis=1, keepdims=True)
-        spot = jnp.where(slot >= 0, slot + float(k * SLOTS), -1.0)
-        total = total + jnp.where(wide == spot, gate, 0.0)
-    for part in range(3):
+def mix_kernel(quarter_count, top_ref, bottom_ref, router_ref, mix_ref, slots_ref, gates_ref):
+    half = LANES // 2
+    rows = jnp.concatenate([message_rows(ref, half) for ref in (top_ref, bottom_ref)], axis=0)
+    rest, terms = router_ref[...], []
+    for _ in range(3):
+        terms.append(rest.astype(jnp.bfloat16).astype(jnp.float32))
+        rest = rest - terms[-1]
+    experts = rest.shape[0]
+    router = jnp.concatenate([*terms, jnp.zeros_like(rest)], axis=0).astype(jnp.bfloat16)
+    products = lax.dot_general(
+        router, rows, (((1,), (1,)), ((), ())), preferred_element_type=jnp.float32
+    )
+    logits = products[:experts] + (
+        products[experts : 2 * experts] + products[2 * experts : 3 * experts]
+    )
+    slots = message_codes(top_ref)[:experts]
+    logits = jnp.where(slots >= 0, logits, -jnp.inf)
+    raised = jnp.exp(logits - jnp.max(logits, axis=0, keepdims=True))
+    slots_ref[...] = slots
+    gates_ref[...] = raised / jnp.sum(raised, axis=0, keepdims=True)
+    tok_count = slots.shape[1]
+    order = lax.broadcasted_iota(jnp.int32, (SLOTS, tok_count), 0).astype(jnp.float32)
+    parts = []
+    for k in range(mix_ref.shape[1] // SLOTS):
+        expert = pl.ds((lax.axis_index("ctx") ^ k) // quarter_count, 1)
+        parts.append(jnp.where(order == slots_ref[expert, :], gates_ref[expert, :], 0.0))
+    total = jnp.concatenate(parts, axis=0).T
+    for part in range(TERMS):
         term = total.astype(jnp.bfloat16)
         mix_ref[pl.ds(part * tok_count, tok_count), :] = term
         total = total - term.astype(jnp.float32)
 
 
-def gate_mix(quarter_count, halves, logits, count):
-    half, width = halves[0].shape
-    tok_count = 2 * half
-    lanes = width // LANES - 1
+def gate_mix(quarter_count, halves, router, count):
+    tok_count = LANES
+    held = pltpu.VMEM((router.shape[0], tok_count), jnp.float32)
     return pl.pallas_call(
         functools.partial(mix_kernel, quarter_count),
-        grid=(1,),
-        in_specs=[pl.BlockSpec((half, LANES), lambda n: (0, lanes))] * 2
-        + [pl.BlockSpec((tok_count, LANES), lambda n: (0, 0))],
-        out_specs=pl.BlockSpec((3 * tok_count, count * SLOTS), lambda n: (0, 0)),
-        out_shape=jax.ShapeDtypeStruct((3 * tok_count, count * SLOTS), jnp.bfloat16),
+        in_specs=[WHOLE] * 3,
+        out_specs=WHOLE,
+        out_shape=jax.ShapeDtypeStruct((TERMS * tok_count, count * SLOTS), jnp.bfloat16),
+        scratch_shapes=[held, held],
         compiler_params=pltpu.CompilerParams(vmem_limit_bytes=16 * MIB),
         name="gate_mix",
-    )(*halves, logits)
+    )(*halves, router)
 
 
 def combine_kernel(mix_ref, *refs):
@@ -383,14 +403,14 @@
             rows += [piece[:, cols].astype(jnp.float32), spare]
         rows = jnp.concatenate(rows, axis=0).astype(jnp.bfloat16)
         product = jnp.dot(mix_ref[...], rows, preferred_element_type=jnp.float32)
-        total = product[:tok_count] + (
-            product[tok_count : 2 * tok_count] + product[2 * tok_count :]
-        )
+        total = product[-tok_count:]
+        for part in range(TERMS - 2, -1, -1):
+            total = product[part * tok_count : (part + 1) * tok_count] + total
         out_ref[:, cols] = total.astype(jnp.bfloat16)
 
 
 def combine(mix, pieces):
-    tok_count = mix.shape[0] // 3
+    tok_count = mix.shape[0] // TERMS
     model_width = pieces[0].shape[1]
     return pl.pallas_call(
         combine_kernel,
@@ -422,6 +442,7 @@
         value_weight = lax.dynamic_slice_in_dim(value_weight, first, head_width, axis=1)
 
     halves = norm_rows(tokens, norm_gain, routes)
+    token_half = tok_count // 2
     steps = ctx_count // 2
     plan = [[0]] + [[-step, step] for step in range(1, steps)] + [[steps]]
     own, other, picked, queries, positions = [], [], [], [], []
@@ -439,7 +460,7 @@
     lead = send([halves[0], halves[1]])
     rest = send([halves[1], halves[0]])
     for step in range(steps):
-        keys, mark = project_keys(blocks, key_weight)
+        keys, mark = project_keys(token_half, blocks, key_weight)
         following = [lead[0], rest[0], rest[1], lead[1]]
         if step == steps - 2:
             queries = project_queries(picked, query_slab)
@@ -448,7 +469,7 @@
             mark, *lead_next = tie(mark, *lead, *queries)
             queries = lead_next[2:]
             lead = send(lead_next[:2])
-        panel, rows, position = project_values(blocks, plan[step], mark, keys, value_weight)
+        panel, rows, position = project_values(token_half, blocks, plan[step], mark, keys, value_weight)
         if step < steps - 2:
             position, *rest_next = tie(position, *rest)
             rest = send(rest_next)
@@ -460,8 +481,8 @@
         blocks = following
     own[-1], *blocks = tie(own[-1], *lead)
     other.append(hand_over(own[-1]))
-    keys, mark = project_keys(blocks, key_weight)
-    panel, rows, position = project_values(blocks, plan[-1], mark, keys, value_weight)
+    keys, mark = project_keys(token_half, blocks, key_weight)
+    panel, rows, position = project_values(token_half, blocks, plan[-1], mark, keys, value_weight)
     own.append(panel)
     other.append(hand_over(panel))
     positions.append(position)
@@ -481,14 +502,10 @@
             far.append([swap(piece, start + r) for r, piece in enumerate(pieces)])
         else:
             near = pieces
-    tied = tie(*near, *far[0])
-    near, far[0] = tied[:half], tied[half:]
+    *near, far[0][0] = tie(*near, far[0][0])
     near = [near[0]] + [swap(near[r], r) for r in range(1, half)]
 
-    normed = jnp.concatenate([part[:, :model_width] for part in halves], axis=0)
-    logits = jnp.dot(normed.astype(jnp.float32), router_weight, precision=lax.Precision.HIGHEST)
-    logits = jnp.pad(logits, ((0, 0), (0, LANES - EXPERTS)))
-    mix = gate_mix(quarter_count, halves, logits, ctx_count)
+    mix = gate_mix(quarter_count, halves, router_weight.T, ctx_count)
     return combine(mix, [*near, *far[0], *far[1]])
 
 

time: 97.4 us -> 93.2 us (0.957)
  starting transfers between devices: 27.6 us -> 24.7 us
    ppermute x7, starting transfers between devices: 11.3 us -> 8.31 us  [swap(): return lax.ppermute(piece, 'ctx', [(c, c ^ k) for c in range(ctx_count)])]
    ppermute x7, waiting for transfers between devices: 12 us -> 13.3 us  [swap(): return lax.ppermute(piece, 'ctx', [(c, c ^ k) for c in range(ctx_count)])]
  transfers between devices with their start and end apart: 26 -> 26, of which waited for: 17 -> 17; matrix products, arithmetic and copies ran while one was open for 1% -> 0% of each run, Pallas kernels for 26% -> 26%
where the time goes in v9:
time: 93.2 us; the launch traced here: 92.8 us
  Pallas kernels  31.3 us (34%)
  waiting for transfers between devices  28.3 us (30%)
  starting transfers between devices  24.7 us (27%)
  local copies, waits for them, and re-layouts  8.3 us (9%)
    pallas_call x3, Pallas kernels, attend(): pl.pallas_call(functools.partial(attend_kernel, lots, heads), in_specs=[W...  14.6 us
    ppermute x7, waiting for transfers between devices, swap(): return lax.ppermute(piece, 'ctx', [(c, c ^ k) for c in range(ctx_count)])  13.3 us
    ppermute x7, waiting for transfers between devices, send(): lax.ppermute(parts[1], 'ctx', backward)  11.5 us
    ppermute x7, starting transfers between devices, send(): lax.ppermute(parts[0], 'ctx', forward)  11.1 us
    ppermute x7, starting transfers between devices, swap(): return lax.ppermute(piece, 'ctx', [(c, c ^ k) for c in range(ctx_count)])  8.31 us
    unnamed x20, local copies, waits for them, and re-layouts  8.3 us
    pallas_call x5, Pallas kernels, project_values(): pl.pallas_call(functools.partial(values_kernel, half, offsets, len(blocks...  6.15 us
    pallas_call x5, Pallas kernels, project_keys(): pl.pallas_call(functools.partial(keys_kernel, half, len(blocks)), in_spec...  5.27 us
  transfers between devices with their start and end apart: 26, of which 17 were waited for; matrix products, arithmetic and copies ran while one was open for 0% of the time, Pallas kernels for 26%

profile of v9, /device:TPU:0, one launch (start us, length us, event | category | flops | bytes accessed | tf_op | source)
XLA Modules:
  0.0 92.8 jit_solution(1379319203692305081)
XLA Ops:
  0.0 1.0 %copy-done.6 = bf16[128,2048]{1,0:T(8,128)(2,1)S(1)} copy-done((bf16[128,2048]{1,0:T(8,128)(2,1)S(1)}, bf16[128,2048]{1,0:T(8,128)(2,1)}, u32[]{:S(2)}) %copy-start.6) | copy-done | bytes 524312
  1.0 0.7 copy-done.8
  1.7 0.7 copy-done.9
  2.4 0.3 norm_rows.1
  2.7 3.1 %collective-permute-start = (bf16[1040,128]{1,0:T(8,128)(2,1)S(1)}, bf16[1040,128]{1,0:T(8,128)(2,1)S(1)}, u32[]{:S(2)}, u32[]{:S(2)}) collective-permute-start(bf16[1040,128]{1,0:T(8,128)(2,1)S(1)} %get-tuple-element.79.top_ref.refs_0_), channel_id=1, source_target_pairs={{0,4},{4,8},{8,12},{12,14},{14,10},{10,6},{6,2},{2,0},{1,5},{5,9},... | collective-permute-start | bytes 798728 | tf_op jit(solution)/shard_map/ppermute | solution.py:451
  5.8 2.0 %collective-permute-start.3 = (bf16[1040,128]{1,0:T(8,128)(2,1)S(1)}, bf16[1040,128]{1,0:T(8,128)(2,1)S(1)}, u32[]{:S(2)}, u32[]{:S(2)}) collective-permute-start(bf16[1040,128]{1,0:T(8,128)(2,1)S(1)} %get-tuple-element.79.top_ref.refs_0_), channel_id=1, source_target_pairs={{4,0},{8,4},{12,8},{14,12},{10,14},{6,10},{2,6},{0,2},{5,1},{9,5},... | collective-permute-start | bytes 798728 | tf_op jit(solution)/shard_map/ppermute | solution.py:451
  7.8 0.1 collective-permute-start.2
  7.9 2.2 %copy-done = bf16[2048,1024]{1,0:T(8,128)(2,1)S(1)} copy-done((bf16[2048,1024]{1,0:T(8,128)(2,1)S(1)}, bf16[2048,1024]{1,0:T(8,128)(2,1)}, u32[]{:S(2)}) %copy-start) | copy-done | bytes 4194328
  10.1 0.7 project_keys.5
  10.8 2.2 %collective-permute-done.refs_0_ = bf16[1040,128]{1,0:T(8,128)(2,1)S(1)} collective-permute-done((bf16[1040,128]{1,0:T(8,128)(2,1)S(1)}, bf16[1040,128]{1,0:T(8,128)(2,1)S(1)}, u32[]{:S(2)}, u32[]{:S(2)}) %collective-permute-start) | collective-permute-done | bytes 266272 | tf_op jit(solution)/shard_map/ppermute | solution.py:451
  13.0 2.2 %collective-permute-done.1.refs_3_ = bf16[1040,128]{1,0:T(8,128)(2,1)S(1)} collective-permute-done((bf16[1040,128]{1,0:T(8,128)(2,1)S(1)}, bf16[1040,128]{1,0:T(8,128)(2,1)S(1)}, u32[]{:S(2)}, u32[]{:S(2)}) %collective-permute-start.1) | collective-permute-done | bytes 266272 | tf_op jit(solution)/shard_map/ppermute | solution.py:451
  15.1 1.6 %collective-permute-start.4 = (bf16[1040,128]{1,0:T(8,128)(2,1)S(1)}, bf16[1040,128]{1,0:T(8,128)(2,1)S(1)}, u32[]{:S(2)}, u32[]{:S(2)}) collective-permute-start(bf16[1040,128]{1,0:T(8,128)(2,1)S(1)} %collective-permute-done.refs_0_), channel_id=1, source_target_pairs={{0,4},{4,8},{8,12},{12,14},{14,10},{10,6},{6,2},{2,0},{1,5},{5,9},... | collective-permute-start | bytes 798728 | tf_op jit(solution)/shard_map/ppermute | solution.py:451
  16.7 0.4 collective-permute-start.5
  17.2 2.2 %copy-done.2 = bf16[2048,1024]{1,0:T(8,128)(2,1)S(1)} copy-done((bf16[2048,1024]{1,0:T(8,128)(2,1)S(1)}, bf16[2048,1024]{1,0:T(8,128)(2,1)}, u32[]{:S(2)}) %copy-start.2) | copy-done | bytes 4194328
  19.3 0.8 project_values.5
  20.2 0.6 collective-permute-done.3.refs_2_
  20.8 1.6 %collective-permute-start.6 = (bf16[1040,128]{1,0:T(8,128)(2,1)S(1)}, bf16[1040,128]{1,0:T(8,128)(2,1)S(1)}, u32[]{:S(2)}, u32[]{:S(2)}) collective-permute-start(bf16[1040,128]{1,0:T(8,128)(2,1)S(1)} %collective-permute-done.2.refs_1_), channel_id=1, source_target_pairs={{0,4},{4,8},{8,12},{12,14},{14,10},{10,6},{6,2},{2,0},{1,5},{5,9},... | collective-permute-start | bytes 798728 | tf_op jit(solution)/shard_map/ppermute | solution.py:451
  22.4 0.4 collective-permute-start.7
  22.9 1.3 %project_keys.6 = (bf16[256,1024]{1,0:T(8,128)(2,1)S(1)}, f32[8,128]{1,0:T(8,128)S(1)}) custom-call(bf16[1040,128]{1,0:T(8,128)(2,1)S(1)} %collective-permute-done.refs_0_, bf16[1040,128]{1,0:T(8,128)(2,1)S(1)} %collective-permute-done.2.refs_1_, bf16[1040,128]{1,0:T(8,128)(2,1)S(1)} %collective-permute-done.3.refs_2_, ...), custom_call_target="tpu_custom_call" | custom-call | tf_op jit(solution)/shard_map/project_keys/pallas_call | solution.py:115
  24.2 0.3 collective-permute-done.4.refs_0_
  24.5 2.1 %collective-permute-done.5.refs_3_ = bf16[1040,128]{1,0:T(8,128)(2,1)S(1)} collective-permute-done((bf16[1040,128]{1,0:T(8,128)(2,1)S(1)}, bf16[1040,128]{1,0:T(8,128)(2,1)S(1)}, u32[]{:S(2)}, u32[]{:S(2)}) %collective-permute-start.5) | collective-permute-done | bytes 266272 | tf_op jit(solution)/shard_map/ppermute | solution.py:451
  26.5 1.6 %collective-permute-start.8 = (bf16[1040,128]{1,0:T(8,128)(2,1)S(1)}, bf16[1040,128]{1,0:T(8,128)(2,1)S(1)}, u32[]{:S(2)}, u32[]{:S(2)}) collective-permute-start(bf16[1040,128]{1,0:T(8,128)(2,1)S(1)} %collective-permute-done.4.refs_0_), channel_id=1, source_target_pairs={{0,4},{4,8},{8,12},{12,14},{14,10},{10,6},{6,2},{2,0},{1,5},{5,9},... | collective-permute-start | bytes 798728 | tf_op jit(solution)/shard_map/ppermute | solution.py:451
  28.1 0.4 collective-permute-start.9
  28.6 1.5 %project_values.6 = (bf16[2,256,1024]{2,1,0:T(8,128)(2,1)S(1)}, bf16[2,48,2048]{2,1,0:T(8,128)(2,1)S(1)}, f32[2,48,128]{2,1,0:T(8,128)S(1)}) custom-call(f32[8,128]{1,0:T(8,128)S(1)} %get-tuple-element.88.mark_ref, bf16[256,1024]{1,0:T(8,128)(2,1)S(1)} %get-tuple-element.89.keys_ref, bf16[1040,128]{1,0:T(8,128)(2,1)S(1)} %collective-permute-done.refs_0_, ...), custom_call_target="tpu_custom_call" | custom-call | tf_op jit(solution)/shard_map/project_values/pallas_call | solution.py:160
  30.1 0.1 collective-permute-done.6.refs_1_
  30.2 2.1 %collective-permute-done.7.refs_2_ = bf16[1040,128]{1,0:T(8,128)(2,1)S(1)} collective-permute-done((bf16[1040,128]{1,0:T(8,128)(2,1)S(1)}, bf16[1040,128]{1,0:T(8,128)(2,1)S(1)}, u32[]{:S(2)}, u32[]{:S(2)}) %collective-permute-start.7) | collective-permute-done | bytes 266272 | tf_op jit(solution)/shard_map/ppermute | solution.py:451
  32.2 1.6 %collective-permute-start.10 = (bf16[1040,128]{1,0:T(8,128)(2,1)S(1)}, bf16[1040,128]{1,0:T(8,128)(2,1)S(1)}, u32[]{:S(2)}, u32[]{:S(2)}) collective-permute-start(bf16[1040,128]{1,0:T(8,128)(2,1)S(1)} %collective-permute-done.6.refs_1_), channel_id=1, source_target_pairs={{0,4},{4,8},{8,12},{12,14},{14,10},{10,6},{6,2},{2,0},{1,5},{5,9},... | collective-permute-start | bytes 798728 | tf_op jit(solution)/shard_map/ppermute | solution.py:451
  33.8 0.4 collective-permute-start.11
  34.3 0.8 project_queries.2
  35.1 1.3 %project_keys.7 = (bf16[256,1024]{1,0:T(8,128)(2,1)S(1)}, f32[8,128]{1,0:T(8,128)S(1)}) custom-call(bf16[1040,128]{1,0:T(8,128)(2,1)S(1)} %collective-permute-done.4.refs_0_, bf16[1040,128]{1,0:T(8,128)(2,1)S(1)} %collective-permute-done.6.refs_1_, bf16[1040,128]{1,0:T(8,128)(2,1)S(1)} %collective-permute-done.7.refs_2_, ...), custom_call_target="tpu_custom_call" | custom-call | tf_op jit(solution)/shard_map/project_keys/pallas_call | solution.py:115
  36.4 1.6 %collective-permute-done.9.refs_3_ = bf16[1040,128]{1,0:T(8,128)(2,1)S(1)} collective-permute-done((bf16[1040,128]{1,0:T(8,128)(2,1)S(1)}, bf16[1040,128]{1,0:T(8,128)(2,1)S(1)}, u32[]{:S(2)}, u32[]{:S(2)}) %collective-permute-start.9) | collective-permute-done | bytes 266272 | tf_op jit(solution)/shard_map/ppermute | solution.py:451
  38.0 1.6 %collective-permute-start.12 = (bf16[1040,128]{1,0:T(8,128)(2,1)S(1)}, bf16[1040,128]{1,0:T(8,128)(2,1)S(1)}, u32[]{:S(2)}, u32[]{:S(2)}) collective-permute-start(bf16[1040,128]{1,0:T(8,128)(2,1)S(1)} %collective-permute-done.8.refs_0_), channel_id=1, source_target_pairs={{0,4},{4,8},{8,12},{12,14},{14,10},{10,6},{6,2},{2,0},{1,5},{5,9},... | collective-permute-start | bytes 798728 | tf_op jit(solution)/shard_map/ppermute | solution.py:451
  39.5 0.4 collective-permute-start.13
  40.0 1.5 %project_values.7 = (bf16[2,256,1024]{2,1,0:T(8,128)(2,1)S(1)}, bf16[2,48,2048]{2,1,0:T(8,128)(2,1)S(1)}, f32[2,48,128]{2,1,0:T(8,128)S(1)}) custom-call(f32[8,128]{1,0:T(8,128)S(1)} %get-tuple-element.101.mark_ref, bf16[256,1024]{1,0:T(8,128)(2,1)S(1)} %get-tuple-element.102.keys_ref, bf16[1040,128]{1,0:T(8,128)(2,1)S(1)} %collective-permute-done.4.refs_0_, ...), custom_call_target="tpu_custom_call" | custom-call | tf_op jit(solution)/shard_map/project_values/pallas_call | solution.py:160
  41.5 0.1 collective-permute-done.10.refs_1_
  41.6 0.5 collective-permute-start.16
  42.1 1.6 %collective-permute-done.11.refs_2_ = bf16[1040,128]{1,0:T(8,128)(2,1)S(1)} collective-permute-done((bf16[1040,128]{1,0:T(8,128)(2,1)S(1)}, bf16[1040,128]{1,0:T(8,128)(2,1)S(1)}, u32[]{:S(2)}, u32[]{:S(2)}) %collective-permute-start.11) | collective-permute-done | bytes 266272 | tf_op jit(solution)/shard_map/ppermute | solution.py:451
  43.7 1.3 %project_keys.8 = (bf16[256,1024]{1,0:T(8,128)(2,1)S(1)}, f32[8,128]{1,0:T(8,128)S(1)}) custom-call(bf16[1040,128]{1,0:T(8,128)(2,1)S(1)} %collective-permute-done.8.refs_0_, bf16[1040,128]{1,0:T(8,128)(2,1)S(1)} %collective-permute-done.10.refs_1_, bf16[1040,128]{1,0:T(8,128)(2,1)S(1)} %collective-permute-done.11.refs_2_, ...), custom_call_target="tpu_custom_call" | custom-call | tf_op jit(solution)/shard_map/project_keys/pallas_call | solution.py:115
  44.9 1.5 %project_values.8 = (bf16[2,256,1024]{2,1,0:T(8,128)(2,1)S(1)}, bf16[2,48,2048]{2,1,0:T(8,128)(2,1)S(1)}, f32[2,48,128]{2,1,0:T(8,128)S(1)}) custom-call(f32[8,128]{1,0:T(8,128)S(1)} %get-tuple-element.107.mark_ref, bf16[256,1024]{1,0:T(8,128)(2,1)S(1)} %get-tuple-element.108.keys_ref, bf16[1040,128]{1,0:T(8,128)(2,1)S(1)} %collective-permute-done.8.refs_0_, ...), custom_call_target="tpu_custom_call" | custom-call | tf_op jit(solution)/shard_map/project_values/pallas_call | solution.py:160
  46.5 1.4 %collective-permute-done.13.refs_1_ = bf16[1040,128]{1,0:T(8,128)(2,1)S(1)} collective-permute-done((bf16[1040,128]{1,0:T(8,128)(2,1)S(1)}, bf16[1040,128]{1,0:T(8,128)(2,1)S(1)}, u32[]{:S(2)}, u32[]{:S(2)}) %collective-permute-start.13) | collective-permute-done | bytes 266272 | tf_op jit(solution)/shard_map/ppermute | solution.py:451
  47.9 0.5 collective-permute-start.14
  48.4 0.7 project_keys.9
  49.2 0.8 project_values.9
  50.0 0.1 collective-permute-start.18
  50.1 1.2 %project_queries.3 = (bf16[2,48,1024]{2,1,0:T(8,128)(2,1)S(1)}, bf16[2,48,1024]{2,1,0:T(8,128)(2,1)S(1)}, bf16[1,48,1024]{2,1,0:T(8,128)(2,1)S(1)}) custom-call(bf16[2,48,2048]{2,1,0:T(8,128)(2,1)S(1)} %get-tuple-element.120.refs_0_, bf16[2,48,2048]{2,1,0:T(8,128)(2,1)S(1)} %get-tuple-element.121.refs_1_, ...), custom_call_target="tpu_custom_call" | custom-call | tf_op jit(solution)/shard_map/project_queries/pallas_call | solution.py:189
  51.3 0.7 collective-permute-done.18.refs_9_
  52.1 0.7 arrange.1
  52.8 1.5 %copy-done.4 = bf16[1,1024,2048]{2,1,0:T(8,128)(2,1)S(1)} copy-done((bf16[1,1024,2048]{2,1,0:T(8,128)(2,1)S(1)}, bf16[1,1024,2048]{2,1,0:T(8,128)(2,1)}, u32[]{:S(2)}) %copy-start.4) | copy-done | bytes 4194328
  54.3 4.5 %attend.3 = (bf16[40,2048]{1,0:T(8,128)(2,1)S(1)}, bf16[40,2048]{1,0:T(8,128)(2,1)S(1)}) custom-call(bf16[2,16,128,1024]{3,2,1,0:T(8,128)(2,1)S(1)} %get-tuple-element.131.panel_ref, bf16[8,48,1024]{2,1,0:T(8,128)(2,1)S(1)} %get-tuple-element.132.queries_ref, f32[8,48,128]{2,1,0:T(8,128)S(1)} %get-tuple-element.139.places_ref, bf16[1024,2048]{1,0:T(8,128)(2,1)S(1)} %bitcast.5), custom_call_target="tpu_custom_call" | custom-call | flops 1207959552 | bytes 8388608 | tf_op jit(solution)/shard_map/attend/pallas_call | solution.py:327
  58.7 0.5 collective-permute-start.19
  59.2 2.2 %collective-permute-start.23 = (bf16[40,2048]{1,0:T(8,128)(2,1)S(1)}, bf16[40,2048]{1,0:T(8,128)(2,1)S(1)}, u32[]{:S(2)}, u32[]{:S(2)}) collective-permute-start(bf16[40,2048]{1,0:T(8,128)(2,1)S(1)} %get-tuple-element.150), channel_id=1, source_target_pairs={{0,10},{2,8},{4,14},{6,12},{8,2},{10,0},{12,6},{14,4},{1,11},{3,9}... | collective-permute-start | bytes 491528 | tf_op jit(solution)/shard_map/ppermute | solution.py:493
  61.4 5.3 %attend.4 = (bf16[40,2048]{1,0:T(8,128)(2,1)S(1)}, bf16[40,2048]{1,0:T(8,128)(2,1)S(1)}) custom-call(bf16[2,16,128,1024]{3,2,1,0:T(8,128)(2,1)S(1)} %get-tuple-element.131.panel_ref, bf16[8,48,1024]{2,1,0:T(8,128)(2,1)S(1)} %get-tuple-element.132.queries_ref, f32[8,48,128]{2,1,0:T(8,128)S(1)} %get-tuple-element.139.places_ref, bf16[1024,2048]{1,0:T(8,128)(2,1)S(1)} %bitcast.6), custom_call_target="tpu_custom_call" | custom-call | flops 1207959552 | bytes 8388608 | tf_op jit(solution)/shard_map/attend/pallas_call | solution.py:327
  66.7 0.1 collective-permute-start.24
  66.8 5.0 %collective-permute-start.25 = (bf16[40,2048]{1,0:T(8,128)(2,1)S(1)}, bf16[40,2048]{1,0:T(8,128)(2,1)S(1)}, u32[]{:S(2)}, u32[]{:S(2)}) collective-permute-start(bf16[40,2048]{1,0:T(8,128)(2,1)S(1)} %get-tuple-element.152), channel_id=1, source_target_pairs={{0,14},{2,12},{4,10},{6,8},{8,6},{10,4},{12,2},{14,0},{1,15},{3,13... | collective-permute-start | bytes 491528 | tf_op jit(solution)/shard_map/ppermute | solution.py:493
  71.8 4.9 %attend.5 = (bf16[40,2048]{1,0:T(8,128)(2,1)S(1)}, bf16[40,2048]{1,0:T(8,128)(2,1)S(1)}, bf16[40,2048]{1,0:T(8,128)(2,1)S(1)}, bf16[40,2048]{1,0:T(8,128)(2,1)S(1)}) custom-call(bf16[2,16,128,1024]{3,2,1,0:T(8,128)(2,1)S(1)} %get-tuple-element.131.panel_ref, bf16[8,48,1024]{2,1,0:T(8,128)(2,1)S(1)} %get-tuple-element.132.queries_ref, ...), custom_call_target="tpu_custom_call" | custom-call | flops 2415919104 | bytes 8388608 | tf_op jit(solution)/shard_map/attend/pallas_call | solution.py:327
  76.7 4.1 %collective-permute-done.19.refs_4_ = bf16[40,2048]{1,0:T(8,128)(2,1)S(1)} collective-permute-done((bf16[40,2048]{1,0:T(8,128)(2,1)S(1)}, bf16[40,2048]{1,0:T(8,128)(2,1)S(1)}, u32[]{:S(2)}, u32[]{:S(2)}) %collective-permute-start.19) | collective-permute-done | bytes 163872 | tf_op jit(solution)/shard_map/ppermute | solution.py:493
  80.8 0.3 collective-permute-start.20
  81.1 2.9 %collective-permute-done.23.refs_5_ = bf16[40,2048]{1,0:T(8,128)(2,1)S(1)} collective-permute-done((bf16[40,2048]{1,0:T(8,128)(2,1)S(1)}, bf16[40,2048]{1,0:T(8,128)(2,1)S(1)}, u32[]{:S(2)}, u32[]{:S(2)}) %collective-permute-start.23) | collective-permute-done | bytes 163872 | tf_op jit(solution)/shard_map/ppermute | solution.py:493
  84.0 0.3 collective-permute-start.22
  84.3 0.5 gate_mix.1.mix_ref
  84.7 2.7 %collective-permute-done.20.refs_1_ = bf16[40,2048]{1,0:T(8,128)(2,1)S(1)} collective-permute-done((bf16[40,2048]{1,0:T(8,128)(2,1)S(1)}, bf16[40,2048]{1,0:T(8,128)(2,1)S(1)}, u32[]{:S(2)}, u32[]{:S(2)}) %collective-permute-start.20) | collective-permute-done | bytes 163872 | tf_op jit(solution)/shard_map/ppermute | solution.py:493
  87.4 0.3 collective-permute-done.21.refs_2_
  87.7 3.3 %collective-permute-done.22.refs_3_ = bf16[40,2048]{1,0:T(8,128)(2,1)S(1)} collective-permute-done((bf16[40,2048]{1,0:T(8,128)(2,1)S(1)}, bf16[40,2048]{1,0:T(8,128)(2,1)S(1)}, u32[]{:S(2)}, u32[]{:S(2)}) %collective-permute-start.22) | collective-permute-done | bytes 163872 | tf_op jit(solution)/shard_map/ppermute | solution.py:493
  91.1 1.8 %combine.1 = bf16[128,2048]{1,0:T(8,128)(2,1)} custom-call(bf16[384,384]{1,0:T(8,128)(2,1)S(1)} %gate_mix.1.mix_ref, bf16[40,2048]{1,0:T(8,128)(2,1)S(1)} %get-tuple-element.145.refs_0_, bf16[40,2048]{1,0:T(8,128)(2,1)S(1)} %collective-permute-done.20.refs_1_, bf16[40,2048]{1,0:T(8,128)(2,1)S(1)} %collective-permute-done.21.refs_2_, ...), custom_call_target="tpu_custom_call" | custom-call | tf_op jit(solution)/shard_map/combine/pallas_call | solution.py:415
  (27 shorter events, 0.1 us)
Async XLA Ops:
  0.0 1.0 %copy-start.6 = (bf16[128,2048]{1,0:T(8,128)(2,1)S(1)}, bf16[128,2048]{1,0:T(8,128)(2,1)}, u32[]{:S(2)}) copy-start(bf16[128,2048]{1,0:T(8,128)(2,1)} %refs_0_.1) | copy-start | bytes 1572868
  1.0 0.7 copy-start.8
  1.7 0.7 copy-start.9
  2.7 10.2 %collective-permute-start = (bf16[1040,128]{1,0:T(8,128)(2,1)S(1)}, bf16[1040,128]{1,0:T(8,128)(2,1)S(1)}, u32[]{:S(2)}, u32[]{:S(2)}) collective-permute-start(bf16[1040,128]{1,0:T(8,128)(2,1)S(1)} %get-tuple-element.79.top_ref.refs_0_), channel_id=1, source_target_pairs={{0,4},{4,8},{8,12},{12,14},{14,10},{10,6},{6,2},{2,0},{1,5},{5,9},... | collective-permute-start | bytes 798728 | tf_op jit(solution)/shard_map/ppermute | solution.py:451
  5.8 9.3 %collective-permute-start.1 = (bf16[1040,128]{1,0:T(8,128)(2,1)S(1)}, bf16[1040,128]{1,0:T(8,128)(2,1)S(1)}, u32[]{:S(2)}, u32[]{:S(2)}) collective-permute-start(bf16[1040,128]{1,0:T(8,128)(2,1)S(1)} %get-tuple-element.80.bottom_ref.refs_1_), channel_id=1, source_target_pairs={{4,0},{8,4},{12,8},{14,12},{10,14},{6,10},{2,6},{0,2},{5,1},{9,5},... | collective-permute-start | bytes 798728 | tf_op jit(solution)/shard_map/ppermute | solution.py:451
  5.8 15.0 %collective-permute-start.3 = (bf16[1040,128]{1,0:T(8,128)(2,1)S(1)}, bf16[1040,128]{1,0:T(8,128)(2,1)S(1)}, u32[]{:S(2)}, u32[]{:S(2)}) collective-permute-start(bf16[1040,128]{1,0:T(8,128)(2,1)S(1)} %get-tuple-element.79.top_ref.refs_0_), channel_id=1, source_target_pairs={{4,0},{8,4},{12,8},{14,12},{10,14},{6,10},{2,6},{0,2},{5,1},{9,5},... | collective-permute-start | bytes 798728 | tf_op jit(solution)/shard_map/ppermute | solution.py:451
  7.8 13.1 %collective-permute-start.2 = (bf16[1040,128]{1,0:T(8,128)(2,1)S(1)}, bf16[1040,128]{1,0:T(8,128)(2,1)S(1)}, u32[]{:S(2)}, u32[]{:S(2)}) collective-permute-start(bf16[1040,128]{1,0:T(8,128)(2,1)S(1)} %get-tuple-element.80.bottom_ref.refs_1_), channel_id=1, source_target_pairs={{0,4},{4,8},{8,12},{12,14},{14,10},{10,6},{6,2},{2,0},{1,5},{5,9},... | collective-permute-start | bytes 798728 | tf_op jit(solution)/shard_map/ppermute | solution.py:451
  7.9 2.2 %copy-start = (bf16[2048,1024]{1,0:T(8,128)(2,1)S(1)}, bf16[2048,1024]{1,0:T(8,128)(2,1)}, u32[]{:S(2)}) copy-start(bf16[2048,1024]{1,0:T(8,128)(2,1)} %refs_2_.6) | copy-start | bytes 12582916
  10.1 12.8 %copy-start.1 = (bf16[2048,1024]{1,0:T(8,128)(2,1)S(1)}, bf16[2048,1024]{1,0:T(8,128)(2,1)}, u32[]{:S(2)}) copy-start(bf16[2048,1024]{1,0:T(8,128)(2,1)} %refs_2_.6) | copy-start | bytes 12582916
  15.1 9.3 %collective-permute-start.4 = (bf16[1040,128]{1,0:T(8,128)(2,1)S(1)}, bf16[1040,128]{1,0:T(8,128)(2,1)S(1)}, u32[]{:S(2)}, u32[]{:S(2)}) collective-permute-start(bf16[1040,128]{1,0:T(8,128)(2,1)S(1)} %collective-permute-done.refs_0_), channel_id=1, source_target_pairs={{0,4},{4,8},{8,12},{12,14},{14,10},{10,6},{6,2},{2,0},{1,5},{5,9},... | collective-permute-start | bytes 798728 | tf_op jit(solution)/shard_map/ppermute | solution.py:451
  16.7 9.8 %collective-permute-start.5 = (bf16[1040,128]{1,0:T(8,128)(2,1)S(1)}, bf16[1040,128]{1,0:T(8,128)(2,1)S(1)}, u32[]{:S(2)}, u32[]{:S(2)}) collective-permute-start(bf16[1040,128]{1,0:T(8,128)(2,1)S(1)} %collective-permute-done.1.refs_3_), channel_id=1, source_target_pairs={{4,0},{8,4},{12,8},{14,12},{10,14},{6,10},{2,6},{0,2},{5,1},{9,5},... | collective-permute-start | bytes 798728 | tf_op jit(solution)/shard_map/ppermute | solution.py:451
  17.2 2.2 %copy-start.2 = (bf16[2048,1024]{1,0:T(8,128)(2,1)S(1)}, bf16[2048,1024]{1,0:T(8,128)(2,1)}, u32[]{:S(2)}) copy-start(bf16[2048,1024]{1,0:T(8,128)(2,1)} %refs_2_.7) | copy-start | bytes 12582916
  19.3 9.2 %copy-start.3 = (bf16[2048,1024]{1,0:T(8,128)(2,1)S(1)}, bf16[2048,1024]{1,0:T(8,128)(2,1)}, u32[]{:S(2)}) copy-start(bf16[2048,1024]{1,0:T(8,128)(2,1)} %refs_2_.7) | copy-start | bytes 12582916
  20.8 9.3 %collective-permute-start.6 = (bf16[1040,128]{1,0:T(8,128)(2,1)S(1)}, bf16[1040,128]{1,0:T(8,128)(2,1)S(1)}, u32[]{:S(2)}, u32[]{:S(2)}) collective-permute-start(bf16[1040,128]{1,0:T(8,128)(2,1)S(1)} %collective-permute-done.2.refs_1_), channel_id=1, source_target_pairs={{0,4},{4,8},{8,12},{12,14},{14,10},{10,6},{6,2},{2,0},{1,5},{5,9},... | collective-permute-start | bytes 798728 | tf_op jit(solution)/shard_map/ppermute | solution.py:451
  22.4 9.8 %collective-permute-start.7 = (bf16[1040,128]{1,0:T(8,128)(2,1)S(1)}, bf16[1040,128]{1,0:T(8,128)(2,1)S(1)}, u32[]{:S(2)}, u32[]{:S(2)}) collective-permute-start(bf16[1040,128]{1,0:T(8,128)(2,1)S(1)} %collective-permute-done.3.refs_2_), channel_id=1, source_target_pairs={{4,0},{8,4},{12,8},{14,12},{10,14},{6,10},{2,6},{0,2},{5,1},{9,5},... | collective-permute-start | bytes 798728 | tf_op jit(solution)/shard_map/ppermute | solution.py:451
  24.1 10.1 %copy-start.5 = (bf16[1,2048,1024]{2,1,0:T(8,128)(2,1)S(1)}, bf16[1,2048,1024]{2,1,0:T(8,128)(2,1)}, u32[]{:S(2)}) copy-start(bf16[1,2048,1024]{2,1,0:T(8,128)(2,1)} %param.14) | copy-start | bytes 12582916
  26.5 9.8 %collective-permute-start.8 = (bf16[1040,128]{1,0:T(8,128)(2,1)S(1)}, bf16[1040,128]{1,0:T(8,128)(2,1)S(1)}, u32[]{:S(2)}, u32[]{:S(2)}) collective-permute-start(bf16[1040,128]{1,0:T(8,128)(2,1)S(1)} %collective-permute-done.4.refs_0_), channel_id=1, source_target_pairs={{0,4},{4,8},{8,12},{12,14},{14,10},{10,6},{6,2},{2,0},{1,5},{5,9},... | collective-permute-start | bytes 798728 | tf_op jit(solution)/shard_map/ppermute | solution.py:451
  28.1 9.8 %collective-permute-start.9 = (bf16[1040,128]{1,0:T(8,128)(2,1)S(1)}, bf16[1040,128]{1,0:T(8,128)(2,1)S(1)}, u32[]{:S(2)}, u32[]{:S(2)}) collective-permute-start(bf16[1040,128]{1,0:T(8,128)(2,1)S(1)} %collective-permute-done.5.refs_3_), channel_id=1, source_target_pairs={{4,0},{8,4},{12,8},{14,12},{10,14},{6,10},{2,6},{0,2},{5,1},{9,5},... | collective-permute-start | bytes 798728 | tf_op jit(solution)/shard_map/ppermute | solution.py:451
  32.2 9.3 %collective-permute-start.10 = (bf16[1040,128]{1,0:T(8,128)(2,1)S(1)}, bf16[1040,128]{1,0:T(8,128)(2,1)S(1)}, u32[]{:S(2)}, u32[]{:S(2)}) collective-permute-start(bf16[1040,128]{1,0:T(8,128)(2,1)S(1)} %collective-permute-done.6.refs_1_), channel_id=1, source_target_pairs={{0,4},{4,8},{8,12},{12,14},{14,10},{10,6},{6,2},{2,0},{1,5},{5,9},... | collective-permute-start | bytes 798728 | tf_op jit(solution)/shard_map/ppermute | solution.py:451
  33.8 9.8 %collective-permute-start.11 = (bf16[1040,128]{1,0:T(8,128)(2,1)S(1)}, bf16[1040,128]{1,0:T(8,128)(2,1)S(1)}, u32[]{:S(2)}, u32[]{:S(2)}) collective-permute-start(bf16[1040,128]{1,0:T(8,128)(2,1)S(1)} %collective-permute-done.7.refs_2_), channel_id=1, source_target_pairs={{4,0},{8,4},{12,8},{14,12},{10,14},{6,10},{2,6},{0,2},{5,1},{9,5},... | collective-permute-start | bytes 798728 | tf_op jit(solution)/shard_map/ppermute | solution.py:451
  38.0 8.5 %collective-permute-start.12 = (bf16[1040,128]{1,0:T(8,128)(2,1)S(1)}, bf16[1040,128]{1,0:T(8,128)(2,1)S(1)}, u32[]{:S(2)}, u32[]{:S(2)}) collective-permute-start(bf16[1040,128]{1,0:T(8,128)(2,1)S(1)} %collective-permute-done.8.refs_0_), channel_id=1, source_target_pairs={{0,4},{4,8},{8,12},{12,14},{14,10},{10,6},{6,2},{2,0},{1,5},{5,9},... | collective-permute-start | bytes 798728 | tf_op jit(solution)/shard_map/ppermute | solution.py:451
  39.5 8.4 %collective-permute-start.13 = (bf16[1040,128]{1,0:T(8,128)(2,1)S(1)}, bf16[1040,128]{1,0:T(8,128)(2,1)S(1)}, u32[]{:S(2)}, u32[]{:S(2)}) collective-permute-start(bf16[1040,128]{1,0:T(8,128)(2,1)S(1)} %collective-permute-done.9.refs_3_), channel_id=1, source_target_pairs={{4,0},{8,4},{12,8},{14,12},{10,14},{6,10},{2,6},{0,2},{5,1},{9,5},... | collective-permute-start | bytes 798728 | tf_op jit(solution)/shard_map/ppermute | solution.py:451
  40.0 11.3 %collective-permute-start.15 = (bf16[2,256,1024]{2,1,0:T(8,128)(2,1)S(1)}, bf16[2,256,1024]{2,1,0:T(8,128)(2,1)S(1)}, u32[]{:S(2)}, u32[]{:S(2)}) collective-permute-start(bf16[2,256,1024]{2,1,0:T(8,128)(2,1)S(1)} %get-tuple-element.90.refs_1_), channel_id=1, source_target_pairs={{0,1},{1,0},{2,3},{3,2},{4,5},{5,4},{6,7},{7,6},{8,9},{9,8},{10,11... | collective-permute-start | bytes 3145736 | tf_op jit(solution)/shard_map/ppermute | solution.py:454
  41.6 10.5 %collective-permute-start.16 = (bf16[2,256,1024]{2,1,0:T(8,128)(2,1)S(1)}, bf16[2,256,1024]{2,1,0:T(8,128)(2,1)S(1)}, u32[]{:S(2)}, u32[]{:S(2)}) collective-permute-start(bf16[2,256,1024]{2,1,0:T(8,128)(2,1)S(1)} %get-tuple-element.103.refs_2_), channel_id=1, source_target_pairs={{0,1},{1,0},{2,3},{3,2},{4,5},{5,4},{6,7},{7,6},{8,9},{9,8},{10,11... | collective-permute-start | bytes 3145736 | tf_op jit(solution)/shard_map/ppermute | solution.py:454
  47.9 4.2 %collective-permute-start.17 = (bf16[2,256,1024]{2,1,0:T(8,128)(2,1)S(1)}, bf16[2,256,1024]{2,1,0:T(8,128)(2,1)S(1)}, u32[]{:S(2)}, u32[]{:S(2)}) collective-permute-start(bf16[2,256,1024]{2,1,0:T(8,128)(2,1)S(1)} %get-tuple-element.112.refs_3_), channel_id=1, source_target_pairs={{0,1},{1,0},{2,3},{3,2},{4,5},{5,4},{6,7},{7,6},{8,9},{9,8},{10,11... | collective-permute-start | bytes 3145736 | tf_op jit(solution)/shard_map/ppermute | solution.py:454
  47.9 3.4 %collective-permute-start.14 = (bf16[2,128,1024]{2,1,0:T(8,128)(2,1)S(1)}, bf16[2,128,1024]{2,1,0:T(8,128)(2,1)S(1)}, u32[]{:S(2)}, u32[]{:S(2)}) collective-permute-start(bf16[2,128,1024]{2,1,0:T(8,128)(2,1)S(1)} %get-tuple-element.84.refs_0_), channel_id=1, source_target_pairs={{0,1},{1,0},{2,3},{3,2},{4,5},{5,4},{6,7},{7,6},{8,9},{9,8},{10,11... | collective-permute-start | bytes 1572872 | tf_op jit(solution)/shard_map/ppermute | solution.py:454
  50.0 2.1 %collective-permute-start.18 = (bf16[2,128,1024]{2,1,0:T(8,128)(2,1)S(1)}, bf16[2,128,1024]{2,1,0:T(8,128)(2,1)S(1)}, u32[]{:S(2)}, u32[]{:S(2)}) collective-permute-start(bf16[2,128,1024]{2,1,0:T(8,128)(2,1)S(1)} %get-tuple-element.117.refs_4_), channel_id=1, source_target_pairs={{0,1},{1,0},{2,3},{3,2},{4,5},{5,4},{6,7},{7,6},{8,9},{9,8},{10,11... | collective-permute-start | bytes 1572872 | tf_op jit(solution)/shard_map/ppermute | solution.py:454
  52.1 2.2 %copy-start.4 = (bf16[1,1024,2048]{2,1,0:T(8,128)(2,1)S(1)}, bf16[1,1024,2048]{2,1,0:T(8,128)(2,1)}, u32[]{:S(2)}) copy-start(bf16[1,1024,2048]{2,1,0:T(8,128)(2,1)} %param.15) | copy-start | bytes 12582916
  58.7 22.1 %collective-permute-start.19 = (bf16[40,2048]{1,0:T(8,128)(2,1)S(1)}, bf16[40,2048]{1,0:T(8,128)(2,1)S(1)}, u32[]{:S(2)}, u32[]{:S(2)}) collective-permute-start(bf16[40,2048]{1,0:T(8,128)(2,1)S(1)} %get-tuple-element.144), channel_id=1, source_target_pairs={{0,8},{2,10},{4,12},{6,14},{8,0},{10,2},{12,4},{14,6},{1,9},{3,11}... | collective-permute-start | bytes 491528 | tf_op jit(solution)/shard_map/ppermute | solution.py:493
  59.2 24.8 %collective-permute-start.23 = (bf16[40,2048]{1,0:T(8,128)(2,1)S(1)}, bf16[40,2048]{1,0:T(8,128)(2,1)S(1)}, u32[]{:S(2)}, u32[]{:S(2)}) collective-permute-start(bf16[40,2048]{1,0:T(8,128)(2,1)S(1)} %get-tuple-element.150), channel_id=1, source_target_pairs={{0,10},{2,8},{4,14},{6,12},{8,2},{10,0},{12,6},{14,4},{1,11},{3,9}... | collective-permute-start | bytes 491528 | tf_op jit(solution)/shard_map/ppermute | solution.py:493
  66.7 17.5 %copy-start.7 = (f32[2048,8]{0,1:T(8,128)S(1)}, f32[2048,8]{0,1:T(8,128)}, u32[]{:S(2)}) copy-start(f32[2048,8]{0,1:T(8,128)} %param.10) | copy-start | bytes 196612
  66.7 18.0 %collective-permute-start.24 = (bf16[40,2048]{1,0:T(8,128)(2,1)S(1)}, bf16[40,2048]{1,0:T(8,128)(2,1)S(1)}, u32[]{:S(2)}, u32[]{:S(2)}) collective-permute-start(bf16[40,2048]{1,0:T(8,128)(2,1)S(1)} %get-tuple-element.151), channel_id=1, source_target_pairs={{0,12},{2,14},{4,8},{6,10},{8,4},{10,6},{12,0},{14,2},{1,13},{3,15... | collective-permute-start | bytes 491528 | tf_op jit(solution)/shard_map/ppermute | solution.py:493
  66.8 17.9 %collective-permute-start.25 = (bf16[40,2048]{1,0:T(8,128)(2,1)S(1)}, bf16[40,2048]{1,0:T(8,128)(2,1)S(1)}, u32[]{:S(2)}, u32[]{:S(2)}) collective-permute-start(bf16[40,2048]{1,0:T(8,128)(2,1)S(1)} %get-tuple-element.152), channel_id=1, source_target_pairs={{0,14},{2,12},{4,10},{6,8},{8,6},{10,4},{12,2},{14,0},{1,15},{3,13... | collective-permute-start | bytes 491528 | tf_op jit(solution)/shard_map/ppermute | solution.py:493
  80.8 6.6 %collective-permute-start.20 = (bf16[40,2048]{1,0:T(8,128)(2,1)S(1)}, bf16[40,2048]{1,0:T(8,128)(2,1)S(1)}, u32[]{:S(2)}, u32[]{:S(2)}) collective-permute-start(bf16[40,2048]{1,0:T(8,128)(2,1)S(1)} %get-tuple-element.146), channel_id=1, source_target_pairs={{0,2},{2,0},{4,6},{6,4},{8,10},{10,8},{12,14},{14,12},{1,3},{3,1},... | collective-permute-start | bytes 491528 | tf_op jit(solution)/shard_map/ppermute | solution.py:493
  81.1 6.7 %collective-permute-start.21 = (bf16[40,2048]{1,0:T(8,128)(2,1)S(1)}, bf16[40,2048]{1,0:T(8,128)(2,1)S(1)}, u32[]{:S(2)}, u32[]{:S(2)}) collective-permute-start(bf16[40,2048]{1,0:T(8,128)(2,1)S(1)} %get-tuple-element.147), channel_id=1, source_target_pairs={{0,4},{2,6},{4,0},{6,2},{8,12},{10,14},{12,8},{14,10},{1,5},{3,7},... | collective-permute-start | bytes 491528 | tf_op jit(solution)/shard_map/ppermute | solution.py:493
  84.0 7.1 %collective-permute-start.22 = (bf16[40,2048]{1,0:T(8,128)(2,1)S(1)}, bf16[40,2048]{1,0:T(8,128)(2,1)S(1)}, u32[]{:S(2)}, u32[]{:S(2)}) collective-permute-start(bf16[40,2048]{1,0:T(8,128)(2,1)S(1)} %get-tuple-element.148), channel_id=1, source_target_pairs={{0,6},{2,4},{4,2},{6,0},{8,14},{10,12},{12,10},{14,8},{1,7},{3,5},... | collective-permute-start | bytes 491528 | tf_op jit(solution)/shard_map/ppermute | solution.py:493

commit v10 on v9

--- a/solution.py
+++ b/solution.py
@@ -15,7 +15,7 @@
 MASKED = -1e30
 LANES = 128
 CODES = 16
-TERMS = 3
+TERMS = 2
 MIB = 1 << 20
 WHOLE = pl.BlockSpec(memory_space=pltpu.VMEM)
 
@@ -89,7 +89,7 @@
         out_shape=[half, half],
         scratch_shapes=[pltpu.VMEM(x.shape, x.dtype) for x in operands]
         + [pltpu.SemaphoreType.DMA((3,))],
-        compiler_params=pltpu.CompilerParams(vmem_limit_bytes=8 * MIB),
+        compiler_params=pltpu.CompilerParams(vmem_limit_bytes=60 * MIB),
         name="norm_rows",
     )(*operands)
 
@@ -172,8 +172,8 @@
 
 
 def queries_kernel(*refs):
-    count = len(refs) // 2
-    picked, weight_ref, outs = refs[:count], refs[count], refs[count + 1 :]
+    count = len(refs) // 2 - 1
+    picked, weight_ref, outs = refs[:count], refs[count], refs[count + 2 :]
     rows = jnp.concatenate([ref[g] for ref in picked for g in range(ref.shape[0])], axis=0)
     places = [(ref, g) for ref in outs for g in range(ref.shape[0])]
     for cols in column_parts(weight_ref):
@@ -182,20 +182,20 @@
             ref[g, :, cols] = product[i * SLOTS : (i + 1) * SLOTS].astype(jnp.bfloat16)
 
 
-def project_queries(picked, query_slab):
+def project_queries(picked, query_slab, next_slab):
     model_width, width = query_slab.shape
     owners = sum(rows.shape[0] for rows in picked)
-    held = 2 * model_width * width + owners * SLOTS * (4 * model_width + 4 * width)
+    held = 4 * model_width * width + owners * SLOTS * (4 * model_width + 4 * width)
     return pl.pallas_call(
         queries_kernel,
-        in_specs=[WHOLE] * (len(picked) + 1),
+        in_specs=[WHOLE] * (len(picked) + 2),
         out_specs=[WHOLE] * len(picked),
         out_shape=[
             jax.ShapeDtypeStruct((rows.shape[0], SLOTS, width), jnp.bfloat16) for rows in picked
         ],
         compiler_params=pltpu.CompilerParams(vmem_limit_bytes=held + 6 * MIB),
         name="project_queries",
-    )(*picked, query_slab)
+    )(*picked, query_slab, next_slab)
 
 
 def arrange_kernel(plan, *refs):
@@ -256,47 +256,58 @@
         reach = (part_id + 1) * span
         pair = pl.ds(2 * number, 2)
         spots = places_ref[pair].reshape(tile, LANES)
-        for h in range(heads):
-            held = queries_ref[pair, :, lanes[h]].reshape(tile, HS)
-            for j in range(part_id + 1):
-                key_part = panel_ref[0, per_span * j : per_span * (j + 1), :, lanes[h]]
-                scores[h, :, pl.ds(j * span, span)] = lax.dot_general(
-                    held,
-                    key_part.reshape(span, HS),
-                    (((1,), (1,)), ((), ())),
-                    preferred_element_type=jnp.float32,
-                )
-        for h in range(heads):
-            for sub in range(0, tile, 16):
-                rows = pl.ds(sub, 16)
-                part = scores[h, rows, pl.ds(0, reach)]
-                last = part[:, reach - span :]
-                key_index = lax.broadcasted_iota(jnp.int32, last.shape, 1) + (reach - span)
-                spot = spots[sub : sub + 16, 0:1]
-                last = jnp.where(key_index.astype(jnp.float32) <= spot, last, MASKED)
-                if part_id > 0:
-                    part = jnp.concatenate([part[:, : reach - span], last], axis=1)
-                else:
-                    part = last
-                peak = jnp.max(part, axis=1, keepdims=True)
-                raised = jnp.exp2((part - peak) * rate)
-                total = jnp.sum(raised, axis=1, keepdims=True)
-                weights[h, rows, pl.ds(0, reach)] = (raised * (1.0 / total)).astype(jnp.bfloat16)
-        for h in range(heads):
-            total = None
-            for j in range(part_id + 1):
-                value_part = panel_ref[1, per_span * j : per_span * (j + 1), :, lanes[h]]
-                product = jnp.dot(
-                    weights[h, :, pl.ds(j * span, span)],
-                    value_part.reshape(span, HS),
-                    preferred_element_type=jnp.float32,
-                )
-                total = product if total is None else total + product
-            total = total.astype(jnp.bfloat16)
-            for side in range(2):
-                attended[2 * lot + (side ^ (rank % 2)), :, lanes[h]] = total[
-                    side * SLOTS : (side + 1) * SLOTS
-                ]
+        held, sums = {}, {}
+
+        def score(h, j):
+            if j == 0:
+                held[h] = queries_ref[pair, :, lanes[h]].reshape(tile, HS)
+            key_part = panel_ref[0, per_span * j : per_span * (j + 1), :, lanes[h]]
+            scores[h, :, pl.ds(j * span, span)] = lax.dot_general(
+                held[h],
+                key_part.reshape(span, HS),
+                (((1,), (1,)), ((), ())),
+                preferred_element_type=jnp.float32,
+            )
+
+        def weigh(h, sub):
+            rows = pl.ds(sub * 16, 16)
+            part = scores[h, rows, pl.ds(0, reach)]
+            last = part[:, reach - span :]
+            key_index = lax.broadcasted_iota(jnp.int32, last.shape, 1) + (reach - span)
+            spot = spots[sub * 16 : sub * 16 + 16, 0:1]
+            last = jnp.where(key_index.astype(jnp.float32) <= spot, last, MASKED)
+            if part_id > 0:
+                part = jnp.concatenate([part[:, : reach - span], last], axis=1)
+            else:
+                part = last
+            peak = jnp.max(part, axis=1, keepdims=True)
+            raised = jnp.exp2((part - peak) * rate)
+            total = jnp.sum(raised, axis=1, keepdims=True)
+            weights[h, rows, pl.ds(0, reach)] = (raised * (1.0 / total)).astype(jnp.bfloat16)
+
+        def gather(h, j):
+            value_part = panel_ref[1, per_span * j : per_span * (j + 1), :, lanes[h]]
+            product = jnp.dot(
+                weights[h, :, pl.ds(j * span, span)],
+                value_part.reshape(span, HS),
+                preferred_element_type=jnp.float32,
+            )
+            sums[h] = product if j == 0 else sums[h] + product
+            if j == part_id:
+                total = sums[h].astype(jnp.bfloat16)
+                for side in range(2):
+                    attended[2 * lot + (side ^ (rank % 2)), :, lanes[h]] = total[
+                        side * SLOTS : (side + 1) * SLOTS
+                    ]
+
+        for h in range(heads + 2):
+            for i in range(max(tile // 16, parts)):
+                if 0 < h <= heads and i < tile // 16:
+                    weigh(h - 1, i)
+                if h < heads and i <= part_id:
+                    score(h, i)
+                if h > 1 and i <= part_id:
+                    gather(h - 2, i)
 
     def one(at, carry):
         lot, now = at // passes, at % passes
@@ -463,7 +474,7 @@
         keys, mark = project_keys(token_half, blocks, key_weight)
         following = [lead[0], rest[0], rest[1], lead[1]]
         if step == steps - 2:
-            queries = project_queries(picked, query_slab)
+            queries = project_queries(picked, query_slab, output_slab)
             picked = []
         if step < steps - 1:
             mark, *lead_next = tie(mark, *lead, *queries)
@@ -479,14 +490,15 @@
         if step < steps - 1:
             other.append(hand_over(panel))
         blocks = following
-    own[-1], *blocks = tie(own[-1], *lead)
+    queries = [*queries, *project_queries(picked, query_slab, output_slab)]
+    own[-1], queries[-1], *blocks = tie(own[-1], queries[-1], *lead)
     other.append(hand_over(own[-1]))
     keys, mark = project_keys(token_half, blocks, key_weight)
     panel, rows, position = project_values(token_half, blocks, plan[-1], mark, keys, value_weight)
     own.append(panel)
     other.append(hand_over(panel))
     positions.append(position)
-    queries = [*queries, *project_queries(picked + [rows], query_slab)]
+    queries = [*queries, *project_queries([rows], query_slab, output_slab)]
     held = arrange(ctx_count, plan, own, other, queries, positions)
 
     def swap(piece, k):

time: 93.2 us -> 91 us (0.976)
  waiting for transfers between devices: 28.3 us -> 24.8 us
  Pallas kernels: 31.3 us -> 34.7 us
  local copies, waits for them, and re-layouts: 8.3 us -> 6.31 us
    unnamed x20 -> x22, local copies, waits for them, and re-layouts: 8.3 us -> 6.31 us
    ppermute x7, waiting for transfers between devices: 2.71 us -> 0.97 us  [send(): lax.ppermute(parts[0], 'ctx', forward)]
    pallas_call x1, Pallas kernels: 0.31 us -> 2.03 us  [norm_rows(): pl.pallas_call(norm_kernel, in_specs=[pl.BlockSpec(memory_space=pltpu.HBM...]
    pallas_call x3, Pallas kernels: 14.6 us -> 15.9 us  [attend(): pl.pallas_call(functools.partial(attend_kernel, lots, heads), in_specs=[W...]
    ppermute x7, waiting for transfers between devices: 13.3 us -> 12.2 us  [swap(): return lax.ppermute(piece, 'ctx', [(c, c ^ k) for c in range(ctx_count)])]
    ppermute x7, waiting for transfers between devices: 11.5 us -> 10.5 us  [send(): lax.ppermute(parts[1], 'ctx', backward)]
    pallas_call x2 -> x3, Pallas kernels: 2.01 us -> 2.63 us  [project_queries(): pl.pallas_call(queries_kernel, in_specs=[WHOLE] * (len(picked) + 2), out_...]
  transfers between devices with their start and end apart: 26 -> 26, of which waited for: 17 -> 18; matrix products, arithmetic and copies ran while one was open for 0% -> 0% of each run, Pallas kernels for 26% -> 29%
where the time goes in v10:
time: 91 us; the launch traced here: 90.7 us
  Pallas kernels  34.7 us (38%)
  waiting for transfers between devices  24.8 us (27%)
  starting transfers between devices  24.7 us (27%)
  local copies, waits for them, and re-layouts  6.31 us (7%)
    pallas_call x3, Pallas kernels, attend(): pl.pallas_call(functools.partial(attend_kernel, lots, heads), in_specs=[W...  15.9 us
    ppermute x7, waiting for transfers between devices, swap(): return lax.ppermute(piece, 'ctx', [(c, c ^ k) for c in range(ctx_count)])  12.2 us
    ppermute x7, starting transfers between devices, send(): lax.ppermute(parts[0], 'ctx', forward)  11.1 us
    ppermute x7, waiting for transfers between devices, send(): lax.ppermute(parts[1], 'ctx', backward)  10.5 us
    ppermute x7, starting transfers between devices, swap(): return lax.ppermute(piece, 'ctx', [(c, c ^ k) for c in range(ctx_count)])  8.31 us
    unnamed x22, local copies, waits for them, and re-layouts  6.31 us
    pallas_call x5, Pallas kernels, project_values(): pl.pallas_call(functools.partial(values_kernel, half, offsets, len(blocks...  6.15 us
    pallas_call x5, Pallas kernels, project_keys(): pl.pallas_call(functools.partial(keys_kernel, half, len(blocks)), in_spec...  5.3 us
  transfers between devices with their start and end apart: 26, of which 18 were waited for; matrix products, arithmetic and copies ran while one was open for 0% of the time, Pallas kernels for 29%

profile of v10, /device:TPU:0, one launch (start us, length us, event | category | flops | bytes accessed | tf_op | source)
XLA Modules:
  0.0 90.7 jit_solution(8720855407373620513)
XLA Ops:
  0.0 2.0 %norm_rows.1 = (bf16[1040,128]{1,0:T(8,128)(2,1)}, bf16[1040,128]{1,0:T(8,128)(2,1)}) custom-call(bf16[128,2048]{1,0:T(8,128)(2,1)} %refs_0_.1, f32[1,2048]{1,0:T(1,128)} %bitcast.15, s32[2,128]{1,0:T(2,128)} %bitcast.16), custom_call_target="tpu_custom_call" | custom-call | tf_op jit(solution)/shard_map/norm_rows/pallas_call | solution.py:85
  2.0 3.1 %collective-permute-start = (bf16[1040,128]{1,0:T(8,128)(2,1)}, bf16[1040,128]{1,0:T(8,128)(2,1)S(1)}, u32[]{:S(2)}, u32[]{:S(2)}) collective-permute-start(bf16[1040,128]{1,0:T(8,128)(2,1)} %get-tuple-element.79.top_ref.refs_0_), channel_id=1, source_target_pairs={{0,4},{4,8},{8,12},{12,14},{14,10},{10,6},{6,2},{2,0},{1,5},{5,9},... | collective-permute-start | bytes 798728 | tf_op jit(solution)/shard_map/ppermute | solution.py:462
  5.1 2.0 %collective-permute-start.3 = (bf16[1040,128]{1,0:T(8,128)(2,1)}, bf16[1040,128]{1,0:T(8,128)(2,1)S(1)}, u32[]{:S(2)}, u32[]{:S(2)}) collective-permute-start(bf16[1040,128]{1,0:T(8,128)(2,1)} %get-tuple-element.79.top_ref.refs_0_), channel_id=1, source_target_pairs={{4,0},{8,4},{12,8},{14,12},{10,14},{6,10},{2,6},{0,2},{5,1},{9,5},... | collective-permute-start | bytes 798728 | tf_op jit(solution)/shard_map/ppermute | solution.py:462
  7.1 0.1 collective-permute-start.2
  7.2 2.2 %copy-done.1 = bf16[2048,1024]{1,0:T(8,128)(2,1)S(1)} copy-done((bf16[2048,1024]{1,0:T(8,128)(2,1)S(1)}, bf16[2048,1024]{1,0:T(8,128)(2,1)}, u32[]{:S(2)}) %copy-start.1) | copy-done | bytes 4194328
  9.4 0.9 %copy-done.6 = bf16[1040,128]{1,0:T(8,128)(2,1)S(1)} copy-done((bf16[1040,128]{1,0:T(8,128)(2,1)S(1)}, bf16[1040,128]{1,0:T(8,128)(2,1)}, u32[]{:S(2)}) %copy-start.6) | copy-done | bytes 266264
  10.3 0.9 %copy-done.8 = bf16[1040,128]{1,0:T(8,128)(2,1)S(1)} copy-done((bf16[1040,128]{1,0:T(8,128)(2,1)S(1)}, bf16[1040,128]{1,0:T(8,128)(2,1)}, u32[]{:S(2)}) %copy-start.8) | copy-done | bytes 266264
  11.3 0.7 project_keys.5
  12.0 0.5 collective-permute-done.refs_0_
  12.5 2.2 %collective-permute-done.1.refs_3_ = bf16[1040,128]{1,0:T(8,128)(2,1)S(1)} collective-permute-done((bf16[1040,128]{1,0:T(8,128)(2,1)}, bf16[1040,128]{1,0:T(8,128)(2,1)S(1)}, u32[]{:S(2)}, u32[]{:S(2)}) %collective-permute-start.1) | collective-permute-done | bytes 266272 | tf_op jit(solution)/shard_map/ppermute | solution.py:462
  14.6 1.6 %collective-permute-start.4 = (bf16[1040,128]{1,0:T(8,128)(2,1)S(1)}, bf16[1040,128]{1,0:T(8,128)(2,1)S(1)}, u32[]{:S(2)}, u32[]{:S(2)}) collective-permute-start(bf16[1040,128]{1,0:T(8,128)(2,1)S(1)} %collective-permute-done.refs_0_), channel_id=1, source_target_pairs={{0,4},{4,8},{8,12},{12,14},{14,10},{10,6},{6,2},{2,0},{1,5},{5,9},... | collective-permute-start | bytes 798728 | tf_op jit(solution)/shard_map/ppermute | solution.py:462
  16.2 0.4 collective-permute-start.5
  16.7 2.2 %copy-done.3 = bf16[2048,1024]{1,0:T(8,128)(2,1)S(1)} copy-done((bf16[2048,1024]{1,0:T(8,128)(2,1)S(1)}, bf16[2048,1024]{1,0:T(8,128)(2,1)}, u32[]{:S(2)}) %copy-start.3) | copy-done | bytes 4194328
  18.9 0.8 project_values.5
  19.7 0.7 collective-permute-done.3.refs_2_
  20.4 1.6 %collective-permute-start.6 = (bf16[1040,128]{1,0:T(8,128)(2,1)S(1)}, bf16[1040,128]{1,0:T(8,128)(2,1)S(1)}, u32[]{:S(2)}, u32[]{:S(2)}) collective-permute-start(bf16[1040,128]{1,0:T(8,128)(2,1)S(1)} %collective-permute-done.2.refs_1_), channel_id=1, source_target_pairs={{0,4},{4,8},{8,12},{12,14},{14,10},{10,6},{6,2},{2,0},{1,5},{5,9},... | collective-permute-start | bytes 798728 | tf_op jit(solution)/shard_map/ppermute | solution.py:462
  21.9 0.4 collective-permute-start.7
  22.4 1.3 %project_keys.6 = (bf16[256,1024]{1,0:T(8,128)(2,1)S(1)}, f32[8,128]{1,0:T(8,128)S(1)}) custom-call(bf16[1040,128]{1,0:T(8,128)(2,1)S(1)} %collective-permute-done.refs_0_, bf16[1040,128]{1,0:T(8,128)(2,1)S(1)} %collective-permute-done.2.refs_1_, bf16[1040,128]{1,0:T(8,128)(2,1)S(1)} %collective-permute-done.3.refs_2_, ...), custom_call_target="tpu_custom_call" | custom-call | tf_op jit(solution)/shard_map/project_keys/pallas_call | solution.py:115
  23.7 0.3 collective-permute-done.4.refs_0_
  24.0 2.1 %collective-permute-done.5.refs_3_ = bf16[1040,128]{1,0:T(8,128)(2,1)S(1)} collective-permute-done((bf16[1040,128]{1,0:T(8,128)(2,1)S(1)}, bf16[1040,128]{1,0:T(8,128)(2,1)S(1)}, u32[]{:S(2)}, u32[]{:S(2)}) %collective-permute-start.5) | collective-permute-done | bytes 266272 | tf_op jit(solution)/shard_map/ppermute | solution.py:462
  26.1 1.6 %collective-permute-start.8 = (bf16[1040,128]{1,0:T(8,128)(2,1)S(1)}, bf16[1040,128]{1,0:T(8,128)(2,1)S(1)}, u32[]{:S(2)}, u32[]{:S(2)}) collective-permute-start(bf16[1040,128]{1,0:T(8,128)(2,1)S(1)} %collective-permute-done.4.refs_0_), channel_id=1, source_target_pairs={{0,4},{4,8},{8,12},{12,14},{14,10},{10,6},{6,2},{2,0},{1,5},{5,9},... | collective-permute-start | bytes 798728 | tf_op jit(solution)/shard_map/ppermute | solution.py:462
  27.6 0.4 collective-permute-start.9
  28.1 1.5 %project_values.6 = (bf16[2,256,1024]{2,1,0:T(8,128)(2,1)S(1)}, bf16[2,48,2048]{2,1,0:T(8,128)(2,1)S(1)}, f32[2,48,128]{2,1,0:T(8,128)S(1)}) custom-call(f32[8,128]{1,0:T(8,128)S(1)} %get-tuple-element.88.mark_ref, bf16[256,1024]{1,0:T(8,128)(2,1)S(1)} %get-tuple-element.89.keys_ref, bf16[1040,128]{1,0:T(8,128)(2,1)S(1)} %collective-permute-done.refs_0_, ...), custom_call_target="tpu_custom_call" | custom-call | tf_op jit(solution)/shard_map/project_values/pallas_call | solution.py:160
  29.6 0.1 collective-permute-done.6.refs_1_
  29.7 2.1 %collective-permute-done.7.refs_2_ = bf16[1040,128]{1,0:T(8,128)(2,1)S(1)} collective-permute-done((bf16[1040,128]{1,0:T(8,128)(2,1)S(1)}, bf16[1040,128]{1,0:T(8,128)(2,1)S(1)}, u32[]{:S(2)}, u32[]{:S(2)}) %collective-permute-start.7) | collective-permute-done | bytes 266272 | tf_op jit(solution)/shard_map/ppermute | solution.py:462
  31.8 1.6 %collective-permute-start.10 = (bf16[1040,128]{1,0:T(8,128)(2,1)S(1)}, bf16[1040,128]{1,0:T(8,128)(2,1)S(1)}, u32[]{:S(2)}, u32[]{:S(2)}) collective-permute-start(bf16[1040,128]{1,0:T(8,128)(2,1)S(1)} %collective-permute-done.6.refs_1_), channel_id=1, source_target_pairs={{0,4},{4,8},{8,12},{12,14},{14,10},{10,6},{6,2},{2,0},{1,5},{5,9},... | collective-permute-start | bytes 798728 | tf_op jit(solution)/shard_map/ppermute | solution.py:462
  33.3 0.4 collective-permute-start.11
  33.8 0.8 project_queries.3
  34.6 1.3 %project_keys.7 = (bf16[256,1024]{1,0:T(8,128)(2,1)S(1)}, f32[8,128]{1,0:T(8,128)S(1)}) custom-call(bf16[1040,128]{1,0:T(8,128)(2,1)S(1)} %collective-permute-done.4.refs_0_, bf16[1040,128]{1,0:T(8,128)(2,1)S(1)} %collective-permute-done.6.refs_1_, bf16[1040,128]{1,0:T(8,128)(2,1)S(1)} %collective-permute-done.7.refs_2_, ...), custom_call_target="tpu_custom_call" | custom-call | tf_op jit(solution)/shard_map/project_keys/pallas_call | solution.py:115
  35.9 1.6 %collective-permute-done.9.refs_3_ = bf16[1040,128]{1,0:T(8,128)(2,1)S(1)} collective-permute-done((bf16[1040,128]{1,0:T(8,128)(2,1)S(1)}, bf16[1040,128]{1,0:T(8,128)(2,1)S(1)}, u32[]{:S(2)}, u32[]{:S(2)}) %collective-permute-start.9) | collective-permute-done | bytes 266272 | tf_op jit(solution)/shard_map/ppermute | solution.py:462
  37.5 1.6 %collective-permute-start.12 = (bf16[1040,128]{1,0:T(8,128)(2,1)S(1)}, bf16[1040,128]{1,0:T(8,128)(2,1)S(1)}, u32[]{:S(2)}, u32[]{:S(2)}) collective-permute-start(bf16[1040,128]{1,0:T(8,128)(2,1)S(1)} %collective-permute-done.8.refs_0_), channel_id=1, source_target_pairs={{0,4},{4,8},{8,12},{12,14},{14,10},{10,6},{6,2},{2,0},{1,5},{5,9},... | collective-permute-start | bytes 798728 | tf_op jit(solution)/shard_map/ppermute | solution.py:462
  39.0 0.4 collective-permute-start.13
  39.5 1.5 %project_values.7 = (bf16[2,256,1024]{2,1,0:T(8,128)(2,1)S(1)}, bf16[2,48,2048]{2,1,0:T(8,128)(2,1)S(1)}, f32[2,48,128]{2,1,0:T(8,128)S(1)}) custom-call(f32[8,128]{1,0:T(8,128)S(1)} %get-tuple-element.101.mark_ref, bf16[256,1024]{1,0:T(8,128)(2,1)S(1)} %get-tuple-element.102.keys_ref, bf16[1040,128]{1,0:T(8,128)(2,1)S(1)} %collective-permute-done.4.refs_0_, ...), custom_call_target="tpu_custom_call" | custom-call | tf_op jit(solution)/shard_map/project_values/pallas_call | solution.py:160
  41.0 0.1 collective-permute-done.10.refs_1_
  41.1 0.5 collective-permute-start.16
  41.6 1.6 %collective-permute-done.11.refs_2_ = bf16[1040,128]{1,0:T(8,128)(2,1)S(1)} collective-permute-done((bf16[1040,128]{1,0:T(8,128)(2,1)S(1)}, bf16[1040,128]{1,0:T(8,128)(2,1)S(1)}, u32[]{:S(2)}, u32[]{:S(2)}) %collective-permute-start.11) | collective-permute-done | bytes 266272 | tf_op jit(solution)/shard_map/ppermute | solution.py:462
  43.2 1.3 %project_keys.8 = (bf16[256,1024]{1,0:T(8,128)(2,1)S(1)}, f32[8,128]{1,0:T(8,128)S(1)}) custom-call(bf16[1040,128]{1,0:T(8,128)(2,1)S(1)} %collective-permute-done.8.refs_0_, bf16[1040,128]{1,0:T(8,128)(2,1)S(1)} %collective-permute-done.10.refs_1_, bf16[1040,128]{1,0:T(8,128)(2,1)S(1)} %collective-permute-done.11.refs_2_, ...), custom_call_target="tpu_custom_call" | custom-call | tf_op jit(solution)/shard_map/project_keys/pallas_call | solution.py:115
  44.5 1.5 %project_values.8 = (bf16[2,256,1024]{2,1,0:T(8,128)(2,1)S(1)}, bf16[2,48,2048]{2,1,0:T(8,128)(2,1)S(1)}, f32[2,48,128]{2,1,0:T(8,128)S(1)}) custom-call(f32[8,128]{1,0:T(8,128)S(1)} %get-tuple-element.107.mark_ref, bf16[256,1024]{1,0:T(8,128)(2,1)S(1)} %get-tuple-element.108.keys_ref, bf16[1040,128]{1,0:T(8,128)(2,1)S(1)} %collective-permute-done.8.refs_0_, ...), custom_call_target="tpu_custom_call" | custom-call | tf_op jit(solution)/shard_map/project_values/pallas_call | solution.py:160
  46.0 1.0 %project_queries.4 = (bf16[2,48,1024]{2,1,0:T(8,128)(2,1)S(1)}, bf16[2,48,1024]{2,1,0:T(8,128)(2,1)S(1)}) custom-call(bf16[2,48,2048]{2,1,0:T(8,128)(2,1)S(1)} %get-tuple-element.110.refs_0_, bf16[2,48,2048]{2,1,0:T(8,128)(2,1)S(1)} %get-tuple-element.111.refs_1_, bf16[2048,1024]{1,0:T(8,128)(2,1)S(1)} %bitcast.12, bf16[1024,2048]{1,0:T(8,128)(2,1)S(1)} %bitcast.6), custom_call_target="tpu_custom_call" | custom-call | tf_op jit(solution)/shard_map/project_queries/pallas_call | solution.py:189
  47.0 0.4 collective-permute-done.13.refs_1_
  47.4 0.5 collective-permute-start.14
  47.9 0.7 project_keys.9
  48.7 0.8 project_values.9
  49.5 0.1 collective-permute-start.18
  49.6 0.8 project_queries.5.refs_14_
  50.4 0.4 collective-permute-done.14.refs_5_
  50.8 0.7 collective-permute-done.18.refs_9_
  51.6 0.7 arrange.1
  52.2 4.6 %attend.3 = (bf16[40,2048]{1,0:T(8,128)(2,1)S(1)}, bf16[40,2048]{1,0:T(8,128)(2,1)S(1)}) custom-call(bf16[2,16,128,1024]{3,2,1,0:T(8,128)(2,1)S(1)} %get-tuple-element.131.panel_ref, bf16[8,48,1024]{2,1,0:T(8,128)(2,1)S(1)} %get-tuple-element.132.queries_ref, f32[8,48,128]{2,1,0:T(8,128)S(1)} %get-tuple-element.139.places_ref, bf16[1024,2048]{1,0:T(8,128)(2,1)S(1)} %bitcast.8), custom_call_target="tpu_custom_call" | custom-call | flops 1207959552 | bytes 8388608 | tf_op jit(solution)/shard_map/attend/pallas_call | solution.py:338
  56.9 0.9 collective-permute-start.19
  57.8 1.8 %collective-permute-start.23 = (bf16[40,2048]{1,0:T(8,128)(2,1)S(1)}, bf16[40,2048]{1,0:T(8,128)(2,1)S(1)}, u32[]{:S(2)}, u32[]{:S(2)}) collective-permute-start(bf16[40,2048]{1,0:T(8,128)(2,1)S(1)} %get-tuple-element.150), channel_id=1, source_target_pairs={{0,10},{2,8},{4,14},{6,12},{8,2},{10,0},{12,6},{14,4},{1,11},{3,9}... | collective-permute-start | bytes 491528 | tf_op jit(solution)/shard_map/ppermute | solution.py:505
  59.6 6.0 %attend.4 = (bf16[40,2048]{1,0:T(8,128)(2,1)S(1)}, bf16[40,2048]{1,0:T(8,128)(2,1)S(1)}) custom-call(bf16[2,16,128,1024]{3,2,1,0:T(8,128)(2,1)S(1)} %get-tuple-element.131.panel_ref, bf16[8,48,1024]{2,1,0:T(8,128)(2,1)S(1)} %get-tuple-element.132.queries_ref, f32[8,48,128]{2,1,0:T(8,128)S(1)} %get-tuple-element.139.places_ref, bf16[1024,2048]{1,0:T(8,128)(2,1)S(1)} %bitcast.9), custom_call_target="tpu_custom_call" | custom-call | flops 1207959552 | bytes 8388608 | tf_op jit(solution)/shard_map/attend/pallas_call | solution.py:338
  65.6 0.1 collective-permute-start.24
  65.6 5.0 %collective-permute-start.25 = (bf16[40,2048]{1,0:T(8,128)(2,1)S(1)}, bf16[40,2048]{1,0:T(8,128)(2,1)S(1)}, u32[]{:S(2)}, u32[]{:S(2)}) collective-permute-start(bf16[40,2048]{1,0:T(8,128)(2,1)S(1)} %get-tuple-element.152), channel_id=1, source_target_pairs={{0,14},{2,12},{4,10},{6,8},{8,6},{10,4},{12,2},{14,0},{1,15},{3,13... | collective-permute-start | bytes 491528 | tf_op jit(solution)/shard_map/ppermute | solution.py:505
  70.6 5.4 %attend.5 = (bf16[40,2048]{1,0:T(8,128)(2,1)S(1)}, bf16[40,2048]{1,0:T(8,128)(2,1)S(1)}, bf16[40,2048]{1,0:T(8,128)(2,1)S(1)}, bf16[40,2048]{1,0:T(8,128)(2,1)S(1)}) custom-call(bf16[2,16,128,1024]{3,2,1,0:T(8,128)(2,1)S(1)} %get-tuple-element.131.panel_ref, bf16[8,48,1024]{2,1,0:T(8,128)(2,1)S(1)} %get-tuple-element.132.queries_ref, ...), custom_call_target="tpu_custom_call" | custom-call | flops 2415919104 | bytes 8388608 | tf_op jit(solution)/shard_map/attend/pallas_call | solution.py:338
  76.0 2.9 %collective-permute-done.19.refs_4_ = bf16[40,2048]{1,0:T(8,128)(2,1)S(1)} collective-permute-done((bf16[40,2048]{1,0:T(8,128)(2,1)S(1)}, bf16[40,2048]{1,0:T(8,128)(2,1)S(1)}, u32[]{:S(2)}, u32[]{:S(2)}) %collective-permute-start.19) | collective-permute-done | bytes 163872 | tf_op jit(solution)/shard_map/ppermute | solution.py:505
  78.9 0.3 collective-permute-start.20
  79.2 2.9 %collective-permute-done.23.refs_5_ = bf16[40,2048]{1,0:T(8,128)(2,1)S(1)} collective-permute-done((bf16[40,2048]{1,0:T(8,128)(2,1)S(1)}, bf16[40,2048]{1,0:T(8,128)(2,1)S(1)}, u32[]{:S(2)}, u32[]{:S(2)}) %collective-permute-start.23) | collective-permute-done | bytes 163872 | tf_op jit(solution)/shard_map/ppermute | solution.py:505
  82.2 0.3 collective-permute-start.22
  82.4 0.5 gate_mix.1.mix_ref
  82.9 2.7 %collective-permute-done.20.refs_1_ = bf16[40,2048]{1,0:T(8,128)(2,1)S(1)} collective-permute-done((bf16[40,2048]{1,0:T(8,128)(2,1)S(1)}, bf16[40,2048]{1,0:T(8,128)(2,1)S(1)}, u32[]{:S(2)}, u32[]{:S(2)}) %collective-permute-start.20) | collective-permute-done | bytes 163872 | tf_op jit(solution)/shard_map/ppermute | solution.py:505
  85.6 0.3 collective-permute-done.21.refs_2_
  85.9 3.3 %collective-permute-done.22.refs_3_ = bf16[40,2048]{1,0:T(8,128)(2,1)S(1)} collective-permute-done((bf16[40,2048]{1,0:T(8,128)(2,1)S(1)}, bf16[40,2048]{1,0:T(8,128)(2,1)S(1)}, u32[]{:S(2)}, u32[]{:S(2)}) %collective-permute-start.22) | collective-permute-done | bytes 163872 | tf_op jit(solution)/shard_map/ppermute | solution.py:505
  89.2 1.5 %combine.1 = bf16[128,2048]{1,0:T(8,128)(2,1)} custom-call(bf16[256,384]{1,0:T(8,128)(2,1)S(1)} %gate_mix.1.mix_ref, bf16[40,2048]{1,0:T(8,128)(2,1)S(1)} %get-tuple-element.145.refs_0_, bf16[40,2048]{1,0:T(8,128)(2,1)S(1)} %collective-permute-done.20.refs_1_, bf16[40,2048]{1,0:T(8,128)(2,1)S(1)} %collective-permute-done.21.refs_2_, ...), custom_call_target="tpu_custom_call" | custom-call | tf_op jit(solution)/shard_map/combine/pallas_call | solution.py:426
  (30 shorter events, 0.1 us)
Async XLA Ops:
  2.0 10.5 %collective-permute-start = (bf16[1040,128]{1,0:T(8,128)(2,1)}, bf16[1040,128]{1,0:T(8,128)(2,1)S(1)}, u32[]{:S(2)}, u32[]{:S(2)}) collective-permute-start(bf16[1040,128]{1,0:T(8,128)(2,1)} %get-tuple-element.79.top_ref.refs_0_), channel_id=1, source_target_pairs={{0,4},{4,8},{8,12},{12,14},{14,10},{10,6},{6,2},{2,0},{1,5},{5,9},... | collective-permute-start | bytes 798728 | tf_op jit(solution)/shard_map/ppermute | solution.py:462
  5.1 9.5 %collective-permute-start.1 = (bf16[1040,128]{1,0:T(8,128)(2,1)}, bf16[1040,128]{1,0:T(8,128)(2,1)S(1)}, u32[]{:S(2)}, u32[]{:S(2)}) collective-permute-start(bf16[1040,128]{1,0:T(8,128)(2,1)} %get-tuple-element.80.bottom_ref.refs_1_), channel_id=1, source_target_pairs={{4,0},{8,4},{12,8},{14,12},{10,14},{6,10},{2,6},{0,2},{5,1},{9,5},... | collective-permute-start | bytes 798728 | tf_op jit(solution)/shard_map/ppermute | solution.py:462
  5.1 15.2 %collective-permute-start.3 = (bf16[1040,128]{1,0:T(8,128)(2,1)}, bf16[1040,128]{1,0:T(8,128)(2,1)S(1)}, u32[]{:S(2)}, u32[]{:S(2)}) collective-permute-start(bf16[1040,128]{1,0:T(8,128)(2,1)} %get-tuple-element.79.top_ref.refs_0_), channel_id=1, source_target_pairs={{4,0},{8,4},{12,8},{14,12},{10,14},{6,10},{2,6},{0,2},{5,1},{9,5},... | collective-permute-start | bytes 798728 | tf_op jit(solution)/shard_map/ppermute | solution.py:462
  7.1 13.3 %collective-permute-start.2 = (bf16[1040,128]{1,0:T(8,128)(2,1)}, bf16[1040,128]{1,0:T(8,128)(2,1)S(1)}, u32[]{:S(2)}, u32[]{:S(2)}) collective-permute-start(bf16[1040,128]{1,0:T(8,128)(2,1)} %get-tuple-element.80.bottom_ref.refs_1_), channel_id=1, source_target_pairs={{0,4},{4,8},{8,12},{12,14},{14,10},{10,6},{6,2},{2,0},{1,5},{5,9},... | collective-permute-start | bytes 798728 | tf_op jit(solution)/shard_map/ppermute | solution.py:462
  7.2 2.2 %copy-start.1 = (bf16[2048,1024]{1,0:T(8,128)(2,1)S(1)}, bf16[2048,1024]{1,0:T(8,128)(2,1)}, u32[]{:S(2)}) copy-start(bf16[2048,1024]{1,0:T(8,128)(2,1)} %refs_2_.6) | copy-start | bytes 12582916
  9.4 1.0 %copy-start.6 = (bf16[1040,128]{1,0:T(8,128)(2,1)S(1)}, bf16[1040,128]{1,0:T(8,128)(2,1)}, u32[]{:S(2)}) copy-start(bf16[1040,128]{1,0:T(8,128)(2,1)} %get-tuple-element.79.top_ref.refs_0_) | copy-start | bytes 798724
  10.3 1.0 %copy-start.8 = (bf16[1040,128]{1,0:T(8,128)(2,1)S(1)}, bf16[1040,128]{1,0:T(8,128)(2,1)}, u32[]{:S(2)}) copy-start(bf16[1040,128]{1,0:T(8,128)(2,1)} %get-tuple-element.80.bottom_ref.refs_1_) | copy-start | bytes 798724
  11.3 11.1 %copy-start.2 = (bf16[2048,1024]{1,0:T(8,128)(2,1)S(1)}, bf16[2048,1024]{1,0:T(8,128)(2,1)}, u32[]{:S(2)}) copy-start(bf16[2048,1024]{1,0:T(8,128)(2,1)} %refs_2_.6) | copy-start | bytes 12582916
  14.6 9.3 %collective-permute-start.4 = (bf16[1040,128]{1,0:T(8,128)(2,1)S(1)}, bf16[1040,128]{1,0:T(8,128)(2,1)S(1)}, u32[]{:S(2)}, u32[]{:S(2)}) collective-permute-start(bf16[1040,128]{1,0:T(8,128)(2,1)S(1)} %collective-permute-done.refs_0_), channel_id=1, source_target_pairs={{0,4},{4,8},{8,12},{12,14},{14,10},{10,6},{6,2},{2,0},{1,5},{5,9},... | collective-permute-start | bytes 798728 | tf_op jit(solution)/shard_map/ppermute | solution.py:462
  16.2 9.8 %collective-permute-start.5 = (bf16[1040,128]{1,0:T(8,128)(2,1)S(1)}, bf16[1040,128]{1,0:T(8,128)(2,1)S(1)}, u32[]{:S(2)}, u32[]{:S(2)}) collective-permute-start(bf16[1040,128]{1,0:T(8,128)(2,1)S(1)} %collective-permute-done.1.refs_3_), channel_id=1, source_target_pairs={{4,0},{8,4},{12,8},{14,12},{10,14},{6,10},{2,6},{0,2},{5,1},{9,5},... | collective-permute-start | bytes 798728 | tf_op jit(solution)/shard_map/ppermute | solution.py:462
  16.7 2.2 %copy-start.3 = (bf16[2048,1024]{1,0:T(8,128)(2,1)S(1)}, bf16[2048,1024]{1,0:T(8,128)(2,1)}, u32[]{:S(2)}) copy-start(bf16[2048,1024]{1,0:T(8,128)(2,1)} %refs_2_.7) | copy-start | bytes 12582916
  18.9 9.2 %copy-start.4 = (bf16[2048,1024]{1,0:T(8,128)(2,1)S(1)}, bf16[2048,1024]{1,0:T(8,128)(2,1)}, u32[]{:S(2)}) copy-start(bf16[2048,1024]{1,0:T(8,128)(2,1)} %refs_2_.7) | copy-start | bytes 12582916
  20.4 9.3 %collective-permute-start.6 = (bf16[1040,128]{1,0:T(8,128)(2,1)S(1)}, bf16[1040,128]{1,0:T(8,128)(2,1)S(1)}, u32[]{:S(2)}, u32[]{:S(2)}) collective-permute-start(bf16[1040,128]{1,0:T(8,128)(2,1)S(1)} %collective-permute-done.2.refs_1_), channel_id=1, source_target_pairs={{0,4},{4,8},{8,12},{12,14},{14,10},{10,6},{6,2},{2,0},{1,5},{5,9},... | collective-permute-start | bytes 798728 | tf_op jit(solution)/shard_map/ppermute | solution.py:462
  21.9 9.8 %collective-permute-start.7 = (bf16[1040,128]{1,0:T(8,128)(2,1)S(1)}, bf16[1040,128]{1,0:T(8,128)(2,1)S(1)}, u32[]{:S(2)}, u32[]{:S(2)}) collective-permute-start(bf16[1040,128]{1,0:T(8,128)(2,1)S(1)} %collective-permute-done.3.refs_2_), channel_id=1, source_target_pairs={{4,0},{8,4},{12,8},{14,12},{10,14},{6,10},{2,6},{0,2},{5,1},{9,5},... | collective-permute-start | bytes 798728 | tf_op jit(solution)/shard_map/ppermute | solution.py:462
  22.4 11.4 %copy-start.5 = (bf16[1,2048,1024]{2,1,0:T(8,128)(2,1)S(1)}, bf16[1,2048,1024]{2,1,0:T(8,128)(2,1)}, u32[]{:S(2)}) copy-start(bf16[1,2048,1024]{2,1,0:T(8,128)(2,1)} %param.14) | copy-start | bytes 12582916
  23.7 10.1 %copy-start = (bf16[1,1024,2048]{2,1,0:T(8,128)(2,1)S(1)}, bf16[1,1024,2048]{2,1,0:T(8,128)(2,1)}, u32[]{:S(2)}) copy-start(bf16[1,1024,2048]{2,1,0:T(8,128)(2,1)} %param.15) | copy-start | bytes 12582916
  26.1 9.8 %collective-permute-start.8 = (bf16[1040,128]{1,0:T(8,128)(2,1)S(1)}, bf16[1040,128]{1,0:T(8,128)(2,1)S(1)}, u32[]{:S(2)}, u32[]{:S(2)}) collective-permute-start(bf16[1040,128]{1,0:T(8,128)(2,1)S(1)} %collective-permute-done.4.refs_0_), channel_id=1, source_target_pairs={{0,4},{4,8},{8,12},{12,14},{14,10},{10,6},{6,2},{2,0},{1,5},{5,9},... | collective-permute-start | bytes 798728 | tf_op jit(solution)/shard_map/ppermute | solution.py:462
  27.6 9.8 %collective-permute-start.9 = (bf16[1040,128]{1,0:T(8,128)(2,1)S(1)}, bf16[1040,128]{1,0:T(8,128)(2,1)S(1)}, u32[]{:S(2)}, u32[]{:S(2)}) collective-permute-start(bf16[1040,128]{1,0:T(8,128)(2,1)S(1)} %collective-permute-done.5.refs_3_), channel_id=1, source_target_pairs={{4,0},{8,4},{12,8},{14,12},{10,14},{6,10},{2,6},{0,2},{5,1},{9,5},... | collective-permute-start | bytes 798728 | tf_op jit(solution)/shard_map/ppermute | solution.py:462
  31.8 9.3 %collective-permute-start.10 = (bf16[1040,128]{1,0:T(8,128)(2,1)S(1)}, bf16[1040,128]{1,0:T(8,128)(2,1)S(1)}, u32[]{:S(2)}, u32[]{:S(2)}) collective-permute-start(bf16[1040,128]{1,0:T(8,128)(2,1)S(1)} %collective-permute-done.6.refs_1_), channel_id=1, source_target_pairs={{0,4},{4,8},{8,12},{12,14},{14,10},{10,6},{6,2},{2,0},{1,5},{5,9},... | collective-permute-start | bytes 798728 | tf_op jit(solution)/shard_map/ppermute | solution.py:462
  33.3 9.8 %collective-permute-start.11 = (bf16[1040,128]{1,0:T(8,128)(2,1)S(1)}, bf16[1040,128]{1,0:T(8,128)(2,1)S(1)}, u32[]{:S(2)}, u32[]{:S(2)}) collective-permute-start(bf16[1040,128]{1,0:T(8,128)(2,1)S(1)} %collective-permute-done.7.refs_2_), channel_id=1, source_target_pairs={{4,0},{8,4},{12,8},{14,12},{10,14},{6,10},{2,6},{0,2},{5,1},{9,5},... | collective-permute-start | bytes 798728 | tf_op jit(solution)/shard_map/ppermute | solution.py:462
  37.5 9.5 %collective-permute-start.12 = (bf16[1040,128]{1,0:T(8,128)(2,1)S(1)}, bf16[1040,128]{1,0:T(8,128)(2,1)S(1)}, u32[]{:S(2)}, u32[]{:S(2)}) collective-permute-start(bf16[1040,128]{1,0:T(8,128)(2,1)S(1)} %collective-permute-done.8.refs_0_), channel_id=1, source_target_pairs={{0,4},{4,8},{8,12},{12,14},{14,10},{10,6},{6,2},{2,0},{1,5},{5,9},... | collective-permute-start | bytes 798728 | tf_op jit(solution)/shard_map/ppermute | solution.py:462
  39.0 8.4 %collective-permute-start.13 = (bf16[1040,128]{1,0:T(8,128)(2,1)S(1)}, bf16[1040,128]{1,0:T(8,128)(2,1)S(1)}, u32[]{:S(2)}, u32[]{:S(2)}) collective-permute-start(bf16[1040,128]{1,0:T(8,128)(2,1)S(1)} %collective-permute-done.9.refs_3_), channel_id=1, source_target_pairs={{4,0},{8,4},{12,8},{14,12},{10,14},{6,10},{2,6},{0,2},{5,1},{9,5},... | collective-permute-start | bytes 798728 | tf_op jit(solution)/shard_map/ppermute | solution.py:462
  39.5 11.3 %collective-permute-start.15 = (bf16[2,256,1024]{2,1,0:T(8,128)(2,1)S(1)}, bf16[2,256,1024]{2,1,0:T(8,128)(2,1)S(1)}, u32[]{:S(2)}, u32[]{:S(2)}) collective-permute-start(bf16[2,256,1024]{2,1,0:T(8,128)(2,1)S(1)} %get-tuple-element.90.refs_1_), channel_id=1, source_target_pairs={{0,1},{1,0},{2,3},{3,2},{4,5},{5,4},{6,7},{7,6},{8,9},{9,8},{10,11... | collective-permute-start | bytes 3145736 | tf_op jit(solution)/shard_map/ppermute | solution.py:465
  41.1 10.5 %collective-permute-start.16 = (bf16[2,256,1024]{2,1,0:T(8,128)(2,1)S(1)}, bf16[2,256,1024]{2,1,0:T(8,128)(2,1)S(1)}, u32[]{:S(2)}, u32[]{:S(2)}) collective-permute-start(bf16[2,256,1024]{2,1,0:T(8,128)(2,1)S(1)} %get-tuple-element.103.refs_2_), channel_id=1, source_target_pairs={{0,1},{1,0},{2,3},{3,2},{4,5},{5,4},{6,7},{7,6},{8,9},{9,8},{10,11... | collective-permute-start | bytes 3145736 | tf_op jit(solution)/shard_map/ppermute | solution.py:465
  47.4 4.2 %collective-permute-start.17 = (bf16[2,256,1024]{2,1,0:T(8,128)(2,1)S(1)}, bf16[2,256,1024]{2,1,0:T(8,128)(2,1)S(1)}, u32[]{:S(2)}, u32[]{:S(2)}) collective-permute-start(bf16[2,256,1024]{2,1,0:T(8,128)(2,1)S(1)} %get-tuple-element.115.refs_3_), channel_id=1, source_target_pairs={{0,1},{1,0},{2,3},{3,2},{4,5},{5,4},{6,7},{7,6},{8,9},{9,8},{10,11... | collective-permute-start | bytes 3145736 | tf_op jit(solution)/shard_map/ppermute | solution.py:465
  47.4 3.4 %collective-permute-start.14 = (bf16[2,128,1024]{2,1,0:T(8,128)(2,1)S(1)}, bf16[2,128,1024]{2,1,0:T(8,128)(2,1)S(1)}, u32[]{:S(2)}, u32[]{:S(2)}) collective-permute-start(bf16[2,128,1024]{2,1,0:T(8,128)(2,1)S(1)} %get-tuple-element.84.refs_0_), channel_id=1, source_target_pairs={{0,1},{1,0},{2,3},{3,2},{4,5},{5,4},{6,7},{7,6},{8,9},{9,8},{10,11... | collective-permute-start | bytes 1572872 | tf_op jit(solution)/shard_map/ppermute | solution.py:465
  49.5 2.1 %collective-permute-start.18 = (bf16[2,128,1024]{2,1,0:T(8,128)(2,1)S(1)}, bf16[2,128,1024]{2,1,0:T(8,128)(2,1)S(1)}, u32[]{:S(2)}, u32[]{:S(2)}) collective-permute-start(bf16[2,128,1024]{2,1,0:T(8,128)(2,1)S(1)} %get-tuple-element.120.refs_4_), channel_id=1, source_target_pairs={{0,1},{1,0},{2,3},{3,2},{4,5},{5,4},{6,7},{7,6},{8,9},{9,8},{10,11... | collective-permute-start | bytes 1572872 | tf_op jit(solution)/shard_map/ppermute | solution.py:465
  56.9 22.1 %collective-permute-start.19 = (bf16[40,2048]{1,0:T(8,128)(2,1)S(1)}, bf16[40,2048]{1,0:T(8,128)(2,1)S(1)}, u32[]{:S(2)}, u32[]{:S(2)}) collective-permute-start(bf16[40,2048]{1,0:T(8,128)(2,1)S(1)} %get-tuple-element.144), channel_id=1, source_target_pairs={{0,8},{2,10},{4,12},{6,14},{8,0},{10,2},{12,4},{14,6},{1,9},{3,11}... | collective-permute-start | bytes 491528 | tf_op jit(solution)/shard_map/ppermute | solution.py:505
  57.8 24.4 %collective-permute-start.23 = (bf16[40,2048]{1,0:T(8,128)(2,1)S(1)}, bf16[40,2048]{1,0:T(8,128)(2,1)S(1)}, u32[]{:S(2)}, u32[]{:S(2)}) collective-permute-start(bf16[40,2048]{1,0:T(8,128)(2,1)S(1)} %get-tuple-element.150), channel_id=1, source_target_pairs={{0,10},{2,8},{4,14},{6,12},{8,2},{10,0},{12,6},{14,4},{1,11},{3,9}... | collective-permute-start | bytes 491528 | tf_op jit(solution)/shard_map/ppermute | solution.py:505
  65.5 16.9 %copy-start.7 = (bf16[1040,128]{1,0:T(8,128)(2,1)S(1)}, bf16[1040,128]{1,0:T(8,128)(2,1)}, u32[]{:S(2)}) copy-start(bf16[1040,128]{1,0:T(8,128)(2,1)} %get-tuple-element.79.top_ref.refs_0_) | copy-start | bytes 798724
  65.5 16.9 %copy-start.9 = (bf16[1040,128]{1,0:T(8,128)(2,1)S(1)}, bf16[1040,128]{1,0:T(8,128)(2,1)}, u32[]{:S(2)}) copy-start(bf16[1040,128]{1,0:T(8,128)(2,1)} %get-tuple-element.80.bottom_ref.refs_1_) | copy-start | bytes 798724
  65.6 16.9 %copy-start.10 = (f32[2048,8]{0,1:T(8,128)S(1)}, f32[2048,8]{0,1:T(8,128)}, u32[]{:S(2)}) copy-start(f32[2048,8]{0,1:T(8,128)} %param.10) | copy-start | bytes 196612
  65.6 17.3 %collective-permute-start.24 = (bf16[40,2048]{1,0:T(8,128)(2,1)S(1)}, bf16[40,2048]{1,0:T(8,128)(2,1)S(1)}, u32[]{:S(2)}, u32[]{:S(2)}) collective-permute-start(bf16[40,2048]{1,0:T(8,128)(2,1)S(1)} %get-tuple-element.151), channel_id=1, source_target_pairs={{0,12},{2,14},{4,8},{6,10},{8,4},{10,6},{12,0},{14,2},{1,13},{3,15... | collective-permute-start | bytes 491528 | tf_op jit(solution)/shard_map/ppermute | solution.py:505
  65.6 17.2 %collective-permute-start.25 = (bf16[40,2048]{1,0:T(8,128)(2,1)S(1)}, bf16[40,2048]{1,0:T(8,128)(2,1)S(1)}, u32[]{:S(2)}, u32[]{:S(2)}) collective-permute-start(bf16[40,2048]{1,0:T(8,128)(2,1)S(1)} %get-tuple-element.152), channel_id=1, source_target_pairs={{0,14},{2,12},{4,10},{6,8},{8,6},{10,4},{12,2},{14,0},{1,15},{3,13... | collective-permute-start | bytes 491528 | tf_op jit(solution)/shard_map/ppermute | solution.py:505
  78.9 6.6 %collective-permute-start.20 = (bf16[40,2048]{1,0:T(8,128)(2,1)S(1)}, bf16[40,2048]{1,0:T(8,128)(2,1)S(1)}, u32[]{:S(2)}, u32[]{:S(2)}) collective-permute-start(bf16[40,2048]{1,0:T(8,128)(2,1)S(1)} %get-tuple-element.146), channel_id=1, source_target_pairs={{0,2},{2,0},{4,6},{6,4},{8,10},{10,8},{12,14},{14,12},{1,3},{3,1},... | collective-permute-start | bytes 491528 | tf_op jit(solution)/shard_map/ppermute | solution.py:505
  79.2 6.7 %collective-permute-start.21 = (bf16[40,2048]{1,0:T(8,128)(2,1)S(1)}, bf16[40,2048]{1,0:T(8,128)(2,1)S(1)}, u32[]{:S(2)}, u32[]{:S(2)}) collective-permute-start(bf16[40,2048]{1,0:T(8,128)(2,1)S(1)} %get-tuple-element.147), channel_id=1, source_target_pairs={{0,4},{2,6},{4,0},{6,2},{8,12},{10,14},{12,8},{14,10},{1,5},{3,7},... | collective-permute-start | bytes 491528 | tf_op jit(solution)/shard_map/ppermute | solution.py:505
  82.2 7.1 %collective-permute-start.22 = (bf16[40,2048]{1,0:T(8,128)(2,1)S(1)}, bf16[40,2048]{1,0:T(8,128)(2,1)S(1)}, u32[]{:S(2)}, u32[]{:S(2)}) collective-permute-start(bf16[40,2048]{1,0:T(8,128)(2,1)S(1)} %get-tuple-element.148), channel_id=1, source_target_pairs={{0,6},{2,4},{4,2},{6,0},{8,14},{10,12},{12,10},{14,8},{1,7},{3,5},... | collective-permute-start | bytes 491528 | tf_op jit(solution)/shard_map/ppermute | solution.py:505

commit v11 on v9

--- a/solution.py
+++ b/solution.py
@@ -15,7 +15,7 @@
 MASKED = -1e30
 LANES = 128
 CODES = 16
-TERMS = 3
+TERMS = 2
 MIB = 1 << 20
 WHOLE = pl.BlockSpec(memory_space=pltpu.VMEM)
 
@@ -89,7 +89,7 @@
         out_shape=[half, half],
         scratch_shapes=[pltpu.VMEM(x.shape, x.dtype) for x in operands]
         + [pltpu.SemaphoreType.DMA((3,))],
-        compiler_params=pltpu.CompilerParams(vmem_limit_bytes=8 * MIB),
+        compiler_params=pltpu.CompilerParams(vmem_limit_bytes=60 * MIB),
         name="norm_rows",
     )(*operands)
 
@@ -172,8 +172,8 @@
 
 
 def queries_kernel(*refs):
-    count = len(refs) // 2
-    picked, weight_ref, outs = refs[:count], refs[count], refs[count + 1 :]
+    count = len(refs) // 2 - 1
+    picked, weight_ref, outs = refs[:count], refs[count], refs[count + 2 :]
     rows = jnp.concatenate([ref[g] for ref in picked for g in range(ref.shape[0])], axis=0)
     places = [(ref, g) for ref in outs for g in range(ref.shape[0])]
     for cols in column_parts(weight_ref):
@@ -182,20 +182,20 @@
             ref[g, :, cols] = product[i * SLOTS : (i + 1) * SLOTS].astype(jnp.bfloat16)
 
 
-def project_queries(picked, query_slab):
+def project_queries(picked, query_slab, next_slab):
     model_width, width = query_slab.shape
     owners = sum(rows.shape[0] for rows in picked)
-    held = 2 * model_width * width + owners * SLOTS * (4 * model_width + 4 * width)
+    held = 4 * model_width * width + owners * SLOTS * (4 * model_width + 4 * width)
     return pl.pallas_call(
         queries_kernel,
-        in_specs=[WHOLE] * (len(picked) + 1),
+        in_specs=[WHOLE] * (len(picked) + 2),
         out_specs=[WHOLE] * len(picked),
         out_shape=[
             jax.ShapeDtypeStruct((rows.shape[0], SLOTS, width), jnp.bfloat16) for rows in picked
         ],
         compiler_params=pltpu.CompilerParams(vmem_limit_bytes=held + 6 * MIB),
         name="project_queries",
-    )(*picked, query_slab)
+    )(*picked, query_slab, next_slab)
 
 
 def arrange_kernel(plan, *refs):
@@ -320,7 +320,7 @@
     first, count = lots
     _, blocks, tok_count, width = panel.shape
     length = blocks * tok_count
-    heads = min(4, width // HS) if blocks <= 16 else 1
+    heads = min(2, width // HS) if blocks <= 16 else 1
     model_width = output_slab.shape[1]
     held = heads * 2 * SLOTS * length * 6 + 2 * length * width * 2 + width * model_width * 2
     held += 2 * count * SLOTS * (model_width * 8 + width * 2)
@@ -342,6 +342,10 @@
         ),
         name="attend",
     )(panel, queries, places, output_slab)
+
+
+def order_of_pieces(count):
+    return [0, *range(count // 2 - 1, 0, -1), *range(count // 2, count)]
 
 
 def mix_kernel(quarter_count, top_ref, bottom_ref, router_ref, mix_ref, slots_ref, gates_ref):
@@ -367,7 +371,7 @@
     tok_count = slots.shape[1]
     order = lax.broadcasted_iota(jnp.int32, (SLOTS, tok_count), 0).astype(jnp.float32)
     parts = []
-    for k in range(mix_ref.shape[1] // SLOTS):
+    for k in order_of_pieces(mix_ref.shape[1] // SLOTS):
         expert = pl.ds((lax.axis_index("ctx") ^ k) // quarter_count, 1)
         parts.append(jnp.where(order == slots_ref[expert, :], gates_ref[expert, :], 0.0))
     total = jnp.concatenate(parts, axis=0).T
@@ -463,7 +467,7 @@
         keys, mark = project_keys(token_half, blocks, key_weight)
         following = [lead[0], rest[0], rest[1], lead[1]]
         if step == steps - 2:
-            queries = project_queries(picked, query_slab)
+            queries = project_queries(picked, query_slab, output_slab)
             picked = []
         if step < steps - 1:
             mark, *lead_next = tie(mark, *lead, *queries)
@@ -479,14 +483,15 @@
         if step < steps - 1:
             other.append(hand_over(panel))
         blocks = following
-    own[-1], *blocks = tie(own[-1], *lead)
+    queries = [*queries, *project_queries(picked, query_slab, output_slab)]
+    own[-1], queries[-1], other[0], *blocks = tie(own[-1], queries[-1], other[0], *lead)
     other.append(hand_over(own[-1]))
     keys, mark = project_keys(token_half, blocks, key_weight)
     panel, rows, position = project_values(token_half, blocks, plan[-1], mark, keys, value_weight)
     own.append(panel)
     other.append(hand_over(panel))
     positions.append(position)
-    queries = [*queries, *project_queries(picked + [rows], query_slab)]
+    queries = [*queries, *project_queries([rows], query_slab, output_slab)]
     held = arrange(ctx_count, plan, own, other, queries, positions)
 
     def swap(piece, k):
@@ -506,7 +511,8 @@
     near = [near[0]] + [swap(near[r], r) for r in range(1, half)]
 
     mix = gate_mix(quarter_count, halves, router_weight.T, ctx_count)
-    return combine(mix, [*near, *far[0], *far[1]])
+    pieces = [*near, *far[0], *far[1]]
+    return combine(mix, [pieces[k] for k in order_of_pieces(ctx_count)])
 
 
 def solution(mesh):

time: 93.2 us -> 91.7 us (0.984)
  waiting for transfers between devices: 28.3 us -> 20.4 us
  Pallas kernels: 31.3 us -> 36.3 us
  starting transfers between devices: 24.7 us -> 27.2 us
  local copies, waits for them, and re-layouts: 8.3 us -> 6.31 us
    ppermute x7, waiting for transfers between devices: 13.3 us -> 7.68 us  [swap(): return lax.ppermute(piece, 'ctx', [(c, c ^ k) for c in range(ctx_count)])]
    ppermute x7, starting transfers between devices: 8.31 us -> 11.3 us  [swap(): return lax.ppermute(piece, 'ctx', [(c, c ^ k) for c in range(ctx_count)])]
    pallas_call x3, Pallas kernels: 14.6 us -> 17.6 us  [attend(): pl.pallas_call(functools.partial(attend_kernel, lots, heads), in_specs=[W...]
    unnamed x20 -> x22, local copies, waits for them, and re-layouts: 8.3 us -> 6.31 us
    ppermute x7, waiting for transfers between devices: 2.71 us -> 0.98 us  [send(): lax.ppermute(parts[0], 'ctx', forward)]
    pallas_call x1, Pallas kernels: 0.31 us -> 2.03 us  [norm_rows(): pl.pallas_call(norm_kernel, in_specs=[pl.BlockSpec(memory_space=pltpu.HBM...]
    pallas_call x2 -> x3, Pallas kernels: 2.01 us -> 2.6 us  [project_queries(): pl.pallas_call(queries_kernel, in_specs=[WHOLE] * (len(picked) + 2), out_...]
  transfers between devices with their start and end apart: 26 -> 26, of which waited for: 17 -> 16; matrix products, arithmetic and copies ran while one was open for 0% -> 0% of each run, Pallas kernels for 26% -> 30%
where the time goes in v11:
time: 91.7 us; the launch traced here: 90.4 us
  Pallas kernels  36.3 us (40%)
  starting transfers between devices  27.2 us (30%)
  waiting for transfers between devices  20.4 us (22%)
  local copies, waits for them, and re-layouts  6.31 us (7%)
    pallas_call x3, Pallas kernels, attend(): pl.pallas_call(functools.partial(attend_kernel, lots, heads), in_specs=[W...  17.6 us
    ppermute x7, starting transfers between devices, swap(): return lax.ppermute(piece, 'ctx', [(c, c ^ k) for c in range(ctx_count)])  11.3 us
    ppermute x7, starting transfers between devices, send(): lax.ppermute(parts[0], 'ctx', forward)  11.1 us
    ppermute x7, waiting for transfers between devices, send(): lax.ppermute(parts[1], 'ctx', backward)  11 us
    ppermute x7, waiting for transfers between devices, swap(): return lax.ppermute(piece, 'ctx', [(c, c ^ k) for c in range(ctx_count)])  7.68 us
    unnamed x22, local copies, waits for them, and re-layouts  6.31 us
    pallas_call x5, Pallas kernels, project_values(): pl.pallas_call(functools.partial(values_kernel, half, offsets, len(blocks...  6.14 us
    pallas_call x5, Pallas kernels, project_keys(): pl.pallas_call(functools.partial(keys_kernel, half, len(blocks)), in_spec...  5.28 us
  transfers between devices with their start and end apart: 26, of which 16 were waited for; matrix products, arithmetic and copies ran while one was open for 0% of the time, Pallas kernels for 30%

profile of v11, /device:TPU:0, one launch (start us, length us, event | category | flops | bytes accessed | tf_op | source)
XLA Modules:
  0.0 90.4 jit_solution(16097583839877614429)
XLA Ops:
  0.0 2.0 %norm_rows.1 = (bf16[1040,128]{1,0:T(8,128)(2,1)}, bf16[1040,128]{1,0:T(8,128)(2,1)}) custom-call(bf16[128,2048]{1,0:T(8,128)(2,1)} %refs_0_.1, f32[1,2048]{1,0:T(1,128)} %bitcast.15, s32[2,128]{1,0:T(2,128)} %bitcast.16), custom_call_target="tpu_custom_call" | custom-call | tf_op jit(solution)/shard_map/norm_rows/pallas_call | solution.py:85
  2.0 3.1 %collective-permute-start = (bf16[1040,128]{1,0:T(8,128)(2,1)}, bf16[1040,128]{1,0:T(8,128)(2,1)S(1)}, u32[]{:S(2)}, u32[]{:S(2)}) collective-permute-start(bf16[1040,128]{1,0:T(8,128)(2,1)} %get-tuple-element.80.top_ref.refs_0_), channel_id=1, source_target_pairs={{0,4},{4,8},{8,12},{12,14},{14,10},{10,6},{6,2},{2,0},{1,5},{5,9},... | collective-permute-start | bytes 798728 | tf_op jit(solution)/shard_map/ppermute | solution.py:455
  5.1 0.0 collective-permute-start.1
  5.1 2.0 %collective-permute-start.3 = (bf16[1040,128]{1,0:T(8,128)(2,1)}, bf16[1040,128]{1,0:T(8,128)(2,1)S(1)}, u32[]{:S(2)}, u32[]{:S(2)}) collective-permute-start(bf16[1040,128]{1,0:T(8,128)(2,1)} %get-tuple-element.80.top_ref.refs_0_), channel_id=1, source_target_pairs={{4,0},{8,4},{12,8},{14,12},{10,14},{6,10},{2,6},{0,2},{5,1},{9,5},... | collective-permute-start | bytes 798728 | tf_op jit(solution)/shard_map/ppermute | solution.py:455
  7.1 0.1 collective-permute-start.2
  7.2 2.2 %copy-done.1 = bf16[2048,1024]{1,0:T(8,128)(2,1)S(1)} copy-done((bf16[2048,1024]{1,0:T(8,128)(2,1)S(1)}, bf16[2048,1024]{1,0:T(8,128)(2,1)}, u32[]{:S(2)}) %copy-start.1) | copy-done | bytes 4194328
  9.4 0.9 %copy-done.6 = bf16[1040,128]{1,0:T(8,128)(2,1)S(1)} copy-done((bf16[1040,128]{1,0:T(8,128)(2,1)S(1)}, bf16[1040,128]{1,0:T(8,128)(2,1)}, u32[]{:S(2)}) %copy-start.6) | copy-done | bytes 266264
  10.3 0.9 %copy-done.8 = bf16[1040,128]{1,0:T(8,128)(2,1)S(1)} copy-done((bf16[1040,128]{1,0:T(8,128)(2,1)S(1)}, bf16[1040,128]{1,0:T(8,128)(2,1)}, u32[]{:S(2)}) %copy-start.8) | copy-done | bytes 266264
  11.3 0.7 project_keys.5
  12.0 0.5 collective-permute-done.refs_0_
  12.5 2.2 %collective-permute-done.1.refs_3_ = bf16[1040,128]{1,0:T(8,128)(2,1)S(1)} collective-permute-done((bf16[1040,128]{1,0:T(8,128)(2,1)}, bf16[1040,128]{1,0:T(8,128)(2,1)S(1)}, u32[]{:S(2)}, u32[]{:S(2)}) %collective-permute-start.1) | collective-permute-done | bytes 266272 | tf_op jit(solution)/shard_map/ppermute | solution.py:455
  14.6 1.6 %collective-permute-start.4 = (bf16[1040,128]{1,0:T(8,128)(2,1)S(1)}, bf16[1040,128]{1,0:T(8,128)(2,1)S(1)}, u32[]{:S(2)}, u32[]{:S(2)}) collective-permute-start(bf16[1040,128]{1,0:T(8,128)(2,1)S(1)} %collective-permute-done.refs_0_), channel_id=1, source_target_pairs={{0,4},{4,8},{8,12},{12,14},{14,10},{10,6},{6,2},{2,0},{1,5},{5,9},... | collective-permute-start | bytes 798728 | tf_op jit(solution)/shard_map/ppermute | solution.py:455
  16.2 0.4 collective-permute-start.5
  16.7 2.2 %copy-done.3 = bf16[2048,1024]{1,0:T(8,128)(2,1)S(1)} copy-done((bf16[2048,1024]{1,0:T(8,128)(2,1)S(1)}, bf16[2048,1024]{1,0:T(8,128)(2,1)}, u32[]{:S(2)}) %copy-start.3) | copy-done | bytes 4194328
  18.9 0.8 project_values.5
  19.7 0.7 collective-permute-done.3.refs_2_
  20.4 1.6 %collective-permute-start.6 = (bf16[1040,128]{1,0:T(8,128)(2,1)S(1)}, bf16[1040,128]{1,0:T(8,128)(2,1)S(1)}, u32[]{:S(2)}, u32[]{:S(2)}) collective-permute-start(bf16[1040,128]{1,0:T(8,128)(2,1)S(1)} %collective-permute-done.2.refs_1_), channel_id=1, source_target_pairs={{0,4},{4,8},{8,12},{12,14},{14,10},{10,6},{6,2},{2,0},{1,5},{5,9},... | collective-permute-start | bytes 798728 | tf_op jit(solution)/shard_map/ppermute | solution.py:455
  21.9 0.4 collective-permute-start.7
  22.4 1.3 %project_keys.6 = (bf16[256,1024]{1,0:T(8,128)(2,1)S(1)}, f32[8,128]{1,0:T(8,128)S(1)}) custom-call(bf16[1040,128]{1,0:T(8,128)(2,1)S(1)} %collective-permute-done.refs_0_, bf16[1040,128]{1,0:T(8,128)(2,1)S(1)} %collective-permute-done.2.refs_1_, bf16[1040,128]{1,0:T(8,128)(2,1)S(1)} %collective-permute-done.3.refs_2_, ...), custom_call_target="tpu_custom_call" | custom-call | tf_op jit(solution)/shard_map/project_keys/pallas_call | solution.py:115
  23.7 0.0 copy-start
  23.7 0.3 collective-permute-done.4.refs_0_
  24.0 2.1 %collective-permute-done.5.refs_3_ = bf16[1040,128]{1,0:T(8,128)(2,1)S(1)} collective-permute-done((bf16[1040,128]{1,0:T(8,128)(2,1)S(1)}, bf16[1040,128]{1,0:T(8,128)(2,1)S(1)}, u32[]{:S(2)}, u32[]{:S(2)}) %collective-permute-start.5) | collective-permute-done | bytes 266272 | tf_op jit(solution)/shard_map/ppermute | solution.py:455
  26.1 1.6 %collective-permute-start.8 = (bf16[1040,128]{1,0:T(8,128)(2,1)S(1)}, bf16[1040,128]{1,0:T(8,128)(2,1)S(1)}, u32[]{:S(2)}, u32[]{:S(2)}) collective-permute-start(bf16[1040,128]{1,0:T(8,128)(2,1)S(1)} %collective-permute-done.4.refs_0_), channel_id=1, source_target_pairs={{0,4},{4,8},{8,12},{12,14},{14,10},{10,6},{6,2},{2,0},{1,5},{5,9},... | collective-permute-start | bytes 798728 | tf_op jit(solution)/shard_map/ppermute | solution.py:455
  27.6 0.4 collective-permute-start.9
  28.1 1.5 %project_values.6 = (bf16[2,256,1024]{2,1,0:T(8,128)(2,1)S(1)}, bf16[2,48,2048]{2,1,0:T(8,128)(2,1)S(1)}, f32[2,48,128]{2,1,0:T(8,128)S(1)}) custom-call(f32[8,128]{1,0:T(8,128)S(1)} %get-tuple-element.89.mark_ref, bf16[256,1024]{1,0:T(8,128)(2,1)S(1)} %get-tuple-element.90.keys_ref, bf16[1040,128]{1,0:T(8,128)(2,1)S(1)} %collective-permute-done.refs_0_, ...), custom_call_target="tpu_custom_call" | custom-call | tf_op jit(solution)/shard_map/project_values/pallas_call | solution.py:160
  29.6 0.1 collective-permute-done.6.refs_1_
  29.7 2.1 %collective-permute-done.7.refs_2_ = bf16[1040,128]{1,0:T(8,128)(2,1)S(1)} collective-permute-done((bf16[1040,128]{1,0:T(8,128)(2,1)S(1)}, bf16[1040,128]{1,0:T(8,128)(2,1)S(1)}, u32[]{:S(2)}, u32[]{:S(2)}) %collective-permute-start.7) | collective-permute-done | bytes 266272 | tf_op jit(solution)/shard_map/ppermute | solution.py:455
  31.8 1.6 %collective-permute-start.10 = (bf16[1040,128]{1,0:T(8,128)(2,1)S(1)}, bf16[1040,128]{1,0:T(8,128)(2,1)S(1)}, u32[]{:S(2)}, u32[]{:S(2)}) collective-permute-start(bf16[1040,128]{1,0:T(8,128)(2,1)S(1)} %collective-permute-done.6.refs_1_), channel_id=1, source_target_pairs={{0,4},{4,8},{8,12},{12,14},{14,10},{10,6},{6,2},{2,0},{1,5},{5,9},... | collective-permute-start | bytes 798728 | tf_op jit(solution)/shard_map/ppermute | solution.py:455
  33.3 0.4 collective-permute-start.11
  33.8 0.8 project_queries.3
  34.6 1.3 %project_keys.7 = (bf16[256,1024]{1,0:T(8,128)(2,1)S(1)}, f32[8,128]{1,0:T(8,128)S(1)}) custom-call(bf16[1040,128]{1,0:T(8,128)(2,1)S(1)} %collective-permute-done.4.refs_0_, bf16[1040,128]{1,0:T(8,128)(2,1)S(1)} %collective-permute-done.6.refs_1_, bf16[1040,128]{1,0:T(8,128)(2,1)S(1)} %collective-permute-done.7.refs_2_, ...), custom_call_target="tpu_custom_call" | custom-call | tf_op jit(solution)/shard_map/project_keys/pallas_call | solution.py:115
  35.9 1.6 %collective-permute-done.9.refs_3_ = bf16[1040,128]{1,0:T(8,128)(2,1)S(1)} collective-permute-done((bf16[1040,128]{1,0:T(8,128)(2,1)S(1)}, bf16[1040,128]{1,0:T(8,128)(2,1)S(1)}, u32[]{:S(2)}, u32[]{:S(2)}) %collective-permute-start.9) | collective-permute-done | bytes 266272 | tf_op jit(solution)/shard_map/ppermute | solution.py:455
  37.5 1.6 %collective-permute-start.13 = (bf16[1040,128]{1,0:T(8,128)(2,1)S(1)}, bf16[1040,128]{1,0:T(8,128)(2,1)S(1)}, u32[]{:S(2)}, u32[]{:S(2)}) collective-permute-start(bf16[1040,128]{1,0:T(8,128)(2,1)S(1)} %collective-permute-done.8.refs_0_), channel_id=1, source_target_pairs={{0,4},{4,8},{8,12},{12,14},{14,10},{10,6},{6,2},{2,0},{1,5},{5,9},... | collective-permute-start | bytes 798728 | tf_op jit(solution)/shard_map/ppermute | solution.py:455
  39.0 0.4 collective-permute-start.14
  39.5 1.5 %project_values.7 = (bf16[2,256,1024]{2,1,0:T(8,128)(2,1)S(1)}, bf16[2,48,2048]{2,1,0:T(8,128)(2,1)S(1)}, f32[2,48,128]{2,1,0:T(8,128)S(1)}) custom-call(f32[8,128]{1,0:T(8,128)S(1)} %get-tuple-element.102.mark_ref, bf16[256,1024]{1,0:T(8,128)(2,1)S(1)} %get-tuple-element.103.keys_ref, bf16[1040,128]{1,0:T(8,128)(2,1)S(1)} %collective-permute-done.4.refs_0_, ...), custom_call_target="tpu_custom_call" | custom-call | tf_op jit(solution)/shard_map/project_values/pallas_call | solution.py:160
  41.0 0.1 collective-permute-done.10.refs_1_
  41.1 2.1 %collective-permute-done.11.refs_2_ = bf16[1040,128]{1,0:T(8,128)(2,1)S(1)} collective-permute-done((bf16[1040,128]{1,0:T(8,128)(2,1)S(1)}, bf16[1040,128]{1,0:T(8,128)(2,1)S(1)}, u32[]{:S(2)}, u32[]{:S(2)}) %collective-permute-start.11) | collective-permute-done | bytes 266272 | tf_op jit(solution)/shard_map/ppermute | solution.py:455
  43.2 1.3 %project_keys.8 = (bf16[256,1024]{1,0:T(8,128)(2,1)S(1)}, f32[8,128]{1,0:T(8,128)S(1)}) custom-call(bf16[1040,128]{1,0:T(8,128)(2,1)S(1)} %collective-permute-done.8.refs_0_, bf16[1040,128]{1,0:T(8,128)(2,1)S(1)} %collective-permute-done.10.refs_1_, bf16[1040,128]{1,0:T(8,128)(2,1)S(1)} %collective-permute-done.11.refs_2_, ...), custom_call_target="tpu_custom_call" | custom-call | tf_op jit(solution)/shard_map/project_keys/pallas_call | solution.py:115
  44.5 1.5 %project_values.8 = (bf16[2,256,1024]{2,1,0:T(8,128)(2,1)S(1)}, bf16[2,48,2048]{2,1,0:T(8,128)(2,1)S(1)}, f32[2,48,128]{2,1,0:T(8,128)S(1)}) custom-call(f32[8,128]{1,0:T(8,128)S(1)} %get-tuple-element.108.mark_ref, bf16[256,1024]{1,0:T(8,128)(2,1)S(1)} %get-tuple-element.109.keys_ref, bf16[1040,128]{1,0:T(8,128)(2,1)S(1)} %collective-permute-done.8.refs_0_, ...), custom_call_target="tpu_custom_call" | custom-call | tf_op jit(solution)/shard_map/project_values/pallas_call | solution.py:160
  46.0 1.0 %project_queries.4 = (bf16[2,48,1024]{2,1,0:T(8,128)(2,1)S(1)}, bf16[2,48,1024]{2,1,0:T(8,128)(2,1)S(1)}) custom-call(bf16[2,48,2048]{2,1,0:T(8,128)(2,1)S(1)} %get-tuple-element.111.refs_0_, bf16[2,48,2048]{2,1,0:T(8,128)(2,1)S(1)} %get-tuple-element.112.refs_1_, bf16[2048,1024]{1,0:T(8,128)(2,1)S(1)} %bitcast.12, bf16[1024,2048]{1,0:T(8,128)(2,1)S(1)} %bitcast.6), custom_call_target="tpu_custom_call" | custom-call | tf_op jit(solution)/shard_map/project_queries/pallas_call | solution.py:189
  47.0 0.4 collective-permute-done.14.refs_1_
  47.4 0.2 collective-permute-start.17
  47.6 0.7 project_keys.9
  48.3 0.8 project_values.9
  49.1 0.4 collective-permute-start.18
  49.6 0.8 project_queries.5.refs_14_
  50.4 0.0 collective-permute-done.15.refs_6_
  50.4 0.7 collective-permute-done.18.refs_9_
  51.1 0.7 arrange.1
  51.8 5.1 %attend.3 = (bf16[40,2048]{1,0:T(8,128)(2,1)S(1)}, bf16[40,2048]{1,0:T(8,128)(2,1)S(1)}) custom-call(bf16[2,16,128,1024]{3,2,1,0:T(8,128)(2,1)S(1)} %get-tuple-element.133.panel_ref, bf16[8,48,1024]{2,1,0:T(8,128)(2,1)S(1)} %get-tuple-element.134.queries_ref, f32[8,48,128]{2,1,0:T(8,128)S(1)} %get-tuple-element.141.places_ref, bf16[1024,2048]{1,0:T(8,128)(2,1)S(1)} %bitcast.8), custom_call_target="tpu_custom_call" | custom-call | flops 1207959552 | bytes 8388608 | tf_op jit(solution)/shard_map/attend/pallas_call | solution.py:327
  56.9 0.9 collective-permute-start.19
  57.8 1.8 %collective-permute-start.23 = (bf16[40,2048]{1,0:T(8,128)(2,1)S(1)}, bf16[40,2048]{1,0:T(8,128)(2,1)S(1)}, u32[]{:S(2)}, u32[]{:S(2)}) collective-permute-start(bf16[40,2048]{1,0:T(8,128)(2,1)S(1)} %get-tuple-element.152), channel_id=1, source_target_pairs={{0,10},{2,8},{4,14},{6,12},{8,2},{10,0},{12,6},{14,4},{1,11},{3,9}... | collective-permute-start | bytes 491528 | tf_op jit(solution)/shard_map/ppermute | solution.py:498
  59.6 6.0 %attend.4 = (bf16[40,2048]{1,0:T(8,128)(2,1)S(1)}, bf16[40,2048]{1,0:T(8,128)(2,1)S(1)}) custom-call(bf16[2,16,128,1024]{3,2,1,0:T(8,128)(2,1)S(1)} %get-tuple-element.133.panel_ref, bf16[8,48,1024]{2,1,0:T(8,128)(2,1)S(1)} %get-tuple-element.134.queries_ref, f32[8,48,128]{2,1,0:T(8,128)S(1)} %get-tuple-element.141.places_ref, bf16[1024,2048]{1,0:T(8,128)(2,1)S(1)} %bitcast.9), custom_call_target="tpu_custom_call" | custom-call | flops 1207959552 | bytes 8388608 | tf_op jit(solution)/shard_map/attend/pallas_call | solution.py:327
  65.7 0.1 collective-permute-start.24
  65.7 5.0 %collective-permute-start.25 = (bf16[40,2048]{1,0:T(8,128)(2,1)S(1)}, bf16[40,2048]{1,0:T(8,128)(2,1)S(1)}, u32[]{:S(2)}, u32[]{:S(2)}) collective-permute-start(bf16[40,2048]{1,0:T(8,128)(2,1)S(1)} %get-tuple-element.154), channel_id=1, source_target_pairs={{0,14},{2,12},{4,10},{6,8},{8,6},{10,4},{12,2},{14,0},{1,15},{3,13... | collective-permute-start | bytes 491528 | tf_op jit(solution)/shard_map/ppermute | solution.py:498
  70.7 6.5 %attend.5 = (bf16[40,2048]{1,0:T(8,128)(2,1)S(1)}, bf16[40,2048]{1,0:T(8,128)(2,1)S(1)}, bf16[40,2048]{1,0:T(8,128)(2,1)S(1)}, bf16[40,2048]{1,0:T(8,128)(2,1)S(1)}) custom-call(bf16[2,16,128,1024]{3,2,1,0:T(8,128)(2,1)S(1)} %get-tuple-element.133.panel_ref, bf16[8,48,1024]{2,1,0:T(8,128)(2,1)S(1)} %get-tuple-element.134.queries_ref, ...), custom_call_target="tpu_custom_call" | custom-call | flops 2415919104 | bytes 8388608 | tf_op jit(solution)/shard_map/attend/pallas_call | solution.py:327
  77.2 1.7 %collective-permute-done.19.refs_4_ = bf16[40,2048]{1,0:T(8,128)(2,1)S(1)} collective-permute-done((bf16[40,2048]{1,0:T(8,128)(2,1)S(1)}, bf16[40,2048]{1,0:T(8,128)(2,1)S(1)}, u32[]{:S(2)}, u32[]{:S(2)}) %collective-permute-start.19) | collective-permute-done | bytes 163872 | tf_op jit(solution)/shard_map/ppermute | solution.py:498
  79.0 1.7 %collective-permute-start.21 = (bf16[40,2048]{1,0:T(8,128)(2,1)S(1)}, bf16[40,2048]{1,0:T(8,128)(2,1)S(1)}, u32[]{:S(2)}, u32[]{:S(2)}) collective-permute-start(bf16[40,2048]{1,0:T(8,128)(2,1)S(1)} %get-tuple-element.149), channel_id=1, source_target_pairs={{0,4},{2,6},{4,0},{6,2},{8,12},{10,14},{12,8},{14,10},{1,5},{3,7},... | collective-permute-start | bytes 491528 | tf_op jit(solution)/shard_map/ppermute | solution.py:498
  80.7 1.5 %collective-permute-done.23.refs_5_ = bf16[40,2048]{1,0:T(8,128)(2,1)S(1)} collective-permute-done((bf16[40,2048]{1,0:T(8,128)(2,1)S(1)}, bf16[40,2048]{1,0:T(8,128)(2,1)S(1)}, u32[]{:S(2)}, u32[]{:S(2)}) %collective-permute-start.23) | collective-permute-done | bytes 163872 | tf_op jit(solution)/shard_map/ppermute | solution.py:498
  82.2 1.8 %collective-permute-start.22 = (bf16[40,2048]{1,0:T(8,128)(2,1)S(1)}, bf16[40,2048]{1,0:T(8,128)(2,1)S(1)}, u32[]{:S(2)}, u32[]{:S(2)}) collective-permute-start(bf16[40,2048]{1,0:T(8,128)(2,1)S(1)} %get-tuple-element.150), channel_id=1, source_target_pairs={{0,2},{2,0},{4,6},{6,4},{8,10},{10,8},{12,14},{14,12},{1,3},{3,1},... | collective-permute-start | bytes 491528 | tf_op jit(solution)/shard_map/ppermute | solution.py:498
  84.0 0.5 gate_mix.1.mix_ref
  84.5 2.5 %collective-permute-done.20.refs_1_ = bf16[40,2048]{1,0:T(8,128)(2,1)S(1)} collective-permute-done((bf16[40,2048]{1,0:T(8,128)(2,1)S(1)}, bf16[40,2048]{1,0:T(8,128)(2,1)S(1)}, u32[]{:S(2)}, u32[]{:S(2)}) %collective-permute-start.20) | collective-permute-done | bytes 163872 | tf_op jit(solution)/shard_map/ppermute | solution.py:498
  87.0 1.9 %collective-permute-done.21.refs_2_ = bf16[40,2048]{1,0:T(8,128)(2,1)S(1)} collective-permute-done((bf16[40,2048]{1,0:T(8,128)(2,1)S(1)}, bf16[40,2048]{1,0:T(8,128)(2,1)S(1)}, u32[]{:S(2)}, u32[]{:S(2)}) %collective-permute-start.21) | collective-permute-done | bytes 163872 | tf_op jit(solution)/shard_map/ppermute | solution.py:498
  88.9 1.5 %combine.1 = bf16[128,2048]{1,0:T(8,128)(2,1)} custom-call(bf16[256,384]{1,0:T(8,128)(2,1)S(1)} %gate_mix.1.mix_ref, bf16[40,2048]{1,0:T(8,128)(2,1)S(1)} %get-tuple-element.147.refs_0_, bf16[40,2048]{1,0:T(8,128)(2,1)S(1)} %collective-permute-done.20.refs_1_, bf16[40,2048]{1,0:T(8,128)(2,1)S(1)} %collective-permute-done.21.refs_2_, ...), custom_call_target="tpu_custom_call" | custom-call | tf_op jit(solution)/shard_map/combine/pallas_call | solution.py:419
  (30 shorter events, 0.1 us)
Async XLA Ops:
  2.0 10.5 %collective-permute-start = (bf16[1040,128]{1,0:T(8,128)(2,1)}, bf16[1040,128]{1,0:T(8,128)(2,1)S(1)}, u32[]{:S(2)}, u32[]{:S(2)}) collective-permute-start(bf16[1040,128]{1,0:T(8,128)(2,1)} %get-tuple-element.80.top_ref.refs_0_), channel_id=1, source_target_pairs={{0,4},{4,8},{8,12},{12,14},{14,10},{10,6},{6,2},{2,0},{1,5},{5,9},... | collective-permute-start | bytes 798728 | tf_op jit(solution)/shard_map/ppermute | solution.py:455
  5.1 9.5 %collective-permute-start.1 = (bf16[1040,128]{1,0:T(8,128)(2,1)}, bf16[1040,128]{1,0:T(8,128)(2,1)S(1)}, u32[]{:S(2)}, u32[]{:S(2)}) collective-permute-start(bf16[1040,128]{1,0:T(8,128)(2,1)} %get-tuple-element.81.bottom_ref.refs_1_), channel_id=1, source_target_pairs={{4,0},{8,4},{12,8},{14,12},{10,14},{6,10},{2,6},{0,2},{5,1},{9,5},... | collective-permute-start | bytes 798728 | tf_op jit(solution)/shard_map/ppermute | solution.py:455
  5.1 15.2 %collective-permute-start.3 = (bf16[1040,128]{1,0:T(8,128)(2,1)}, bf16[1040,128]{1,0:T(8,128)(2,1)S(1)}, u32[]{:S(2)}, u32[]{:S(2)}) collective-permute-start(bf16[1040,128]{1,0:T(8,128)(2,1)} %get-tuple-element.80.top_ref.refs_0_), channel_id=1, source_target_pairs={{4,0},{8,4},{12,8},{14,12},{10,14},{6,10},{2,6},{0,2},{5,1},{9,5},... | collective-permute-start | bytes 798728 | tf_op jit(solution)/shard_map/ppermute | solution.py:455
  7.1 13.3 %collective-permute-start.2 = (bf16[1040,128]{1,0:T(8,128)(2,1)}, bf16[1040,128]{1,0:T(8,128)(2,1)S(1)}, u32[]{:S(2)}, u32[]{:S(2)}) collective-permute-start(bf16[1040,128]{1,0:T(8,128)(2,1)} %get-tuple-element.81.bottom_ref.refs_1_), channel_id=1, source_target_pairs={{0,4},{4,8},{8,12},{12,14},{14,10},{10,6},{6,2},{2,0},{1,5},{5,9},... | collective-permute-start | bytes 798728 | tf_op jit(solution)/shard_map/ppermute | solution.py:455
  7.2 2.2 %copy-start.1 = (bf16[2048,1024]{1,0:T(8,128)(2,1)S(1)}, bf16[2048,1024]{1,0:T(8,128)(2,1)}, u32[]{:S(2)}) copy-start(bf16[2048,1024]{1,0:T(8,128)(2,1)} %refs_2_.6) | copy-start | bytes 12582916
  9.4 1.0 %copy-start.6 = (bf16[1040,128]{1,0:T(8,128)(2,1)S(1)}, bf16[1040,128]{1,0:T(8,128)(2,1)}, u32[]{:S(2)}) copy-start(bf16[1040,128]{1,0:T(8,128)(2,1)} %get-tuple-element.80.top_ref.refs_0_) | copy-start | bytes 798724
  10.3 1.0 %copy-start.8 = (bf16[1040,128]{1,0:T(8,128)(2,1)S(1)}, bf16[1040,128]{1,0:T(8,128)(2,1)}, u32[]{:S(2)}) copy-start(bf16[1040,128]{1,0:T(8,128)(2,1)} %get-tuple-element.81.bottom_ref.refs_1_) | copy-start | bytes 798724
  11.3 11.1 %copy-start.2 = (bf16[2048,1024]{1,0:T(8,128)(2,1)S(1)}, bf16[2048,1024]{1,0:T(8,128)(2,1)}, u32[]{:S(2)}) copy-start(bf16[2048,1024]{1,0:T(8,128)(2,1)} %refs_2_.6) | copy-start | bytes 12582916
  14.6 9.3 %collective-permute-start.4 = (bf16[1040,128]{1,0:T(8,128)(2,1)S(1)}, bf16[1040,128]{1,0:T(8,128)(2,1)S(1)}, u32[]{:S(2)}, u32[]{:S(2)}) collective-permute-start(bf16[1040,128]{1,0:T(8,128)(2,1)S(1)} %collective-permute-done.refs_0_), channel_id=1, source_target_pairs={{0,4},{4,8},{8,12},{12,14},{14,10},{10,6},{6,2},{2,0},{1,5},{5,9},... | collective-permute-start | bytes 798728 | tf_op jit(solution)/shard_map/ppermute | solution.py:455
  16.2 9.8 %collective-permute-start.5 = (bf16[1040,128]{1,0:T(8,128)(2,1)S(1)}, bf16[1040,128]{1,0:T(8,128)(2,1)S(1)}, u32[]{:S(2)}, u32[]{:S(2)}) collective-permute-start(bf16[1040,128]{1,0:T(8,128)(2,1)S(1)} %collective-permute-done.1.refs_3_), channel_id=1, source_target_pairs={{4,0},{8,4},{12,8},{14,12},{10,14},{6,10},{2,6},{0,2},{5,1},{9,5},... | collective-permute-start | bytes 798728 | tf_op jit(solution)/shard_map/ppermute | solution.py:455
  16.7 2.2 %copy-start.3 = (bf16[2048,1024]{1,0:T(8,128)(2,1)S(1)}, bf16[2048,1024]{1,0:T(8,128)(2,1)}, u32[]{:S(2)}) copy-start(bf16[2048,1024]{1,0:T(8,128)(2,1)} %refs_2_.7) | copy-start | bytes 12582916
  18.9 9.2 %copy-start.4 = (bf16[2048,1024]{1,0:T(8,128)(2,1)S(1)}, bf16[2048,1024]{1,0:T(8,128)(2,1)}, u32[]{:S(2)}) copy-start(bf16[2048,1024]{1,0:T(8,128)(2,1)} %refs_2_.7) | copy-start | bytes 12582916
  20.4 9.3 %collective-permute-start.6 = (bf16[1040,128]{1,0:T(8,128)(2,1)S(1)}, bf16[1040,128]{1,0:T(8,128)(2,1)S(1)}, u32[]{:S(2)}, u32[]{:S(2)}) collective-permute-start(bf16[1040,128]{1,0:T(8,128)(2,1)S(1)} %collective-permute-done.2.refs_1_), channel_id=1, source_target_pairs={{0,4},{4,8},{8,12},{12,14},{14,10},{10,6},{6,2},{2,0},{1,5},{5,9},... | collective-permute-start | bytes 798728 | tf_op jit(solution)/shard_map/ppermute | solution.py:455
  21.9 9.8 %collective-permute-start.7 = (bf16[1040,128]{1,0:T(8,128)(2,1)S(1)}, bf16[1040,128]{1,0:T(8,128)(2,1)S(1)}, u32[]{:S(2)}, u32[]{:S(2)}) collective-permute-start(bf16[1040,128]{1,0:T(8,128)(2,1)S(1)} %collective-permute-done.3.refs_2_), channel_id=1, source_target_pairs={{4,0},{8,4},{12,8},{14,12},{10,14},{6,10},{2,6},{0,2},{5,1},{9,5},... | collective-permute-start | bytes 798728 | tf_op jit(solution)/shard_map/ppermute | solution.py:455
  22.4 11.4 %copy-start.5 = (bf16[1,2048,1024]{2,1,0:T(8,128)(2,1)S(1)}, bf16[1,2048,1024]{2,1,0:T(8,128)(2,1)}, u32[]{:S(2)}) copy-start(bf16[1,2048,1024]{2,1,0:T(8,128)(2,1)} %param.14) | copy-start | bytes 12582916
  23.7 10.1 %copy-start = (bf16[1,1024,2048]{2,1,0:T(8,128)(2,1)S(1)}, bf16[1,1024,2048]{2,1,0:T(8,128)(2,1)}, u32[]{:S(2)}) copy-start(bf16[1,1024,2048]{2,1,0:T(8,128)(2,1)} %param.15) | copy-start | bytes 12582916
  26.1 9.8 %collective-permute-start.8 = (bf16[1040,128]{1,0:T(8,128)(2,1)S(1)}, bf16[1040,128]{1,0:T(8,128)(2,1)S(1)}, u32[]{:S(2)}, u32[]{:S(2)}) collective-permute-start(bf16[1040,128]{1,0:T(8,128)(2,1)S(1)} %collective-permute-done.4.refs_0_), channel_id=1, source_target_pairs={{0,4},{4,8},{8,12},{12,14},{14,10},{10,6},{6,2},{2,0},{1,5},{5,9},... | collective-permute-start | bytes 798728 | tf_op jit(solution)/shard_map/ppermute | solution.py:455
  27.6 9.8 %collective-permute-start.9 = (bf16[1040,128]{1,0:T(8,128)(2,1)S(1)}, bf16[1040,128]{1,0:T(8,128)(2,1)S(1)}, u32[]{:S(2)}, u32[]{:S(2)}) collective-permute-start(bf16[1040,128]{1,0:T(8,128)(2,1)S(1)} %collective-permute-done.5.refs_3_), channel_id=1, source_target_pairs={{4,0},{8,4},{12,8},{14,12},{10,14},{6,10},{2,6},{0,2},{5,1},{9,5},... | collective-permute-start | bytes 798728 | tf_op jit(solution)/shard_map/ppermute | solution.py:455
  28.1 18.9 %collective-permute-start.12 = (bf16[2,128,1024]{2,1,0:T(8,128)(2,1)S(1)}, bf16[2,128,1024]{2,1,0:T(8,128)(2,1)S(1)}, u32[]{:S(2)}, u32[]{:S(2)}) collective-permute-start(bf16[2,128,1024]{2,1,0:T(8,128)(2,1)S(1)} %get-tuple-element.85.refs_0_), channel_id=1, source_target_pairs={{0,1},{1,0},{2,3},{3,2},{4,5},{5,4},{6,7},{7,6},{8,9},{9,8},{10,11... | collective-permute-start | bytes 1572872 | tf_op jit(solution)/shard_map/ppermute | solution.py:458
  31.8 9.3 %collective-permute-start.10 = (bf16[1040,128]{1,0:T(8,128)(2,1)S(1)}, bf16[1040,128]{1,0:T(8,128)(2,1)S(1)}, u32[]{:S(2)}, u32[]{:S(2)}) collective-permute-start(bf16[1040,128]{1,0:T(8,128)(2,1)S(1)} %collective-permute-done.6.refs_1_), channel_id=1, source_target_pairs={{0,4},{4,8},{8,12},{12,14},{14,10},{10,6},{6,2},{2,0},{1,5},{5,9},... | collective-permute-start | bytes 798728 | tf_op jit(solution)/shard_map/ppermute | solution.py:455
  33.3 9.8 %collective-permute-start.11 = (bf16[1040,128]{1,0:T(8,128)(2,1)S(1)}, bf16[1040,128]{1,0:T(8,128)(2,1)S(1)}, u32[]{:S(2)}, u32[]{:S(2)}) collective-permute-start(bf16[1040,128]{1,0:T(8,128)(2,1)S(1)} %collective-permute-done.7.refs_2_), channel_id=1, source_target_pairs={{4,0},{8,4},{12,8},{14,12},{10,14},{6,10},{2,6},{0,2},{5,1},{9,5},... | collective-permute-start | bytes 798728 | tf_op jit(solution)/shard_map/ppermute | solution.py:455
  37.5 9.5 %collective-permute-start.13 = (bf16[1040,128]{1,0:T(8,128)(2,1)S(1)}, bf16[1040,128]{1,0:T(8,128)(2,1)S(1)}, u32[]{:S(2)}, u32[]{:S(2)}) collective-permute-start(bf16[1040,128]{1,0:T(8,128)(2,1)S(1)} %collective-permute-done.8.refs_0_), channel_id=1, source_target_pairs={{0,4},{4,8},{8,12},{12,14},{14,10},{10,6},{6,2},{2,0},{1,5},{5,9},... | collective-permute-start | bytes 798728 | tf_op jit(solution)/shard_map/ppermute | solution.py:455
  39.0 8.4 %collective-permute-start.14 = (bf16[1040,128]{1,0:T(8,128)(2,1)S(1)}, bf16[1040,128]{1,0:T(8,128)(2,1)S(1)}, u32[]{:S(2)}, u32[]{:S(2)}) collective-permute-start(bf16[1040,128]{1,0:T(8,128)(2,1)S(1)} %collective-permute-done.9.refs_3_), channel_id=1, source_target_pairs={{4,0},{8,4},{12,8},{14,12},{10,14},{6,10},{2,6},{0,2},{5,1},{9,5},... | collective-permute-start | bytes 798728 | tf_op jit(solution)/shard_map/ppermute | solution.py:455
  41.1 9.3 %collective-permute-start.15 = (bf16[2,256,1024]{2,1,0:T(8,128)(2,1)S(1)}, bf16[2,256,1024]{2,1,0:T(8,128)(2,1)S(1)}, u32[]{:S(2)}, u32[]{:S(2)}) collective-permute-start(bf16[2,256,1024]{2,1,0:T(8,128)(2,1)S(1)} %get-tuple-element.91.refs_1_), channel_id=1, source_target_pairs={{0,1},{1,0},{2,3},{3,2},{4,5},{5,4},{6,7},{7,6},{8,9},{9,8},{10,11... | collective-permute-start | bytes 3145736 | tf_op jit(solution)/shard_map/ppermute | solution.py:458
  43.2 7.9 %collective-permute-start.16 = (bf16[2,256,1024]{2,1,0:T(8,128)(2,1)S(1)}, bf16[2,256,1024]{2,1,0:T(8,128)(2,1)S(1)}, u32[]{:S(2)}, u32[]{:S(2)}) collective-permute-start(bf16[2,256,1024]{2,1,0:T(8,128)(2,1)S(1)} %get-tuple-element.104.refs_2_), channel_id=1, source_target_pairs={{0,1},{1,0},{2,3},{3,2},{4,5},{5,4},{6,7},{7,6},{8,9},{9,8},{10,11... | collective-permute-start | bytes 3145736 | tf_op jit(solution)/shard_map/ppermute | solution.py:458
  47.4 3.7 %collective-permute-start.17 = (bf16[2,256,1024]{2,1,0:T(8,128)(2,1)S(1)}, bf16[2,256,1024]{2,1,0:T(8,128)(2,1)S(1)}, u32[]{:S(2)}, u32[]{:S(2)}) collective-permute-start(bf16[2,256,1024]{2,1,0:T(8,128)(2,1)S(1)} %get-tuple-element.116.refs_3_), channel_id=1, source_target_pairs={{0,1},{1,0},{2,3},{3,2},{4,5},{5,4},{6,7},{7,6},{8,9},{9,8},{10,11... | collective-permute-start | bytes 3145736 | tf_op jit(solution)/shard_map/ppermute | solution.py:458
  49.1 2.0 %collective-permute-start.18 = (bf16[2,128,1024]{2,1,0:T(8,128)(2,1)S(1)}, bf16[2,128,1024]{2,1,0:T(8,128)(2,1)S(1)}, u32[]{:S(2)}, u32[]{:S(2)}) collective-permute-start(bf16[2,128,1024]{2,1,0:T(8,128)(2,1)S(1)} %get-tuple-element.121.refs_4_), channel_id=1, source_target_pairs={{0,1},{1,0},{2,3},{3,2},{4,5},{5,4},{6,7},{7,6},{8,9},{9,8},{10,11... | collective-permute-start | bytes 1572872 | tf_op jit(solution)/shard_map/ppermute | solution.py:458
  56.9 22.1 %collective-permute-start.19 = (bf16[40,2048]{1,0:T(8,128)(2,1)S(1)}, bf16[40,2048]{1,0:T(8,128)(2,1)S(1)}, u32[]{:S(2)}, u32[]{:S(2)}) collective-permute-start(bf16[40,2048]{1,0:T(8,128)(2,1)S(1)} %get-tuple-element.146), channel_id=1, source_target_pairs={{0,8},{2,10},{4,12},{6,14},{8,0},{10,2},{12,4},{14,6},{1,9},{3,11}... | collective-permute-start | bytes 491528 | tf_op jit(solution)/shard_map/ppermute | solution.py:498
  57.8 24.4 %collective-permute-start.23 = (bf16[40,2048]{1,0:T(8,128)(2,1)S(1)}, bf16[40,2048]{1,0:T(8,128)(2,1)S(1)}, u32[]{:S(2)}, u32[]{:S(2)}) collective-permute-start(bf16[40,2048]{1,0:T(8,128)(2,1)S(1)} %get-tuple-element.152), channel_id=1, source_target_pairs={{0,10},{2,8},{4,14},{6,12},{8,2},{10,0},{12,6},{14,4},{1,11},{3,9}... | collective-permute-start | bytes 491528 | tf_op jit(solution)/shard_map/ppermute | solution.py:498
  65.6 18.4 %copy-start.7 = (bf16[1040,128]{1,0:T(8,128)(2,1)S(1)}, bf16[1040,128]{1,0:T(8,128)(2,1)}, u32[]{:S(2)}) copy-start(bf16[1040,128]{1,0:T(8,128)(2,1)} %get-tuple-element.80.top_ref.refs_0_) | copy-start | bytes 798724
  65.6 18.4 %copy-start.9 = (bf16[1040,128]{1,0:T(8,128)(2,1)S(1)}, bf16[1040,128]{1,0:T(8,128)(2,1)}, u32[]{:S(2)}) copy-start(bf16[1040,128]{1,0:T(8,128)(2,1)} %get-tuple-element.81.bottom_ref.refs_1_) | copy-start | bytes 798724
  65.6 18.3 %copy-start.10 = (f32[2048,8]{0,1:T(8,128)S(1)}, f32[2048,8]{0,1:T(8,128)}, u32[]{:S(2)}) copy-start(f32[2048,8]{0,1:T(8,128)} %param.10) | copy-start | bytes 196612
  65.7 18.8 %collective-permute-start.24 = (bf16[40,2048]{1,0:T(8,128)(2,1)S(1)}, bf16[40,2048]{1,0:T(8,128)(2,1)S(1)}, u32[]{:S(2)}, u32[]{:S(2)}) collective-permute-start(bf16[40,2048]{1,0:T(8,128)(2,1)S(1)} %get-tuple-element.153), channel_id=1, source_target_pairs={{0,12},{2,14},{4,8},{6,10},{8,4},{10,6},{12,0},{14,2},{1,13},{3,15... | collective-permute-start | bytes 491528 | tf_op jit(solution)/shard_map/ppermute | solution.py:498
  65.7 18.7 %collective-permute-start.25 = (bf16[40,2048]{1,0:T(8,128)(2,1)S(1)}, bf16[40,2048]{1,0:T(8,128)(2,1)S(1)}, u32[]{:S(2)}, u32[]{:S(2)}) collective-permute-start(bf16[40,2048]{1,0:T(8,128)(2,1)S(1)} %get-tuple-element.154), channel_id=1, source_target_pairs={{0,14},{2,12},{4,10},{6,8},{8,6},{10,4},{12,2},{14,0},{1,15},{3,13... | collective-permute-start | bytes 491528 | tf_op jit(solution)/shard_map/ppermute | solution.py:498
  79.0 8.0 %collective-permute-start.20 = (bf16[40,2048]{1,0:T(8,128)(2,1)S(1)}, bf16[40,2048]{1,0:T(8,128)(2,1)S(1)}, u32[]{:S(2)}, u32[]{:S(2)}) collective-permute-start(bf16[40,2048]{1,0:T(8,128)(2,1)S(1)} %get-tuple-element.148), channel_id=1, source_target_pairs={{0,6},{2,4},{4,2},{6,0},{8,14},{10,12},{12,10},{14,8},{1,7},{3,5},... | collective-permute-start | bytes 491528 | tf_op jit(solution)/shard_map/ppermute | solution.py:498
  79.0 9.9 %collective-permute-start.21 = (bf16[40,2048]{1,0:T(8,128)(2,1)S(1)}, bf16[40,2048]{1,0:T(8,128)(2,1)S(1)}, u32[]{:S(2)}, u32[]{:S(2)}) collective-permute-start(bf16[40,2048]{1,0:T(8,128)(2,1)S(1)} %get-tuple-element.149), channel_id=1, source_target_pairs={{0,4},{2,6},{4,0},{6,2},{8,12},{10,14},{12,8},{14,10},{1,5},{3,7},... | collective-permute-start | bytes 491528 | tf_op jit(solution)/shard_map/ppermute | solution.py:498
  82.2 6.7 %collective-permute-start.22 = (bf16[40,2048]{1,0:T(8,128)(2,1)S(1)}, bf16[40,2048]{1,0:T(8,128)(2,1)S(1)}, u32[]{:S(2)}, u32[]{:S(2)}) collective-permute-start(bf16[40,2048]{1,0:T(8,128)(2,1)S(1)} %get-tuple-element.150), channel_id=1, source_target_pairs={{0,2},{2,0},{4,6},{6,4},{8,10},{10,8},{12,14},{14,12},{1,3},{3,1},... | collective-permute-start | bytes 491528 | tf_op jit(solution)/shard_map/ppermute | solution.py:498
